TPU v7x, 32 devices: a whole 2x2x4 slice. The times are simulated.
32 devices in a mesh: rows: 16 (over z, y, x), cols: 2 (over core).
Axes of the slice: x: 2, y: 2, z: 4, core: 2. Of those that a mesh axis runs over, the one named last changes fastest.
Arguments:
- descriptors: bfloat16 [51200, 1024], P('rows', 'cols'), may hold values from -6 to 6
- sparse_points: bfloat16 [4096, 1024], P('cols'), may hold values from -6 to 6
- block_weights: bfloat16 [400], P('rows'), may hold values from 0.29882812 to 3
- block_counts: int32 [16], replicated, may hold values from 1 to 25, as said below
- destinations: int32 [16, 25], replicated, may hold values from 0 to 15, as said below
Outputs:
- projected: float32 [256, 4096], P(None, 'cols')
- remainder: bfloat16 [26624, 4096], P('rows', 'cols')
Inputs may be any that keep to these rules, and one draw needn't show every extreme that they name: Live blocks of owner s are slots 0 to block_counts[s] - 1; the counts sum to 208, and some owner holds 25. `destinations`: entries of live slots name the row owner of the block; every row owner receives exactly 13 live blocks, no owner sends more than 2 live block to one row owner, and entries of slots that are not live are not used.
All inputs are finite; a program needn't handle non-finite values.
Results may differ from a plain program's by a relative error of at most 0.0055.
Values may be sent and summed in bfloat16 or wider, within the bound.
No kernel may reach another device: no remote copies, remote signals or barrier semaphores. Data moves between devices by JAX's collectives and lax.ppermute only.
A program may use at most 128 MiB of HBM per device.

v0:
```python
import math

import jax
import jax.numpy as jnp
from jax import lax
from jax.sharding import PartitionSpec as P

PANEL = 256
BLK = 128
DST_BLK = 13


EPSILON = 1e-06


def broadcast(value, axis, source):
    kept = jnp.where(lax.axis_index(axis) == source, value, 0).astype(value.dtype)
    return lax.psum(kept, axis)


def build_kernel(block_rows, block_wts, sparse_points, sparse_sq):
    block_total = block_rows.shape[0]
    row_count = block_rows.shape[1]
    full_rows = lax.all_gather(block_rows, "cols", axis=2, tiled=True)
    width_all = full_rows.shape[2]
    flat_rows = full_rows.reshape(block_total * row_count, width_all)
    inner = lax.dot_general(
        flat_rows, sparse_points, (((1,), (1,)), ((), ())), preferred_element_type=jnp.float32
    )
    row_sq = (
        jnp.einsum("rf,rf->r", flat_rows, flat_rows, preferred_element_type=jnp.float32) / width_all
        + EPSILON
    )
    weight_rows = jnp.repeat(block_wts.astype(jnp.float32), row_count)
    values = (
        weight_rows[:, None] * inner * inner / (width_all * row_sq[:, None] * sparse_sq[None, :])
    )
    return values.astype(jnp.bfloat16)


def on_device(descriptors, sparse_points, block_weights, block_counts, destinations):
    owners = lax.axis_size("rows")
    self_index = lax.axis_index("rows")
    slot_total = block_weights.shape[0]
    per_pair = -(-slot_total // owners)
    feat_local = descriptors.shape[1]
    col_local = sparse_points.shape[0]
    sparse_sq = (
        jnp.einsum("mf,mf->m", sparse_points, sparse_points, preferred_element_type=jnp.float32)
        / sparse_points.shape[1]
        + EPSILON
    )
    slot_ids = jnp.arange(slot_total, dtype=jnp.int32)
    live_all = slot_ids[None, :] < block_counts[:, None]
    same_dest = destinations[:, :, None] == destinations[:, None, :]
    earlier = slot_ids[None, :] < slot_ids[:, None]
    rank_all = jnp.sum(
        (same_dest & live_all[:, None, :] & earlier[None, :, :]).astype(jnp.int32), axis=2
    )
    my_dest = lax.dynamic_index_in_dim(destinations, self_index, 0, keepdims=False)
    my_live = lax.dynamic_index_in_dim(live_all, self_index, 0, keepdims=False)
    my_rank = lax.dynamic_index_in_dim(rank_all, self_index, 0, keepdims=False)
    target = jnp.arange(owners, dtype=jnp.int32)
    pair_ids = jnp.arange(per_pair, dtype=jnp.int32)
    matches = (
        my_live[None, None, :]
        & (my_dest[None, None, :] == target[:, None, None])
        & (my_rank[None, None, :] == pair_ids[None, :, None])
    )
    is_valid = jnp.any(matches, axis=2)
    source_index = jnp.sum(jnp.where(matches, slot_ids[None, None, :], 0), axis=2)
    toward_self = live_all & (destinations == self_index)
    arriving = jnp.sum(toward_self.astype(jnp.int32), axis=1)
    arrive_live = (pair_ids[None, :] < arriving[:, None]).reshape(owners * per_pair)
    sort_keys = jnp.where(
        arrive_live, jnp.arange(owners * per_pair, dtype=jnp.int32), owners * per_pair
    )
    positions = jnp.sort(sort_keys)[:DST_BLK]
    desc_blocks = descriptors.reshape(slot_total, BLK, feat_local)
    src_kernel = build_kernel(desc_blocks, block_weights, sparse_points, sparse_sq).reshape(
        slot_total, BLK, col_local
    )
    outgoing = jnp.where(
        is_valid[:, :, None, None], src_kernel[source_index], jnp.zeros((), jnp.bfloat16)
    )
    received = lax.all_to_all(outgoing, "rows", split_axis=0, concat_axis=0, tiled=True)
    local_kernel = received.reshape(owners * per_pair, BLK, col_local)[positions].reshape(
        DST_BLK * BLK, col_local
    )
    panel_rows = broadcast(local_kernel[:, :PANEL], "cols", 0)
    contract = (((0,), (0,)), ((), ()))
    gram_matrix = lax.psum(
        lax.dot_general(panel_rows, panel_rows, contract, preferred_element_type=jnp.float32),
        "rows",
    )
    lower_factor = jnp.linalg.cholesky(gram_matrix)
    basis_cols = lax.linalg.triangular_solve(
        lower_factor, panel_rows.astype(jnp.float32).T, left_side=True, lower=True
    )
    projection = lax.psum(
        jnp.dot(
            basis_cols,
            local_kernel,
            precision=lax.Precision.HIGHEST,
            preferred_element_type=jnp.float32,
        ),
        "rows",
    )
    basis_rows = basis_cols.T
    norm_factor = math.sqrt(owners * local_kernel.shape[0])
    rest = local_kernel - jnp.dot(basis_rows, projection, precision=lax.Precision.HIGHEST)
    column = lax.axis_index("cols") * col_local + jnp.arange(col_local, dtype=jnp.int32)
    padded = jnp.pad(basis_rows, ((0, 0), (0, col_local - PANEL))) * norm_factor
    remainder = jnp.where(column[None, :] < PANEL, padded, rest).astype(jnp.bfloat16)
    return (projection / norm_factor, remainder)


def solution(mesh):
    return jax.shard_map(
        on_device,
        mesh=mesh,
        in_specs=(P("rows", "cols"), P("cols", None), P("rows"), P(), P()),
        out_specs=(P(None, "cols"), P("rows", "cols")),
        check_vma=False,
    )
```

profile of v0, /device:TPU:0, one launch (start us, length us, event | category | flops | bytes accessed | tf_op | source)
XLA Modules:
  0.0 864.9 jit_solution(12514857613203194263)
XLA Ops:
  7.2 0.7 all-gather.2.cloned.1.call-update
  7.9 0.8 copy.27
  8.7 0.7 iota_compare_fusion.6
  9.4 1.3 convert_reduce_fusion
  10.7 0.2 dynamic-slice_reduce_fusion
  10.9 0.7 fusion.16
  11.6 0.1 fusion.14
  12.0 0.7 convert_element_type.24
  12.6 0.1 and_reduce_fusion
  12.8 3.1 fusion.3
  16.0 13.4 %all-gather.2.cloned.1.call-done = bf16[25,128,1024]{2,1,0:T(8,128)(2,1)} async-done(((bf16[25,128,512]{2,1,0:T(8,128)(2,1)}), bf16[25,128,1024]{2,1,0:T(8,128)(2,1)}) %all-gather.2.cloned.1.call-update) | async-done | bytes 6553616 | tf_op jit(solution)/shard_map/all_gather | solution.py:24
  29.4 4.2 fusion.2
  33.6 22.0 %fusion.1 = bf16[3200,2048]{1,0:T(8,128)(2,1)} fusion(bf16[3200,1024]{1,0:T(8,128)(2,1)} %bitcast.63, bf16[2048,1024]{1,0:T(8,128)(2,1)} %param.6, f32[2048]{0:T(1024)S(1)} %multiply_add_fusion, f32[3200]{0:T(1024)S(1)} %add_multiply_fusion, f32[3200]{0:T(1024)S(1)} %broadcast_bitcast_fusion), kind=kOutput, calls=%fused_computation.6 | convolution fusion | flops 13454540800 | bytes 23888896 | tf_op jit(solution)/shard_map/dot_general | solution.py:27
  55.6 11.7 %gather_fusion = bf16[32,128,2048]{2,1,0:T(8,128)(2,1)} fusion(bf16[25,128,2048]{2,1,0:T(8,128)(2,1)} %bitcast.60, s32[1024]{0:T(1024)S(1)} %pad_clamp_fusion.1), kind=kCustom, calls=%fused_computation | custom fusion | bytes 33554560 | tf_op jit(solution)/shard_map/gather | solution.py:84
  67.3 14.0 %broadcast_select_fusion = bf16[16,2,128,2048]{3,2,1,0:T(8,128)(2,1)} fusion(bf16[16,2,128,2048]{3,2,1,0:T(8,128)(2,1)} %bitcast.57, pred[16,2]{1,0:T(8,128)(4,1)S(1)} %copy.28), kind=kLoop, calls=%fused_computation.7 | loop fusion | flops 8388608 | bytes 33554464 | tf_op jit(solution)/shard_map/jit(_where)/select_n | solution.py:83
  81.3 7.1 all-to-all-start
  88.5 0.2 all-reduce.6.cloned.1.call-start
  88.7 0.2 convert_reduce_fusion.1
  89.1 1.6 sort.15
  90.7 313.5 %all-to-all-done = bf16[16,2,128,2048]{3,2,1,0:T(8,128)(2,1)} async-done(((bf16[16,2,128,2048]{3,2,1,0:T(8,128)(2,1)}), bf16[16,2,128,2048]{3,2,1,0:T(8,128)(2,1)}, u32[]{:S(2)}, u32[]{:S(2)}) %all-to-all-start) | async-done | bytes 16777248 | tf_op jit(solution)/shard_map/all_to_all | solution.py:86
  404.2 10.2 %gather_fusion.1 = bf16[13,128,2048]{2,1,0:T(8,128)(2,1)} fusion(bf16[32,128,2048]{2,1,0:T(8,128)(2,1)} %bitcast.8, s32[1024]{0:T(1024)S(1)} %pad_clamp_fusion), kind=kCustom, calls=%fused_computation.1 | custom fusion | bytes 13631540 | tf_op jit(solution)/shard_map/gather | solution.py:87
  414.4 9.7 %copy.30 = bf16[1664,2048]{0,1:T(8,128)(2,1)} copy(bf16[1664,2048]{1,0:T(8,128)(2,1)} %bitcast.58) | data formatting | bytes 13631488 | tf_op jit(solution)/shard_map/reshape | solution.py:87
  424.1 2.1 slice_select_fusion
  426.3 88.3 %all-reduce.6.cloned.1.call-done = bf16[1664,256]{0,1:T(8,128)(2,1)} async-done(((bf16[1664,256]{0,1:T(8,128)(2,1)}), bf16[1664,256]{0,1:T(8,128)(2,1)}) %all-reduce.6.cloned.1.call-update) | async-done | bytes 851984 | tf_op jit(solution)/shard_map/psum | solution.py:18
  514.6 2.7 fusion.20
  517.5 111.7 %all-reduce.8.cloned.1.call-done = f32[256,256]{0,1:T(8,128)} async-done(((f32[256,256]{0,1:T(8,128)}), f32[256,256]{0,1:T(8,128)}) %all-reduce.8.cloned.1.call-update) | async-done | bytes 262160 | tf_op jit(solution)/shard_map/psum | solution.py:92
  629.2 1.1 copy.32
  630.3 1.0 fusion.8
  631.3 11.7 %cholesky.50 = f32[128,128]{1,0:T(8,128)S(1)} custom-call(f32[128,128]{1,0:T(8,128)S(1)} %cholesky.118), custom_call_target="Cholesky" | custom-call | tf_op jit(solution)/shard_map/jit(cholesky)/cholesky | solution.py:96
  643.0 9.8 %custom-call.14 = f32[1,128,128]{1,2,0:T(8,128)S(1)} custom-call(f32[1,128,128]{2,1,0:T(8,128)S(1)} %get-tuple-element.34), custom_call_target="InvertDiagBlocksLowerTriangular" | custom-call | tf_op jit(solution)/shard_map/jit(cholesky)/cholesky | solution.py:96
  652.9 0.2 constant_dynamic-update-slice_fusion
  653.1 0.3 convolution_subtract_fusion.1
  653.3 11.7 %cholesky.105 = f32[128,128]{1,0:T(8,128)S(1)} custom-call(f32[128,128]{1,0:T(8,128)S(1)} %convolution_subtract_fusion.1), custom_call_target="Cholesky" | custom-call | tf_op jit(solution)/shard_map/jit(cholesky)/cholesky | solution.py:96
  665.1 0.7 compare_reduce_fusion
  667.2 4.1 while.1
  667.4 0.6 fusion.32
  668.0 1.4 bitcast_dynamic-update-slice_fusion.2
  669.4 0.6 fusion.32
  669.9 1.4 bitcast_dynamic-update-slice_fusion.2
  671.3 19.7 %custom-call.15 = f32[2,128,128]{1,2,0:T(8,128)S(1)} custom-call(f32[2,128,128]{2,1,0:T(8,128)S(1)} %get-tuple-element.12), custom_call_target="InvertDiagBlocksLowerTriangular" | custom-call | tf_op jit(solution)/shard_map/triangular_solve | solution.py:97
  691.0 1.6 fusion.6
  692.6 0.8 convolution_subtract_fusion
  693.4 0.9 fusion.10
  694.3 9.0 %fusion.5 = f32[256,2048]{1,0:T(8,128)} fusion(bf16[1664,2048]{1,0:T(8,128)(2,1)} %bitcast.59, f32[128,1664]{1,0:T(8,128)S(1)} %fusion.10, f32[128,1664]{1,0:T(8,128)S(1)} %fusion.6), kind=kOutput, calls=%fused_computation.17 | convolution fusion | flops 10469408768 | bytes 10616832 | tf_op jit(solution)/shard_map/dot_general | solution.py:101
  703.5 125.0 %all-reduce.10.cloned.1.call-done = f32[256,2048]{1,0:T(8,128)} async-done(((f32[256,2048]{1,0:T(8,128)}), f32[256,2048]{1,0:T(8,128)}) %all-reduce.10.cloned.1.call-update) | async-done | bytes 2097168 | tf_op jit(solution)/shard_map/psum | solution.py:100
  828.5 17.6 %select_convert_fusion = bf16[1664,2048]{0,1:T(8,128)(2,1)} fusion(bf16[1664,2048]{0,1:T(8,128)(2,1)} %copy.30, f32[1664,256]{0,1:T(8,128)S(1)} %fusion.4, f32[256,2048]{1,0:T(8,128)} %all-reduce.10.cloned.1.call-done, pred[2048]{0:T(1024)(128)(4,1)S(1)} %add_compare_fusion, f32[128,1664]{1,0:T(8,128)S(1)} %fusion.10, f32[128,1664]{1,0:T(8,128)S(1)} %fusion.6), kind=kOutput, calls=%fused_computation.8 | convolution fusion | flops 10486448128 | bytes 19138560 | tf_op jit(solution)/shard_map/dot_general | solution.py:111
  846.1 10.4 %copy.35 = bf16[1664,2048]{1,0:T(8,128)(2,1)} copy(bf16[1664,2048]{0,1:T(8,128)(2,1)} %select_convert_fusion) | data formatting | bytes 13631488
  856.5 1.5 broadcast_multiply_fusion
  (44 shorter events, 1.1 us)
Async XLA Ops:
  7.2 22.3 %all-gather.2.cloned.1.call-start = ((), (), s32[]{:S(2)}) async-start(), calls=%async_computation.1 | async-start | bytes 9830400 | tf_op jit(solution)/shard_map/all_gather | solution.py:24
  81.3 7.4 copy-start.2
  81.3 7.4 copy-start.3
  81.3 322.9 %all-to-all-start = ((bf16[16,2,128,2048]{3,2,1,0:T(8,128)(2,1)}), bf16[16,2,128,2048]{3,2,1,0:T(8,128)(2,1)}, u32[]{:S(2)}, u32[]{:S(2)}) async-start(bf16[16,2,128,2048]{3,2,1,0:T(8,128)(2,1)} %broadcast_select_fusion), calls=%async_computation | async-start | bytes 33554432 | tf_op jit(solution)/shard_map/all_to_all | solution.py:86
  88.5 426.2 %all-reduce.6.cloned.1.call-start = ((), (), s32[]{:S(2)}) async-start(), calls=%async_computation.2 | async-start | bytes 1703936 | tf_op jit(solution)/shard_map/psum | solution.py:18
  426.3 202.9 %all-reduce.8.cloned.1.call-start = ((), (), s32[]{:S(2)}) async-start(), calls=%async_computation.3 | async-start | bytes 524288 | tf_op jit(solution)/shard_map/psum | solution.py:92
  514.6 177.9 %copy-start = (bf16[1664,256]{0,1:T(8,128)(2,1)S(1)}, bf16[1664,256]{0,1:T(8,128)(2,1)}, u32[]{:S(2)}) copy-start(bf16[1664,256]{0,1:T(8,128)(2,1)} %all-reduce.6.cloned.1.call-done) | copy-start | bytes 2555908
  517.4 311.1 %all-reduce.10.cloned.1.call-start = ((), (), s32[]{:S(2)}) async-start(), calls=%async_computation.4 | async-start | bytes 4194304 | tf_op jit(solution)/shard_map/psum | solution.py:100
  846.1 10.4 %copy-start.1 = (f32[256,2048]{1,0:T(8,128)S(1)}, f32[256,2048]{1,0:T(8,128)}, u32[]{:S(2)}) copy-start(f32[256,2048]{1,0:T(8,128)} %all-reduce.10.cloned.1.call-done) | copy-start | bytes 6291460
Sparse Core Ops, SparseCore 0:
  9.5 19.8 all-gather.1
  426.4 88.1 all-reduce.5
  521.3 107.8 all-reduce.7
  703.5 124.9 all-reduce.9
where the time goes:
time: 874 us; the launch traced here: 865 us
  waiting for transfers between devices  653 us (75%)
  other arithmetic  84.6 us (10%)
  matrix products  55.1 us (6%)
  local copies, waits for them, and re-layouts  49.2 us (6%)
  between operations  15.7 us (2%)
    all_to_all x1, waiting for transfers between devices, on_device(): lax.all_to_all(outgoing, 'rows', split_axis=0, concat_axis=0, tiled=True)  314 us
    psum x1, waiting for transfers between devices, on_device(): lax.psum(jnp.dot(basis_cols, local_kernel, precision=lax.Precision.HIGHES...  125 us
    psum x1, waiting for transfers between devices, on_device(): lax.psum(lax.dot_general(panel_rows, panel_rows, contract, preferred_elem...  112 us
    psum x1, waiting for transfers between devices, broadcast(): return lax.psum(kept, axis)  88.3 us
    another operation x6, other arithmetic, on_device(): lower_factor = jnp.linalg.cholesky(gram_matrix)  34 us
    dot_general x1, matrix products, build_kernel(): lax.dot_general(flat_rows, sparse_points, (((1,), (1,)), ((), ())), prefe...  22 us
    another operation x3, other arithmetic, on_device(): lax.linalg.triangular_solve(lower_factor, panel_rows.astype(jnp.float32)....  19.7 us
    dot_general x1, matrix products, on_device(): jnp.dot(basis_rows, projection, precision=lax.Precision.HIGHEST)  17.6 us
  transfers between devices with their start and end apart: 5, of which 5 were waited for; matrix products, arithmetic and copies ran while one was open for 1% of the time, Pallas kernels for 0%

commit v1 on v0

v1 whole, which is shorter than its diff:
```python
import functools
import math

import jax
import jax.numpy as jnp
from jax import lax
from jax.experimental import pallas as pl
from jax.experimental.pallas import tpu as pltpu
from jax.sharding import PartitionSpec as P

PANEL = 256
BLK = 128
DST_BLK = 13
EPSILON = 1e-06
VMEM_LIMIT = 56 * 1024 * 1024
HIGH = lax.Precision.HIGHEST
ANY = pl.BlockSpec(memory_space=pl.ANY)
SMEM = pl.BlockSpec(memory_space=pltpu.SMEM)


def params(**kw):
    return pltpu.CompilerParams(vmem_limit_bytes=VMEM_LIMIT, **kw)


def cost(flops, nbytes):
    return pl.CostEstimate(flops=int(flops), bytes_accessed=int(nbytes), transcendentals=0)


def nt(a, b):
    return lax.dot_general(a, b, (((1,), (1,)), ((), ())), preferred_element_type=jnp.float32)


def nn(a, b, precision=None):
    return lax.dot_general(
        a, b, (((1,), (0,)), ((), ())), preferred_element_type=jnp.float32, precision=precision
    )


def pack_kernel(per_pair, me_ref, dest_ref, cnt_ref, desc_ref, out_ref, ctr_ref, sems):
    slots = desc_ref.shape[0]
    owners = ctr_ref.shape[0]
    me = me_ref[0]
    count = cnt_ref[me]

    @pl.loop(0, owners)
    def _(i):
        ctr_ref[i] = 0

    def copy(j, slot):
        return pltpu.make_async_copy(desc_ref.at[j], out_ref.at[slot], sems.at[j])

    @pl.loop(0, slots)
    def _(j):
        @pl.when(j < count)
        def _():
            d = dest_ref[me, j]
            r = ctr_ref[d]
            ctr_ref[d] = r + 1
            copy(j, d * per_pair + r).start()

    @pl.loop(0, slots)
    def _(j):
        @pl.when(j < count)
        def _():
            pltpu.make_async_copy(desc_ref.at[0], out_ref.at[0], sems.at[j]).wait()


def pack(desc_blocks, me, destinations, counts, per_pair):
    slots, blk, feat = desc_blocks.shape
    owners = destinations.shape[0]
    return pl.pallas_call(
        functools.partial(pack_kernel, per_pair),
        out_shape=jax.ShapeDtypeStruct((owners * per_pair, blk, feat), desc_blocks.dtype),
        in_specs=[SMEM, SMEM, SMEM, ANY],
        out_specs=ANY,
        scratch_shapes=[pltpu.SMEM((owners,), jnp.int32), pltpu.SemaphoreType.DMA((slots,))],
        cost_estimate=cost(0, 4 * slots * blk * feat),
        name="pack",
    )(me, destinations, counts, desc_blocks)


def select_kernel(pos_ref, recv_ref, out_ref, sems):
    copies = [
        pltpu.make_async_copy(recv_ref.at[pos_ref[p]], out_ref.at[p], sems.at[p])
        for p in range(DST_BLK)
    ]
    for c in copies:
        c.start()
    for c in copies:
        c.wait()


def select(received, positions):
    _, blk, feat = received.shape
    return pl.pallas_call(
        select_kernel,
        out_shape=jax.ShapeDtypeStruct((DST_BLK, blk, feat), received.dtype),
        in_specs=[SMEM, ANY],
        out_specs=ANY,
        scratch_shapes=[pltpu.SemaphoreType.DMA((DST_BLK,))],
        cost_estimate=cost(0, 4 * DST_BLK * blk * feat),
        name="select",
    )(positions, received)


def share_parts(x):
    groups = lax.axis_size("cols")
    if groups == 2:
        peer = lax.ppermute(x, "cols", [(0, 1), (1, 0)])
        return [x, peer]
    full = lax.all_gather(x, "cols", axis=0, tiled=False)
    return [full[i] for i in range(groups)]


def part_offsets(feat):
    groups = lax.axis_size("cols")
    if groups == 2:
        c = lax.axis_index("cols")
        return jnp.stack([c * feat, (1 - c) * feat]).astype(jnp.int32)
    return jnp.arange(groups, dtype=jnp.int32) * feat


def inner_product(x_parts, rows, off_ref, s_ref):
    feat = x_parts[0].shape[1]
    total = None
    for i, ref in enumerate(x_parts):
        off = pl.multiple_of(off_ref[i], 128)
        term = nt(ref[rows, :], s_ref[:, pl.ds(off, feat)])
        total = term if total is None else total + term
    return total


def row_square(x_parts, rows):
    total = None
    for ref in x_parts:
        x = ref[rows, :].astype(jnp.float32)
        term = jnp.sum(x * x, axis=1, keepdims=True)
        total = term if total is None else total + term
    return total


def source_kernel(nparts, tile, cnt_ref, off_ref, w_ref, *refs):
    parts = refs[:nparts]
    sp_ref, csp_ref, s_ref, cs_ref, gram_ref, g_ref, pt_ref, rs_ref = refs[nparts:]
    width = parts[0].shape[1] * nparts
    rows_all = parts[0].shape[0]
    count = cnt_ref[0]
    step = pl.program_id(0)
    per = tile // BLK
    tiles = rows_all // tile

    @pl.when(step == 0)
    def _():
        gram_ref[...] = jnp.zeros_like(gram_ref)
        for t in range(tiles):
            @pl.when(t * per < count)
            def _():
                for b in range(per):
                    j = t * per + b
                    rows = pl.ds(j * BLK, BLK)
                    sq = row_square(parts, rows) / width + EPSILON
                    w = jnp.where(j < count, w_ref[j], 0.0)
                    rs_ref[rows, :] = w / sq
                rows = pl.ds(t * tile, tile)
                inner = inner_product(parts, rows, off_ref, sp_ref)
                panel = inner * inner * rs_ref[rows, :] * csp_ref[...]
                panel_t = panel.T.astype(jnp.bfloat16)
                pt_ref[t] = panel_t
                gram_ref[...] += nt(panel_t, panel_t)

    g_ref[...] = jnp.zeros_like(g_ref)
    for t in range(tiles):
        @pl.when(t * per < count)
        def _():
            rows = pl.ds(t * tile, tile)
            inner = inner_product(parts, rows, off_ref, s_ref)
            kern = (inner * inner * rs_ref[rows, :] * cs_ref[...]).astype(jnp.bfloat16)
            g_ref[...] += nn(pt_ref[t], kern)


def source_products(parts, offsets, count, weights, sp, csp, s, cs):
    rows, feat = parts[0].shape
    cols, width = s.shape
    blocks = rows // BLK
    per = 5 if blocks % 5 == 0 else 1
    tile = per * BLK
    chunk = min(512, cols)
    once = pl.Buffered(1)
    return pl.pallas_call(
        functools.partial(source_kernel, len(parts), tile),
        grid=(cols // chunk,),
        out_shape=(
            jax.ShapeDtypeStruct((PANEL, PANEL), jnp.float32),
            jax.ShapeDtypeStruct((PANEL, cols), jnp.float32),
        ),
        in_specs=[SMEM, SMEM, SMEM]
        + [pl.BlockSpec((rows, feat), lambda i: (0, 0), pipeline_mode=once)] * len(parts)
        + [
            pl.BlockSpec((PANEL, width), lambda i: (0, 0), pipeline_mode=once),
            pl.BlockSpec((1, PANEL), lambda i: (0, 0), pipeline_mode=once),
            pl.BlockSpec((chunk, width), lambda i: (i, 0)),
            pl.BlockSpec((1, chunk), lambda i: (0, i)),
        ],
        out_specs=(
            pl.BlockSpec((PANEL, PANEL), lambda i: (0, 0)),
            pl.BlockSpec((PANEL, chunk), lambda i: (0, i)),
        ),
        scratch_shapes=[
            pltpu.VMEM((rows // tile, PANEL, tile), jnp.bfloat16),
            pltpu.VMEM((rows, 1), jnp.float32),
        ],
        compiler_params=params(dimension_semantics=("arbitrary",)),
        cost_estimate=cost(
            2 * rows * (width + PANEL) * (cols + PANEL), 2 * rows * width + 2 * cols * width + 4 * PANEL * cols
        ),
        name="source_products",
    )(count, offsets, weights, *parts, sp, csp, s, cs)


def remainder_kernel(nparts, off_ref, w_ref, *refs):
    parts = refs[:nparts]
    sp_ref, csp_ref, s_ref, cs_ref, keep_ref, coef_ref, out_ref, p_ref, rs_ref = refs[nparts:]
    width = parts[0].shape[1] * nparts
    rows_all = parts[0].shape[0]
    step = pl.program_id(0)
    blocks = rows_all // BLK
    bounds = list(range(0, blocks, 4)) + [blocks]
    spans = [pl.ds(a * BLK, (b - a) * BLK) for a, b in zip(bounds, bounds[1:])]

    @pl.when(step == 0)
    def _():
        for j in range(blocks):
            rows = pl.ds(j * BLK, BLK)
            sq = row_square(parts, rows) / width + EPSILON
            rs_ref[rows, :] = w_ref[j] / sq
        for rows in spans:
            inner = inner_product(parts, rows, off_ref, sp_ref)
            panel = inner * inner * rs_ref[rows, :] * csp_ref[...]
            p_ref[rows, :] = panel.astype(jnp.bfloat16)

    coef = coef_ref[...]
    high = coef.astype(jnp.bfloat16)
    low = (coef - high.astype(jnp.float32)).astype(jnp.bfloat16)
    for rows in spans:
        inner = inner_product(parts, rows, off_ref, s_ref)
        kern = (inner * inner * rs_ref[rows, :] * cs_ref[...]).astype(jnp.bfloat16)
        panel = p_ref[rows, :]
        fit = nn(panel, high) + nn(panel, low)
        out_ref[rows, :] = (kern.astype(jnp.float32) * keep_ref[...] - fit).astype(out_ref.dtype)


def remainder_rows(parts, offsets, weights, sp, csp, s, cs, keep, coef):
    rows, feat = parts[0].shape
    cols, width = s.shape
    chunk = min(256, cols)
    once = pl.Buffered(1)
    return pl.pallas_call(
        functools.partial(remainder_kernel, len(parts)),
        grid=(cols // chunk,),
        out_shape=jax.ShapeDtypeStruct((rows, cols), jnp.bfloat16),
        in_specs=[SMEM, SMEM]
        + [pl.BlockSpec((rows, feat), lambda i: (0, 0), pipeline_mode=once)] * len(parts)
        + [
            pl.BlockSpec((PANEL, width), lambda i: (0, 0), pipeline_mode=once),
            pl.BlockSpec((1, PANEL), lambda i: (0, 0), pipeline_mode=once),
            pl.BlockSpec((chunk, width), lambda i: (i, 0)),
            pl.BlockSpec((1, chunk), lambda i: (0, i)),
            pl.BlockSpec((1, chunk), lambda i: (0, i)),
            pl.BlockSpec((PANEL, chunk), lambda i: (0, i)),
        ],
        out_specs=pl.BlockSpec((rows, chunk), lambda i: (0, i)),
        scratch_shapes=[
            pltpu.VMEM((rows, PANEL), jnp.bfloat16),
            pltpu.VMEM((rows, 1), jnp.float32),
        ],
        compiler_params=params(dimension_semantics=("arbitrary",)),
        cost_estimate=cost(
            2 * rows * (width + 2 * PANEL) * cols, 2 * rows * width + 2 * cols * width + 2 * rows * cols
        ),
        name="remainder_rows",
    )(offsets, weights, *parts, sp, csp, s, cs, keep, coef)


def flips(bit, size):
    return [(i, i ^ bit) for i in range(size)]


def butterfly_sum(x, bits):
    size = lax.axis_size("rows")
    me = lax.axis_index("rows")
    for bit in bits:
        half = x.shape[0] // 2
        upper = (me // bit) % 2
        send = lax.dynamic_slice_in_dim(x, (1 - upper) * half, half, 0)
        kept = lax.dynamic_slice_in_dim(x, upper * half, half, 0)
        x = kept + lax.ppermute(send, "rows", flips(bit, size))
    for bit in bits[::-1]:
        upper = (me // bit) % 2
        other = lax.ppermute(x, "rows", flips(bit, size))
        x = jnp.where(
            upper == 0, jnp.concatenate([x, other], 0), jnp.concatenate([other, x], 0)
        )
    return x


def full_sum(x):
    size = lax.axis_size("rows")
    bit = 1
    while bit < size:
        x = x + lax.ppermute(x, "rows", flips(bit, size))
        bit *= 2
    return x


def on_device(descriptors, sparse_points, block_weights, block_counts, destinations):
    owners = lax.axis_size("rows")
    groups = lax.axis_size("cols")
    me = lax.axis_index("rows").astype(jnp.int32)
    group = lax.axis_index("cols").astype(jnp.int32)
    slots = block_weights.shape[0]
    per_pair = -(-slots // owners)
    feat = descriptors.shape[1]
    cols, width = sparse_points.shape
    norm = math.sqrt(owners * DST_BLK * BLK)

    desc_blocks = descriptors.reshape(slots, BLK, feat)
    outgoing = pack(desc_blocks, me[None], destinations, block_counts, per_pair)
    received = lax.all_to_all(outgoing, "rows", split_axis=0, concat_axis=0, tiled=True)

    first = sparse_points[:PANEL]
    if groups == 2:
        moved = lax.ppermute(first, "cols", [(0, 1), (1, 0)])
        panel_points = jnp.where(group == 0, first, moved)
    else:
        panel_points = lax.all_gather(first, "cols", axis=0, tiled=False)[0]

    def column_scale(points):
        sq = jnp.einsum("mf,mf->m", points, points, preferred_element_type=jnp.float32)
        return (1.0 / (width * (sq / width + EPSILON)))[None, :]

    cs = column_scale(sparse_points)
    csp = column_scale(panel_points)
    offsets = part_offsets(feat)

    source_parts = share_parts(descriptors)
    count = lax.dynamic_index_in_dim(block_counts, me, 0)
    weights32 = block_weights.astype(jnp.float32)
    gram_part, g_part = source_products(
        source_parts, offsets, count, weights32, panel_points, csp, sparse_points, cs
    )

    spare = -(-owners * slots // (PANEL * 8)) * 8
    table = lax.dynamic_update_slice(
        jnp.zeros((spare * PANEL,), jnp.float32), weights32, (me * slots,)
    ).reshape(spare, PANEL)
    if groups == 2:
        mine = lax.dynamic_slice_in_dim(gram_part, group * (PANEL // 2), PANEL // 2, 0)
        summed = full_sum(jnp.concatenate([mine, table], 0))
        mine, table = summed[: PANEL // 2], summed[PANEL // 2 :]
        other = lax.ppermute(mine, "cols", [(0, 1), (1, 0)])
        gram = jnp.where(
            group == 0, jnp.concatenate([mine, other], 0), jnp.concatenate([other, mine], 0)
        )
    else:
        summed = full_sum(jnp.concatenate([gram_part, table], 0))
        gram, table = summed[:PANEL], summed[PANEL:]
    all_weights = table.reshape(-1)[: owners * slots]

    lower = jnp.linalg.cholesky(gram)
    inverse = lax.linalg.triangular_solve(
        lower, jnp.eye(PANEL, dtype=jnp.float32), left_side=True, lower=True
    )

    bits = []
    bit = 1
    while bit < owners:
        bits.append(bit)
        bit *= 2
    half = cols // 2
    swapped = [bits[1], bits[0]] + bits[2:]
    g = jnp.concatenate(
        [butterfly_sum(g_part[:, :half], bits), butterfly_sum(g_part[:, half:], swapped)], 1
    )
    projection = nn(inverse, g, HIGH)
    fit = nn(inverse.T, projection, HIGH)
    column = group * cols + jnp.arange(cols, dtype=jnp.int32)
    keep = (column >= PANEL)[None, :]
    basis_map = jnp.pad(inverse.T * (-norm), ((0, 0), (0, cols - PANEL)))
    coef = jnp.where(keep, fit, basis_map)

    slot_ids = jnp.arange(slots, dtype=jnp.int32)
    toward = ((slot_ids[None, :] < block_counts[:, None]) & (destinations == me)).astype(jnp.int32)
    rank = jnp.cumsum(toward, axis=1) - toward
    flat = toward.reshape(-1)
    place = jnp.cumsum(flat) - flat
    where_from = (jnp.arange(owners, dtype=jnp.int32)[:, None] * per_pair + rank).reshape(-1)
    hit = (flat[None, :] == 1) & (place[None, :] == jnp.arange(DST_BLK, dtype=jnp.int32)[:, None])
    positions = jnp.sum(jnp.where(hit, where_from[None, :], 0), axis=1)
    weights_here = jnp.sum(jnp.where(hit, all_weights[None, :], 0.0), axis=1)

    arrived = select(received, positions).reshape(DST_BLK * BLK, feat)
    parts = share_parts(arrived)
    remainder = remainder_rows(
        parts,
        offsets,
        weights_here,
        panel_points,
        csp,
        sparse_points,
        cs,
        keep.astype(jnp.float32),
        coef,
    )
    return (projection / norm, remainder)


def solution(mesh):
    return jax.shard_map(
        on_device,
        mesh=mesh,
        in_specs=(P("rows", "cols"), P("cols", None), P("rows"), P(), P()),
        out_specs=(P(None, "cols"), P("rows", "cols")),
        check_vma=False,
    )
```

time: 874 us -> 406 us (0.46)
  waiting for transfers between devices: 653 us -> 75.3 us
  Pallas kernels: 0 us -> 190 us
  matrix products: 55.1 us -> 7.94 us
  starting transfers between devices: 7.45 us -> 50.7 us
  local copies, waits for them, and re-layouts: 49.2 us -> 11.2 us
  other arithmetic: 84.6 us -> 65.9 us
  between operations: 15.7 us -> 2.95 us
    psum x3 -> x0, waiting for transfers between devices: 325 us -> none  [the longest x1 125 us: on_device(): lax.psum(jnp.dot(basis_cols, local_kernel, precision=lax.Precision.HIGHES...]
    all_to_all x1, waiting for transfers between devices: 314 us -> 0.01 us  [on_device(): lax.all_to_all(outgoing, 'rows', split_axis=0, concat_axis=0, tiled=True)]
    pallas_call x0 -> x4, Pallas kernels: none -> 190 us  [the longest x1 85.6 us: pack(): pl.pallas_call(functools.partial(pack_kernel, per_pair), out_shape=jax.Sh...]
    ppermute x0 -> x24, waiting for transfers between devices: none -> 75.3 us  [the longest x4 47.5 us: full_sum(): x = x + lax.ppermute(x, 'rows', flips(bit, size))]
    dot_general x4 -> x2, matrix products: 51.3 us -> 6.54 us  [nn(): lax.dot_general(a, b, (((1,), (0,)), ((), ())), preferred_element_type=jn...]
    ppermute x0 -> x24, starting transfers between devices: none -> 30.2 us  [the longest x4 11.3 us: full_sum(): x = x + lax.ppermute(x, 'rows', flips(bit, size))]
    gather x2 -> x0, local copies, waits for them, and re-layouts: 21.9 us -> none  [the longest x1 11.7 us: on_device(): src_kernel[source_index]]
    select_n x5 -> x9, other arithmetic: 16.1 us -> 0.37 us  [the longest x8 0.35 us: butterfly_sum(): jnp.where(upper == 0, jnp.concatenate([x, other], 0), jnp.concatenate([ot...]
  transfers between devices with their start and end apart: 5 -> 25, of which waited for: 5 -> 12; matrix products, arithmetic and copies ran while one was open for 1% -> 21% of each run, Pallas kernels for 0% -> 43%
where the time goes in v1:
time: 406 us; the launch traced here: 404 us
  Pallas kernels  190 us (47%)
  waiting for transfers between devices  75.3 us (19%)
  other arithmetic  65.9 us (16%)
  starting transfers between devices  50.7 us (12%)
  local copies, waits for them, and re-layouts  11.2 us (3%)
  matrix products  7.94 us (2%)
    pallas_call x1, Pallas kernels, pack(): pl.pallas_call(functools.partial(pack_kernel, per_pair), out_shape=jax.Sh...  85.6 us
    pallas_call x1, Pallas kernels, select(): pl.pallas_call(select_kernel, out_shape=jax.ShapeDtypeStruct((DST_BLK, bl...  53.5 us
    ppermute x4, waiting for transfers between devices, full_sum(): x = x + lax.ppermute(x, 'rows', flips(bit, size))  47.5 us
    another operation x6, other arithmetic, on_device(): lower = jnp.linalg.cholesky(gram)  34 us
    pallas_call x1, Pallas kernels, source_products(): pl.pallas_call(functools.partial(source_kernel, len(parts), tile), grid=(...  32.8 us
    all_to_all x1, starting transfers between devices, on_device(): lax.all_to_all(outgoing, 'rows', split_axis=0, concat_axis=0, tiled=True)  20.5 us
    another operation x3, other arithmetic, on_device(): lax.linalg.triangular_solve(lower, jnp.eye(PANEL, dtype=jnp.float32), lef...  19.7 us
    pallas_call x1, Pallas kernels, remainder_rows(): pl.pallas_call(functools.partial(remainder_kernel, len(parts)), grid=(col...  18.1 us
  transfers between devices with their start and end apart: 25, of which 12 were waited for; matrix products, arithmetic and copies ran while one was open for 21% of the time, Pallas kernels for 43%

profile of v1, /device:TPU:0, one launch (start us, length us, event | category | flops | bytes accessed | tf_op | source)
XLA Modules:
  0.0 404.0 jit_solution(17936831518170849049)
XLA Ops:
  1.1 1.1 slice.71
  2.3 85.6 %pack.1 = bf16[32,128,512]{2,1,0:T(8,128)(2,1)} custom-call(s32[1]{0:T(128)} %bitcast.11.me_ref, s32[16,25]{1,0:T(8,128)} %dest_ref.1, s32[16]{0:T(128)} %cnt_ref.1, bf16[25,128,512]{2,1,0:T(8,128)(2,1)} %bitcast.47), custom_call_target="tpu_custom_call" | custom-call | bytes 6553600 | tf_op jit(solution)/shard_map/pack/pallas_call | solution.py:71
  88.0 20.5 %all-to-all-start = ((bf16[32,128,512]{2,1,0:T(8,128)(2,1)}), bf16[32,128,512]{2,1,0:T(8,128)(2,1)}, u32[]{:S(2)}, u32[]{:S(2)}) async-start(bf16[32,128,512]{2,1,0:T(8,128)(2,1)} %pack.1), calls=%async_computation | async-start | bytes 8388608 | tf_op jit(solution)/shard_map/all_to_all | solution.py:328
  110.9 0.6 pad_add_fusion.off_ref
  111.7 0.6 select_reduce_fusion.2.pos_ref
  112.3 0.6 compare_convert_fusion.refs_6_
  112.9 3.1 fusion
  116.0 0.6 multiply_divide_fusion
  116.6 2.0 fusion.5
  119.2 32.8 %source_products.1 = (f32[256,256]{1,0:T(8,128)}, f32[256,2048]{1,0:T(8,128)}) custom-call(s32[1]{0:T(128)} %dynamic_slice.55.cnt_ref, s32[2]{0:T(128)} %pad_add_fusion.off_ref, f32[25]{0:T(128)} %convert_element_type.12.w_ref, bf16[3200,512]{1,0:T(8,128)(2,1)} %refs_0_.1, bf16[3200,512]{1,0:T(8,128)(2,1)} %collective-permute-done.refs_1_, ...), custom_call_target="tpu_custom_call" | custom-call | flops 18874368000 | bytes 12845056 | tf_op jit(solution)/shard_map/source_products/pallas_call | solution.py:189
  152.0 1.1 copy.17
  153.2 1.7 fusion.21
  154.9 0.8 constant_dynamic-slice_fusion.4
  155.8 17.8 %collective-permute-done.2 = f32[136,256]{0,1:T(8,128)S(1)} collective-permute-done((f32[136,256]{0,1:T(8,128)S(1)}, f32[136,256]{0,1:T(8,128)S(1)}, u32[]{:S(2)}, u32[]{:S(2)}) %collective-permute-start.2) | collective-permute-done | bytes 139296 | tf_op jit(solution)/shard_map/ppermute | solution.py:310
  173.7 0.8 constant_dynamic-slice_fusion.8
  174.6 1.5 collective-permute-start.7
  176.0 16.3 %collective-permute-done.3 = f32[136,256]{0,1:T(8,128)S(1)} collective-permute-done((f32[136,256]{0,1:T(8,128)S(1)}, f32[136,256]{0,1:T(8,128)S(1)}, u32[]{:S(2)}, u32[]{:S(2)}) %collective-permute-start.3) | collective-permute-done | bytes 139296 | tf_op jit(solution)/shard_map/ppermute | solution.py:310
  192.7 8.1 %collective-permute-done.4 = f32[136,256]{0,1:T(8,128)S(1)} collective-permute-done((f32[136,256]{0,1:T(8,128)S(1)}, f32[136,256]{0,1:T(8,128)S(1)}, u32[]{:S(2)}, u32[]{:S(2)}) %collective-permute-start.4) | collective-permute-done | bytes 139296 | tf_op jit(solution)/shard_map/ppermute | solution.py:310
  200.8 11.1 %collective-permute-start.5 = (f32[136,256]{0,1:T(8,128)S(1)}, f32[136,256]{0,1:T(8,128)S(1)}, u32[]{:S(2)}, u32[]{:S(2)}) collective-permute-start(f32[136,256]{0,1:T(8,128)S(1)} %add.190), channel_id=1, source_target_pairs={{0,16},{2,18},{4,20},{6,22},{8,24},{10,26},{12,28},{14,30},{16,0},... | collective-permute-start | bytes 417800 | tf_op jit(solution)/shard_map/ppermute | solution.py:310
  212.0 1.1 dynamic-slice_add_fusion.1
  213.2 5.3 %collective-permute-done.5 = f32[136,256]{0,1:T(8,128)S(1)} collective-permute-done((f32[136,256]{0,1:T(8,128)S(1)}, f32[136,256]{0,1:T(8,128)S(1)}, u32[]{:S(2)}, u32[]{:S(2)}) %collective-permute-start.5) | collective-permute-done | bytes 139296 | tf_op jit(solution)/shard_map/ppermute | solution.py:310
  218.6 0.7 collective-permute-start.8
  219.4 0.7 select_reduce_fusion.3.w_ref
  220.3 11.7 %cholesky.50 = f32[128,128]{1,0:T(8,128)S(1)} custom-call(f32[128,128]{1,0:T(8,128)S(1)} %cholesky.118), custom_call_target="Cholesky" | custom-call | tf_op jit(solution)/shard_map/jit(cholesky)/cholesky | solution.py:369
  232.1 9.8 %custom-call.14 = f32[1,128,128]{1,2,0:T(8,128)S(1)} custom-call(f32[1,128,128]{2,1,0:T(8,128)S(1)} %get-tuple-element.31), custom_call_target="InvertDiagBlocksLowerTriangular" | custom-call | tf_op jit(solution)/shard_map/jit(cholesky)/cholesky | solution.py:369
  242.4 11.7 %cholesky.105 = f32[128,128]{1,0:T(8,128)S(1)} custom-call(f32[128,128]{1,0:T(8,128)S(1)} %convolution_subtract_fusion.1), custom_call_target="Cholesky" | custom-call | tf_op jit(solution)/shard_map/jit(cholesky)/cholesky | solution.py:369
  254.2 0.7 compare_reduce_fusion
  256.9 1.9 collective-permute-start.9
  258.8 4.2 %collective-permute-done.17 = f32[32,1024]{1,0:T(8,128)S(1)} collective-permute-done((f32[32,1024]{1,0:T(8,128)S(1)}, f32[32,1024]{1,0:T(8,128)S(1)}, u32[]{:S(2)}, u32[]{:S(2)}) %collective-permute-start.17) | collective-permute-done | bytes 131104 | tf_op jit(solution)/shard_map/ppermute | solution.py:296
  263.0 1.5 collective-permute-start.18
  265.1 2.3 collective-permute-start.10
  267.4 2.8 collective-permute-done.18
  270.3 2.7 collective-permute-done.10
  273.3 3.8 collective-permute-done.19
  277.6 0.7 collective-permute-done.11
  278.3 2.2 collective-permute-start.12
  280.5 4.1 %while.1 = (s32[]{:T(128)}, f32[256,256]{1,0:T(8,128)S(1)}, s32[2,2]{1,0:T(2,128)S(1)}, f32[2,128,128]{2,1,0:T(8,128)S(1)}, s32[]{:T(128)}) while((s32[]{:T(128)}, f32[256,256]{1,0:T(8,128)S(1)}, s32[2,2]{1,0:T(2,128)S(1)}, f32[2,128,128]{2,1,0:T(8,128)S(1)}, s32[]{:T(128)}) %tuple.30), condition=%wide.while_cond, body=%wide.while_body.sunk | while | flops 2 | bytes 131189 | solution.py:370
  280.5 0.6 fusion.28
  281.1 1.4 bitcast_dynamic-update-slice_fusion.2
  283.2 1.4 bitcast_dynamic-update-slice_fusion.2
  284.6 19.7 %custom-call.15 = f32[2,128,128]{1,2,0:T(8,128)S(1)} custom-call(f32[2,128,128]{2,1,0:T(8,128)S(1)} %get-tuple-element.13), custom_call_target="InvertDiagBlocksLowerTriangular" | custom-call | tf_op jit(solution)/shard_map/triangular_solve | solution.py:370
  304.4 4.6 %collective-permute-start.21 = (f32[64,1024]{1,0:T(8,128)S(1)}, f32[64,1024]{1,0:T(8,128)S(1)}, u32[]{:S(2)}, u32[]{:S(2)}) collective-permute-start(f32[64,1024]{1,0:T(8,128)S(1)} %maximum_select_fusion.6), channel_id=1, source_target_pairs={{0,2},{2,0},{4,6},{6,4},{8,10},{10,8},{12,14},{14,12},{16,18},{18,... | collective-permute-start | bytes 786440 | tf_op jit(solution)/shard_map/ppermute | solution.py:299
  309.0 1.6 collective-permute-start.13
  310.6 53.5 %select.41 = bf16[13,128,512]{2,1,0:T(8,128)(2,1)} custom-call(s32[13]{0:T(128)} %select_reduce_fusion.2.pos_ref, bf16[32,128,512]{2,1,0:T(8,128)(2,1)} %all-to-all-done.recv_ref), custom_call_target="tpu_custom_call" | custom-call | bytes 3407872 | tf_op jit(solution)/shard_map/select/pallas_call | solution.py:95
  366.0 12.9 %collective-permute-done.22 = f32[128,1024]{1,0:T(8,128)S(1)} collective-permute-done((f32[128,1024]{1,0:T(8,128)S(1)}, f32[128,1024]{1,0:T(8,128)S(1)}, u32[]{:S(2)}, u32[]{:S(2)}) %collective-permute-start.22) | collective-permute-done | bytes 524320 | tf_op jit(solution)/shard_map/ppermute | solution.py:299
  379.4 3.3 broadcast_multiply_fusion
  382.6 3.3 convolution_select_fusion.refs_7_
  385.9 18.1 %remainder_rows.1 = bf16[1664,2048]{1,0:T(8,128)(2,1)} custom-call(s32[2]{0:T(128)} %pad_add_fusion.off_ref, f32[13]{0:T(128)} %select_reduce_fusion.3.w_ref, bf16[1664,512]{1,0:T(8,128)(2,1)} %bitcast.49, bf16[1664,512]{1,0:T(8,128)(2,1)} %collective-permute-done.23.refs_1_, bf16[256,1024]{1,0:T(8,128)(2,1)} %get-tuple-element.23.refs_2_, ...), custom_call_target="tpu_custom_call" | custom-call | flops 10468982784 | bytes 14417920 | tf_op jit(solution)/shard_map/remainder_rows/pallas_call | solution.py:257
  (112 shorter events, 10.1 us)
Async XLA Ops:
  0.6 118.6 %collective-permute-start = (bf16[3200,512]{1,0:T(8,128)(2,1)}, bf16[3200,512]{1,0:T(8,128)(2,1)}, u32[]{:S(2)}, u32[]{:S(2)}) collective-permute-start(bf16[3200,512]{1,0:T(8,128)(2,1)} %refs_0_.1), channel_id=1, source_target_pairs={{0,1},{1,0},{2,3},{3,2},{4,5},{5,4},{6,7},{7,6},{8,9},{9,8},{10,11... | collective-permute-start | bytes 9830408 | tf_op jit(solution)/shard_map/ppermute | solution.py:109
  2.2 114.4 %collective-permute-start.1 = (bf16[256,1024]{1,0:T(8,128)(2,1)S(1)}, bf16[256,1024]{1,0:T(8,128)(2,1)S(1)}, u32[]{:S(2)}, u32[]{:S(2)}) collective-permute-start(bf16[256,1024]{1,0:T(8,128)(2,1)S(1)} %slice.71), channel_id=1, source_target_pairs={{0,1},{1,0},{2,3},{3,2},{4,5},{5,4},{6,7},{7,6},{8,9},{9,8},{10,11... | collective-permute-start | bytes 1572872 | tf_op jit(solution)/shard_map/ppermute | solution.py:332
  88.0 20.6 %copy-start = (s32[16,25]{1,0:T(8,128)S(1)}, s32[16,25]{1,0:T(8,128)}, u32[]{:S(2)}) copy-start(s32[16,25]{1,0:T(8,128)} %dest_ref.1) | copy-start | bytes 4804
  88.0 20.6 %copy-start.1 = (s32[16]{0:T(128)S(1)}, s32[16]{0:T(128)}, u32[]{:S(2)}) copy-start(s32[16]{0:T(128)} %cnt_ref.1) | copy-start | bytes 196
  88.0 21.5 %copy-start.2 = (bf16[25]{0:T(256)(128)(2,1)S(1)}, bf16[25]{0:T(256)(128)(2,1)}, u32[]{:S(2)}) copy-start(bf16[25]{0:T(256)(128)(2,1)} %param.7) | copy-start | bytes 154
  88.0 222.6 %all-to-all-start = ((bf16[32,128,512]{2,1,0:T(8,128)(2,1)}), bf16[32,128,512]{2,1,0:T(8,128)(2,1)}, u32[]{:S(2)}, u32[]{:S(2)}) async-start(bf16[32,128,512]{2,1,0:T(8,128)(2,1)} %pack.1), calls=%async_computation | async-start | bytes 8388608 | tf_op jit(solution)/shard_map/all_to_all | solution.py:328
  153.2 20.4 %collective-permute-start.2 = (f32[136,256]{0,1:T(8,128)S(1)}, f32[136,256]{0,1:T(8,128)S(1)}, u32[]{:S(2)}, u32[]{:S(2)}) collective-permute-start(f32[136,256]{0,1:T(8,128)S(1)} %pad_maximum_fusion), channel_id=1, source_target_pairs={{0,2},{2,0},{4,6},{6,4},{8,10},{10,8},{12,14},{14,12},{16,18},{18,... | collective-permute-start | bytes 417800 | tf_op jit(solution)/shard_map/ppermute | solution.py:310
  155.7 56.1 %collective-permute-start.15 = (f32[128,1024]{1,0:T(8,128)}, f32[128,1024]{1,0:T(8,128)S(1)}, u32[]{:S(2)}, u32[]{:S(2)}) collective-permute-start(f32[128,1024]{1,0:T(8,128)} %constant_dynamic-slice_fusion.4), channel_id=1, source_target_pairs={{0,4},{2,6},{4,0},{6,2},{8,12},{10,14},{12,8},{14,10},{16,20},{18,... | collective-permute-start | bytes 1572872 | tf_op jit(solution)/shard_map/ppermute | solution.py:296
  173.6 18.7 %collective-permute-start.3 = (f32[136,256]{0,1:T(8,128)S(1)}, f32[136,256]{0,1:T(8,128)S(1)}, u32[]{:S(2)}, u32[]{:S(2)}) collective-permute-start(f32[136,256]{0,1:T(8,128)S(1)} %fusion.19), channel_id=1, source_target_pairs={{0,4},{2,6},{4,0},{6,2},{8,12},{10,14},{12,8},{14,10},{16,20},{18,... | collective-permute-start | bytes 417800 | tf_op jit(solution)/shard_map/ppermute | solution.py:310
  174.6 37.5 %collective-permute-start.7 = (f32[128,1024]{1,0:T(8,128)}, f32[128,1024]{1,0:T(8,128)}, u32[]{:S(2)}, u32[]{:S(2)}) collective-permute-start(f32[128,1024]{1,0:T(8,128)} %constant_dynamic-slice_fusion.8), channel_id=1, source_target_pairs={{0,2},{2,0},{4,6},{6,4},{8,10},{10,8},{12,14},{14,12},{16,18},{18,... | collective-permute-start | bytes 1572872 | tf_op jit(solution)/shard_map/ppermute | solution.py:296
  192.4 8.4 %collective-permute-start.4 = (f32[136,256]{0,1:T(8,128)S(1)}, f32[136,256]{0,1:T(8,128)S(1)}, u32[]{:S(2)}, u32[]{:S(2)}) collective-permute-start(f32[136,256]{0,1:T(8,128)S(1)} %add.189), channel_id=1, source_target_pairs={{0,8},{2,10},{4,12},{6,14},{8,0},{10,2},{12,4},{14,6},{16,24},{18,... | collective-permute-start | bytes 417800 | tf_op jit(solution)/shard_map/ppermute | solution.py:310
  200.8 17.7 %collective-permute-start.5 = (f32[136,256]{0,1:T(8,128)S(1)}, f32[136,256]{0,1:T(8,128)S(1)}, u32[]{:S(2)}, u32[]{:S(2)}) collective-permute-start(f32[136,256]{0,1:T(8,128)S(1)} %add.190), channel_id=1, source_target_pairs={{0,16},{2,18},{4,20},{6,22},{8,24},{10,26},{12,28},{14,30},{16,0},... | collective-permute-start | bytes 417800 | tf_op jit(solution)/shard_map/ppermute | solution.py:310
  212.0 44.3 %collective-permute-start.16 = (f32[64,1024]{1,0:T(8,128)S(1)}, f32[64,1024]{1,0:T(8,128)S(1)}, u32[]{:S(2)}, u32[]{:S(2)}) collective-permute-start(f32[64,1024]{1,0:T(8,128)S(1)} %constant_dynamic-slice_fusion.3), channel_id=1, source_target_pairs={{0,2},{2,0},{4,6},{6,4},{8,10},{10,8},{12,14},{14,12},{16,18},{18,... | collective-permute-start | bytes 786440 | tf_op jit(solution)/shard_map/ppermute | solution.py:296
  218.5 1.6 collective-permute-start.6
  218.6 38.2 %collective-permute-start.8 = (f32[64,1024]{1,0:T(8,128)S(1)}, f32[64,1024]{1,0:T(8,128)S(1)}, u32[]{:S(2)}, u32[]{:S(2)}) collective-permute-start(f32[64,1024]{1,0:T(8,128)S(1)} %constant_dynamic-slice_fusion.7), channel_id=1, source_target_pairs={{0,4},{2,6},{4,0},{6,2},{8,12},{10,14},{12,8},{14,10},{16,20},{18,... | collective-permute-start | bytes 786440 | tf_op jit(solution)/shard_map/ppermute | solution.py:296
  256.6 6.4 %collective-permute-start.17 = (f32[32,1024]{1,0:T(8,128)S(1)}, f32[32,1024]{1,0:T(8,128)S(1)}, u32[]{:S(2)}, u32[]{:S(2)}) collective-permute-start(f32[32,1024]{1,0:T(8,128)S(1)} %constant_dynamic-slice_fusion.2), channel_id=1, source_target_pairs={{0,8},{2,10},{4,12},{6,14},{8,0},{10,2},{12,4},{14,6},{16,24},{18,... | collective-permute-start | bytes 393224 | tf_op jit(solution)/shard_map/ppermute | solution.py:296
  256.9 8.2 %collective-permute-start.9 = (f32[32,1024]{1,0:T(8,128)S(1)}, f32[32,1024]{1,0:T(8,128)S(1)}, u32[]{:S(2)}, u32[]{:S(2)}) collective-permute-start(f32[32,1024]{1,0:T(8,128)S(1)} %constant_dynamic-slice_fusion.6), channel_id=1, source_target_pairs={{0,8},{2,10},{4,12},{6,14},{8,0},{10,2},{12,4},{14,6},{16,24},{18,... | collective-permute-start | bytes 393224 | tf_op jit(solution)/shard_map/ppermute | solution.py:296
  263.0 7.2 %collective-permute-start.18 = (f32[16,1024]{1,0:T(8,128)S(1)}, f32[16,1024]{1,0:T(8,128)S(1)}, u32[]{:S(2)}, u32[]{:S(2)}) collective-permute-start(f32[16,1024]{1,0:T(8,128)S(1)} %constant_dynamic-slice_fusion.1), channel_id=1, source_target_pairs={{0,16},{2,18},{4,20},{6,22},{8,24},{10,26},{12,28},{14,30},{16,0},... | collective-permute-start | bytes 196616 | tf_op jit(solution)/shard_map/ppermute | solution.py:296
  265.1 7.9 %collective-permute-start.10 = (f32[16,1024]{1,0:T(8,128)S(1)}, f32[16,1024]{1,0:T(8,128)S(1)}, u32[]{:S(2)}, u32[]{:S(2)}) collective-permute-start(f32[16,1024]{1,0:T(8,128)S(1)} %constant_dynamic-slice_fusion.5), channel_id=1, source_target_pairs={{0,16},{2,18},{4,20},{6,22},{8,24},{10,26},{12,28},{14,30},{16,0},... | collective-permute-start | bytes 196616 | tf_op jit(solution)/shard_map/ppermute | solution.py:296
  270.2 6.9 %collective-permute-start.19 = (f32[16,1024]{1,0:T(8,128)S(1)}, f32[16,1024]{1,0:T(8,128)S(1)}, u32[]{:S(2)}, u32[]{:S(2)}) collective-permute-start(f32[16,1024]{1,0:T(8,128)S(1)} %dynamic-slice_add_fusion.6), channel_id=1, source_target_pairs={{0,16},{2,18},{4,20},{6,22},{8,24},{10,26},{12,28},{14,30},{16,0},... | collective-permute-start | bytes 196616 | tf_op jit(solution)/shard_map/ppermute | solution.py:299
  273.0 5.2 %collective-permute-start.11 = (f32[16,1024]{1,0:T(8,128)S(1)}, f32[16,1024]{1,0:T(8,128)S(1)}, u32[]{:S(2)}, u32[]{:S(2)}) collective-permute-start(f32[16,1024]{1,0:T(8,128)S(1)} %dynamic-slice_add_fusion.7), channel_id=1, source_target_pairs={{0,16},{2,18},{4,20},{6,22},{8,24},{10,26},{12,28},{14,30},{16,0},... | collective-permute-start | bytes 196616 | tf_op jit(solution)/shard_map/ppermute | solution.py:299
  277.2 27.2 %collective-permute-start.20 = (f32[32,1024]{1,0:T(8,128)S(1)}, f32[32,1024]{1,0:T(8,128)S(1)}, u32[]{:S(2)}, u32[]{:S(2)}) collective-permute-start(f32[32,1024]{1,0:T(8,128)S(1)} %maximum_select_fusion.8), channel_id=1, source_target_pairs={{0,8},{2,10},{4,12},{6,14},{8,0},{10,2},{12,4},{14,6},{16,24},{18,... | collective-permute-start | bytes 393224 | tf_op jit(solution)/shard_map/ppermute | solution.py:299
  278.3 30.7 %collective-permute-start.12 = (f32[32,1024]{1,0:T(8,128)S(1)}, f32[32,1024]{1,0:T(8,128)S(1)}, u32[]{:S(2)}, u32[]{:S(2)}) collective-permute-start(f32[32,1024]{1,0:T(8,128)S(1)} %maximum_select_fusion.7), channel_id=1, source_target_pairs={{0,8},{2,10},{4,12},{6,14},{8,0},{10,2},{12,4},{14,6},{16,24},{18,... | collective-permute-start | bytes 393224 | tf_op jit(solution)/shard_map/ppermute | solution.py:299
  304.4 60.1 %collective-permute-start.21 = (f32[64,1024]{1,0:T(8,128)S(1)}, f32[64,1024]{1,0:T(8,128)S(1)}, u32[]{:S(2)}, u32[]{:S(2)}) collective-permute-start(f32[64,1024]{1,0:T(8,128)S(1)} %maximum_select_fusion.6), channel_id=1, source_target_pairs={{0,2},{2,0},{4,6},{6,4},{8,10},{10,8},{12,14},{14,12},{16,18},{18,... | collective-permute-start | bytes 786440 | tf_op jit(solution)/shard_map/ppermute | solution.py:299
  309.0 56.1 %collective-permute-start.13 = (f32[64,1024]{1,0:T(8,128)S(1)}, f32[64,1024]{1,0:T(8,128)S(1)}, u32[]{:S(2)}, u32[]{:S(2)}) collective-permute-start(f32[64,1024]{1,0:T(8,128)S(1)} %maximum_select_fusion.5), channel_id=1, source_target_pairs={{0,4},{2,6},{4,0},{6,2},{8,12},{10,14},{12,8},{14,10},{16,20},{18,... | collective-permute-start | bytes 786440 | tf_op jit(solution)/shard_map/ppermute | solution.py:299
  364.1 21.8 %collective-permute-start.23 = (bf16[1664,512]{1,0:T(8,128)(2,1)}, bf16[1664,512]{1,0:T(8,128)(2,1)}, u32[]{:S(2)}, u32[]{:S(2)}) collective-permute-start(bf16[1664,512]{1,0:T(8,128)(2,1)} %bitcast.48), channel_id=1, source_target_pairs={{0,1},{1,0},{2,3},{3,2},{4,5},{5,4},{6,7},{7,6},{8,9},{9,8},{10,11... | collective-permute-start | bytes 5111816 | tf_op jit(solution)/shard_map/ppermute | solution.py:109
  364.5 14.4 %collective-permute-start.22 = (f32[128,1024]{1,0:T(8,128)S(1)}, f32[128,1024]{1,0:T(8,128)S(1)}, u32[]{:S(2)}, u32[]{:S(2)}) collective-permute-start(f32[128,1024]{1,0:T(8,128)S(1)} %maximum_select_fusion.3), channel_id=1, source_target_pairs={{0,4},{2,6},{4,0},{6,2},{8,12},{10,14},{12,8},{14,10},{16,20},{18,... | collective-permute-start | bytes 1572872 | tf_op jit(solution)/shard_map/ppermute | solution.py:299
  365.1 14.1 %collective-permute-start.14 = (f32[128,1024]{1,0:T(8,128)S(1)}, f32[128,1024]{1,0:T(8,128)S(1)}, u32[]{:S(2)}, u32[]{:S(2)}) collective-permute-start(f32[128,1024]{1,0:T(8,128)S(1)} %maximum_select_fusion.2), channel_id=1, source_target_pairs={{0,2},{2,0},{4,6},{6,4},{8,10},{10,8},{12,14},{14,12},{16,18},{18,... | collective-permute-start | bytes 1572872 | tf_op jit(solution)/shard_map/ppermute | solution.py:299

commit v2 on v1

v2 whole, which is shorter than its diff:
```python
import functools
import math

import jax
import jax.numpy as jnp
from jax import lax
from jax.experimental import pallas as pl
from jax.experimental.pallas import tpu as pltpu
from jax.sharding import PartitionSpec as P

PANEL = 256
BLK = 128
DST_BLK = 13
EPSILON = 1e-06
VMEM_LIMIT = 56 * 1024 * 1024
HIGH = lax.Precision.HIGHEST
ANY = pl.BlockSpec(memory_space=pl.ANY)
VMEM = pl.BlockSpec(memory_space=pltpu.VMEM)
SMEM = pl.BlockSpec(memory_space=pltpu.SMEM)


def params(**kw):
    return pltpu.CompilerParams(vmem_limit_bytes=VMEM_LIMIT, **kw)


def cost(flops, nbytes):
    return pl.CostEstimate(flops=int(flops), bytes_accessed=int(nbytes), transcendentals=0)


def dot(a, b, ca, cb, precision=None):
    return lax.dot_general(
        a, b, (((ca,), (cb,)), ((), ())), preferred_element_type=jnp.float32, precision=precision
    )


def nt(a, b, precision=None):
    return dot(a, b, 1, 1, precision)


def nn(a, b, precision=None):
    return dot(a, b, 1, 0, precision)


def tn(a, b, precision=None):
    return dot(a, b, 0, 0, precision)


def split(x):
    high = x.astype(jnp.bfloat16)
    return high, (x - high.astype(jnp.float32)).astype(jnp.bfloat16)


def pack_kernel(per_pair, me_ref, dest_ref, cnt_ref, desc_ref, out_ref, ctr_ref, sems):
    slots = desc_ref.shape[0]
    owners = ctr_ref.shape[0]
    me = me_ref[0]
    count = cnt_ref[me]

    @pl.loop(0, owners)
    def _(i):
        ctr_ref[i] = 0

    @pl.loop(0, slots)
    def _(j):
        @pl.when(j < count)
        def _():
            d = dest_ref[me, j]
            r = ctr_ref[d]
            ctr_ref[d] = r + 1
            slot = d * per_pair + r
            pltpu.make_async_copy(desc_ref.at[j], out_ref.at[slot], sems.at[j]).start()

    @pl.loop(0, slots)
    def _(j):
        @pl.when(j < count)
        def _():
            pltpu.make_async_copy(desc_ref.at[0], out_ref.at[0], sems.at[j]).wait()


def pack(desc_blocks, me, destinations, counts, per_pair):
    slots, blk, feat = desc_blocks.shape
    owners = destinations.shape[0]
    return pl.pallas_call(
        functools.partial(pack_kernel, per_pair),
        out_shape=jax.ShapeDtypeStruct((owners * per_pair, blk, feat), desc_blocks.dtype),
        in_specs=[SMEM, SMEM, SMEM, VMEM],
        out_specs=ANY,
        scratch_shapes=[pltpu.SMEM((owners,), jnp.int32), pltpu.SemaphoreType.DMA((slots,))],
        compiler_params=params(),
        cost_estimate=cost(0, 4 * slots * blk * feat),
        name="pack",
    )(me, destinations, counts, desc_blocks)


def select_kernel(pos_ref, recv_ref, out_ref, sems):
    copies = [
        pltpu.make_async_copy(recv_ref.at[pos_ref[p]], out_ref.at[p], sems.at[p])
        for p in range(DST_BLK)
    ]
    for c in copies:
        c.start()
    for c in copies:
        c.wait()


def select(received, positions):
    _, blk, feat = received.shape
    return pl.pallas_call(
        select_kernel,
        out_shape=jax.ShapeDtypeStruct((DST_BLK, blk, feat), received.dtype),
        in_specs=[SMEM, ANY],
        out_specs=VMEM,
        scratch_shapes=[pltpu.SemaphoreType.DMA((DST_BLK,))],
        compiler_params=params(),
        cost_estimate=cost(0, 4 * DST_BLK * blk * feat),
        name="select",
    )(positions, received)


def small_factor(a):
    n = a.shape[0]
    row = lax.broadcasted_iota(jnp.int32, (n, 1), 0)
    eye = lax.broadcasted_iota(jnp.int32, (n, n), 0) == lax.broadcasted_iota(jnp.int32, (n, n), 1)
    m = jnp.concatenate([a, eye.astype(jnp.float32)], axis=1)
    out = []
    for j in range(0, n, 2):
        r0 = m[j : j + 1, :]
        r1 = m[j + 1 : j + 2, :]
        p = r0[:, j : j + 1]
        q = r0[:, j + 1 : j + 2]
        s = r1[:, j + 1 : j + 2]
        det = p * s - q * q
        out.append(r0[:, n:] * lax.rsqrt(p))
        out.append((r1[:, n:] - (q / p) * r0[:, n:]) * lax.rsqrt(det / p))
        if j + 2 < n:
            inv = 1.0 / det
            g0 = (s * r0 - q * r1) * inv
            g1 = (p * r1 - q * r0) * inv
            c0 = jnp.where(row > j + 1, m[:, j : j + 1], 0.0)
            c1 = jnp.where(row > j + 1, m[:, j + 1 : j + 2], 0.0)
            m = m - c0 * g0 - c1 * g1
    return out


def factor_kernel(leaf, gram_ref, x_ref, a_ref):
    n = gram_ref.shape[0]
    a_ref[...] = gram_ref[...]
    x_ref[...] = jnp.zeros_like(x_ref)
    for k in range(0, n, leaf):
        e = k + leaf
        for i, r in enumerate(small_factor(a_ref[k:e, k:e])):
            x_ref[k + i : k + i + 1, k:e] = r
        xk = x_ref[k:e, k:e]
        if e < n:
            t = nn(xk, a_ref[k:e, e:], HIGH)
            a_ref[k:e, e:] = t
            a_ref[e:, e:] -= tn(t, t, HIGH)
        if k > 0:
            x_ref[k:e, :k] = -nn(xk, tn(a_ref[:k, k:e], x_ref[:k, :k], HIGH), HIGH)


def factor(gram):
    n = gram.shape[0]
    return pl.pallas_call(
        functools.partial(factor_kernel, 64),
        out_shape=jax.ShapeDtypeStruct((n, n), jnp.float32),
        scratch_shapes=[pltpu.VMEM((n, n), jnp.float32)],
        compiler_params=params(),
        cost_estimate=cost(2e10, 8 * n * n),
        name="factor",
    )(gram)


def share_parts(x):
    groups = lax.axis_size("cols")
    if groups == 2:
        peer = lax.ppermute(x, "cols", [(0, 1), (1, 0)])
        return [x, peer]
    full = lax.all_gather(x, "cols", axis=0, tiled=False)
    return [full[i] for i in range(groups)]


def part_offsets(feat):
    groups = lax.axis_size("cols")
    if groups == 2:
        c = lax.axis_index("cols")
        return jnp.stack([c * feat, (1 - c) * feat]).astype(jnp.int32)
    return jnp.arange(groups, dtype=jnp.int32) * feat


def joined(parts, off_ref, x_ref):
    feat = parts[0].shape[1]
    for i, ref in enumerate(parts):
        x_ref[:, pl.ds(pl.multiple_of(off_ref[i], 128), feat)] = ref[...]


def row_scale(x, weight):
    x = x.astype(jnp.float32)
    return weight / (jnp.sum(x * x, axis=1, keepdims=True) / x.shape[1] + EPSILON)


def panel_kernel(nparts, cnt_ref, off_ref, w_ref, *refs):
    parts = refs[:nparts]
    sp_ref, csp_ref, gram_ref, x_ref, pw_ref = refs[nparts:]
    tile = x_ref.shape[0]
    per = tile // BLK
    count = cnt_ref[0]
    step = pl.program_id(0)

    @pl.when(step == 0)
    def _():
        gram_ref[...] = jnp.zeros_like(gram_ref)

    @pl.when(step * per < count)
    def _():
        joined(parts, off_ref, x_ref)
        scales = []
        for b in range(per):
            j = step * per + b
            w = jnp.where(j < count, w_ref[j], 0.0)
            scales.append(row_scale(x_ref[b * BLK : (b + 1) * BLK, :], w))
        scale = jnp.concatenate(scales, axis=0)
        inner = nt(x_ref[...], sp_ref[...])
        panel = (inner * inner * scale * csp_ref[...]).astype(jnp.bfloat16)
        gram_ref[...] += tn(panel, panel)
        pw_ref[...] = (panel.astype(jnp.float32) * scale).astype(jnp.bfloat16)

    @pl.when(step * per >= count)
    def _():
        pw_ref[...] = jnp.zeros_like(pw_ref)


def panel_products(parts, offsets, count, weights, sp, csp):
    rows, feat = parts[0].shape
    width = sp.shape[1]
    blocks = rows // BLK
    per = 5 if blocks % 5 == 0 else 1
    tile = per * BLK
    return pl.pallas_call(
        functools.partial(panel_kernel, len(parts)),
        grid=(rows // tile,),
        out_shape=(
            jax.ShapeDtypeStruct((PANEL, PANEL), jnp.float32),
            jax.ShapeDtypeStruct((rows, width), jnp.bfloat16),
            jax.ShapeDtypeStruct((rows, PANEL), jnp.bfloat16),
        ),
        in_specs=[SMEM, SMEM, SMEM]
        + [pl.BlockSpec((tile, feat), lambda i: (i, 0))] * len(parts)
        + [pl.BlockSpec((PANEL, width), lambda i: (0, 0)), pl.BlockSpec((1, PANEL), lambda i: (0, 0))],
        out_specs=(
            pl.BlockSpec((PANEL, PANEL), lambda i: (0, 0)),
            pl.BlockSpec((tile, width), lambda i: (i, 0)),
            pl.BlockSpec((tile, PANEL), lambda i: (i, 0)),
        ),
        compiler_params=params(dimension_semantics=("arbitrary",)),
        cost_estimate=cost(2 * rows * PANEL * (width + PANEL), 4 * rows * width),
        name="panel_products",
    )(count, offsets, weights, *parts, sp, csp)


def column_kernel(tile, cnt_ref, x_ref, pw_ref, s_ref, g_ref):
    rows, width = x_ref.shape
    count = cnt_ref[0]
    per = tile // BLK
    s = s_ref[...]
    g_ref[...] = jnp.zeros_like(g_ref)
    for t in range(rows // tile):
        @pl.when(t * per < count)
        def _():
            inner = nt(s, x_ref[t * tile : (t + 1) * tile, :])
            square = (inner * inner).astype(jnp.bfloat16)
            g_ref[...] += nn(square, pw_ref[t * tile : (t + 1) * tile, :])

    wide = s.astype(jnp.float32)
    norm = jnp.sum(wide * wide, axis=1, keepdims=True) / width + EPSILON
    g_ref[...] = g_ref[...] / (width * norm)


def column_products(x, pw, count, s, start, size):
    rows, width = x.shape
    blocks = rows // BLK
    per = 5 if blocks % 5 == 0 else 1
    chunk = min(512, size)
    first = start // chunk
    once = pl.Buffered(1)
    return pl.pallas_call(
        functools.partial(column_kernel, per * BLK),
        grid=(size // chunk,),
        out_shape=jax.ShapeDtypeStruct((size, PANEL), jnp.float32),
        in_specs=[
            SMEM,
            pl.BlockSpec((rows, width), lambda i: (0, 0), pipeline_mode=once),
            pl.BlockSpec((rows, PANEL), lambda i: (0, 0), pipeline_mode=once),
            pl.BlockSpec((chunk, width), lambda i: (first + i, 0)),
        ],
        out_specs=pl.BlockSpec((chunk, PANEL), lambda i: (i, 0)),
        compiler_params=params(dimension_semantics=("arbitrary",)),
        cost_estimate=cost(2 * rows * (width + PANEL) * size, 2 * rows * width),
        name="column_products",
    )(count, x, pw, s)


def remainder_kernel(nparts, norm, off_ref, w_ref, group_ref, *refs):
    parts = refs[:nparts]
    sp_ref, csp_ref, s_ref, cs_ref, inv_ref, rt_ref, out_ref, proj_ref, x_ref, p_ref, rs_ref = refs[nparts:]
    rows_all, width = x_ref.shape
    chunk = s_ref.shape[0]
    step = pl.program_id(0)
    blocks = rows_all // BLK
    bounds = list(range(0, blocks, 4)) + [blocks]
    spans = [(a * BLK, b * BLK) for a, b in zip(bounds, bounds[1:])]

    @pl.when(step == 0)
    def _():
        joined(parts, off_ref, x_ref)
        for j in range(blocks):
            scale = row_scale(x_ref[j * BLK : (j + 1) * BLK, :], w_ref[j])
            rs_ref[j * BLK : (j + 1) * BLK, :] = jnp.broadcast_to(scale, (BLK, 128))
        for a, b in spans:
            inner = nt(x_ref[a:b, :], sp_ref[...])
            scale = jnp.concatenate([rs_ref[a:b, :]] * (PANEL // 128), axis=1)
            p_ref[a:b, :] = (inner * inner * scale * csp_ref[...]).astype(jnp.bfloat16)

    inv_high, inv_low = split(inv_ref[...])
    rt = rt_ref[...]
    coef = (nn(rt, inv_high) + nn(rt, inv_low)).astype(jnp.bfloat16)
    proj_ref[...] = rt.astype(jnp.float32).T * (1.0 / norm)
    for a, b in spans:
        inner = nt(x_ref[a:b, :], s_ref[...])
        scale = jnp.concatenate([rs_ref[a:b, :]] * (chunk // 128), axis=1)
        kern = (inner * inner * scale * cs_ref[...]).astype(jnp.bfloat16)
        fit = nt(p_ref[a:b, :], coef)
        out_ref[a:b, :] = (kern.astype(jnp.float32) - fit).astype(out_ref.dtype)

    @pl.when((step == 0) & (group_ref[0] == 0))
    def _():
        for a, b in spans:
            panel = p_ref[a:b, :]
            basis = nt(panel, inv_high) + nt(panel, inv_low)
            out_ref[a:b, :PANEL] = (basis * norm).astype(out_ref.dtype)


def remainder_rows(parts, offsets, weights, group, sp, csp, s, cs, inverse, rt, norm):
    rows, feat = parts[0].shape
    cols, width = s.shape
    chunk = min(512, cols)
    once = pl.Buffered(1)
    return pl.pallas_call(
        functools.partial(remainder_kernel, len(parts), norm),
        grid=(cols // chunk,),
        out_shape=(
            jax.ShapeDtypeStruct((rows, cols), jnp.bfloat16),
            jax.ShapeDtypeStruct((PANEL, cols), jnp.float32),
        ),
        in_specs=[SMEM, SMEM, SMEM]
        + [pl.BlockSpec((rows, feat), lambda i: (0, 0), pipeline_mode=once)] * len(parts)
        + [
            pl.BlockSpec((PANEL, width), lambda i: (0, 0), pipeline_mode=once),
            pl.BlockSpec((1, PANEL), lambda i: (0, 0), pipeline_mode=once),
            pl.BlockSpec((chunk, width), lambda i: (i, 0)),
            pl.BlockSpec((1, chunk), lambda i: (0, i)),
            pl.BlockSpec((PANEL, PANEL), lambda i: (0, 0), pipeline_mode=once),
            pl.BlockSpec((chunk, PANEL), lambda i: (i, 0)),
        ],
        out_specs=(
            pl.BlockSpec((rows, chunk), lambda i: (0, i)),
            pl.BlockSpec((PANEL, chunk), lambda i: (0, i)),
        ),
        scratch_shapes=[
            pltpu.VMEM((rows, width), jnp.bfloat16),
            pltpu.VMEM((rows, PANEL), jnp.bfloat16),
            pltpu.VMEM((rows, 128), jnp.float32),
        ],
        compiler_params=params(dimension_semantics=("arbitrary",)),
        cost_estimate=cost(
            2 * rows * (width + 2 * PANEL) * cols, 2 * rows * width + 2 * cols * width + 2 * rows * cols
        ),
        name="remainder_rows",
    )(offsets, weights, group, *parts, sp, csp, s, cs, inverse, rt)


def flips(bit, size):
    return [(i, i ^ bit) for i in range(size)]


def scatter_sum(x, bits):
    size = lax.axis_size("rows")
    me = lax.axis_index("rows")
    for bit in bits:
        half = x.shape[0] // 2
        upper = (me // bit) % 2
        send = lax.dynamic_slice_in_dim(x, (1 - upper) * half, half, 0)
        kept = lax.dynamic_slice_in_dim(x, upper * half, half, 0)
        x = kept + lax.ppermute(send, "rows", flips(bit, size))
    return x


def gather_back(x, bits):
    size = lax.axis_size("rows")
    me = lax.axis_index("rows")
    for bit in bits[::-1]:
        upper = (me // bit) % 2
        other = lax.ppermute(x, "rows", flips(bit, size))
        x = jnp.where(
            upper == 0, jnp.concatenate([x, other], 0), jnp.concatenate([other, x], 0)
        )
    return x


def full_sum(x, bits):
    size = lax.axis_size("rows")
    for i in range(0, len(bits), 2):
        pair = bits[i : i + 2]
        if len(pair) == 1:
            x = x + lax.ppermute(x, "rows", flips(pair[0], size))
        else:
            a, b = pair
            xa = lax.ppermute(x, "rows", flips(a, size))
            xb = lax.ppermute(x, "rows", flips(b, size))
            xab = lax.ppermute(x, "rows", flips(a + b, size))
            x = (x + xa) + (xb + xab)
    return x


def on_device(descriptors, sparse_points, block_weights, block_counts, destinations):
    owners = lax.axis_size("rows")
    groups = lax.axis_size("cols")
    me = lax.axis_index("rows").astype(jnp.int32)
    group = lax.axis_index("cols").astype(jnp.int32)
    slots = block_weights.shape[0]
    per_pair = -(-slots // owners)
    feat = descriptors.shape[1]
    cols, width = sparse_points.shape
    norm = math.sqrt(owners * DST_BLK * BLK)
    bits = [1 << i for i in range(owners.bit_length() - 1)]
    swapped = [bits[1], bits[0]] + bits[2:]

    source_parts = share_parts(descriptors)
    desc_blocks = descriptors.reshape(slots, BLK, feat)
    outgoing = pack(desc_blocks, me[None], destinations, block_counts, per_pair)
    received = lax.all_to_all(outgoing, "rows", split_axis=0, concat_axis=0, tiled=True)

    first = sparse_points[:PANEL]
    if groups == 2:
        moved = lax.ppermute(first, "cols", [(0, 1), (1, 0)])
        panel_points = jnp.where(group == 0, first, moved)
    else:
        panel_points = lax.all_gather(first, "cols", axis=0, tiled=False)[0]

    def column_scale(points):
        sq = jnp.einsum("mf,mf->m", points, points, preferred_element_type=jnp.float32)
        return (1.0 / (width * (sq / width + EPSILON)))[None, :]

    cs = column_scale(sparse_points)
    csp = column_scale(panel_points)
    offsets = part_offsets(feat)

    count = lax.dynamic_index_in_dim(block_counts, me, 0)
    weights32 = block_weights.astype(jnp.float32)
    gram_part, x_source, pw = panel_products(
        source_parts, offsets, count, weights32, panel_points, csp
    )

    spare = -(-owners * slots // (PANEL * 8)) * 8
    table = lax.dynamic_update_slice(
        jnp.zeros((spare * PANEL,), jnp.float32), weights32, (me * slots,)
    ).reshape(spare, PANEL)
    if groups == 2:
        mine = lax.dynamic_slice_in_dim(gram_part, group * (PANEL // 2), PANEL // 2, 0)
        summed = full_sum(jnp.concatenate([mine, table], 0), bits)
        mine, table = summed[: PANEL // 2], summed[PANEL // 2 :]
        other = lax.ppermute(mine, "cols", [(0, 1), (1, 0)])
        gram = jnp.where(
            group == 0, jnp.concatenate([mine, other], 0), jnp.concatenate([other, mine], 0)
        )
    else:
        summed = full_sum(jnp.concatenate([gram_part, table], 0), bits)
        gram, table = summed[:PANEL], summed[PANEL:]
    all_weights = table.reshape(-1)[: owners * slots]
    inverse = factor(gram)

    half = cols // 2
    low = scatter_sum(column_products(x_source, pw, count, sparse_points, 0, half), bits)
    high = scatter_sum(column_products(x_source, pw, count, sparse_points, half, half), swapped)
    own = low.shape[0]
    solved = nt(jnp.concatenate([low, high], 0), inverse, HIGH).astype(jnp.bfloat16)
    rt = jnp.concatenate(
        [gather_back(solved[:own], bits), gather_back(solved[own:], swapped)], 0
    )

    slot_ids = jnp.arange(slots, dtype=jnp.int32)
    toward = ((slot_ids[None, :] < block_counts[:, None]) & (destinations == me)).astype(jnp.int32)
    rank = jnp.cumsum(toward, axis=1) - toward
    flat = toward.reshape(-1)
    place = jnp.cumsum(flat) - flat
    where_from = (jnp.arange(owners, dtype=jnp.int32)[:, None] * per_pair + rank).reshape(-1)
    hit = (flat[None, :] == 1) & (place[None, :] == jnp.arange(DST_BLK, dtype=jnp.int32)[:, None])
    positions = jnp.sum(jnp.where(hit, where_from[None, :], 0), axis=1)
    weights_here = jnp.sum(jnp.where(hit, all_weights[None, :], 0.0), axis=1)

    arrived = select(received, positions).reshape(DST_BLK * BLK, feat)
    remainder, projected = remainder_rows(
        share_parts(arrived),
        offsets,
        weights_here,
        group[None],
        panel_points,
        csp,
        sparse_points,
        cs,
        inverse,
        rt,
        norm,
    )
    return (projected, remainder)


def solution(mesh):
    return jax.shard_map(
        on_device,
        mesh=mesh,
        in_specs=(P("rows", "cols"), P("cols", None), P("rows"), P(), P()),
        out_specs=(P(None, "cols"), P("rows", "cols")),
        check_vma=False,
    )
```

time: 406 us -> 220 us (0.54)
  Pallas kernels: 190 us -> 97.8 us
  other arithmetic: 65.9 us -> 12.4 us
  waiting for transfers between devices: 75.3 us -> 60.6 us
  starting transfers between devices: 50.7 us -> 42.1 us
  matrix products: 7.94 us -> 0.4 us
  local copies, waits for them, and re-layouts: 11.2 us -> 5.41 us
    pallas_call x1, Pallas kernels: 85.6 us -> 3.91 us  [pack(): pl.pallas_call(functools.partial(pack_kernel, per_pair), out_shape=jax.Sh...]
    another operation x12 -> x3, other arithmetic: 54.2 us -> 0.41 us  [the longest x6 34 us: on_device(): lower = jnp.linalg.cholesky(gram)]
    pallas_call x1, Pallas kernels: 53.5 us -> 3.48 us  [select(): pl.pallas_call(select_kernel, out_shape=jax.ShapeDtypeStruct((DST_BLK, bl...]
    pallas_call x2 -> x5, Pallas kernels: 50.8 us -> 90.4 us  [the longest x2 38.7 us: column_products(): pl.pallas_call(functools.partial(column_kernel, per * BLK), grid=(size //...]
    ppermute x20 -> x22, waiting for transfers between devices: 75.3 us -> 60.6 us  [the longest x2 29.2 us: full_sum(): xb = lax.ppermute(x, 'rows', flips(b, size))]
    all_to_all x1, starting transfers between devices: 20.5 us -> 7.89 us  [on_device(): lax.all_to_all(outgoing, 'rows', split_axis=0, concat_axis=0, tiled=True)]
    dot_general x2 -> x1, matrix products: 6.54 us -> 0.4 us  [dot(): lax.dot_general(a, b, (((ca,), (cb,)), ((), ())), preferred_element_type=...]
    another operation x13 -> x1, local copies, waits for them, and re-layouts: 4.44 us -> 0.11 us
  transfers between devices with their start and end apart: 25 -> 27, of which waited for: 12 -> 12; matrix products, arithmetic and copies ran while one was open for 21% -> 8% of each run, Pallas kernels for 43% -> 37%
where the time goes in v2:
time: 220 us
  Pallas kernels  97.8 us (44%)
  waiting for transfers between devices  60.6 us (28%)
  starting transfers between devices  42.1 us (19%)
  other arithmetic  12.4 us (6%)
  local copies, waits for them, and re-layouts  5.41 us (2%)
    pallas_call x2, Pallas kernels, column_products(): pl.pallas_call(functools.partial(column_kernel, per * BLK), grid=(size //...  38.7 us
    ppermute x2, waiting for transfers between devices, full_sum(): xb = lax.ppermute(x, 'rows', flips(b, size))  29.2 us
    pallas_call x1, Pallas kernels, factor(): pl.pallas_call(functools.partial(factor_kernel, 64), out_shape=jax.ShapeD...  24.1 us
    pallas_call x1, Pallas kernels, remainder_rows(): pl.pallas_call(functools.partial(remainder_kernel, len(parts), norm), gri...  17.4 us
    ppermute x8, waiting for transfers between devices, scatter_sum(): x = kept + lax.ppermute(send, 'rows', flips(bit, size))  14.5 us
    ppermute x8, starting transfers between devices, scatter_sum(): x = kept + lax.ppermute(send, 'rows', flips(bit, size))  14.2 us
    ppermute x8, starting transfers between devices, gather_back(): other = lax.ppermute(x, 'rows', flips(bit, size))  11.2 us
    pallas_call x1, Pallas kernels, panel_products(): pl.pallas_call(functools.partial(panel_kernel, len(parts)), grid=(rows //...  10.2 us
  transfers between devices with their start and end apart: 27, of which 12 were waited for; matrix products, arithmetic and copies ran while one was open for 8% of the time, Pallas kernels for 37%

profile of v2, /device:TPU:0, one launch (start us, length us, event | category | flops | bytes accessed | tf_op | source)
XLA Modules:
  0.0 219.7 jit_solution(7885556408776985715)
XLA Ops:
  1.1 1.1 slice.31
  2.3 3.9 %pack.1 = bf16[32,128,512]{2,1,0:T(8,128)(2,1)} custom-call(s32[1]{0:T(128)} %bitcast.6.me_ref, s32[16,25]{1,0:T(8,128)} %dest_ref.1, s32[16]{0:T(128)} %cnt_ref.1, bf16[25,128,512]{2,1,0:T(8,128)(2,1)} %bitcast.16), custom_call_target="tpu_custom_call" | custom-call | bytes 6553600 | tf_op jit(solution)/shard_map/pack/pallas_call | solution.py:83
  6.3 7.9 %all-to-all-start = ((bf16[32,128,512]{2,1,0:T(8,128)(2,1)}), bf16[32,128,512]{2,1,0:T(8,128)(2,1)}, u32[]{:S(2)}, u32[]{:S(2)}) async-start(bf16[32,128,512]{2,1,0:T(8,128)(2,1)} %pack.1), calls=%async_computation | async-start | bytes 8388608 | tf_op jit(solution)/shard_map/all_to_all | solution.py:441
  15.9 0.6 dynamic_slice.55.cnt_ref
  16.6 0.6 pad_add_fusion.off_ref
  17.2 3.1 %fusion = f32[2048]{0:T(1024)S(1)} fusion(bf16[2048,1024]{1,0:T(8,128)(2,1)} %refs_4_.1), kind=kLoop, calls=%fused_computation.1 | loop fusion | flops 6289408 | bytes 4202496 | tf_op jit(solution)/shard_map/mf,mf->m/dot_general | solution.py:451
  20.3 2.0 fusion.1
  22.3 0.5 multiply_divide_fusion.1
  22.9 10.2 %panel_products.1 = (f32[256,256]{1,0:T(8,128)}, bf16[3200,1024]{1,0:T(8,128)(2,1)}, bf16[3200,256]{1,0:T(8,128)(2,1)}) custom-call(s32[1]{0:T(128)} %dynamic_slice.55.cnt_ref, s32[2]{0:T(128)} %pad_add_fusion.off_ref, f32[25]{0:T(128)} %convert_element_type.10.w_ref, bf16[3200,512]{1,0:T(8,128)(2,1)} %refs_0_.1, ...), custom_call_target="tpu_custom_call" | custom-call | flops 2097152000 | bytes 13107200 | tf_op jit(solution)/shard_map/panel_products/pallas_call | solution.py:239
  33.1 0.9 constant_dynamic-slice_fusion.8
  34.1 1.3 collective-permute-start.2
  35.6 2.0 collective-permute-start.4
  37.6 19.3 %column_products.2 = f32[1024,256]{1,0:T(8,128)} custom-call(s32[1]{0:T(128)} %dynamic_slice.55.cnt_ref, bf16[3200,1024]{1,0:T(8,128)(2,1)} %get-tuple-element.8.x_ref, bf16[3200,256]{1,0:T(8,128)(2,1)} %get-tuple-element.9.pw_ref, bf16[2048,1024]{1,0:T(8,128)(2,1)} %refs_4_.1), custom_call_target="tpu_custom_call" | custom-call | flops 8388608000 | bytes 6553600 | tf_op jit(solution)/shard_map/column_products/pallas_call | solution.py:286
  57.1 4.3 %collective-permute-start.7 = (f32[136,256]{1,0:T(8,128)S(1)}, f32[136,256]{1,0:T(8,128)S(1)}, u32[]{:S(2)}, u32[]{:S(2)}) collective-permute-start(f32[136,256]{1,0:T(8,128)S(1)} %add_add_fusion.1), channel_id=1, source_target_pairs={{0,24},{2,26},{4,28},{6,30},{8,16},{10,18},{12,20},{14,22},{16,8},... | collective-permute-start | bytes 417800 | tf_op jit(solution)/shard_map/ppermute | solution.py:420
  61.4 19.5 %column_products.3 = f32[1024,256]{1,0:T(8,128)} custom-call(s32[1]{0:T(128)} %dynamic_slice.55.cnt_ref, bf16[3200,1024]{1,0:T(8,128)(2,1)} %get-tuple-element.8.x_ref, bf16[3200,256]{1,0:T(8,128)(2,1)} %get-tuple-element.9.pw_ref, bf16[2048,1024]{1,0:T(8,128)(2,1)} %refs_4_.1), custom_call_target="tpu_custom_call" | custom-call | flops 8388608000 | bytes 6553600 | tf_op jit(solution)/shard_map/column_products/pallas_call | solution.py:286
  80.9 7.5 %collective-permute-done.5 = f32[136,256]{1,0:T(8,128)S(1)} collective-permute-done((f32[136,256]{1,0:T(8,128)S(1)}, f32[136,256]{1,0:T(8,128)S(1)}, u32[]{:S(2)}, u32[]{:S(2)}) %collective-permute-start.5) | collective-permute-done | bytes 139296 | tf_op jit(solution)/shard_map/ppermute | solution.py:418
  88.3 29.2 %collective-permute-done.6 = f32[136,256]{1,0:T(8,128)S(1)} collective-permute-done((f32[136,256]{1,0:T(8,128)S(1)}, f32[136,256]{1,0:T(8,128)S(1)}, u32[]{:S(2)}, u32[]{:S(2)}) %collective-permute-start.6) | collective-permute-done | bytes 139296 | tf_op jit(solution)/shard_map/ppermute | solution.py:419
  117.7 3.1 %collective-permute-start.10 = (f32[512,256]{1,0:T(8,128)S(1)}, f32[512,256]{1,0:T(8,128)S(1)}, u32[]{:S(2)}, u32[]{:S(2)}) collective-permute-start(f32[512,256]{1,0:T(8,128)S(1)} %constant_dynamic-slice_fusion.7), channel_id=1, source_target_pairs={{0,2},{2,0},{4,6},{6,4},{8,10},{10,8},{12,14},{14,12},{16,18},{18,... | collective-permute-start | bytes 1572872 | tf_op jit(solution)/shard_map/ppermute | solution.py:394
  120.8 1.1 constant_dynamic-slice_fusion.3
  121.9 3.0 %collective-permute-start.14 = (f32[512,256]{1,0:T(8,128)S(1)}, f32[512,256]{1,0:T(8,128)S(1)}, u32[]{:S(2)}, u32[]{:S(2)}) collective-permute-start(f32[512,256]{1,0:T(8,128)S(1)} %constant_dynamic-slice_fusion.3), channel_id=1, source_target_pairs={{0,4},{2,6},{4,0},{6,2},{8,12},{10,14},{12,8},{14,10},{16,20},{18,... | collective-permute-start | bytes 1572872 | tf_op jit(solution)/shard_map/ppermute | solution.py:394
  124.8 0.7 maximum_select_fusion.2.gram_ref
  125.6 24.1 %factor.1.refs_6_ = f32[256,256]{1,0:T(8,128)} custom-call(f32[256,256]{1,0:T(8,128)} %maximum_select_fusion.2.gram_ref), custom_call_target="tpu_custom_call" | custom-call | flops 20000000000 | bytes 524288 | tf_op jit(solution)/shard_map/factor/pallas_call | solution.py:164
  150.0 2.1 collective-permute-start.15
  152.1 6.2 %collective-permute-done.11 = f32[256,256]{1,0:T(8,128)S(1)} collective-permute-done((f32[256,256]{1,0:T(8,128)S(1)}, f32[256,256]{1,0:T(8,128)S(1)}, u32[]{:S(2)}, u32[]{:S(2)}) %collective-permute-start.11) | collective-permute-done | bytes 262176 | tf_op jit(solution)/shard_map/ppermute | solution.py:394
  158.3 2.6 %collective-permute-start.12 = (f32[128,256]{1,0:T(8,128)S(1)}, f32[128,256]{1,0:T(8,128)S(1)}, u32[]{:S(2)}, u32[]{:S(2)}) collective-permute-start(f32[128,256]{1,0:T(8,128)S(1)} %constant_dynamic-slice_fusion.5), channel_id=1, source_target_pairs={{0,8},{2,10},{4,12},{6,14},{8,0},{10,2},{12,4},{14,6},{16,24},{18,... | collective-permute-start | bytes 393224 | tf_op jit(solution)/shard_map/ppermute | solution.py:394
  161.1 4.0 %collective-permute-done.12 = f32[128,256]{1,0:T(8,128)S(1)} collective-permute-done((f32[128,256]{1,0:T(8,128)S(1)}, f32[128,256]{1,0:T(8,128)S(1)}, u32[]{:S(2)}, u32[]{:S(2)}) %collective-permute-start.12) | collective-permute-done | bytes 131104 | tf_op jit(solution)/shard_map/ppermute | solution.py:394
  165.2 1.8 collective-permute-start.13
  167.5 1.5 collective-permute-start.17
  169.0 2.4 %collective-permute-done.13 = f32[64,256]{1,0:T(8,128)S(1)} collective-permute-done((f32[64,256]{1,0:T(8,128)S(1)}, f32[64,256]{1,0:T(8,128)S(1)}, u32[]{:S(2)}, u32[]{:S(2)}) %collective-permute-start.13) | collective-permute-done | bytes 65568 | tf_op jit(solution)/shard_map/ppermute | solution.py:394
  171.4 1.4 collective-permute-done.17
  173.2 1.5 collective-permute-start.18
  174.7 0.6 select_reduce_fusion.pos_ref
  175.3 1.5 collective-permute-start.22
  176.8 3.5 %select.24 = bf16[13,128,512]{2,1,0:T(8,128)(2,1)} custom-call(s32[13]{0:T(128)} %select_reduce_fusion.pos_ref, bf16[32,128,512]{2,1,0:T(8,128)(2,1)} %all-to-all-done.recv_ref), custom_call_target="tpu_custom_call" | custom-call | bytes 3407872 | tf_op jit(solution)/shard_map/select/pallas_call | solution.py:108
  180.4 1.8 collective-permute-start.19
  182.6 2.4 %collective-permute-done.19 = bf16[128,256]{1,0:T(8,128)(2,1)S(1)} collective-permute-done((bf16[128,256]{1,0:T(8,128)(2,1)S(1)}, bf16[128,256]{1,0:T(8,128)(2,1)S(1)}, u32[]{:S(2)}, u32[]{:S(2)}) %collective-permute-start.19) | collective-permute-done | bytes 65568 | tf_op jit(solution)/shard_map/ppermute | solution.py:403
  185.0 1.0 collective-permute-start.20
  186.0 0.6 collective-permute-done.23
  186.6 2.2 %collective-permute-start.24 = (bf16[256,256]{1,0:T(8,128)(2,1)S(1)}, bf16[256,256]{1,0:T(8,128)(2,1)S(1)}, u32[]{:S(2)}, u32[]{:S(2)}) collective-permute-start(bf16[256,256]{1,0:T(8,128)(2,1)S(1)} %maximum_select_fusion.6), channel_id=1, source_target_pairs={{0,2},{2,0},{4,6},{6,4},{8,10},{10,8},{12,14},{14,12},{16,18},{18,... | collective-permute-start | bytes 393224 | tf_op jit(solution)/shard_map/ppermute | solution.py:403
  188.8 0.6 multiply_divide_fusion
  189.4 0.8 collective-permute-done.20
  190.3 2.4 %collective-permute-start.21 = (bf16[512,256]{1,0:T(8,128)(2,1)S(1)}, bf16[512,256]{1,0:T(8,128)(2,1)S(1)}, u32[]{:S(2)}, u32[]{:S(2)}) collective-permute-start(bf16[512,256]{1,0:T(8,128)(2,1)S(1)} %maximum_select_fusion.3), channel_id=1, source_target_pairs={{0,2},{2,0},{4,6},{6,4},{8,10},{10,8},{12,14},{14,12},{16,18},{18,... | collective-permute-start | bytes 786440 | tf_op jit(solution)/shard_map/ppermute | solution.py:403
  193.2 0.6 select_reduce_fusion.1.w_ref
  193.9 4.3 %collective-permute-done.21 = bf16[512,256]{1,0:T(8,128)(2,1)S(1)} collective-permute-done((bf16[512,256]{1,0:T(8,128)(2,1)S(1)}, bf16[512,256]{1,0:T(8,128)(2,1)S(1)}, u32[]{:S(2)}, u32[]{:S(2)}) %collective-permute-start.21) | collective-permute-done | bytes 262176 | tf_op jit(solution)/shard_map/ppermute | solution.py:403
  198.4 1.4 collective-permute-done.25
  200.1 1.0 pad_maximum_fusion.refs_7_
  201.1 1.2 copy-done.5
  202.3 17.4 %remainder_rows.1 = (bf16[1664,2048]{1,0:T(8,128)(2,1)}, f32[256,2048]{1,0:T(8,128)}) custom-call(s32[2]{0:T(128)} %pad_add_fusion.off_ref, f32[13]{0:T(128)} %select_reduce_fusion.1.w_ref, s32[1]{0:T(128)} %bitcast.5.group_ref, bf16[1664,512]{1,0:T(8,128)(2,1)} %bitcast.18, bf16[1664,512]{1,0:T(8,128)(2,1)} %copy-done.5, ...), custom_call_target="tpu_custom_call" | custom-call | flops 10468982784 | bytes 14417920 | tf_op jit(solution)/shard_map/remainder_rows/pallas_call | solution.py:348
  (90 shorter events, 6.1 us)
Async XLA Ops:
  0.6 22.3 %collective-permute-start = (bf16[3200,512]{1,0:T(8,128)(2,1)}, bf16[3200,512]{1,0:T(8,128)(2,1)}, u32[]{:S(2)}, u32[]{:S(2)}) collective-permute-start(bf16[3200,512]{1,0:T(8,128)(2,1)} %refs_0_.1), channel_id=1, source_target_pairs={{0,1},{1,0},{2,3},{3,2},{4,5},{5,4},{6,7},{7,6},{8,9},{9,8},{10,11... | collective-permute-start | bytes 9830408 | tf_op jit(solution)/shard_map/ppermute | solution.py:177
  2.2 18.1 %collective-permute-start.1 = (bf16[256,1024]{1,0:T(8,128)(2,1)S(1)}, bf16[256,1024]{1,0:T(8,128)(2,1)S(1)}, u32[]{:S(2)}, u32[]{:S(2)}) collective-permute-start(bf16[256,1024]{1,0:T(8,128)(2,1)S(1)} %slice.31), channel_id=1, source_target_pairs={{0,1},{1,0},{2,3},{3,2},{4,5},{5,4},{6,7},{7,6},{8,9},{9,8},{10,11... | collective-permute-start | bytes 1572872 | tf_op jit(solution)/shard_map/ppermute | solution.py:445
  6.3 7.9 %copy-start.3 = (s32[16,25]{1,0:T(8,128)S(1)}, s32[16,25]{1,0:T(8,128)}, u32[]{:S(2)}) copy-start(s32[16,25]{1,0:T(8,128)} %dest_ref.1) | copy-start | bytes 4804
  6.3 7.9 %copy-start.4 = (s32[16]{0:T(128)S(1)}, s32[16]{0:T(128)}, u32[]{:S(2)}) copy-start(s32[16]{0:T(128)} %cnt_ref.1) | copy-start | bytes 196
  6.3 9.0 %copy-start.6 = (bf16[25]{0:T(256)(128)(2,1)S(1)}, bf16[25]{0:T(256)(128)(2,1)}, u32[]{:S(2)}) copy-start(bf16[25]{0:T(256)(128)(2,1)} %param.7) | copy-start | bytes 154
  6.3 170.5 %all-to-all-start = ((bf16[32,128,512]{2,1,0:T(8,128)(2,1)}), bf16[32,128,512]{2,1,0:T(8,128)(2,1)}, u32[]{:S(2)}, u32[]{:S(2)}) async-start(bf16[32,128,512]{2,1,0:T(8,128)(2,1)} %pack.1), calls=%async_computation | async-start | bytes 8388608 | tf_op jit(solution)/shard_map/all_to_all | solution.py:441
  34.1 22.8 %collective-permute-start.2 = (f32[136,256]{1,0:T(8,128)S(1)}, f32[136,256]{1,0:T(8,128)S(1)}, u32[]{:S(2)}, u32[]{:S(2)}) collective-permute-start(f32[136,256]{1,0:T(8,128)S(1)} %pad_maximum_fusion.1), channel_id=1, source_target_pairs={{0,2},{2,0},{4,6},{6,4},{8,10},{10,8},{12,14},{14,12},{16,18},{18,... | collective-permute-start | bytes 417800 | tf_op jit(solution)/shard_map/ppermute | solution.py:418
  35.4 21.5 %collective-permute-start.3 = (f32[136,256]{1,0:T(8,128)S(1)}, f32[136,256]{1,0:T(8,128)S(1)}, u32[]{:S(2)}, u32[]{:S(2)}) collective-permute-start(f32[136,256]{1,0:T(8,128)S(1)} %pad_maximum_fusion.1), channel_id=1, source_target_pairs={{0,4},{2,6},{4,0},{6,2},{8,12},{10,14},{12,8},{14,10},{16,20},{18,... | collective-permute-start | bytes 417800 | tf_op jit(solution)/shard_map/ppermute | solution.py:419
  35.6 21.3 %collective-permute-start.4 = (f32[136,256]{1,0:T(8,128)S(1)}, f32[136,256]{1,0:T(8,128)S(1)}, u32[]{:S(2)}, u32[]{:S(2)}) collective-permute-start(f32[136,256]{1,0:T(8,128)S(1)} %pad_maximum_fusion.1), channel_id=1, source_target_pairs={{0,6},{2,4},{4,2},{6,0},{8,14},{10,12},{12,10},{14,8},{16,22},{18,... | collective-permute-start | bytes 417800 | tf_op jit(solution)/shard_map/ppermute | solution.py:420
  56.9 60.7 %copy-start = (f32[1024,256]{1,0:T(8,128)S(1)}, f32[1024,256]{1,0:T(8,128)}, u32[]{:S(2)}) copy-start(f32[1024,256]{1,0:T(8,128)} %column_products.2) | copy-start | bytes 3145732
  57.0 31.4 %collective-permute-start.5 = (f32[136,256]{1,0:T(8,128)S(1)}, f32[136,256]{1,0:T(8,128)S(1)}, u32[]{:S(2)}, u32[]{:S(2)}) collective-permute-start(f32[136,256]{1,0:T(8,128)S(1)} %add_add_fusion.1), channel_id=1, source_target_pairs={{0,8},{2,10},{4,12},{6,14},{8,0},{10,2},{12,4},{14,6},{16,24},{18,... | collective-permute-start | bytes 417800 | tf_op jit(solution)/shard_map/ppermute | solution.py:418
  57.0 60.5 %collective-permute-start.6 = (f32[136,256]{1,0:T(8,128)S(1)}, f32[136,256]{1,0:T(8,128)S(1)}, u32[]{:S(2)}, u32[]{:S(2)}) collective-permute-start(f32[136,256]{1,0:T(8,128)S(1)} %add_add_fusion.1), channel_id=1, source_target_pairs={{0,16},{2,18},{4,20},{6,22},{8,24},{10,26},{12,28},{14,30},{16,0},... | collective-permute-start | bytes 417800 | tf_op jit(solution)/shard_map/ppermute | solution.py:419
  57.1 60.4 %collective-permute-start.7 = (f32[136,256]{1,0:T(8,128)S(1)}, f32[136,256]{1,0:T(8,128)S(1)}, u32[]{:S(2)}, u32[]{:S(2)}) collective-permute-start(f32[136,256]{1,0:T(8,128)S(1)} %add_add_fusion.1), channel_id=1, source_target_pairs={{0,24},{2,26},{4,28},{6,30},{8,16},{10,18},{12,20},{14,22},{16,8},... | collective-permute-start | bytes 417800 | tf_op jit(solution)/shard_map/ppermute | solution.py:420
  117.6 7.3 %collective-permute-start.9 = (f32[128,256]{1,0:T(8,128)S(1)}, f32[128,256]{1,0:T(8,128)S(1)}, u32[]{:S(2)}, u32[]{:S(2)}) collective-permute-start(f32[128,256]{1,0:T(8,128)S(1)} %slice.39), channel_id=1, source_target_pairs={{0,1},{1,0},{2,3},{3,2},{4,5},{5,4},{6,7},{7,6},{8,9},{9,8},{10,11... | collective-permute-start | bytes 393224 | tf_op jit(solution)/shard_map/ppermute | solution.py:472
  117.7 32.0 %collective-permute-start.10 = (f32[512,256]{1,0:T(8,128)S(1)}, f32[512,256]{1,0:T(8,128)S(1)}, u32[]{:S(2)}, u32[]{:S(2)}) collective-permute-start(f32[512,256]{1,0:T(8,128)S(1)} %constant_dynamic-slice_fusion.7), channel_id=1, source_target_pairs={{0,2},{2,0},{4,6},{6,4},{8,10},{10,8},{12,14},{14,12},{16,18},{18,... | collective-permute-start | bytes 1572872 | tf_op jit(solution)/shard_map/ppermute | solution.py:394
  121.9 28.0 %collective-permute-start.14 = (f32[512,256]{1,0:T(8,128)S(1)}, f32[512,256]{1,0:T(8,128)S(1)}, u32[]{:S(2)}, u32[]{:S(2)}) collective-permute-start(f32[512,256]{1,0:T(8,128)S(1)} %constant_dynamic-slice_fusion.3), channel_id=1, source_target_pairs={{0,4},{2,6},{4,0},{6,2},{8,12},{10,14},{12,8},{14,10},{16,20},{18,... | collective-permute-start | bytes 1572872 | tf_op jit(solution)/shard_map/ppermute | solution.py:394
  125.6 24.3 %copy-start.1 = (f32[1024,256]{1,0:T(8,128)S(1)}, f32[1024,256]{1,0:T(8,128)}, u32[]{:S(2)}) copy-start(f32[1024,256]{1,0:T(8,128)} %column_products.3) | copy-start | bytes 3145732
  149.7 23.1 %copy-start.2 = (f32[256,256]{1,0:T(8,128)S(1)}, f32[256,256]{1,0:T(8,128)}, u32[]{:S(2)}) copy-start(f32[256,256]{1,0:T(8,128)} %factor.1.refs_6_) | copy-start | bytes 786436
  149.8 8.5 %collective-permute-start.11 = (f32[256,256]{1,0:T(8,128)S(1)}, f32[256,256]{1,0:T(8,128)S(1)}, u32[]{:S(2)}, u32[]{:S(2)}) collective-permute-start(f32[256,256]{1,0:T(8,128)S(1)} %constant_dynamic-slice_fusion.6), channel_id=1, source_target_pairs={{0,4},{2,6},{4,0},{6,2},{8,12},{10,14},{12,8},{14,10},{16,20},{18,... | collective-permute-start | bytes 786440 | tf_op jit(solution)/shard_map/ppermute | solution.py:394
  150.0 10.9 %collective-permute-start.15 = (f32[256,256]{1,0:T(8,128)S(1)}, f32[256,256]{1,0:T(8,128)S(1)}, u32[]{:S(2)}, u32[]{:S(2)}) collective-permute-start(f32[256,256]{1,0:T(8,128)S(1)} %constant_dynamic-slice_fusion.2), channel_id=1, source_target_pairs={{0,2},{2,0},{4,6},{6,4},{8,10},{10,8},{12,14},{14,12},{16,18},{18,... | collective-permute-start | bytes 786440 | tf_op jit(solution)/shard_map/ppermute | solution.py:394
  158.3 6.8 %collective-permute-start.12 = (f32[128,256]{1,0:T(8,128)S(1)}, f32[128,256]{1,0:T(8,128)S(1)}, u32[]{:S(2)}, u32[]{:S(2)}) collective-permute-start(f32[128,256]{1,0:T(8,128)S(1)} %constant_dynamic-slice_fusion.5), channel_id=1, source_target_pairs={{0,8},{2,10},{4,12},{6,14},{8,0},{10,2},{12,4},{14,6},{16,24},{18,... | collective-permute-start | bytes 393224 | tf_op jit(solution)/shard_map/ppermute | solution.py:394
  161.0 6.5 %collective-permute-start.16 = (f32[128,256]{1,0:T(8,128)S(1)}, f32[128,256]{1,0:T(8,128)S(1)}, u32[]{:S(2)}, u32[]{:S(2)}) collective-permute-start(f32[128,256]{1,0:T(8,128)S(1)} %constant_dynamic-slice_fusion.1), channel_id=1, source_target_pairs={{0,8},{2,10},{4,12},{6,14},{8,0},{10,2},{12,4},{14,6},{16,24},{18,... | collective-permute-start | bytes 393224 | tf_op jit(solution)/shard_map/ppermute | solution.py:394
  165.2 6.2 %collective-permute-start.13 = (f32[64,256]{1,0:T(8,128)S(1)}, f32[64,256]{1,0:T(8,128)S(1)}, u32[]{:S(2)}, u32[]{:S(2)}) collective-permute-start(f32[64,256]{1,0:T(8,128)S(1)} %constant_dynamic-slice_fusion.4), channel_id=1, source_target_pairs={{0,16},{2,18},{4,20},{6,22},{8,24},{10,26},{12,28},{14,30},{16,0},... | collective-permute-start | bytes 196616 | tf_op jit(solution)/shard_map/ppermute | solution.py:394
  167.5 5.3 %collective-permute-start.17 = (f32[64,256]{1,0:T(8,128)S(1)}, f32[64,256]{1,0:T(8,128)S(1)}, u32[]{:S(2)}, u32[]{:S(2)}) collective-permute-start(f32[64,256]{1,0:T(8,128)S(1)} %constant_dynamic-slice_fusion), channel_id=1, source_target_pairs={{0,16},{2,18},{4,20},{6,22},{8,24},{10,26},{12,28},{14,30},{16,0},... | collective-permute-start | bytes 196616 | tf_op jit(solution)/shard_map/ppermute | solution.py:394
  173.2 7.2 %collective-permute-start.18 = (bf16[64,256]{1,0:T(8,128)(2,1)S(1)}, bf16[64,256]{1,0:T(8,128)(2,1)S(1)}, u32[]{:S(2)}, u32[]{:S(2)}) collective-permute-start(bf16[64,256]{1,0:T(8,128)(2,1)S(1)} %get-tuple-element.14), channel_id=1, source_target_pairs={{0,16},{2,18},{4,20},{6,22},{8,24},{10,26},{12,28},{14,30},{16,0},... | collective-permute-start | bytes 98312 | tf_op jit(solution)/shard_map/ppermute | solution.py:403
  175.3 6.9 %collective-permute-start.22 = (bf16[64,256]{1,0:T(8,128)(2,1)S(1)}, bf16[64,256]{1,0:T(8,128)(2,1)S(1)}, u32[]{:S(2)}, u32[]{:S(2)}) collective-permute-start(bf16[64,256]{1,0:T(8,128)(2,1)S(1)} %get-tuple-element.15), channel_id=1, source_target_pairs={{0,16},{2,18},{4,20},{6,22},{8,24},{10,26},{12,28},{14,30},{16,0},... | collective-permute-start | bytes 98312 | tf_op jit(solution)/shard_map/ppermute | solution.py:403
  180.3 20.8 %collective-permute-start.8 = (bf16[1664,512]{1,0:T(8,128)(2,1)}, bf16[1664,512]{1,0:T(8,128)(2,1)S(1)}, u32[]{:S(2)}, u32[]{:S(2)}) collective-permute-start(bf16[1664,512]{1,0:T(8,128)(2,1)} %bitcast.17), channel_id=1, source_target_pairs={{0,1},{1,0},{2,3},{3,2},{4,5},{5,4},{6,7},{7,6},{8,9},{9,8},{10,11... | collective-permute-start | bytes 5111816 | tf_op jit(solution)/shard_map/ppermute | solution.py:177
  180.4 4.5 %collective-permute-start.19 = (bf16[128,256]{1,0:T(8,128)(2,1)S(1)}, bf16[128,256]{1,0:T(8,128)(2,1)S(1)}, u32[]{:S(2)}, u32[]{:S(2)}) collective-permute-start(bf16[128,256]{1,0:T(8,128)(2,1)S(1)} %maximum_select_fusion.7), channel_id=1, source_target_pairs={{0,8},{2,10},{4,12},{6,14},{8,0},{10,2},{12,4},{14,6},{16,24},{18,... | collective-permute-start | bytes 196616 | tf_op jit(solution)/shard_map/ppermute | solution.py:403
  182.2 4.3 %collective-permute-start.23 = (bf16[128,256]{1,0:T(8,128)(2,1)S(1)}, bf16[128,256]{1,0:T(8,128)(2,1)S(1)}, u32[]{:S(2)}, u32[]{:S(2)}) collective-permute-start(bf16[128,256]{1,0:T(8,128)(2,1)S(1)} %maximum_select_fusion.8), channel_id=1, source_target_pairs={{0,8},{2,10},{4,12},{6,14},{8,0},{10,2},{12,4},{14,6},{16,24},{18,... | collective-permute-start | bytes 196616 | tf_op jit(solution)/shard_map/ppermute | solution.py:403
  185.0 5.2 %collective-permute-start.20 = (bf16[256,256]{1,0:T(8,128)(2,1)S(1)}, bf16[256,256]{1,0:T(8,128)(2,1)S(1)}, u32[]{:S(2)}, u32[]{:S(2)}) collective-permute-start(bf16[256,256]{1,0:T(8,128)(2,1)S(1)} %maximum_select_fusion.5), channel_id=1, source_target_pairs={{0,4},{2,6},{4,0},{6,2},{8,12},{10,14},{12,8},{14,10},{16,20},{18,... | collective-permute-start | bytes 393224 | tf_op jit(solution)/shard_map/ppermute | solution.py:403
  186.6 6.1 %collective-permute-start.24 = (bf16[256,256]{1,0:T(8,128)(2,1)S(1)}, bf16[256,256]{1,0:T(8,128)(2,1)S(1)}, u32[]{:S(2)}, u32[]{:S(2)}) collective-permute-start(bf16[256,256]{1,0:T(8,128)(2,1)S(1)} %maximum_select_fusion.6), channel_id=1, source_target_pairs={{0,2},{2,0},{4,6},{6,4},{8,10},{10,8},{12,14},{14,12},{16,18},{18,... | collective-permute-start | bytes 393224 | tf_op jit(solution)/shard_map/ppermute | solution.py:403
  190.3 7.9 %collective-permute-start.21 = (bf16[512,256]{1,0:T(8,128)(2,1)S(1)}, bf16[512,256]{1,0:T(8,128)(2,1)S(1)}, u32[]{:S(2)}, u32[]{:S(2)}) collective-permute-start(bf16[512,256]{1,0:T(8,128)(2,1)S(1)} %maximum_select_fusion.3), channel_id=1, source_target_pairs={{0,2},{2,0},{4,6},{6,4},{8,10},{10,8},{12,14},{14,12},{16,18},{18,... | collective-permute-start | bytes 786440 | tf_op jit(solution)/shard_map/ppermute | solution.py:403
  192.8 7.0 %collective-permute-start.25 = (bf16[512,256]{1,0:T(8,128)(2,1)S(1)}, bf16[512,256]{1,0:T(8,128)(2,1)S(1)}, u32[]{:S(2)}, u32[]{:S(2)}) collective-permute-start(bf16[512,256]{1,0:T(8,128)(2,1)S(1)} %maximum_select_fusion.4), channel_id=1, source_target_pairs={{0,4},{2,6},{4,0},{6,2},{8,12},{10,14},{12,8},{14,10},{16,20},{18,... | collective-permute-start | bytes 786440 | tf_op jit(solution)/shard_map/ppermute | solution.py:403
  201.1 1.2 copy-start.5

commit v3 on v2

v3 whole, which is shorter than its diff:
```python
import functools
import math

import jax
import jax.numpy as jnp
from jax import lax
from jax.experimental import pallas as pl
from jax.experimental.pallas import tpu as pltpu
from jax.sharding import PartitionSpec as P

PANEL = 256
BLK = 128
DST_BLK = 13
EPSILON = 1e-06
VMEM_LIMIT = 56 * 1024 * 1024
HIGH = lax.Precision.HIGHEST
ANY = pl.BlockSpec(memory_space=pl.ANY)
VMEM = pl.BlockSpec(memory_space=pltpu.VMEM)
SMEM = pl.BlockSpec(memory_space=pltpu.SMEM)


def params(**kw):
    return pltpu.CompilerParams(vmem_limit_bytes=VMEM_LIMIT, **kw)


def cost(flops, nbytes):
    return pl.CostEstimate(flops=int(flops), bytes_accessed=int(nbytes), transcendentals=0)


def dot(a, b, ca, cb, precision=None):
    return lax.dot_general(
        a, b, (((ca,), (cb,)), ((), ())), preferred_element_type=jnp.float32, precision=precision
    )


def nt(a, b, precision=None):
    return dot(a, b, 1, 1, precision)


def nn(a, b, precision=None):
    return dot(a, b, 1, 0, precision)


def tn(a, b, precision=None):
    return dot(a, b, 0, 0, precision)


def split(x):
    high = x.astype(jnp.bfloat16)
    return high, (x - high.astype(jnp.float32)).astype(jnp.bfloat16)


def pack_kernel(per_pair, me_ref, dest_ref, cnt_ref, desc_ref, out_ref, ctr_ref, sems):
    slots = desc_ref.shape[0]
    owners = ctr_ref.shape[0]
    me = me_ref[0]
    count = cnt_ref[me]

    @pl.loop(0, owners)
    def _(i):
        ctr_ref[i] = 0

    @pl.loop(0, slots)
    def _(j):
        @pl.when(j < count)
        def _():
            d = dest_ref[me, j]
            r = ctr_ref[d]
            ctr_ref[d] = r + 1
            slot = d * per_pair + r
            pltpu.make_async_copy(desc_ref.at[j], out_ref.at[slot], sems.at[j]).start()

    @pl.loop(0, slots)
    def _(j):
        @pl.when(j < count)
        def _():
            pltpu.make_async_copy(desc_ref.at[0], out_ref.at[0], sems.at[j]).wait()


def pack(desc_blocks, me, destinations, counts, per_pair):
    slots, blk, feat = desc_blocks.shape
    owners = destinations.shape[0]
    return pl.pallas_call(
        functools.partial(pack_kernel, per_pair),
        out_shape=jax.ShapeDtypeStruct((owners * per_pair, blk, feat), desc_blocks.dtype),
        in_specs=[SMEM, SMEM, SMEM, VMEM],
        out_specs=ANY,
        scratch_shapes=[pltpu.SMEM((owners,), jnp.int32), pltpu.SemaphoreType.DMA((slots,))],
        compiler_params=params(),
        cost_estimate=cost(0, 4 * slots * blk * feat),
        name="pack",
    )(me, destinations, counts, desc_blocks)


def select_kernel(pos_ref, recv_ref, out_ref, sems):
    copies = [
        pltpu.make_async_copy(recv_ref.at[pos_ref[p]], out_ref.at[p], sems.at[p])
        for p in range(DST_BLK)
    ]
    for c in copies:
        c.start()
    for c in copies:
        c.wait()


def select(received, positions):
    _, blk, feat = received.shape
    return pl.pallas_call(
        select_kernel,
        out_shape=jax.ShapeDtypeStruct((DST_BLK, blk, feat), received.dtype),
        in_specs=[SMEM, ANY],
        out_specs=VMEM,
        scratch_shapes=[pltpu.SemaphoreType.DMA((DST_BLK,))],
        compiler_params=params(),
        cost_estimate=cost(0, 4 * DST_BLK * blk * feat),
        name="select",
    )(positions, received)


def small_factor(a):
    n = a.shape[0]
    row = lax.broadcasted_iota(jnp.int32, (n, 1), 0)
    eye = lax.broadcasted_iota(jnp.int32, (n, n), 0) == lax.broadcasted_iota(jnp.int32, (n, n), 1)
    m = jnp.concatenate([a, eye.astype(jnp.float32)], axis=1)
    out = []
    for j in range(0, n, 2):
        r0 = m[j : j + 1, :]
        r1 = m[j + 1 : j + 2, :]
        p = r0[:, j : j + 1]
        q = r0[:, j + 1 : j + 2]
        s = r1[:, j + 1 : j + 2]
        det = p * s - q * q
        out.append(r0[:, n:] * lax.rsqrt(p))
        out.append((r1[:, n:] - (q / p) * r0[:, n:]) * lax.rsqrt(det / p))
        if j + 2 < n:
            inv = 1.0 / det
            g0 = (s * r0 - q * r1) * inv
            g1 = (p * r1 - q * r0) * inv
            c0 = jnp.where(row > j + 1, m[:, j : j + 1], 0.0)
            c1 = jnp.where(row > j + 1, m[:, j + 1 : j + 2], 0.0)
            m = m - c0 * g0 - c1 * g1
    return out


def factor_kernel(leaf, gram_ref, x_ref, a_ref):
    n = gram_ref.shape[0]
    a_ref[...] = gram_ref[...]
    x_ref[...] = jnp.zeros_like(x_ref)
    for k in range(0, n, leaf):
        e = k + leaf
        for i, r in enumerate(small_factor(a_ref[k:e, k:e])):
            x_ref[k + i : k + i + 1, k:e] = r
        xk = x_ref[k:e, k:e]
        if e < n:
            t = nn(xk, a_ref[k:e, e:], HIGH)
            a_ref[k:e, e:] = t
            a_ref[e:, e:] -= tn(t, t, HIGH)
        if k > 0:
            x_ref[k:e, :k] = -nn(xk, tn(a_ref[:k, k:e], x_ref[:k, :k], HIGH), HIGH)


def factor(gram):
    n = gram.shape[0]
    return pl.pallas_call(
        functools.partial(factor_kernel, 64),
        out_shape=jax.ShapeDtypeStruct((n, n), jnp.float32),
        scratch_shapes=[pltpu.VMEM((n, n), jnp.float32)],
        compiler_params=params(),
        cost_estimate=cost(2e10, 8 * n * n),
        name="factor",
    )(gram)


def share_parts(x):
    groups = lax.axis_size("cols")
    if groups == 2:
        peer = lax.ppermute(x, "cols", [(0, 1), (1, 0)])
        return [x, peer]
    full = lax.all_gather(x, "cols", axis=0, tiled=False)
    return [full[i] for i in range(groups)]


def part_offsets(feat):
    groups = lax.axis_size("cols")
    if groups == 2:
        c = lax.axis_index("cols")
        return jnp.stack([c * feat, (1 - c) * feat]).astype(jnp.int32)
    return jnp.arange(groups, dtype=jnp.int32) * feat


def join_copies(parts, off_ref, x_ref, sems, spans):
    feat = parts[0].shape[1]
    return [
        [
            pltpu.make_async_copy(
                ref.at[pl.ds(start, size)],
                x_ref.at[pl.ds(start, size), pl.ds(pl.multiple_of(off_ref[i], 128), feat)],
                sems.at[t, i],
            )
            for i, ref in enumerate(parts)
        ]
        for t, (start, size) in enumerate(spans)
    ]


def row_scale(x, weight):
    x = x.astype(jnp.float32)
    return weight / (jnp.sum(x * x, axis=1, keepdims=True) / x.shape[1] + EPSILON)


def column_scale(s):
    s = s.astype(jnp.float32)
    width = s.shape[1]
    scale = 1.0 / (width * (jnp.sum(s * s, axis=1, keepdims=True) / width + EPSILON))
    return jnp.broadcast_to(scale, (s.shape[0], 128)).T[:1, :]


def row_tiles(rows):
    blocks = rows // BLK
    per = 5 if blocks % 5 == 0 else 1
    return per, [(i * BLK, per * BLK) for i in range(0, blocks, per)]


def panel_kernel(nparts, cnt_ref, off_ref, w_ref, *refs):
    parts = refs[:nparts]
    sp_ref, gram_ref, pw_ref, x_ref, sems = refs[nparts:]
    per, tiles = row_tiles(x_ref.shape[0])
    count = cnt_ref[0]
    copies = join_copies(parts, off_ref, x_ref, sems, tiles)
    for group in copies:
        for c in group:
            c.start()
    gram_ref[...] = jnp.zeros_like(gram_ref)
    pw_ref[...] = jnp.zeros_like(pw_ref)
    points = column_scale(sp_ref[...])
    for t, (start, size) in enumerate(tiles):
        for c in copies[t]:
            c.wait()

        @pl.when(t * per < count)
        def _():
            scales = []
            for b in range(per):
                j = t * per + b
                w = jnp.where(j < count, w_ref[j], 0.0)
                scales.append(row_scale(x_ref[j * BLK : (j + 1) * BLK, :], w))
            scale = jnp.concatenate(scales, axis=0)
            inner = nt(x_ref[start : start + size, :], sp_ref[...])
            panel = (inner * inner * scale * points).astype(jnp.bfloat16)
            gram_ref[...] += tn(panel, panel)
            pw_ref[start : start + size, :] = (panel.astype(jnp.float32) * scale).astype(
                jnp.bfloat16
            )


def panel_products(parts, offsets, count, weights, sp):
    rows, feat = parts[0].shape
    width = sp.shape[1]
    tiles = len(row_tiles(rows)[1])
    return pl.pallas_call(
        functools.partial(panel_kernel, len(parts)),
        out_shape=(
            jax.ShapeDtypeStruct((PANEL, PANEL), jnp.float32),
            jax.ShapeDtypeStruct((rows, PANEL), jnp.bfloat16),
        ),
        in_specs=[SMEM, SMEM, SMEM] + [ANY] * len(parts) + [VMEM],
        out_specs=(VMEM, VMEM),
        scratch_shapes=[
            pltpu.VMEM((rows, width), jnp.bfloat16),
            pltpu.SemaphoreType.DMA((tiles, len(parts))),
        ],
        compiler_params=params(),
        cost_estimate=cost(2 * rows * PANEL * (width + PANEL), 2 * rows * width),
        name="panel_products",
    )(count, offsets, weights, *parts, sp)


def column_kernel(nparts, off_ref, *refs):
    parts = refs[:nparts]
    pw_ref, s_ref, g_ref, x_ref, sems = refs[nparts:]
    width = x_ref.shape[1]

    @pl.when(pl.program_id(0) == 0)
    def _():
        copies = join_copies(parts, off_ref, x_ref, sems, row_tiles(x_ref.shape[0])[1])
        for group in copies:
            for c in group:
                c.start()
        for group in copies:
            for c in group:
                c.wait()

    s = s_ref[...]
    inner = nt(s, x_ref[...])
    products = nn((inner * inner).astype(jnp.bfloat16), pw_ref[...])
    wide = s.astype(jnp.float32)
    square = jnp.sum(wide * wide, axis=1, keepdims=True) / width + EPSILON
    g_ref[...] = products / (width * square)


def column_products(parts, offsets, pw, s, start, size):
    rows, feat = parts[0].shape
    width = s.shape[1]
    chunk = min(512, size)
    first = start // chunk
    tiles = len(row_tiles(rows)[1])
    once = pl.Buffered(1)
    return pl.pallas_call(
        functools.partial(column_kernel, len(parts)),
        grid=(size // chunk,),
        out_shape=jax.ShapeDtypeStruct((size, PANEL), jnp.float32),
        in_specs=[SMEM]
        + [ANY] * len(parts)
        + [
            pl.BlockSpec((rows, PANEL), lambda i: (0, 0), pipeline_mode=once),
            pl.BlockSpec((chunk, width), lambda i: (first + i, 0)),
        ],
        out_specs=pl.BlockSpec((chunk, PANEL), lambda i: (i, 0)),
        scratch_shapes=[
            pltpu.VMEM((rows, width), jnp.bfloat16),
            pltpu.SemaphoreType.DMA((tiles, len(parts))),
        ],
        compiler_params=params(dimension_semantics=("arbitrary",)),
        cost_estimate=cost(2 * rows * (width + PANEL) * size, 2 * rows * width),
        name="column_products",
    )(offsets, *parts, pw, s)


def remainder_kernel(nparts, norm, quarter_ref, off_ref, w_ref, group_ref, *refs):
    parts = refs[:nparts]
    sp_ref, s_ref, inv_ref, rt_ref, out_ref, proj_ref, x_ref, p_ref, rs_ref, sems = refs[nparts:]
    rows_all, width = x_ref.shape
    chunk = s_ref.shape[0]
    step = pl.program_id(0)
    blocks = rows_all // BLK
    bounds = list(range(0, blocks, 7)) + [blocks]
    spans = [(a * BLK, b * BLK) for a, b in zip(bounds, bounds[1:])]

    @pl.when(step == 0)
    def _():
        copies = join_copies(parts, off_ref, x_ref, sems, [(a, b - a) for a, b in spans])
        for group in copies:
            for c in group:
                c.start()
        points = column_scale(sp_ref[...])
        for (a, b), group in zip(spans, copies):
            for c in group:
                c.wait()
            for j in range(a // BLK, b // BLK):
                scale = row_scale(x_ref[j * BLK : (j + 1) * BLK, :], w_ref[j])
                rs_ref[j * BLK : (j + 1) * BLK, :] = jnp.broadcast_to(scale, (BLK, 128))
            inner = nt(x_ref[a:b, :], sp_ref[...])
            scale = jnp.concatenate([rs_ref[a:b, :]] * (PANEL // 128), axis=1)
            p_ref[a:b, :] = (inner * inner * scale * points).astype(jnp.bfloat16)

    inv_high, inv_low = split(inv_ref[...])
    rt = rt_ref[0]
    coef = (nn(rt, inv_high) + nn(rt, inv_low)).astype(jnp.bfloat16)
    proj_ref[...] = rt.astype(jnp.float32).T * (1.0 / norm)
    columns = column_scale(s_ref[...])
    for a, b in spans:
        inner = nt(x_ref[a:b, :], s_ref[...])
        scale = jnp.concatenate([rs_ref[a:b, :]] * (chunk // 128), axis=1)
        kern = (inner * inner * scale * columns).astype(jnp.bfloat16)
        fit = nt(p_ref[a:b, :], coef)
        out_ref[a:b, :] = (kern.astype(jnp.float32) - fit).astype(out_ref.dtype)

    for i in range(-(-PANEL // chunk)):
        part = min(chunk, PANEL)

        @pl.when((step == i) & (group_ref[0] == 0))
        def _():
            for a, b in spans:
                panel = p_ref[a:b, :]
                rows = slice(i * part, (i + 1) * part)
                basis = nt(panel, inv_high[rows, :]) + nt(panel, inv_low[rows, :])
                out_ref[a:b, :part] = (basis * norm).astype(out_ref.dtype)


def remainder_rows(parts, offsets, weights, group, quarter, sp, s, inverse, rt, norm):
    rows, feat = parts[0].shape
    cols, width = s.shape
    chunk = rt.shape[1]
    once = pl.Buffered(1)
    spec = pltpu.PrefetchScalarGridSpec(
        num_scalar_prefetch=1,
        grid=(cols // chunk,),
        in_specs=[SMEM, SMEM, SMEM]
        + [ANY] * len(parts)
        + [
            pl.BlockSpec((PANEL, width), lambda i, q: (0, 0), pipeline_mode=once),
            pl.BlockSpec((chunk, width), lambda i, q: (i, 0)),
            pl.BlockSpec((PANEL, PANEL), lambda i, q: (0, 0), pipeline_mode=once),
            pl.BlockSpec((1, chunk, PANEL), lambda i, q: (i ^ q[0], 0, 0)),
        ],
        out_specs=(
            pl.BlockSpec((rows, chunk), lambda i, q: (0, i)),
            pl.BlockSpec((PANEL, chunk), lambda i, q: (0, i)),
        ),
        scratch_shapes=[
            pltpu.VMEM((rows, width), jnp.bfloat16),
            pltpu.VMEM((rows, PANEL), jnp.bfloat16),
            pltpu.VMEM((rows, 128), jnp.float32),
            pltpu.SemaphoreType.DMA((2, len(parts))),
        ],
    )
    return pl.pallas_call(
        functools.partial(remainder_kernel, len(parts), norm),
        grid_spec=spec,
        out_shape=(
            jax.ShapeDtypeStruct((rows, cols), jnp.bfloat16),
            jax.ShapeDtypeStruct((PANEL, cols), jnp.float32),
        ),
        compiler_params=params(dimension_semantics=("arbitrary",)),
        cost_estimate=cost(
            2 * rows * (width + 2 * PANEL) * cols, 2 * rows * width + 2 * cols * width + 2 * rows * cols
        ),
        name="remainder_rows",
    )(quarter, offsets, weights, group, *parts, sp, s, inverse, rt)


def flips(bit, size):
    return [(i, i ^ bit) for i in range(size)]


def quarter_of(pair):
    me = lax.axis_index("rows").astype(jnp.int32)
    return (me // pair[0]) % 2 + 2 * ((me // pair[1]) % 2)


def trade(x, pair, k):
    bit = pair[0] * (k & 1) + pair[1] * (k >> 1)
    return lax.ppermute(x, "rows", flips(bit, lax.axis_size("rows")))


def scatter_sum(x, pair):
    n = x.shape[0] // 4
    q = quarter_of(pair)
    pieces = [lax.dynamic_slice_in_dim(x, (q ^ k) * n, n, 0) for k in range(4)]
    got = [pieces[0]] + [trade(pieces[k], pair, k) for k in range(1, 4)]
    return (got[0] + got[1]) + (got[2] + got[3])


def gather_pieces(x, pair):
    return [x] + [trade(x, pair, k) for k in range(1, 4)]


def gather_back(x, pair):
    n = x.shape[0]
    q = quarter_of(pair)
    pieces = gather_pieces(x, pair)
    return jnp.concatenate(
        [lax.select_n(q ^ i, *pieces) for i in range(4)], 0
    )


def pair_sum(x, pair):
    got = gather_pieces(x, pair)
    return (got[0] + got[1]) + (got[2] + got[3])


def on_device(descriptors, sparse_points, block_weights, block_counts, destinations):
    owners = lax.axis_size("rows")
    groups = lax.axis_size("cols")
    me = lax.axis_index("rows").astype(jnp.int32)
    group = lax.axis_index("cols").astype(jnp.int32)
    slots = block_weights.shape[0]
    per_pair = -(-slots // owners)
    feat = descriptors.shape[1]
    cols, width = sparse_points.shape
    norm = math.sqrt(owners * DST_BLK * BLK)
    pairs = [(1 << i, 2 << i) for i in range(0, owners.bit_length() - 1, 2)]

    first = sparse_points[:PANEL]
    source_parts = share_parts(descriptors)
    if groups == 2:
        moved = lax.ppermute(first, "cols", [(0, 1), (1, 0)])
        panel_points = jnp.where(group == 0, first, moved)
    else:
        panel_points = lax.all_gather(first, "cols", axis=0, tiled=False)[0]
    desc_blocks = descriptors.reshape(slots, BLK, feat)
    outgoing = pack(desc_blocks, me[None], destinations, block_counts, per_pair)
    received = lax.all_to_all(outgoing, "rows", split_axis=0, concat_axis=0, tiled=True)

    offsets = part_offsets(feat)
    count = lax.dynamic_index_in_dim(block_counts, me, 0)
    weights32 = block_weights.astype(jnp.float32)
    gram_part, pw = panel_products(source_parts, offsets, count, weights32, panel_points)
    half = cols // 2
    low = column_products(source_parts, offsets, pw, sparse_points, 0, half)

    spare = -(-owners * slots // (PANEL * 8)) * 8
    table = lax.dynamic_update_slice(
        jnp.zeros((spare * PANEL,), jnp.float32), weights32, (me * slots,)
    ).reshape(spare, PANEL)
    if groups == 2:
        gram_part = lax.dynamic_slice_in_dim(gram_part, group * (PANEL // 2), PANEL // 2, 0)
    summed = pair_sum(jnp.concatenate([gram_part, table], 0), pairs[0])
    pw, summed = lax.optimization_barrier((pw, summed))
    high = column_products(source_parts, offsets, pw, sparse_points, half, half)
    for pair in pairs[1:]:
        summed = pair_sum(summed, pair)
    gram, table = summed[:-spare], summed[-spare:]
    if groups == 2:
        other = lax.ppermute(gram, "cols", [(0, 1), (1, 0)])
        gram = jnp.where(
            group == 0, jnp.concatenate([gram, other], 0), jnp.concatenate([other, gram], 0)
        )
    all_weights = table.reshape(-1)[: owners * slots]
    inverse = factor(gram)

    g = jnp.concatenate([low, high], 0)
    for pair in pairs:
        g = scatter_sum(g, pair)
    rt = nt(g, inverse, HIGH).astype(jnp.bfloat16)
    for pair in pairs[:0:-1]:
        rt = gather_back(rt, pair)
    slot_ids = jnp.arange(slots, dtype=jnp.int32)
    toward = ((slot_ids[None, :] < block_counts[:, None]) & (destinations == me)).astype(jnp.int32)
    rank = jnp.cumsum(toward, axis=1) - toward
    flat = toward.reshape(-1)
    place = jnp.cumsum(flat) - flat
    where_from = (jnp.arange(owners, dtype=jnp.int32)[:, None] * per_pair + rank).reshape(-1)
    hit = (flat[None, :] == 1) & (place[None, :] == jnp.arange(DST_BLK, dtype=jnp.int32)[:, None])
    positions = jnp.sum(jnp.where(hit, where_from[None, :], 0), axis=1)
    weights_here = jnp.sum(jnp.where(hit, all_weights[None, :], 0.0), axis=1)

    rt, positions = lax.optimization_barrier((rt, positions))
    rt = jnp.stack(gather_pieces(rt, pairs[0]))
    arrived = select(received, positions).reshape(DST_BLK * BLK, feat)
    remainder, projected = remainder_rows(
        share_parts(arrived),
        offsets,
        weights_here,
        group[None],
        quarter_of(pairs[0])[None],
        panel_points,
        sparse_points,
        inverse,
        rt,
        norm,
    )
    return (projected, remainder)


def solution(mesh):
    return jax.shard_map(
        on_device,
        mesh=mesh,
        in_specs=(P("rows", "cols"), P("cols", None), P("rows"), P(), P()),
        out_specs=(P(None, "cols"), P("rows", "cols")),
        check_vma=False,
    )
```

time: 220 us -> 211 us (0.959)
  Pallas kernels: 97.8 us -> 88.8 us
  starting transfers between devices: 42.1 us -> 45.4 us
  other arithmetic: 12.4 us -> 9.23 us
    pallas_call x3, Pallas kernels: 48.9 us -> 39.6 us  [the longest x2 30.3 us: column_products(): pl.pallas_call(functools.partial(column_kernel, len(parts)), grid=(size /...]
    dot_general x2 -> x0, other arithmetic: 5.08 us -> none  [column_scale(): jnp.einsum('mf,mf->m', points, points, preferred_element_type=jnp.float32)]
    ppermute x23 -> x19, starting transfers between devices: 33.5 us -> 36.5 us  [the longest x18 36.5 us: trade(): return lax.ppermute(x, 'rows', flips(bit, lax.axis_size('rows')))]
    ppermute x23 -> x19, waiting for transfers between devices: 60.6 us -> 59.2 us  [the longest x18 57.9 us: trade(): return lax.ppermute(x, 'rows', flips(bit, lax.axis_size('rows')))]
  transfers between devices with their start and end apart: 27 -> 23, of which waited for: 12 -> 9; matrix products, arithmetic and copies ran while one was open for 8% -> 7% of each run, Pallas kernels for 37% -> 32%
where the time goes in v3:
time: 211 us; the launch traced here: 209 us
  Pallas kernels  88.8 us (42%)
  waiting for transfers between devices  59.2 us (28%)
  starting transfers between devices  45.4 us (22%)
  other arithmetic  9.23 us (4%)
  local copies, waits for them, and re-layouts  4.29 us (2%)
    ppermute x18, waiting for transfers between devices, trade(): return lax.ppermute(x, 'rows', flips(bit, lax.axis_size('rows')))  57.9 us
    ppermute x18, starting transfers between devices, trade(): return lax.ppermute(x, 'rows', flips(bit, lax.axis_size('rows')))  36.5 us
    pallas_call x2, Pallas kernels, column_products(): pl.pallas_call(functools.partial(column_kernel, len(parts)), grid=(size /...  30.3 us
    pallas_call x1, Pallas kernels, factor(): pl.pallas_call(functools.partial(factor_kernel, 64), out_shape=jax.ShapeD...  24 us
    pallas_call x1, Pallas kernels, remainder_rows(): pl.pallas_call(functools.partial(remainder_kernel, len(parts), norm), gri...  17.9 us
    pallas_call x1, Pallas kernels, panel_products(): pl.pallas_call(functools.partial(panel_kernel, len(parts)), out_shape=(ja...  9.31 us
    all_to_all x1, starting transfers between devices, on_device(): lax.all_to_all(outgoing, 'rows', split_axis=0, concat_axis=0, tiled=True)  8 us
  transfers between devices with their start and end apart: 23, of which 9 were waited for; matrix products, arithmetic and copies ran while one was open for 7% of the time, Pallas kernels for 32%

profile of v3, /device:TPU:0, one launch (start us, length us, event | category | flops | bytes accessed | tf_op | source)
XLA Modules:
  0.0 209.4 jit_solution(1250920441810260341)
XLA Ops:
  0.6 0.5 collective-permute-start
  1.1 3.8 %pack.1 = bf16[32,128,512]{2,1,0:T(8,128)(2,1)} custom-call(s32[1]{0:T(128)} %bitcast.6.me_ref, s32[16,25]{1,0:T(8,128)} %dest_ref.1, s32[16]{0:T(128)} %cnt_ref.1, bf16[25,128,512]{2,1,0:T(8,128)(2,1)} %bitcast.19), custom_call_target="tpu_custom_call" | custom-call | bytes 6553600 | tf_op jit(solution)/shard_map/pack/pallas_call | solution.py:83
  5.0 8.0 %all-to-all-start = ((bf16[32,128,512]{2,1,0:T(8,128)(2,1)}), bf16[32,128,512]{2,1,0:T(8,128)(2,1)}, u32[]{:S(2)}, u32[]{:S(2)}) async-start(bf16[32,128,512]{2,1,0:T(8,128)(2,1)} %pack.1), calls=%async_computation | async-start | bytes 8388608 | tf_op jit(solution)/shard_map/all_to_all | solution.py:483
  13.0 1.1 slice.25
  14.1 0.3 collective-permute-start.1
  14.5 0.2 reduce_window_sum.28
  14.7 0.6 dynamic_slice.31.cnt_ref
  15.3 0.6 convert_element_type.10.w_ref
  16.1 0.3 reduce-window.9
  16.6 0.1 slice_reduce_fusion
  16.8 0.6 pad_add_fusion.off_ref
  17.4 1.9 broadcast_select_fusion.refs_2_
  19.3 9.3 %panel_products.1 = (f32[256,256]{1,0:T(8,128)}, bf16[3200,256]{1,0:T(8,128)(2,1)}) custom-call(s32[1]{0:T(128)} %dynamic_slice.31.cnt_ref, s32[2]{0:T(128)} %pad_add_fusion.off_ref, f32[25]{0:T(128)} %convert_element_type.10.w_ref, bf16[3200,512]{1,0:T(8,128)(2,1)} %refs_0_.5, bf16[3200,512]{1,0:T(8,128)(2,1)} %collective-permute-done.refs_1_, ...), custom_call_target="tpu_custom_call" | custom-call | flops 2097152000 | bytes 6553600 | tf_op jit(solution)/shard_map/panel_products/pallas_call | solution.py:260
  28.6 0.9 constant_dynamic-slice_fusion.3
  29.7 2.8 %collective-permute-start.4 = (f32[136,256]{1,0:T(8,128)S(1)}, f32[136,256]{1,0:T(8,128)S(1)}, u32[]{:S(2)}, u32[]{:S(2)}) collective-permute-start(f32[136,256]{1,0:T(8,128)S(1)} %pad_maximum_fusion.2), channel_id=1, source_target_pairs={{0,6},{2,4},{4,2},{6,0},{8,14},{10,12},{12,10},{14,8},{16,22},{18,... | collective-permute-start | bytes 417800 | tf_op jit(solution)/shard_map/ppermute | solution.py:433
  32.5 0.7 collective-permute-start.2
  33.1 15.2 %column_products.2 = f32[1024,256]{1,0:T(8,128)} custom-call(s32[2]{0:T(128)} %pad_add_fusion.off_ref, bf16[3200,512]{1,0:T(8,128)(2,1)} %refs_0_.5, bf16[3200,512]{1,0:T(8,128)(2,1)} %collective-permute-done.refs_1_, bf16[3200,256]{1,0:T(8,128)(2,1)} %get-tuple-element.13.refs_2_, bf16[2048,1024]{1,0:T(8,128)(2,1)} %refs_3_.5), custom_call_target="tpu_custom_call" | custom-call | flops 8388608000 | bytes 6553600 | tf_op jit(solution)/shard_map/column_products/pallas_call | solution.py:308
  48.4 4.4 %collective-permute-start.7 = (f32[136,256]{1,0:T(8,128)S(1)}, f32[136,256]{1,0:T(8,128)S(1)}, u32[]{:S(2)}, u32[]{:S(2)}) collective-permute-start(f32[136,256]{1,0:T(8,128)S(1)} %add_add_fusion.1), channel_id=1, source_target_pairs={{0,24},{2,26},{4,28},{6,30},{8,16},{10,18},{12,20},{14,22},{16,8},... | collective-permute-start | bytes 417800 | tf_op jit(solution)/shard_map/ppermute | solution.py:433
  52.8 0.6 collective-permute-start.5
  53.4 15.1 %column_products.3 = f32[1024,256]{1,0:T(8,128)} custom-call(s32[2]{0:T(128)} %pad_add_fusion.off_ref, bf16[3200,512]{1,0:T(8,128)(2,1)} %refs_0_.5, bf16[3200,512]{1,0:T(8,128)(2,1)} %collective-permute-done.refs_1_, bf16[3200,256]{1,0:T(8,128)(2,1)} %get-tuple-element.13.refs_2_, bf16[2048,1024]{1,0:T(8,128)(2,1)} %refs_3_.5), custom_call_target="tpu_custom_call" | custom-call | flops 8388608000 | bytes 6553600 | tf_op jit(solution)/shard_map/column_products/pallas_call | solution.py:308
  68.6 1.8 fusion
  70.4 2.5 %collective-permute-start.10 = (f32[512,256]{1,0:T(8,128)S(1)}, f32[512,256]{1,0:T(8,128)S(1)}, u32[]{:S(2)}, u32[]{:S(2)}) collective-permute-start(f32[512,256]{1,0:T(8,128)S(1)} %get-tuple-element.18), channel_id=1, source_target_pairs={{0,6},{2,4},{4,2},{6,0},{8,14},{10,12},{12,10},{14,8},{16,22},{18,... | collective-permute-start | bytes 1572872 | tf_op jit(solution)/shard_map/ppermute | solution.py:433
  72.9 19.1 %collective-permute-done.7 = f32[136,256]{1,0:T(8,128)S(1)} collective-permute-done((f32[136,256]{1,0:T(8,128)S(1)}, f32[136,256]{1,0:T(8,128)S(1)}, u32[]{:S(2)}, u32[]{:S(2)}) %collective-permute-start.7) | collective-permute-done | bytes 139296 | tf_op jit(solution)/shard_map/ppermute | solution.py:433
  92.0 5.6 %collective-permute-start.9 = (f32[512,256]{1,0:T(8,128)S(1)}, f32[512,256]{1,0:T(8,128)S(1)}, u32[]{:S(2)}, u32[]{:S(2)}) collective-permute-start(f32[512,256]{1,0:T(8,128)S(1)} %get-tuple-element.20), channel_id=1, source_target_pairs={{0,4},{2,6},{4,0},{6,2},{8,12},{10,14},{12,8},{14,10},{16,20},{18,... | collective-permute-start | bytes 1572872 | tf_op jit(solution)/shard_map/ppermute | solution.py:433
  97.6 24.8 %collective-permute-done.6 = f32[136,256]{1,0:T(8,128)S(1)} collective-permute-done((f32[136,256]{1,0:T(8,128)S(1)}, f32[136,256]{1,0:T(8,128)S(1)}, u32[]{:S(2)}, u32[]{:S(2)}) %collective-permute-start.6) | collective-permute-done | bytes 139296 | tf_op jit(solution)/shard_map/ppermute | solution.py:433
  122.6 1.3 collective-permute-done.14
  123.9 0.7 maximum_select_fusion.gram_ref
  124.6 0.3 fusion.3
  124.9 8.6 %collective-permute-start.11 = (f32[128,256]{1,0:T(8,128)S(1)}, f32[128,256]{1,0:T(8,128)S(1)}, u32[]{:S(2)}, u32[]{:S(2)}) collective-permute-start(f32[128,256]{1,0:T(8,128)S(1)} %get-tuple-element.21), channel_id=1, source_target_pairs={{0,8},{2,10},{4,12},{6,14},{8,0},{10,2},{12,4},{14,6},{16,24},{18,... | collective-permute-start | bytes 393224 | tf_op jit(solution)/shard_map/ppermute | solution.py:433
  133.6 1.6 collective-permute-start.13
  135.1 24.0 %factor.1.refs_4_ = f32[256,256]{1,0:T(8,128)} custom-call(f32[256,256]{1,0:T(8,128)} %maximum_select_fusion.gram_ref), custom_call_target="tpu_custom_call" | custom-call | flops 20000000000 | bytes 524288 | tf_op jit(solution)/shard_map/factor/pallas_call | solution.py:164
  159.1 1.4 convolution_convert_fusion
  160.5 2.3 %collective-permute-start.17 = (bf16[128,256]{1,0:T(8,128)(2,1)S(1)}, bf16[128,256]{1,0:T(8,128)(2,1)S(1)}, u32[]{:S(2)}, u32[]{:S(2)}) collective-permute-start(bf16[128,256]{1,0:T(8,128)(2,1)S(1)} %convolution_convert_fusion), channel_id=1, source_target_pairs={{0,24},{2,26},{4,28},{6,30},{8,16},{10,18},{12,20},{14,22},{16,8},... | collective-permute-start | bytes 196616 | tf_op jit(solution)/shard_map/ppermute | solution.py:433
  162.8 2.0 collective-permute-start.16
  164.9 0.6 select_reduce_fusion.pos_ref
  165.6 1.1 collective-permute-done.17
  166.6 1.4 collective-permute-done.16
  168.0 1.1 collective-permute-done.15
  169.2 3.5 %select.24 = bf16[13,128,512]{2,1,0:T(8,128)(2,1)} custom-call(s32[13]{0:T(128)} %select_reduce_fusion.pos_ref, bf16[32,128,512]{2,1,0:T(8,128)(2,1)} %all-to-all-done.recv_ref), custom_call_target="tpu_custom_call" | custom-call | bytes 3407872 | tf_op jit(solution)/shard_map/select/pallas_call | solution.py:108
  172.7 3.5 %collective-permute-start.21 = (bf16[512,256]{1,0:T(8,128)(2,1)S(1)}, bf16[512,256]{1,0:T(8,128)(2,1)S(1)}, u32[]{:S(2)}, u32[]{:S(2)}) collective-permute-start(bf16[512,256]{1,0:T(8,128)(2,1)S(1)} %pad_maximum_fusion.1), channel_id=1, source_target_pairs={{0,6},{2,4},{4,2},{6,0},{8,14},{10,12},{12,10},{14,8},{16,22},{18,... | collective-permute-start | bytes 786440 | tf_op jit(solution)/shard_map/ppermute | solution.py:433
  176.2 1.7 collective-permute-start.20
  178.0 0.6 select_reduce_fusion.1.w_ref
  178.6 4.8 %collective-permute-done.21 = bf16[512,256]{1,0:T(8,128)(2,1)S(1)} collective-permute-done((bf16[512,256]{1,0:T(8,128)(2,1)S(1)}, bf16[512,256]{1,0:T(8,128)(2,1)S(1)}, u32[]{:S(2)}, u32[]{:S(2)}) %collective-permute-start.21) | collective-permute-done | bytes 262176 | tf_op jit(solution)/shard_map/ppermute | solution.py:433
  183.4 5.3 %collective-permute-done.20 = bf16[512,256]{1,0:T(8,128)(2,1)S(1)} collective-permute-done((bf16[512,256]{1,0:T(8,128)(2,1)S(1)}, bf16[512,256]{1,0:T(8,128)(2,1)S(1)}, u32[]{:S(2)}, u32[]{:S(2)}) %collective-permute-start.20) | collective-permute-done | bytes 262176 | tf_op jit(solution)/shard_map/ppermute | solution.py:433
  188.7 0.3 collective-permute-done.19
  189.0 1.1 pad_maximum_fusion.refs_5_
  190.2 1.2 copy-done.4
  191.4 17.9 %remainder_rows.1 = (bf16[1664,2048]{1,0:T(8,128)(2,1)}, f32[256,2048]{1,0:T(8,128)}) custom-call(s32[1]{0:T(128)} %bitcast.quarter_ref, s32[2]{0:T(128)} %pad_add_fusion.off_ref, f32[13]{0:T(128)} %select_reduce_fusion.1.w_ref, s32[1]{0:T(128)} %bitcast.5.group_ref, bf16[1664,512]{1,0:T(8,128)(2,1)} %bitcast.21, bf16[1664,512]{1,0:T(8,128)(2,1)} %copy-done.4, ...), custom_call_target="tpu_custom_call" | custom-call | flops 10468982784 | bytes 14417920 | tf_op jit(solution)/shard_map/remainder_rows/pallas_call | solution.py:407
  (57 shorter events, 1.2 us)
Async XLA Ops:
  0.6 18.7 %collective-permute-start = (bf16[3200,512]{1,0:T(8,128)(2,1)}, bf16[3200,512]{1,0:T(8,128)(2,1)}, u32[]{:S(2)}, u32[]{:S(2)}) collective-permute-start(bf16[3200,512]{1,0:T(8,128)(2,1)} %refs_0_.5), channel_id=1, source_target_pairs={{0,1},{1,0},{2,3},{3,2},{4,5},{5,4},{6,7},{7,6},{8,9},{9,8},{10,11... | collective-permute-start | bytes 9830408 | tf_op jit(solution)/shard_map/ppermute | solution.py:177
  5.0 9.4 %copy-start.2 = (s32[16,25]{1,0:T(8,128)S(1)}, s32[16,25]{1,0:T(8,128)}, u32[]{:S(2)}) copy-start(s32[16,25]{1,0:T(8,128)} %dest_ref.1) | copy-start | bytes 4804
  5.0 9.4 %copy-start.3 = (s32[16]{0:T(128)S(1)}, s32[16]{0:T(128)}, u32[]{:S(2)}) copy-start(s32[16]{0:T(128)} %cnt_ref.1) | copy-start | bytes 196
  5.0 10.3 %copy-start.5 = (bf16[25]{0:T(256)(128)(2,1)S(1)}, bf16[25]{0:T(256)(128)(2,1)}, u32[]{:S(2)}) copy-start(bf16[25]{0:T(256)(128)(2,1)} %param.7) | copy-start | bytes 154
  5.0 164.2 %all-to-all-start = ((bf16[32,128,512]{2,1,0:T(8,128)(2,1)}), bf16[32,128,512]{2,1,0:T(8,128)(2,1)}, u32[]{:S(2)}, u32[]{:S(2)}) async-start(bf16[32,128,512]{2,1,0:T(8,128)(2,1)} %pack.1), calls=%async_computation | async-start | bytes 8388608 | tf_op jit(solution)/shard_map/all_to_all | solution.py:483
  14.1 3.3 %collective-permute-start.1 = (bf16[256,1024]{1,0:T(8,128)(2,1)S(1)}, bf16[256,1024]{1,0:T(8,128)(2,1)S(1)}, u32[]{:S(2)}, u32[]{:S(2)}) collective-permute-start(bf16[256,1024]{1,0:T(8,128)(2,1)S(1)} %slice.25), channel_id=1, source_target_pairs={{0,1},{1,0},{2,3},{3,2},{4,5},{5,4},{6,7},{7,6},{8,9},{9,8},{10,11... | collective-permute-start | bytes 1572872 | tf_op jit(solution)/shard_map/ppermute | solution.py:477
  29.6 18.8 %collective-permute-start.3 = (f32[136,256]{1,0:T(8,128)S(1)}, f32[136,256]{1,0:T(8,128)S(1)}, u32[]{:S(2)}, u32[]{:S(2)}) collective-permute-start(f32[136,256]{1,0:T(8,128)S(1)} %pad_maximum_fusion.2), channel_id=1, source_target_pairs={{0,4},{2,6},{4,0},{6,2},{8,12},{10,14},{12,8},{14,10},{16,20},{18,... | collective-permute-start | bytes 417800 | tf_op jit(solution)/shard_map/ppermute | solution.py:433
  29.7 18.7 %collective-permute-start.4 = (f32[136,256]{1,0:T(8,128)S(1)}, f32[136,256]{1,0:T(8,128)S(1)}, u32[]{:S(2)}, u32[]{:S(2)}) collective-permute-start(f32[136,256]{1,0:T(8,128)S(1)} %pad_maximum_fusion.2), channel_id=1, source_target_pairs={{0,6},{2,4},{4,2},{6,0},{8,14},{10,12},{12,10},{14,8},{16,22},{18,... | collective-permute-start | bytes 417800 | tf_op jit(solution)/shard_map/ppermute | solution.py:433
  32.5 15.9 %collective-permute-start.2 = (f32[136,256]{1,0:T(8,128)S(1)}, f32[136,256]{1,0:T(8,128)S(1)}, u32[]{:S(2)}, u32[]{:S(2)}) collective-permute-start(f32[136,256]{1,0:T(8,128)S(1)} %pad_maximum_fusion.2), channel_id=1, source_target_pairs={{0,2},{2,0},{4,6},{6,4},{8,10},{10,8},{12,14},{14,12},{16,18},{18,... | collective-permute-start | bytes 417800 | tf_op jit(solution)/shard_map/ppermute | solution.py:433
  48.4 20.2 %copy-start = (f32[1024,256]{1,0:T(8,128)S(1)}, f32[1024,256]{1,0:T(8,128)}, u32[]{:S(2)}) copy-start(f32[1024,256]{1,0:T(8,128)} %column_products.2) | copy-start | bytes 3145732
  48.4 43.6 %collective-permute-start.7 = (f32[136,256]{1,0:T(8,128)S(1)}, f32[136,256]{1,0:T(8,128)S(1)}, u32[]{:S(2)}, u32[]{:S(2)}) collective-permute-start(f32[136,256]{1,0:T(8,128)S(1)} %add_add_fusion.1), channel_id=1, source_target_pairs={{0,24},{2,26},{4,28},{6,30},{8,16},{10,18},{12,20},{14,22},{16,8},... | collective-permute-start | bytes 417800 | tf_op jit(solution)/shard_map/ppermute | solution.py:433
  52.8 69.6 %collective-permute-start.6 = (f32[136,256]{1,0:T(8,128)S(1)}, f32[136,256]{1,0:T(8,128)S(1)}, u32[]{:S(2)}, u32[]{:S(2)}) collective-permute-start(f32[136,256]{1,0:T(8,128)S(1)} %add_add_fusion.1), channel_id=1, source_target_pairs={{0,16},{2,18},{4,20},{6,22},{8,24},{10,26},{12,28},{14,30},{16,0},... | collective-permute-start | bytes 417800 | tf_op jit(solution)/shard_map/ppermute | solution.py:433
  52.8 69.6 %collective-permute-start.5 = (f32[136,256]{1,0:T(8,128)S(1)}, f32[136,256]{1,0:T(8,128)S(1)}, u32[]{:S(2)}, u32[]{:S(2)}) collective-permute-start(f32[136,256]{1,0:T(8,128)S(1)} %add_add_fusion.1), channel_id=1, source_target_pairs={{0,8},{2,10},{4,12},{6,14},{8,0},{10,2},{12,4},{14,6},{16,24},{18,... | collective-permute-start | bytes 417800 | tf_op jit(solution)/shard_map/ppermute | solution.py:433
  68.6 56.0 %copy-start.1 = (f32[1024,256]{1,0:T(8,128)S(1)}, f32[1024,256]{1,0:T(8,128)}, u32[]{:S(2)}) copy-start(f32[1024,256]{1,0:T(8,128)} %column_products.3) | copy-start | bytes 3145732
  70.4 54.2 %collective-permute-start.10 = (f32[512,256]{1,0:T(8,128)S(1)}, f32[512,256]{1,0:T(8,128)S(1)}, u32[]{:S(2)}, u32[]{:S(2)}) collective-permute-start(f32[512,256]{1,0:T(8,128)S(1)} %get-tuple-element.18), channel_id=1, source_target_pairs={{0,6},{2,4},{4,2},{6,0},{8,14},{10,12},{12,10},{14,8},{16,22},{18,... | collective-permute-start | bytes 1572872 | tf_op jit(solution)/shard_map/ppermute | solution.py:433
  72.9 51.7 %collective-permute-start.8 = (f32[512,256]{1,0:T(8,128)S(1)}, f32[512,256]{1,0:T(8,128)S(1)}, u32[]{:S(2)}, u32[]{:S(2)}) collective-permute-start(f32[512,256]{1,0:T(8,128)S(1)} %get-tuple-element.19), channel_id=1, source_target_pairs={{0,2},{2,0},{4,6},{6,4},{8,10},{10,8},{12,14},{14,12},{16,18},{18,... | collective-permute-start | bytes 1572872 | tf_op jit(solution)/shard_map/ppermute | solution.py:433
  92.0 32.6 %collective-permute-start.9 = (f32[512,256]{1,0:T(8,128)S(1)}, f32[512,256]{1,0:T(8,128)S(1)}, u32[]{:S(2)}, u32[]{:S(2)}) collective-permute-start(f32[512,256]{1,0:T(8,128)S(1)} %get-tuple-element.20), channel_id=1, source_target_pairs={{0,4},{2,6},{4,0},{6,2},{8,12},{10,14},{12,8},{14,10},{16,20},{18,... | collective-permute-start | bytes 1572872 | tf_op jit(solution)/shard_map/ppermute | solution.py:433
  122.5 1.4 collective-permute-start.14
  124.9 34.2 %collective-permute-start.11 = (f32[128,256]{1,0:T(8,128)S(1)}, f32[128,256]{1,0:T(8,128)S(1)}, u32[]{:S(2)}, u32[]{:S(2)}) collective-permute-start(f32[128,256]{1,0:T(8,128)S(1)} %get-tuple-element.21), channel_id=1, source_target_pairs={{0,8},{2,10},{4,12},{6,14},{8,0},{10,2},{12,4},{14,6},{16,24},{18,... | collective-permute-start | bytes 393224 | tf_op jit(solution)/shard_map/ppermute | solution.py:433
  133.6 25.6 %collective-permute-start.13 = (f32[128,256]{1,0:T(8,128)S(1)}, f32[128,256]{1,0:T(8,128)S(1)}, u32[]{:S(2)}, u32[]{:S(2)}) collective-permute-start(f32[128,256]{1,0:T(8,128)S(1)} %get-tuple-element.22), channel_id=1, source_target_pairs={{0,24},{2,26},{4,28},{6,30},{8,16},{10,18},{12,20},{14,22},{16,8},... | collective-permute-start | bytes 393224 | tf_op jit(solution)/shard_map/ppermute | solution.py:433
  135.1 24.0 %collective-permute-start.12 = (f32[128,256]{1,0:T(8,128)S(1)}, f32[128,256]{1,0:T(8,128)S(1)}, u32[]{:S(2)}, u32[]{:S(2)}) collective-permute-start(f32[128,256]{1,0:T(8,128)S(1)} %get-tuple-element.23), channel_id=1, source_target_pairs={{0,16},{2,18},{4,20},{6,22},{8,24},{10,26},{12,28},{14,30},{16,0},... | collective-permute-start | bytes 393224 | tf_op jit(solution)/shard_map/ppermute | solution.py:433
  160.5 6.2 %collective-permute-start.17 = (bf16[128,256]{1,0:T(8,128)(2,1)S(1)}, bf16[128,256]{1,0:T(8,128)(2,1)S(1)}, u32[]{:S(2)}, u32[]{:S(2)}) collective-permute-start(bf16[128,256]{1,0:T(8,128)(2,1)S(1)} %convolution_convert_fusion), channel_id=1, source_target_pairs={{0,24},{2,26},{4,28},{6,30},{8,16},{10,18},{12,20},{14,22},{16,8},... | collective-permute-start | bytes 196616 | tf_op jit(solution)/shard_map/ppermute | solution.py:433
  162.8 5.2 %collective-permute-start.16 = (bf16[128,256]{1,0:T(8,128)(2,1)S(1)}, bf16[128,256]{1,0:T(8,128)(2,1)S(1)}, u32[]{:S(2)}, u32[]{:S(2)}) collective-permute-start(bf16[128,256]{1,0:T(8,128)(2,1)S(1)} %convolution_convert_fusion), channel_id=1, source_target_pairs={{0,16},{2,18},{4,20},{6,22},{8,24},{10,26},{12,28},{14,30},{16,0},... | collective-permute-start | bytes 196616 | tf_op jit(solution)/shard_map/ppermute | solution.py:433
  164.8 4.3 %collective-permute-start.15 = (bf16[128,256]{1,0:T(8,128)(2,1)S(1)}, bf16[128,256]{1,0:T(8,128)(2,1)S(1)}, u32[]{:S(2)}, u32[]{:S(2)}) collective-permute-start(bf16[128,256]{1,0:T(8,128)(2,1)S(1)} %convolution_convert_fusion), channel_id=1, source_target_pairs={{0,8},{2,10},{4,12},{6,14},{8,0},{10,2},{12,4},{14,6},{16,24},{18,... | collective-permute-start | bytes 196616 | tf_op jit(solution)/shard_map/ppermute | solution.py:433
  172.7 17.5 %collective-permute-start.18 = (bf16[1664,512]{1,0:T(8,128)(2,1)}, bf16[1664,512]{1,0:T(8,128)(2,1)S(1)}, u32[]{:S(2)}, u32[]{:S(2)}) collective-permute-start(bf16[1664,512]{1,0:T(8,128)(2,1)} %bitcast.20), channel_id=1, source_target_pairs={{0,1},{1,0},{2,3},{3,2},{4,5},{5,4},{6,7},{7,6},{8,9},{9,8},{10,11... | collective-permute-start | bytes 5111816 | tf_op jit(solution)/shard_map/ppermute | solution.py:177
  172.7 10.7 %collective-permute-start.21 = (bf16[512,256]{1,0:T(8,128)(2,1)S(1)}, bf16[512,256]{1,0:T(8,128)(2,1)S(1)}, u32[]{:S(2)}, u32[]{:S(2)}) collective-permute-start(bf16[512,256]{1,0:T(8,128)(2,1)S(1)} %pad_maximum_fusion.1), channel_id=1, source_target_pairs={{0,6},{2,4},{4,2},{6,0},{8,14},{10,12},{12,10},{14,8},{16,22},{18,... | collective-permute-start | bytes 786440 | tf_op jit(solution)/shard_map/ppermute | solution.py:433
  176.2 12.5 %collective-permute-start.20 = (bf16[512,256]{1,0:T(8,128)(2,1)S(1)}, bf16[512,256]{1,0:T(8,128)(2,1)S(1)}, u32[]{:S(2)}, u32[]{:S(2)}) collective-permute-start(bf16[512,256]{1,0:T(8,128)(2,1)S(1)} %pad_maximum_fusion.1), channel_id=1, source_target_pairs={{0,4},{2,6},{4,0},{6,2},{8,12},{10,14},{12,8},{14,10},{16,20},{18,... | collective-permute-start | bytes 786440 | tf_op jit(solution)/shard_map/ppermute | solution.py:433
  177.9 11.1 %collective-permute-start.19 = (bf16[512,256]{1,0:T(8,128)(2,1)S(1)}, bf16[512,256]{1,0:T(8,128)(2,1)S(1)}, u32[]{:S(2)}, u32[]{:S(2)}) collective-permute-start(bf16[512,256]{1,0:T(8,128)(2,1)S(1)} %pad_maximum_fusion.1), channel_id=1, source_target_pairs={{0,2},{2,0},{4,6},{6,4},{8,10},{10,8},{12,14},{14,12},{16,18},{18,... | collective-permute-start | bytes 786440 | tf_op jit(solution)/shard_map/ppermute | solution.py:433
  190.2 1.2 copy-start.4

commit v4 on v3

--- a/solution.py
+++ b/solution.py
@@ -50,11 +50,30 @@
     return high, (x - high.astype(jnp.float32)).astype(jnp.bfloat16)
 
 
-def pack_kernel(per_pair, me_ref, dest_ref, cnt_ref, desc_ref, out_ref, ctr_ref, sems):
+HEAD = 64
+
+
+def block_copies(rank, whole_ref, outer, first_ref, last_ref, sems):
+    if rank == 0:
+        pairs = [(whole_ref, first_ref.at[outer, pl.ds(0, BLK)])]
+    else:
+        pairs = [
+            (whole_ref.at[pl.ds(0, HEAD)], first_ref.at[outer, pl.ds(BLK, HEAD)]),
+            (whole_ref.at[pl.ds(HEAD, BLK - HEAD)], last_ref.at[outer]),
+        ]
+    return [(a, b, sems.at[i]) for i, (a, b) in enumerate(pairs)]
+
+
+def pack_kernel(per_pair, me_ref, dest_ref, cnt_ref, desc_ref, *refs):
+    out_refs, (ctr_ref, rank_ref, sems) = refs[:per_pair], refs[per_pair:]
     slots = desc_ref.shape[0]
     owners = ctr_ref.shape[0]
     me = me_ref[0]
     count = cnt_ref[me]
+
+    def copies(j, d, rank):
+        moves = block_copies(rank, desc_ref.at[j], d, out_refs[0], out_refs[-1], sems.at[j])
+        return [pltpu.make_async_copy(a, b, sem) for a, b, sem in moves]
 
     @pl.loop(0, owners)
     def _(i):
@@ -65,56 +84,77 @@
         @pl.when(j < count)
         def _():
             d = dest_ref[me, j]
-            r = ctr_ref[d]
-            ctr_ref[d] = r + 1
-            slot = d * per_pair + r
-            pltpu.make_async_copy(desc_ref.at[j], out_ref.at[slot], sems.at[j]).start()
+            rank = ctr_ref[d]
+            ctr_ref[d] = rank + 1
+            rank_ref[j] = rank
+            for r in range(per_pair):
+                @pl.when(rank == r)
+                def _():
+                    for c in copies(j, d, r):
+                        c.start()
 
     @pl.loop(0, slots)
     def _(j):
         @pl.when(j < count)
         def _():
-            pltpu.make_async_copy(desc_ref.at[0], out_ref.at[0], sems.at[j]).wait()
+            for r in range(per_pair):
+                @pl.when(rank_ref[j] == r)
+                def _():
+                    for c in copies(j, 0, r):
+                        c.wait()
 
 
 def pack(desc_blocks, me, destinations, counts, per_pair):
     slots, blk, feat = desc_blocks.shape
     owners = destinations.shape[0]
+    heights = [blk] if per_pair == 1 else [blk + HEAD, blk - HEAD]
     return pl.pallas_call(
         functools.partial(pack_kernel, per_pair),
-        out_shape=jax.ShapeDtypeStruct((owners * per_pair, blk, feat), desc_blocks.dtype),
+        out_shape=[
+            jax.ShapeDtypeStruct((owners, h, feat), desc_blocks.dtype) for h in heights
+        ],
         in_specs=[SMEM, SMEM, SMEM, VMEM],
-        out_specs=ANY,
-        scratch_shapes=[pltpu.SMEM((owners,), jnp.int32), pltpu.SemaphoreType.DMA((slots,))],
+        out_specs=[ANY] * per_pair,
+        scratch_shapes=[
+            pltpu.SMEM((owners,), jnp.int32),
+            pltpu.SMEM((slots,), jnp.int32),
+            pltpu.SemaphoreType.DMA((slots, 2)),
+        ],
         compiler_params=params(),
         cost_estimate=cost(0, 4 * slots * blk * feat),
         name="pack",
     )(me, destinations, counts, desc_blocks)
 
 
-def select_kernel(pos_ref, recv_ref, out_ref, sems):
-    copies = [
-        pltpu.make_async_copy(recv_ref.at[pos_ref[p]], out_ref.at[p], sems.at[p])
-        for p in range(DST_BLK)
-    ]
-    for c in copies:
-        c.start()
-    for c in copies:
-        c.wait()
+def select_kernel(per_pair, pos_ref, *refs):
+    recv_refs, (out_ref, sems) = refs[:per_pair], refs[per_pair:]
+
+    def copies(p, rank):
+        owner = pos_ref[p] // per_pair
+        moves = block_copies(rank, out_ref.at[p], owner, recv_refs[0], recv_refs[-1], sems.at[p])
+        return [pltpu.make_async_copy(b, a, sem) for a, b, sem in moves]
+
+    for act in ("start", "wait"):
+        for p in range(DST_BLK):
+            for r in range(per_pair):
+                @pl.when(pos_ref[p] % per_pair == r)
+                def _():
+                    for c in copies(p, r):
+                        getattr(c, act)()
 
 
 def select(received, positions):
-    _, blk, feat = received.shape
+    feat = received[0].shape[-1]
     return pl.pallas_call(
-        select_kernel,
-        out_shape=jax.ShapeDtypeStruct((DST_BLK, blk, feat), received.dtype),
-        in_specs=[SMEM, ANY],
+        functools.partial(select_kernel, len(received)),
+        out_shape=jax.ShapeDtypeStruct((DST_BLK, BLK, feat), received[0].dtype),
+        in_specs=[SMEM] + [ANY] * len(received),
         out_specs=VMEM,
-        scratch_shapes=[pltpu.SemaphoreType.DMA((DST_BLK,))],
+        scratch_shapes=[pltpu.SemaphoreType.DMA((DST_BLK, 2))],
         compiler_params=params(),
-        cost_estimate=cost(0, 4 * DST_BLK * blk * feat),
+        cost_estimate=cost(0, 4 * DST_BLK * BLK * feat),
         name="select",
-    )(positions, received)
+    )(positions, *received)
 
 
 def small_factor(a):
@@ -298,11 +338,10 @@
     g_ref[...] = products / (width * square)
 
 
-def column_products(parts, offsets, pw, s, start, size):
+def column_products(parts, offsets, pw, s):
     rows, feat = parts[0].shape
-    width = s.shape[1]
+    size, width = s.shape
     chunk = min(512, size)
-    first = start // chunk
     tiles = len(row_tiles(rows)[1])
     once = pl.Buffered(1)
     return pl.pallas_call(
@@ -313,7 +352,7 @@
         + [ANY] * len(parts)
         + [
             pl.BlockSpec((rows, PANEL), lambda i: (0, 0), pipeline_mode=once),
-            pl.BlockSpec((chunk, width), lambda i: (first + i, 0)),
+            pl.BlockSpec((chunk, width), lambda i: (i, 0)),
         ],
         out_specs=pl.BlockSpec((chunk, PANEL), lambda i: (i, 0)),
         scratch_shapes=[
@@ -441,6 +480,14 @@
     return (got[0] + got[1]) + (got[2] + got[3])
 
 
+def halve_sum(x, bit):
+    half = x.shape[0] // 2
+    upper = (lax.axis_index("rows") // bit) % 2
+    send = lax.dynamic_slice_in_dim(x, (1 - upper) * half, half, 0)
+    kept = lax.dynamic_slice_in_dim(x, upper * half, half, 0)
+    return kept + lax.ppermute(send, "rows", flips(bit, lax.axis_size("rows")))
+
+
 def gather_pieces(x, pair):
     return [x] + [trade(x, pair, k) for k in range(1, 4)]
 
@@ -469,7 +516,8 @@
     feat = descriptors.shape[1]
     cols, width = sparse_points.shape
     norm = math.sqrt(owners * DST_BLK * BLK)
-    pairs = [(1 << i, 2 << i) for i in range(0, owners.bit_length() - 1, 2)]
+    near = (1, 2)
+    far = [1 << i for i in range(2, owners.bit_length() - 1)]
 
     first = sparse_points[:PANEL]
     source_parts = share_parts(descriptors)
@@ -480,26 +528,21 @@
         panel_points = lax.all_gather(first, "cols", axis=0, tiled=False)[0]
     desc_blocks = descriptors.reshape(slots, BLK, feat)
     outgoing = pack(desc_blocks, me[None], destinations, block_counts, per_pair)
-    received = lax.all_to_all(outgoing, "rows", split_axis=0, concat_axis=0, tiled=True)
+    received = [lax.all_to_all(outgoing[0], "rows", split_axis=0, concat_axis=0, tiled=True)]
 
     offsets = part_offsets(feat)
     count = lax.dynamic_index_in_dim(block_counts, me, 0)
     weights32 = block_weights.astype(jnp.float32)
     gram_part, pw = panel_products(source_parts, offsets, count, weights32, panel_points)
-    half = cols // 2
-    low = column_products(source_parts, offsets, pw, sparse_points, 0, half)
-
     spare = -(-owners * slots // (PANEL * 8)) * 8
     table = lax.dynamic_update_slice(
         jnp.zeros((spare * PANEL,), jnp.float32), weights32, (me * slots,)
     ).reshape(spare, PANEL)
     if groups == 2:
         gram_part = lax.dynamic_slice_in_dim(gram_part, group * (PANEL // 2), PANEL // 2, 0)
-    summed = pair_sum(jnp.concatenate([gram_part, table], 0), pairs[0])
-    pw, summed = lax.optimization_barrier((pw, summed))
-    high = column_products(source_parts, offsets, pw, sparse_points, half, half)
-    for pair in pairs[1:]:
-        summed = pair_sum(summed, pair)
+    summed = pair_sum(jnp.concatenate([gram_part, table], 0), near)
+    for bit in far:
+        summed = summed + lax.ppermute(summed, "rows", flips(bit, owners))
     gram, table = summed[:-spare], summed[-spare:]
     if groups == 2:
         other = lax.ppermute(gram, "cols", [(0, 1), (1, 0)])
@@ -509,12 +552,16 @@
     all_weights = table.reshape(-1)[: owners * slots]
     inverse = factor(gram)
 
-    g = jnp.concatenate([low, high], 0)
-    for pair in pairs:
-        g = scatter_sum(g, pair)
+    g = scatter_sum(column_products(source_parts, offsets, pw, sparse_points), near)
+    for bit in far:
+        g = halve_sum(g, bit)
+    if per_pair > 1:
+        g, last = lax.optimization_barrier((g, outgoing[1]))
+        received.append(lax.all_to_all(last, "rows", split_axis=0, concat_axis=0, tiled=True))
     rt = nt(g, inverse, HIGH).astype(jnp.bfloat16)
-    for pair in pairs[:0:-1]:
-        rt = gather_back(rt, pair)
+    for i in range(len(far) - 1, 0, -2):
+        rt = gather_back(rt, (far[i], far[i - 1]))
+
     slot_ids = jnp.arange(slots, dtype=jnp.int32)
     toward = ((slot_ids[None, :] < block_counts[:, None]) & (destinations == me)).astype(jnp.int32)
     rank = jnp.cumsum(toward, axis=1) - toward
@@ -526,14 +573,14 @@
     weights_here = jnp.sum(jnp.where(hit, all_weights[None, :], 0.0), axis=1)
 
     rt, positions = lax.optimization_barrier((rt, positions))
-    rt = jnp.stack(gather_pieces(rt, pairs[0]))
+    rt = jnp.stack(gather_pieces(rt, near))
     arrived = select(received, positions).reshape(DST_BLK * BLK, feat)
     remainder, projected = remainder_rows(
         share_parts(arrived),
         offsets,
         weights_here,
         group[None],
-        quarter_of(pairs[0])[None],
+        quarter_of(near)[None],
         panel_points,
         sparse_points,
         inverse,

time: 211 us -> 213 us (level)
  waiting for transfers between devices: 59.2 us -> 45.2 us
  local copies, waits for them, and re-layouts: 4.29 us -> 15.6 us
  other arithmetic: 9.23 us -> 18.5 us
  Pallas kernels: 88.8 us -> 82.3 us
    ppermute x18 -> x12, starting transfers between devices: 36.5 us -> 15.8 us  [trade(): return lax.ppermute(x, 'rows', flips(bit, lax.axis_size('rows')))]
    ppermute x18 -> x12, waiting for transfers between devices: 57.9 us -> 42.1 us  [trade(): return lax.ppermute(x, 'rows', flips(bit, lax.axis_size('rows')))]
    ppermute x0 -> x4, starting transfers between devices: none -> 15.8 us  [the longest x2 9.35 us: on_device(): summed = summed + lax.ppermute(summed, 'rows', flips(bit, owners))]
    all_to_all x1 -> x2, starting transfers between devices: 8 us -> 14.9 us  [the longest x1 7.45 us: on_device(): lax.all_to_all(last, 'rows', split_axis=0, concat_axis=0, tiled=True)]
    pallas_call x2 -> x1, Pallas kernels: 30.3 us -> 24.8 us  [column_products(): pl.pallas_call(functools.partial(column_kernel, len(parts)), grid=(size /...]
    ppermute x0 -> x4, waiting for transfers between devices: none -> 3.09 us  [the longest x2 3.08 us: on_device(): summed = summed + lax.ppermute(summed, 'rows', flips(bit, owners))]
    add x0 -> x4, other arithmetic: none -> 2.68 us  [the longest x2 2.64 us: halve_sum(): return kept + lax.ppermute(send, 'rows', flips(bit, lax.axis_size('rows')))]
    dynamic_slice x1, local copies, waits for them, and re-layouts: 0.04 us -> 2.57 us  [scatter_sum(): pieces = [lax.dynamic_slice_in_dim(x, (q ^ k) * n, n, 0) for k in range(4)]]
  transfers between devices with their start and end apart: 23 -> 22, of which waited for: 9 -> 8; matrix products, arithmetic and copies ran while one was open for 7% -> 16% of each run, Pallas kernels for 32% -> 29%
where the time goes in v4:
time: 213 us; the launch traced here: 211 us
  Pallas kernels  82.3 us (39%)
  starting transfers between devices  47.2 us (22%)
  waiting for transfers between devices  45.2 us (21%)
  other arithmetic  18.5 us (9%)
  local copies, waits for them, and re-layouts  15.6 us (7%)
    ppermute x12, waiting for transfers between devices, trade(): return lax.ppermute(x, 'rows', flips(bit, lax.axis_size('rows')))  42.1 us
    pallas_call x1, Pallas kernels, column_products(): pl.pallas_call(functools.partial(column_kernel, len(parts)), grid=(size /...  24.8 us
    pallas_call x1, Pallas kernels, factor(): pl.pallas_call(functools.partial(factor_kernel, 64), out_shape=jax.ShapeD...  24 us
    pallas_call x1, Pallas kernels, remainder_rows(): pl.pallas_call(functools.partial(remainder_kernel, len(parts), norm), gri...  17.9 us
    ppermute x12, starting transfers between devices, trade(): return lax.ppermute(x, 'rows', flips(bit, lax.axis_size('rows')))  15.8 us
    ppermute x2, starting transfers between devices, on_device(): summed = summed + lax.ppermute(summed, 'rows', flips(bit, owners))  9.35 us
    pallas_call x1, Pallas kernels, panel_products(): pl.pallas_call(functools.partial(panel_kernel, len(parts)), out_shape=(ja...  8.16 us
    all_to_all x1, starting transfers between devices, on_device(): lax.all_to_all(last, 'rows', split_axis=0, concat_axis=0, tiled=True)  7.45 us
  transfers between devices with their start and end apart: 22, of which 8 were waited for; matrix products, arithmetic and copies ran while one was open for 16% of the time, Pallas kernels for 29%

profile of v4, /device:TPU:0, one launch (start us, length us, event | category | flops | bytes accessed | tf_op | source)
XLA Modules:
  0.0 211.3 jit_solution(7552945511999022264)
XLA Ops:
  1.1 4.0 %pack.1 = (bf16[16,192,512]{2,1,0:T(8,128)(2,1)}, bf16[16,64,512]{2,1,0:T(8,128)(2,1)}) custom-call(s32[1]{0:T(128)} %bitcast.6.me_ref, s32[16,25]{1,0:T(8,128)} %dest_ref.1, s32[16]{0:T(128)} %cnt_ref.1, bf16[25,128,512]{2,1,0:T(8,128)(2,1)} %bitcast.20), custom_call_target="tpu_custom_call" | custom-call | bytes 6553600 | tf_op jit(solution)/shard_map/pack/pallas_call | solution.py:111
  5.1 7.4 %all-to-all-start = ((bf16[16,192,512]{2,1,0:T(8,128)(2,1)}), bf16[16,192,512]{2,1,0:T(8,128)(2,1)S(1)}, u32[]{:S(2)}, u32[]{:S(2)}) async-start(bf16[16,192,512]{2,1,0:T(8,128)(2,1)} %get-tuple-element.17), calls=%async_computation | async-start | bytes 6291456 | tf_op jit(solution)/shard_map/all_to_all | solution.py:531
  12.6 1.9 slice.25
  16.0 0.8 reduce_window_sum.28
  17.4 1.9 broadcast_select_fusion.refs_2_
  19.4 8.2 %panel_products.1 = (f32[256,256]{1,0:T(8,128)}, bf16[3200,256]{1,0:T(8,128)(2,1)}) custom-call(s32[1]{0:T(128)} %dynamic_slice.31.cnt_ref, s32[2]{0:T(128)} %pad_add_fusion.off_ref, f32[25]{0:T(128)} %convert_element_type.10.w_ref, bf16[3200,512]{1,0:T(8,128)(2,1)} %refs_0_.3, bf16[3200,512]{1,0:T(8,128)(2,1)} %collective-permute-done.refs_1_, ...), custom_call_target="tpu_custom_call" | custom-call | flops 2097152000 | bytes 6553600 | tf_op jit(solution)/shard_map/panel_products/pallas_call | solution.py:300
  27.5 0.9 constant_dynamic-slice_fusion.5
  28.5 2.8 %collective-permute-start.3 = (f32[136,256]{1,0:T(8,128)S(1)}, f32[136,256]{1,0:T(8,128)S(1)}, u32[]{:S(2)}, u32[]{:S(2)}) collective-permute-start(f32[136,256]{1,0:T(8,128)S(1)} %pad_maximum_fusion.2), channel_id=1, source_target_pairs={{0,4},{2,6},{4,0},{6,2},{8,12},{10,14},{12,8},{14,10},{16,20},{18,... | collective-permute-start | bytes 417800 | tf_op jit(solution)/shard_map/ppermute | solution.py:472
  31.2 24.8 %column_products.1 = f32[2048,256]{1,0:T(8,128)} custom-call(s32[2]{0:T(128)} %pad_add_fusion.off_ref, bf16[3200,512]{1,0:T(8,128)(2,1)} %refs_0_.3, bf16[3200,512]{1,0:T(8,128)(2,1)} %collective-permute-done.refs_1_, bf16[3200,256]{1,0:T(8,128)(2,1)} %get-tuple-element.13.refs_2_, bf16[2048,1024]{1,0:T(8,128)(2,1)} %refs_3_.3), custom_call_target="tpu_custom_call" | custom-call | flops 16777216000 | bytes 6553600 | tf_op jit(solution)/shard_map/column_products/pallas_call | solution.py:347
  56.0 2.6 %constant_dynamic-slice_fusion.4 = (f32[512,256]{1,0:T(8,128)}, f32[512,256]{1,0:T(8,128)}, f32[512,256]{1,0:T(8,128)}) fusion(f32[2048,256]{1,0:T(8,128)} %column_products.1, s32[]{:T(128)S(6)} %select_n.226, s32[]{:T(128)S(6)} %select_n.228, s32[]{:T(128)S(6)} %select_n.227), kind=kLoop, calls=%fused_computation.27 | loop fusion | bytes 3145740 | tf_op jit(solution)/shard_map/dynamic_slice | solution.py:478
  58.6 1.5 collective-permute-start.9
  60.1 2.0 collective-permute-start.8
  62.8 1.4 broadcast_in_dim_reshape.4
  64.2 1.5 collective-permute-start.2
  65.7 1.3 pad_bitcast_fusion
  66.9 1.5 reduce-window.9
  68.5 1.3 slice.22
  69.7 1.2 reduce-window.12
  71.0 0.8 slice_reduce_fusion
  71.8 24.1 %collective-permute-done.4 = f32[136,256]{1,0:T(8,128)} collective-permute-done((f32[136,256]{1,0:T(8,128)S(1)}, f32[136,256]{1,0:T(8,128)}, u32[]{:S(2)}, u32[]{:S(2)}) %collective-permute-start.4) | collective-permute-done | bytes 139296 | tf_op jit(solution)/shard_map/ppermute | solution.py:472
  95.9 2.9 %collective-permute-done.2 = f32[136,256]{1,0:T(8,128)} collective-permute-done((f32[136,256]{1,0:T(8,128)S(1)}, f32[136,256]{1,0:T(8,128)}, u32[]{:S(2)}, u32[]{:S(2)}) %collective-permute-start.2) | collective-permute-done | bytes 139296 | tf_op jit(solution)/shard_map/ppermute | solution.py:472
  98.8 1.0 add_add_fusion.1
  100.4 1.7 add_add_fusion
  102.1 0.8 copy-done.1
  103.6 1.5 collective-permute-start.10
  105.2 8.8 %collective-permute-start.6 = (f32[136,256]{1,0:T(8,128)S(1)}, f32[136,256]{1,0:T(8,128)S(1)}, u32[]{:S(2)}, u32[]{:S(2)}) collective-permute-start(f32[136,256]{1,0:T(8,128)S(1)} %add.111), channel_id=1, source_target_pairs={{0,16},{2,18},{4,20},{6,22},{8,24},{10,26},{12,28},{14,30},{16,0},... | collective-permute-start | bytes 417800 | tf_op jit(solution)/shard_map/ppermute | solution.py:545
  114.0 3.1 %collective-permute-done.6 = f32[136,256]{1,0:T(8,128)S(1)} collective-permute-done((f32[136,256]{1,0:T(8,128)S(1)}, f32[136,256]{1,0:T(8,128)S(1)}, u32[]{:S(2)}, u32[]{:S(2)}) %collective-permute-start.6) | collective-permute-done | bytes 139296 | tf_op jit(solution)/shard_map/ppermute | solution.py:545
  117.8 1.1 dynamic-slice_add_fusion
  119.5 4.9 %collective-permute-start.11 = (f32[128,256]{1,0:T(8,128)}, f32[128,256]{1,0:T(8,128)}, u32[]{:S(2)}, u32[]{:S(2)}) collective-permute-start(f32[128,256]{1,0:T(8,128)} %constant_dynamic-slice_fusion), channel_id=1, source_target_pairs={{0,16},{2,18},{4,20},{6,22},{8,24},{10,26},{12,28},{14,30},{16,0},... | collective-permute-start | bytes 393224 | tf_op jit(solution)/shard_map/ppermute | solution.py:488
  124.4 1.3 broadcast_compare_fusion
  125.6 0.8 broadcast_in_dim.50
  126.4 1.8 maximum_select_fusion.gram_ref
  128.3 1.6 dynamic-slice_add_fusion.1
  129.9 7.4 %all-to-all-start.1 = ((bf16[16,64,512]{2,1,0:T(8,128)(2,1)}), bf16[16,64,512]{2,1,0:T(8,128)(2,1)}, u32[]{:S(2)}, u32[]{:S(2)}) async-start(bf16[16,64,512]{2,1,0:T(8,128)(2,1)} %get-tuple-element.18), calls=%async_computation.1 | async-start | bytes 2097152 | tf_op jit(solution)/shard_map/all_to_all | solution.py:560
  137.3 24.0 %factor.1.refs_4_ = f32[256,256]{1,0:T(8,128)} custom-call(f32[256,256]{1,0:T(8,128)} %maximum_select_fusion.gram_ref), custom_call_target="tpu_custom_call" | custom-call | flops 20000000000 | bytes 524288 | tf_op jit(solution)/shard_map/factor/pallas_call | solution.py:204
  161.4 1.3 convolution_convert_fusion
  162.7 3.7 %collective-permute-start.15 = (bf16[128,256]{1,0:T(8,128)(2,1)S(1)}, bf16[128,256]{1,0:T(8,128)(2,1)S(1)}, u32[]{:S(2)}, u32[]{:S(2)}) collective-permute-start(bf16[128,256]{1,0:T(8,128)(2,1)S(1)} %convolution_convert_fusion), channel_id=1, source_target_pairs={{0,24},{2,26},{4,28},{6,30},{8,16},{10,18},{12,20},{14,22},{16,8},... | collective-permute-start | bytes 196616 | tf_op jit(solution)/shard_map/ppermute | solution.py:472
  166.5 0.7 collective-permute-start.13
  167.8 1.6 collective-permute-done.15
  169.4 1.7 collective-permute-done.14
  171.1 0.9 collective-permute-done.13
  172.0 3.6 %select.24 = bf16[13,128,512]{2,1,0:T(8,128)(2,1)} custom-call(s32[13]{0:T(128)} %select_reduce_fusion.pos_ref, bf16[16,192,512]{2,1,0:T(8,128)(2,1)} %copy-done, bf16[16,64,512]{2,1,0:T(8,128)(2,1)} %all-to-all-done.1.refs_1_), custom_call_target="tpu_custom_call" | custom-call | bytes 3407872 | tf_op jit(solution)/shard_map/select/pallas_call | solution.py:148
  175.7 2.4 %collective-permute-start.19 = (bf16[512,256]{1,0:T(8,128)(2,1)S(1)}, bf16[512,256]{1,0:T(8,128)(2,1)S(1)}, u32[]{:S(2)}, u32[]{:S(2)}) collective-permute-start(bf16[512,256]{1,0:T(8,128)(2,1)S(1)} %pad_maximum_fusion.1), channel_id=1, source_target_pairs={{0,6},{2,4},{4,2},{6,0},{8,14},{10,12},{12,10},{14,8},{16,22},{18,... | collective-permute-start | bytes 786440 | tf_op jit(solution)/shard_map/ppermute | solution.py:472
  179.9 5.9 %collective-permute-done.19 = bf16[512,256]{1,0:T(8,128)(2,1)S(1)} collective-permute-done((bf16[512,256]{1,0:T(8,128)(2,1)S(1)}, bf16[512,256]{1,0:T(8,128)(2,1)S(1)}, u32[]{:S(2)}, u32[]{:S(2)}) %collective-permute-start.19) | collective-permute-done | bytes 262176 | tf_op jit(solution)/shard_map/ppermute | solution.py:472
  185.8 5.1 %collective-permute-done.18 = bf16[512,256]{1,0:T(8,128)(2,1)S(1)} collective-permute-done((bf16[512,256]{1,0:T(8,128)(2,1)S(1)}, bf16[512,256]{1,0:T(8,128)(2,1)S(1)}, u32[]{:S(2)}, u32[]{:S(2)}) %collective-permute-start.18) | collective-permute-done | bytes 262176 | tf_op jit(solution)/shard_map/ppermute | solution.py:472
  190.9 1.1 pad_maximum_fusion.refs_5_
  192.1 1.2 copy-done.13
  193.3 17.9 %remainder_rows.1 = (bf16[1664,2048]{1,0:T(8,128)(2,1)}, f32[256,2048]{1,0:T(8,128)}) custom-call(s32[1]{0:T(128)} %bitcast.quarter_ref, s32[2]{0:T(128)} %pad_add_fusion.off_ref, f32[13]{0:T(128)} %select_reduce_fusion.1.w_ref, s32[1]{0:T(128)} %bitcast.5.group_ref, bf16[1664,512]{1,0:T(8,128)(2,1)} %bitcast.22, bf16[1664,512]{1,0:T(8,128)(2,1)} %copy-done.13, ...), custom_call_target="tpu_custom_call" | custom-call | flops 10468982784 | bytes 14417920 | tf_op jit(solution)/shard_map/remainder_rows/pallas_call | solution.py:446
  (76 shorter events, 8.9 us)
Async XLA Ops:
  0.6 18.7 %collective-permute-start = (bf16[3200,512]{1,0:T(8,128)(2,1)}, bf16[3200,512]{1,0:T(8,128)(2,1)}, u32[]{:S(2)}, u32[]{:S(2)}) collective-permute-start(bf16[3200,512]{1,0:T(8,128)(2,1)} %refs_0_.3), channel_id=1, source_target_pairs={{0,1},{1,0},{2,3},{3,2},{4,5},{5,4},{6,7},{7,6},{8,9},{9,8},{10,11... | collective-permute-start | bytes 9830408 | tf_op jit(solution)/shard_map/ppermute | solution.py:217
  5.1 9.5 %copy-start.3 = (s32[16,25]{1,0:T(8,128)S(1)}, s32[16,25]{1,0:T(8,128)}, u32[]{:S(2)}) copy-start(s32[16,25]{1,0:T(8,128)} %dest_ref.1) | copy-start | bytes 4804
  5.1 9.5 %copy-start.10 = (s32[16]{0:T(128)S(1)}, s32[16]{0:T(128)}, u32[]{:S(2)}) copy-start(s32[16]{0:T(128)} %cnt_ref.1) | copy-start | bytes 196
  5.1 10.2 %copy-start.14 = (bf16[25]{0:T(256)(128)(2,1)S(1)}, bf16[25]{0:T(256)(128)(2,1)}, u32[]{:S(2)}) copy-start(bf16[25]{0:T(256)(128)(2,1)} %param.7) | copy-start | bytes 154
  5.1 124.7 %all-to-all-start = ((bf16[16,192,512]{2,1,0:T(8,128)(2,1)}), bf16[16,192,512]{2,1,0:T(8,128)(2,1)S(1)}, u32[]{:S(2)}, u32[]{:S(2)}) async-start(bf16[16,192,512]{2,1,0:T(8,128)(2,1)} %get-tuple-element.17), calls=%async_computation | async-start | bytes 6291456 | tf_op jit(solution)/shard_map/all_to_all | solution.py:531
  14.4 3.0 %collective-permute-start.1 = (bf16[256,1024]{1,0:T(8,128)(2,1)}, bf16[256,1024]{1,0:T(8,128)(2,1)}, u32[]{:S(2)}, u32[]{:S(2)}) collective-permute-start(bf16[256,1024]{1,0:T(8,128)(2,1)} %slice.25), channel_id=1, source_target_pairs={{0,1},{1,0},{2,3},{3,2},{4,5},{5,4},{6,7},{7,6},{8,9},{9,8},{10,11... | collective-permute-start | bytes 1572872 | tf_op jit(solution)/shard_map/ppermute | solution.py:525
  14.7 12.8 %copy-start.6 = (s32[16,25]{1,0:T(8,128)}, s32[16,25]{1,0:T(8,128)S(1)}, u32[]{:S(2)}) copy-start(s32[16,25]{1,0:T(8,128)S(1)} %fusion.2) | copy-start | bytes 4804
  16.8 11.6 %copy-start.5 = (f32[8,256]{1,0:T(8,128)}, f32[8,256]{1,0:T(8,128)S(1)}, u32[]{:S(2)}) copy-start(f32[8,256]{1,0:T(8,128)S(1)} %reshape.49) | copy-start | bytes 24580
  28.5 35.7 %collective-permute-start.3 = (f32[136,256]{1,0:T(8,128)S(1)}, f32[136,256]{1,0:T(8,128)S(1)}, u32[]{:S(2)}, u32[]{:S(2)}) collective-permute-start(f32[136,256]{1,0:T(8,128)S(1)} %pad_maximum_fusion.2), channel_id=1, source_target_pairs={{0,4},{2,6},{4,0},{6,2},{8,12},{10,14},{12,8},{14,10},{16,20},{18,... | collective-permute-start | bytes 417800 | tf_op jit(solution)/shard_map/ppermute | solution.py:472
  56.0 6.1 %copy-start.4 = (s32[16,25]{1,0:T(8,128)S(1)}, s32[16,25]{1,0:T(8,128)}, u32[]{:S(2)}) copy-start(s32[16,25]{1,0:T(8,128)} %dest_ref.1) | copy-start | bytes 4804
  56.0 6.1 %copy-start.7 = (s32[16,25]{1,0:T(8,128)S(1)}, s32[16,25]{1,0:T(8,128)}, u32[]{:S(2)}) copy-start(s32[16,25]{1,0:T(8,128)} %reduce_window_sum.28) | copy-start | bytes 4804
  56.0 6.1 %copy-start.11 = (s32[16]{0:T(128)S(1)}, s32[16]{0:T(128)}, u32[]{:S(2)}) copy-start(s32[16]{0:T(128)} %cnt_ref.1) | copy-start | bytes 196
  58.6 41.8 %collective-permute-start.7 = (f32[512,256]{1,0:T(8,128)}, f32[512,256]{1,0:T(8,128)}, u32[]{:S(2)}, u32[]{:S(2)}) collective-permute-start(f32[512,256]{1,0:T(8,128)} %get-tuple-element.22), channel_id=1, source_target_pairs={{0,2},{2,0},{4,6},{6,4},{8,10},{10,8},{12,14},{14,12},{16,18},{18,... | collective-permute-start | bytes 1572872 | tf_op jit(solution)/shard_map/ppermute | solution.py:472
  58.6 41.8 %collective-permute-start.9 = (f32[512,256]{1,0:T(8,128)}, f32[512,256]{1,0:T(8,128)}, u32[]{:S(2)}, u32[]{:S(2)}) collective-permute-start(f32[512,256]{1,0:T(8,128)} %get-tuple-element.23), channel_id=1, source_target_pairs={{0,6},{2,4},{4,2},{6,0},{8,14},{10,12},{12,10},{14,8},{16,22},{18,... | collective-permute-start | bytes 1572872 | tf_op jit(solution)/shard_map/ppermute | solution.py:472
  60.1 40.3 %collective-permute-start.8 = (f32[512,256]{1,0:T(8,128)}, f32[512,256]{1,0:T(8,128)}, u32[]{:S(2)}, u32[]{:S(2)}) collective-permute-start(f32[512,256]{1,0:T(8,128)} %get-tuple-element.24), channel_id=1, source_target_pairs={{0,4},{2,6},{4,0},{6,2},{8,12},{10,14},{12,8},{14,10},{16,20},{18,... | collective-permute-start | bytes 1572872 | tf_op jit(solution)/shard_map/ppermute | solution.py:472
  64.2 31.7 %collective-permute-start.4 = (f32[136,256]{1,0:T(8,128)S(1)}, f32[136,256]{1,0:T(8,128)}, u32[]{:S(2)}, u32[]{:S(2)}) collective-permute-start(f32[136,256]{1,0:T(8,128)S(1)} %pad_maximum_fusion.2), channel_id=1, source_target_pairs={{0,6},{2,4},{4,2},{6,0},{8,14},{10,12},{12,10},{14,8},{16,22},{18,... | collective-permute-start | bytes 417800 | tf_op jit(solution)/shard_map/ppermute | solution.py:472
  64.2 34.6 %collective-permute-start.2 = (f32[136,256]{1,0:T(8,128)S(1)}, f32[136,256]{1,0:T(8,128)}, u32[]{:S(2)}, u32[]{:S(2)}) collective-permute-start(f32[136,256]{1,0:T(8,128)S(1)} %pad_maximum_fusion.2), channel_id=1, source_target_pairs={{0,2},{2,0},{4,6},{6,4},{8,10},{10,8},{12,14},{14,12},{16,18},{18,... | collective-permute-start | bytes 417800 | tf_op jit(solution)/shard_map/ppermute | solution.py:472
  71.0 34.1 %copy-start.9 = (s32[4,128]{1,0:T(4,128)S(1)}, s32[4,128]{1,0:T(4,128)}, u32[]{:S(2)}) copy-start(s32[4,128]{1,0:T(4,128)} %reduce-window.9) | copy-start | bytes 6148
  99.8 14.2 %copy-start.8 = (s32[400]{0:T(512)S(1)}, s32[400]{0:T(512)}, u32[]{:S(2)}) copy-start(s32[400]{0:T(512)} %broadcast_in_dim_reshape.4) | copy-start | bytes 4804
  99.8 5.4 %collective-permute-start.5 = (f32[136,256]{1,0:T(8,128)S(1)}, f32[136,256]{1,0:T(8,128)S(1)}, u32[]{:S(2)}, u32[]{:S(2)}) collective-permute-start(f32[136,256]{1,0:T(8,128)S(1)} %add_add_fusion.1), channel_id=1, source_target_pairs={{0,8},{2,10},{4,12},{6,14},{8,0},{10,2},{12,4},{14,6},{16,24},{18,... | collective-permute-start | bytes 417800 | tf_op jit(solution)/shard_map/ppermute | solution.py:545
  102.0 0.8 copy-start.1
  103.6 14.2 %collective-permute-start.10 = (f32[256,256]{1,0:T(8,128)}, f32[256,256]{1,0:T(8,128)}, u32[]{:S(2)}, u32[]{:S(2)}) collective-permute-start(f32[256,256]{1,0:T(8,128)} %constant_dynamic-slice_fusion.1), channel_id=1, source_target_pairs={{0,8},{2,10},{4,12},{6,14},{8,0},{10,2},{12,4},{14,6},{16,24},{18,... | collective-permute-start | bytes 786440 | tf_op jit(solution)/shard_map/ppermute | solution.py:488
  105.2 11.9 %collective-permute-start.6 = (f32[136,256]{1,0:T(8,128)S(1)}, f32[136,256]{1,0:T(8,128)S(1)}, u32[]{:S(2)}, u32[]{:S(2)}) collective-permute-start(f32[136,256]{1,0:T(8,128)S(1)} %add.111), channel_id=1, source_target_pairs={{0,16},{2,18},{4,20},{6,22},{8,24},{10,26},{12,28},{14,30},{16,0},... | collective-permute-start | bytes 417800 | tf_op jit(solution)/shard_map/ppermute | solution.py:545
  117.7 8.7 %collective-permute-start.12 = (f32[128,256]{1,0:T(8,128)}, f32[128,256]{1,0:T(8,128)}, u32[]{:S(2)}, u32[]{:S(2)}) collective-permute-start(f32[128,256]{1,0:T(8,128)} %slice.31), channel_id=1, source_target_pairs={{0,1},{1,0},{2,3},{3,2},{4,5},{5,4},{6,7},{7,6},{8,9},{9,8},{10,11... | collective-permute-start | bytes 393224 | tf_op jit(solution)/shard_map/ppermute | solution.py:548
  119.5 8.8 %collective-permute-start.11 = (f32[128,256]{1,0:T(8,128)}, f32[128,256]{1,0:T(8,128)}, u32[]{:S(2)}, u32[]{:S(2)}) collective-permute-start(f32[128,256]{1,0:T(8,128)} %constant_dynamic-slice_fusion), channel_id=1, source_target_pairs={{0,16},{2,18},{4,20},{6,22},{8,24},{10,26},{12,28},{14,30},{16,0},... | collective-permute-start | bytes 393224 | tf_op jit(solution)/shard_map/ppermute | solution.py:488
  129.9 31.5 %copy-start = (bf16[16,192,512]{2,1,0:T(8,128)(2,1)}, bf16[16,192,512]{2,1,0:T(8,128)(2,1)S(1)}, u32[]{:S(2)}) copy-start(bf16[16,192,512]{2,1,0:T(8,128)(2,1)S(1)} %all-to-all-done.refs_0_) | copy-start | bytes 9437188
  129.9 42.1 %all-to-all-start.1 = ((bf16[16,64,512]{2,1,0:T(8,128)(2,1)}), bf16[16,64,512]{2,1,0:T(8,128)(2,1)}, u32[]{:S(2)}, u32[]{:S(2)}) async-start(bf16[16,64,512]{2,1,0:T(8,128)(2,1)} %get-tuple-element.18), calls=%async_computation.1 | async-start | bytes 2097152 | tf_op jit(solution)/shard_map/all_to_all | solution.py:560
  137.3 24.1 %copy-start.2 = (f32[128,256]{1,0:T(8,128)S(1)}, f32[128,256]{1,0:T(8,128)}, u32[]{:S(2)}) copy-start(f32[128,256]{1,0:T(8,128)} %dynamic-slice_add_fusion.1) | copy-start | bytes 393220
  137.3 29.9 %copy-start.12 = (pred[400]{0:T(512)(128)(4,1)S(1)}, pred[400]{0:T(512)(128)(4,1)}, u32[]{:S(2)}) copy-start(pred[400]{0:T(512)(128)(4,1)} %broadcast_compare_fusion) | copy-start | bytes 1204
  162.7 6.7 %collective-permute-start.15 = (bf16[128,256]{1,0:T(8,128)(2,1)S(1)}, bf16[128,256]{1,0:T(8,128)(2,1)S(1)}, u32[]{:S(2)}, u32[]{:S(2)}) collective-permute-start(bf16[128,256]{1,0:T(8,128)(2,1)S(1)} %convolution_convert_fusion), channel_id=1, source_target_pairs={{0,24},{2,26},{4,28},{6,30},{8,16},{10,18},{12,20},{14,22},{16,8},... | collective-permute-start | bytes 196616 | tf_op jit(solution)/shard_map/ppermute | solution.py:472
  166.5 4.6 %collective-permute-start.14 = (bf16[128,256]{1,0:T(8,128)(2,1)S(1)}, bf16[128,256]{1,0:T(8,128)(2,1)S(1)}, u32[]{:S(2)}, u32[]{:S(2)}) collective-permute-start(bf16[128,256]{1,0:T(8,128)(2,1)S(1)} %convolution_convert_fusion), channel_id=1, source_target_pairs={{0,8},{2,10},{4,12},{6,14},{8,0},{10,2},{12,4},{14,6},{16,24},{18,... | collective-permute-start | bytes 196616 | tf_op jit(solution)/shard_map/ppermute | solution.py:472
  166.5 5.5 %collective-permute-start.13 = (bf16[128,256]{1,0:T(8,128)(2,1)S(1)}, bf16[128,256]{1,0:T(8,128)(2,1)S(1)}, u32[]{:S(2)}, u32[]{:S(2)}) collective-permute-start(bf16[128,256]{1,0:T(8,128)(2,1)S(1)} %convolution_convert_fusion), channel_id=1, source_target_pairs={{0,16},{2,18},{4,20},{6,22},{8,24},{10,26},{12,28},{14,30},{16,0},... | collective-permute-start | bytes 196616 | tf_op jit(solution)/shard_map/ppermute | solution.py:472
  175.6 16.5 %collective-permute-start.16 = (bf16[1664,512]{1,0:T(8,128)(2,1)}, bf16[1664,512]{1,0:T(8,128)(2,1)S(1)}, u32[]{:S(2)}, u32[]{:S(2)}) collective-permute-start(bf16[1664,512]{1,0:T(8,128)(2,1)} %bitcast.21), channel_id=1, source_target_pairs={{0,1},{1,0},{2,3},{3,2},{4,5},{5,4},{6,7},{7,6},{8,9},{9,8},{10,11... | collective-permute-start | bytes 5111816 | tf_op jit(solution)/shard_map/ppermute | solution.py:217
  175.7 10.1 %collective-permute-start.19 = (bf16[512,256]{1,0:T(8,128)(2,1)S(1)}, bf16[512,256]{1,0:T(8,128)(2,1)S(1)}, u32[]{:S(2)}, u32[]{:S(2)}) collective-permute-start(bf16[512,256]{1,0:T(8,128)(2,1)S(1)} %pad_maximum_fusion.1), channel_id=1, source_target_pairs={{0,6},{2,4},{4,2},{6,0},{8,14},{10,12},{12,10},{14,8},{16,22},{18,... | collective-permute-start | bytes 786440 | tf_op jit(solution)/shard_map/ppermute | solution.py:472
  178.0 12.9 %collective-permute-start.18 = (bf16[512,256]{1,0:T(8,128)(2,1)S(1)}, bf16[512,256]{1,0:T(8,128)(2,1)S(1)}, u32[]{:S(2)}, u32[]{:S(2)}) collective-permute-start(bf16[512,256]{1,0:T(8,128)(2,1)S(1)} %pad_maximum_fusion.1), channel_id=1, source_target_pairs={{0,4},{2,6},{4,0},{6,2},{8,12},{10,14},{12,8},{14,10},{16,20},{18,... | collective-permute-start | bytes 786440 | tf_op jit(solution)/shard_map/ppermute | solution.py:472
  178.6 12.4 %collective-permute-start.17 = (bf16[512,256]{1,0:T(8,128)(2,1)S(1)}, bf16[512,256]{1,0:T(8,128)(2,1)S(1)}, u32[]{:S(2)}, u32[]{:S(2)}) collective-permute-start(bf16[512,256]{1,0:T(8,128)(2,1)S(1)} %pad_maximum_fusion.1), channel_id=1, source_target_pairs={{0,2},{2,0},{4,6},{6,4},{8,10},{10,8},{12,14},{14,12},{16,18},{18,... | collective-permute-start | bytes 786440 | tf_op jit(solution)/shard_map/ppermute | solution.py:472
  192.1 1.2 copy-start.13

commit v5 on v4

--- a/solution.py
+++ b/solution.py
@@ -64,11 +64,11 @@
     return [(a, b, sems.at[i]) for i, (a, b) in enumerate(pairs)]
 
 
-def pack_kernel(per_pair, me_ref, dest_ref, cnt_ref, desc_ref, *refs):
+def pack_kernel(per_pair, dest_ref, cnt_ref, desc_ref, *refs):
     out_refs, (ctr_ref, rank_ref, sems) = refs[:per_pair], refs[per_pair:]
     slots = desc_ref.shape[0]
     owners = ctr_ref.shape[0]
-    me = me_ref[0]
+    me = lax.axis_index("rows")
     count = cnt_ref[me]
 
     def copies(j, d, rank):
@@ -104,7 +104,7 @@
                         c.wait()
 
 
-def pack(desc_blocks, me, destinations, counts, per_pair):
+def pack(desc_blocks, destinations, counts, per_pair):
     slots, blk, feat = desc_blocks.shape
     owners = destinations.shape[0]
     heights = [blk] if per_pair == 1 else [blk + HEAD, blk - HEAD]
@@ -113,7 +113,7 @@
         out_shape=[
             jax.ShapeDtypeStruct((owners, h, feat), desc_blocks.dtype) for h in heights
         ],
-        in_specs=[SMEM, SMEM, SMEM, VMEM],
+        in_specs=[SMEM, SMEM, VMEM],
         out_specs=[ANY] * per_pair,
         scratch_shapes=[
             pltpu.SMEM((owners,), jnp.int32),
@@ -123,7 +123,7 @@
         compiler_params=params(),
         cost_estimate=cost(0, 4 * slots * blk * feat),
         name="pack",
-    )(me, destinations, counts, desc_blocks)
+    )(destinations, counts, desc_blocks)
 
 
 def select_kernel(per_pair, pos_ref, *refs):
@@ -220,21 +220,20 @@
     return [full[i] for i in range(groups)]
 
 
-def part_offsets(feat):
-    groups = lax.axis_size("cols")
-    if groups == 2:
+def part_offset(i, feat):
+    if lax.axis_size("cols") == 2:
         c = lax.axis_index("cols")
-        return jnp.stack([c * feat, (1 - c) * feat]).astype(jnp.int32)
-    return jnp.arange(groups, dtype=jnp.int32) * feat
-
-
-def join_copies(parts, off_ref, x_ref, sems, spans):
+        return (c if i == 0 else 1 - c) * feat
+    return i * feat
+
+
+def join_copies(parts, x_ref, sems, spans):
     feat = parts[0].shape[1]
     return [
         [
             pltpu.make_async_copy(
                 ref.at[pl.ds(start, size)],
-                x_ref.at[pl.ds(start, size), pl.ds(pl.multiple_of(off_ref[i], 128), feat)],
+                x_ref.at[pl.ds(start, size), pl.ds(pl.multiple_of(part_offset(i, feat), 128), feat)],
                 sems.at[t, i],
             )
             for i, ref in enumerate(parts)
@@ -261,17 +260,38 @@
     return per, [(i * BLK, per * BLK) for i in range(0, blocks, per)]
 
 
-def panel_kernel(nparts, cnt_ref, off_ref, w_ref, *refs):
+def panel_kernel(nparts, cnt_ref, w_ref, *refs):
     parts = refs[:nparts]
-    sp_ref, gram_ref, pw_ref, x_ref, sems = refs[nparts:]
+    s_ref, moved_ref, gram_ref, pw_ref, sp_ref, x_ref, sems, sp_sem = refs[nparts:]
     per, tiles = row_tiles(x_ref.shape[0])
-    count = cnt_ref[0]
-    copies = join_copies(parts, off_ref, x_ref, sems, tiles)
-    for group in copies:
-        for c in group:
+    count = cnt_ref[lax.axis_index("rows")]
+    group = lax.axis_index("cols")
+    own = pltpu.make_async_copy(s_ref.at[pl.ds(0, PANEL)], sp_ref, sp_sem)
+    other = pltpu.make_async_copy(moved_ref, sp_ref, sp_sem)
+
+    @pl.when(group == 0)
+    def _():
+        own.start()
+
+    @pl.when(group != 0)
+    def _():
+        other.start()
+
+    copies = join_copies(parts, x_ref, sems, tiles)
+    for moves in copies:
+        for c in moves:
             c.start()
     gram_ref[...] = jnp.zeros_like(gram_ref)
     pw_ref[...] = jnp.zeros_like(pw_ref)
+
+    @pl.when(group == 0)
+    def _():
+        own.wait()
+
+    @pl.when(group != 0)
+    def _():
+        other.wait()
+
     points = column_scale(sp_ref[...])
     for t, (start, size) in enumerate(tiles):
         for c in copies[t]:
@@ -293,36 +313,38 @@
             )
 
 
-def panel_products(parts, offsets, count, weights, sp):
+def panel_products(parts, counts, weights, s, moved):
     rows, feat = parts[0].shape
-    width = sp.shape[1]
+    width = s.shape[1]
     tiles = len(row_tiles(rows)[1])
     return pl.pallas_call(
         functools.partial(panel_kernel, len(parts)),
         out_shape=(
             jax.ShapeDtypeStruct((PANEL, PANEL), jnp.float32),
             jax.ShapeDtypeStruct((rows, PANEL), jnp.bfloat16),
+            jax.ShapeDtypeStruct((PANEL, width), jnp.bfloat16),
         ),
-        in_specs=[SMEM, SMEM, SMEM] + [ANY] * len(parts) + [VMEM],
-        out_specs=(VMEM, VMEM),
+        in_specs=[SMEM, SMEM] + [ANY] * (len(parts) + 2),
+        out_specs=(VMEM, VMEM, VMEM),
         scratch_shapes=[
             pltpu.VMEM((rows, width), jnp.bfloat16),
             pltpu.SemaphoreType.DMA((tiles, len(parts))),
+            pltpu.SemaphoreType.DMA,
         ],
         compiler_params=params(),
         cost_estimate=cost(2 * rows * PANEL * (width + PANEL), 2 * rows * width),
         name="panel_products",
-    )(count, offsets, weights, *parts, sp)
-
-
-def column_kernel(nparts, off_ref, *refs):
+    )(counts, weights, *parts, s, moved)
+
+
+def column_kernel(nparts, *refs):
     parts = refs[:nparts]
     pw_ref, s_ref, g_ref, x_ref, sems = refs[nparts:]
     width = x_ref.shape[1]
 
     @pl.when(pl.program_id(0) == 0)
     def _():
-        copies = join_copies(parts, off_ref, x_ref, sems, row_tiles(x_ref.shape[0])[1])
+        copies = join_copies(parts, x_ref, sems, row_tiles(x_ref.shape[0])[1])
         for group in copies:
             for c in group:
                 c.start()
@@ -338,7 +360,7 @@
     g_ref[...] = products / (width * square)
 
 
-def column_products(parts, offsets, pw, s):
+def column_products(parts, pw, s):
     rows, feat = parts[0].shape
     size, width = s.shape
     chunk = min(512, size)
@@ -348,8 +370,7 @@
         functools.partial(column_kernel, len(parts)),
         grid=(size // chunk,),
         out_shape=jax.ShapeDtypeStruct((size, PANEL), jnp.float32),
-        in_specs=[SMEM]
-        + [ANY] * len(parts)
+        in_specs=[ANY] * len(parts)
         + [
             pl.BlockSpec((rows, PANEL), lambda i: (0, 0), pipeline_mode=once),
             pl.BlockSpec((chunk, width), lambda i: (i, 0)),
@@ -362,28 +383,27 @@
         compiler_params=params(dimension_semantics=("arbitrary",)),
         cost_estimate=cost(2 * rows * (width + PANEL) * size, 2 * rows * width),
         name="column_products",
-    )(offsets, *parts, pw, s)
-
-
-def remainder_kernel(nparts, norm, quarter_ref, off_ref, w_ref, group_ref, *refs):
+    )(*parts, pw, s)
+
+
+def rows_kernel(nparts, w_ref, *refs):
     parts = refs[:nparts]
-    sp_ref, s_ref, inv_ref, rt_ref, out_ref, proj_ref, x_ref, p_ref, rs_ref, sems = refs[nparts:]
-    rows_all, width = x_ref.shape
+    sp_ref, s_ref, kern_ref, p_ref, x_ref, rs_ref, sems = refs[nparts:]
+    rows_all = x_ref.shape[0]
     chunk = s_ref.shape[0]
-    step = pl.program_id(0)
     blocks = rows_all // BLK
     bounds = list(range(0, blocks, 7)) + [blocks]
     spans = [(a * BLK, b * BLK) for a, b in zip(bounds, bounds[1:])]
 
-    @pl.when(step == 0)
+    @pl.when(pl.program_id(0) == 0)
     def _():
-        copies = join_copies(parts, off_ref, x_ref, sems, [(a, b - a) for a, b in spans])
-        for group in copies:
-            for c in group:
+        copies = join_copies(parts, x_ref, sems, [(a, b - a) for a, b in spans])
+        for moves in copies:
+            for c in moves:
                 c.start()
         points = column_scale(sp_ref[...])
-        for (a, b), group in zip(spans, copies):
-            for c in group:
+        for (a, b), moves in zip(spans, copies):
+            for c in moves:
                 c.wait()
             for j in range(a // BLK, b // BLK):
                 scale = row_scale(x_ref[j * BLK : (j + 1) * BLK, :], w_ref[j])
@@ -392,43 +412,78 @@
             scale = jnp.concatenate([rs_ref[a:b, :]] * (PANEL // 128), axis=1)
             p_ref[a:b, :] = (inner * inner * scale * points).astype(jnp.bfloat16)
 
+    columns = column_scale(s_ref[...])
+    for a, b in spans:
+        inner = nt(x_ref[a:b, :], s_ref[...])
+        scale = jnp.concatenate([rs_ref[a:b, :]] * (chunk // 128), axis=1)
+        kern_ref[a:b, :] = (inner * inner * scale * columns).astype(jnp.bfloat16)
+
+
+def kernel_rows(parts, weights, sp, s):
+    rows, feat = parts[0].shape
+    cols, width = s.shape
+    chunk = min(512, cols)
+    once = pl.Buffered(1)
+    return pl.pallas_call(
+        functools.partial(rows_kernel, len(parts)),
+        grid=(cols // chunk,),
+        out_shape=(
+            jax.ShapeDtypeStruct((rows, cols), jnp.bfloat16),
+            jax.ShapeDtypeStruct((rows, PANEL), jnp.bfloat16),
+        ),
+        in_specs=[SMEM]
+        + [ANY] * len(parts)
+        + [
+            pl.BlockSpec((PANEL, width), lambda i: (0, 0), pipeline_mode=once),
+            pl.BlockSpec((chunk, width), lambda i: (i, 0)),
+        ],
+        out_specs=(
+            pl.BlockSpec((rows, chunk), lambda i: (0, i)),
+            pl.BlockSpec((rows, PANEL), lambda i: (0, 0)),
+        ),
+        scratch_shapes=[
+            pltpu.VMEM((rows, width), jnp.bfloat16),
+            pltpu.VMEM((rows, 128), jnp.float32),
+            pltpu.SemaphoreType.DMA((2, len(parts))),
+        ],
+        compiler_params=params(dimension_semantics=("arbitrary",)),
+        cost_estimate=cost(
+            2 * rows * width * (cols + PANEL), 2 * rows * width + 2 * cols * width + 2 * rows * cols
+        ),
+        name="kernel_rows",
+    )(weights, *parts, sp, s)
+
+
+def remainder_kernel(norm, quarter_ref, kern_ref, p_ref, inv_ref, rt_ref, out_ref, proj_ref):
+    chunk = kern_ref.shape[1]
+    step = pl.program_id(0)
     inv_high, inv_low = split(inv_ref[...])
     rt = rt_ref[0]
     coef = (nn(rt, inv_high) + nn(rt, inv_low)).astype(jnp.bfloat16)
     proj_ref[...] = rt.astype(jnp.float32).T * (1.0 / norm)
-    columns = column_scale(s_ref[...])
-    for a, b in spans:
-        inner = nt(x_ref[a:b, :], s_ref[...])
-        scale = jnp.concatenate([rs_ref[a:b, :]] * (chunk // 128), axis=1)
-        kern = (inner * inner * scale * columns).astype(jnp.bfloat16)
-        fit = nt(p_ref[a:b, :], coef)
-        out_ref[a:b, :] = (kern.astype(jnp.float32) - fit).astype(out_ref.dtype)
-
-    for i in range(-(-PANEL // chunk)):
-        part = min(chunk, PANEL)
-
-        @pl.when((step == i) & (group_ref[0] == 0))
+    fit = nt(p_ref[...], coef)
+    out_ref[...] = (kern_ref[...].astype(jnp.float32) - fit).astype(out_ref.dtype)
+
+    part = min(chunk, PANEL)
+    for i in range(PANEL // part):
+        @pl.when((step == i) & (lax.axis_index("cols") == 0))
         def _():
-            for a, b in spans:
-                panel = p_ref[a:b, :]
-                rows = slice(i * part, (i + 1) * part)
-                basis = nt(panel, inv_high[rows, :]) + nt(panel, inv_low[rows, :])
-                out_ref[a:b, :part] = (basis * norm).astype(out_ref.dtype)
-
-
-def remainder_rows(parts, offsets, weights, group, quarter, sp, s, inverse, rt, norm):
-    rows, feat = parts[0].shape
-    cols, width = s.shape
+            panel = p_ref[...]
+            rows = slice(i * part, (i + 1) * part)
+            basis = nt(panel, inv_high[rows, :]) + nt(panel, inv_low[rows, :])
+            out_ref[:, :part] = (basis * norm).astype(out_ref.dtype)
+
+
+def remainder_rows(kern, panel, quarter, inverse, rt, norm):
+    rows, cols = kern.shape
     chunk = rt.shape[1]
     once = pl.Buffered(1)
     spec = pltpu.PrefetchScalarGridSpec(
         num_scalar_prefetch=1,
         grid=(cols // chunk,),
-        in_specs=[SMEM, SMEM, SMEM]
-        + [ANY] * len(parts)
-        + [
-            pl.BlockSpec((PANEL, width), lambda i, q: (0, 0), pipeline_mode=once),
-            pl.BlockSpec((chunk, width), lambda i, q: (i, 0)),
+        in_specs=[
+            pl.BlockSpec((rows, chunk), lambda i, q: (0, i)),
+            pl.BlockSpec((rows, PANEL), lambda i, q: (0, 0), pipeline_mode=once),
             pl.BlockSpec((PANEL, PANEL), lambda i, q: (0, 0), pipeline_mode=once),
             pl.BlockSpec((1, chunk, PANEL), lambda i, q: (i ^ q[0], 0, 0)),
         ],
@@ -436,26 +491,18 @@
             pl.BlockSpec((rows, chunk), lambda i, q: (0, i)),
             pl.BlockSpec((PANEL, chunk), lambda i, q: (0, i)),
         ),
-        scratch_shapes=[
-            pltpu.VMEM((rows, width), jnp.bfloat16),
-            pltpu.VMEM((rows, PANEL), jnp.bfloat16),
-            pltpu.VMEM((rows, 128), jnp.float32),
-            pltpu.SemaphoreType.DMA((2, len(parts))),
-        ],
     )
     return pl.pallas_call(
-        functools.partial(remainder_kernel, len(parts), norm),
+        functools.partial(remainder_kernel, norm),
         grid_spec=spec,
         out_shape=(
             jax.ShapeDtypeStruct((rows, cols), jnp.bfloat16),
             jax.ShapeDtypeStruct((PANEL, cols), jnp.float32),
         ),
         compiler_params=params(dimension_semantics=("arbitrary",)),
-        cost_estimate=cost(
-            2 * rows * (width + 2 * PANEL) * cols, 2 * rows * width + 2 * cols * width + 2 * rows * cols
-        ),
+        cost_estimate=cost(2 * rows * PANEL * cols, 4 * rows * cols),
         name="remainder_rows",
-    )(quarter, offsets, weights, group, *parts, sp, s, inverse, rt)
+    )(quarter, kern, panel, inverse, rt)
 
 
 def flips(bit, size):
@@ -478,14 +525,6 @@
     pieces = [lax.dynamic_slice_in_dim(x, (q ^ k) * n, n, 0) for k in range(4)]
     got = [pieces[0]] + [trade(pieces[k], pair, k) for k in range(1, 4)]
     return (got[0] + got[1]) + (got[2] + got[3])
-
-
-def halve_sum(x, bit):
-    half = x.shape[0] // 2
-    upper = (lax.axis_index("rows") // bit) % 2
-    send = lax.dynamic_slice_in_dim(x, (1 - upper) * half, half, 0)
-    kept = lax.dynamic_slice_in_dim(x, upper * half, half, 0)
-    return kept + lax.ppermute(send, "rows", flips(bit, lax.axis_size("rows")))
 
 
 def gather_pieces(x, pair):
@@ -516,33 +555,34 @@
     feat = descriptors.shape[1]
     cols, width = sparse_points.shape
     norm = math.sqrt(owners * DST_BLK * BLK)
-    near = (1, 2)
-    far = [1 << i for i in range(2, owners.bit_length() - 1)]
+    pairs = [(1 << i, 2 << i) for i in range(0, owners.bit_length() - 1, 2)]
 
     first = sparse_points[:PANEL]
     source_parts = share_parts(descriptors)
     if groups == 2:
         moved = lax.ppermute(first, "cols", [(0, 1), (1, 0)])
-        panel_points = jnp.where(group == 0, first, moved)
     else:
-        panel_points = lax.all_gather(first, "cols", axis=0, tiled=False)[0]
+        moved = lax.all_gather(first, "cols", axis=0, tiled=False)[0]
     desc_blocks = descriptors.reshape(slots, BLK, feat)
-    outgoing = pack(desc_blocks, me[None], destinations, block_counts, per_pair)
+    outgoing = pack(desc_blocks, destinations, block_counts, per_pair)
     received = [lax.all_to_all(outgoing[0], "rows", split_axis=0, concat_axis=0, tiled=True)]
 
-    offsets = part_offsets(feat)
-    count = lax.dynamic_index_in_dim(block_counts, me, 0)
     weights32 = block_weights.astype(jnp.float32)
-    gram_part, pw = panel_products(source_parts, offsets, count, weights32, panel_points)
+    gram_part, pw, panel_points = panel_products(
+        source_parts, block_counts, weights32, sparse_points, moved
+    )
+    g = column_products(source_parts, pw, sparse_points)
+
     spare = -(-owners * slots // (PANEL * 8)) * 8
     table = lax.dynamic_update_slice(
         jnp.zeros((spare * PANEL,), jnp.float32), weights32, (me * slots,)
     ).reshape(spare, PANEL)
     if groups == 2:
         gram_part = lax.dynamic_slice_in_dim(gram_part, group * (PANEL // 2), PANEL // 2, 0)
-    summed = pair_sum(jnp.concatenate([gram_part, table], 0), near)
-    for bit in far:
-        summed = summed + lax.ppermute(summed, "rows", flips(bit, owners))
+    summed = pair_sum(jnp.concatenate([gram_part, table], 0), pairs[0])
+    summed, g = lax.optimization_barrier((summed, g))
+    for pair in pairs[1:]:
+        summed = pair_sum(summed, pair)
     gram, table = summed[:-spare], summed[-spare:]
     if groups == 2:
         other = lax.ppermute(gram, "cols", [(0, 1), (1, 0)])
@@ -550,17 +590,18 @@
             group == 0, jnp.concatenate([gram, other], 0), jnp.concatenate([other, gram], 0)
         )
     all_weights = table.reshape(-1)[: owners * slots]
+
+    g = scatter_sum(g, pairs[0])
+    if per_pair > 1:
+        g, gram, last = lax.optimization_barrier((g, gram, outgoing[1]))
+    for pair in pairs[1:]:
+        g = scatter_sum(g, pair)
+    if per_pair > 1:
+        received.append(lax.all_to_all(last, "rows", split_axis=0, concat_axis=0, tiled=True))
     inverse = factor(gram)
-
-    g = scatter_sum(column_products(source_parts, offsets, pw, sparse_points), near)
-    for bit in far:
-        g = halve_sum(g, bit)
-    if per_pair > 1:
-        g, last = lax.optimization_barrier((g, outgoing[1]))
-        received.append(lax.all_to_all(last, "rows", split_axis=0, concat_axis=0, tiled=True))
     rt = nt(g, inverse, HIGH).astype(jnp.bfloat16)
-    for i in range(len(far) - 1, 0, -2):
-        rt = gather_back(rt, (far[i], far[i - 1]))
+    for pair in pairs[:0:-1]:
+        rt = gather_back(rt, pair)
 
     slot_ids = jnp.arange(slots, dtype=jnp.int32)
     toward = ((slot_ids[None, :] < block_counts[:, None]) & (destinations == me)).astype(jnp.int32)
@@ -573,19 +614,13 @@
     weights_here = jnp.sum(jnp.where(hit, all_weights[None, :], 0.0), axis=1)
 
     rt, positions = lax.optimization_barrier((rt, positions))
-    rt = jnp.stack(gather_pieces(rt, near))
     arrived = select(received, positions).reshape(DST_BLK * BLK, feat)
+    kern, panel = kernel_rows(share_parts(arrived), weights_here, panel_points, sparse_points)
+    pieces = gather_pieces(rt, pairs[0])
+    kern, *pieces = lax.optimization_barrier((kern, *pieces))
+    rt = jnp.stack(pieces)
     remainder, projected = remainder_rows(
-        share_parts(arrived),
-        offsets,
-        weights_here,
-        group[None],
-        quarter_of(near)[None],
-        panel_points,
-        sparse_points,
-        inverse,
-        rt,
-        norm,
+        kern, panel, quarter_of(pairs[0])[None], inverse, rt, norm
     )
     return (projected, remainder)
 

time: 213 us -> 192 us (0.901)
  other arithmetic: 18.5 us -> 6.57 us
  waiting for transfers between devices: 45.2 us -> 35.2 us
  local copies, waits for them, and re-layouts: 15.6 us -> 6.72 us
  starting transfers between devices: 47.2 us -> 53 us
  Pallas kernels: 82.3 us -> 88 us
    ppermute x12 -> x18, starting transfers between devices: 15.8 us -> 39.5 us  [trade(): return lax.ppermute(x, 'rows', flips(bit, lax.axis_size('rows')))]
    ppermute x4 -> x0, starting transfers between devices: 15.8 us -> none  [the longest x2 9.35 us: on_device(): summed = summed + lax.ppermute(summed, 'rows', flips(bit, owners))]
    ppermute x12 -> x18, waiting for transfers between devices: 42.1 us -> 34.2 us  [trade(): return lax.ppermute(x, 'rows', flips(bit, lax.axis_size('rows')))]
    pallas_call x1 -> x2, Pallas kernels: 17.9 us -> 24 us  [the longest x1 14.6 us: kernel_rows(): pl.pallas_call(functools.partial(rows_kernel, len(parts)), grid=(cols //...]
    ppermute x4 -> x0, waiting for transfers between devices: 3.09 us -> none  [the longest x2 3.08 us: on_device(): summed = summed + lax.ppermute(summed, 'rows', flips(bit, owners))]
    another operation x5 -> x4, other arithmetic: 4.55 us -> 1.52 us  [the longest x1 1.1 us: on_device(): rt = jnp.stack(pieces)]
    all_to_all x1, starting transfers between devices: 7.45 us -> 4.56 us  [on_device(): lax.all_to_all(last, 'rows', split_axis=0, concat_axis=0, tiled=True)]
    add x4 -> x0, other arithmetic: 2.68 us -> none  [the longest x2 2.64 us: halve_sum(): return kept + lax.ppermute(send, 'rows', flips(bit, lax.axis_size('rows')))]
  transfers between devices with their start and end apart: 22 -> 24, of which waited for: 8 -> 7; matrix products, arithmetic and copies ran while one was open for 16% -> 7% of each run, Pallas kernels for 29% -> 39%
where the time goes in v5:
time: 192 us
  Pallas kernels  88 us (46%)
  starting transfers between devices  53 us (28%)
  waiting for transfers between devices  35.2 us (18%)
  local copies, waits for them, and re-layouts  6.72 us (4%)
  other arithmetic  6.57 us (3%)
    ppermute x18, starting transfers between devices, trade(): return lax.ppermute(x, 'rows', flips(bit, lax.axis_size('rows')))  39.5 us
    ppermute x18, waiting for transfers between devices, trade(): return lax.ppermute(x, 'rows', flips(bit, lax.axis_size('rows')))  34.2 us
    pallas_call x1, Pallas kernels, column_products(): pl.pallas_call(functools.partial(column_kernel, len(parts)), grid=(size /...  24.7 us
    pallas_call x1, Pallas kernels, factor(): pl.pallas_call(functools.partial(factor_kernel, 64), out_shape=jax.ShapeD...  24 us
    pallas_call x1, Pallas kernels, kernel_rows(): pl.pallas_call(functools.partial(rows_kernel, len(parts)), grid=(cols //...  14.6 us
    pallas_call x1, Pallas kernels, remainder_rows(): pl.pallas_call(functools.partial(remainder_kernel, norm), grid_spec=spec,...  9.43 us
    all_to_all x1, starting transfers between devices, on_device(): lax.all_to_all(outgoing[0], 'rows', split_axis=0, concat_axis=0, tiled=True)  8.07 us
    pallas_call x1, Pallas kernels, panel_products(): pl.pallas_call(functools.partial(panel_kernel, len(parts)), out_shape=(ja...  7.97 us
  transfers between devices with their start and end apart: 24, of which 7 were waited for; matrix products, arithmetic and copies ran while one was open for 7% of the time, Pallas kernels for 39%

profile of v5, /device:TPU:0, one launch (start us, length us, event | category | flops | bytes accessed | tf_op | source)
XLA Modules:
  0.0 192.0 jit_solution(14342863201149200980)
XLA Ops:
  0.6 0.5 collective-permute-start
  1.1 3.7 %pack.1 = (bf16[16,192,512]{2,1,0:T(8,128)(2,1)}, bf16[16,64,512]{2,1,0:T(8,128)(2,1)}) custom-call(s32[16,25]{1,0:T(8,128)} %dest_ref.1, s32[16]{0:T(128)} %cnt_ref.3, bf16[25,128,512]{2,1,0:T(8,128)(2,1)} %bitcast.15), custom_call_target="tpu_custom_call" | custom-call | bytes 6553600 | tf_op jit(solution)/shard_map/pack/pallas_call | solution.py:111
  4.9 8.1 %all-to-all-start = ((bf16[16,192,512]{2,1,0:T(8,128)(2,1)}), bf16[16,192,512]{2,1,0:T(8,128)(2,1)S(1)}, u32[]{:S(2)}, u32[]{:S(2)}) async-start(bf16[16,192,512]{2,1,0:T(8,128)(2,1)} %get-tuple-element.31), calls=%async_computation | async-start | bytes 6291456 | tf_op jit(solution)/shard_map/all_to_all | solution.py:568
  12.9 1.9 slice.25
  14.8 0.2 collective-permute-start.1
  15.2 0.2 reduce_window_sum.28
  15.4 0.5 convert_element_type.10.w_ref
  16.1 0.3 reduce-window.9
  16.5 0.1 convert_dynamic-update-slice_fusion
  16.6 0.1 slice_reduce_fusion
  16.8 0.2 collective-permute-done.1.refs_3_
  17.1 8.0 %panel_products.1 = (f32[256,256]{1,0:T(8,128)}, bf16[3200,256]{1,0:T(8,128)(2,1)}, bf16[256,1024]{1,0:T(8,128)(2,1)}) custom-call(s32[16]{0:T(128)} %cnt_ref.3, f32[25]{0:T(128)} %convert_element_type.10.w_ref, bf16[3200,512]{1,0:T(8,128)(2,1)} %refs_0_.3, bf16[3200,512]{1,0:T(8,128)(2,1)} %collective-permute-done.refs_1_, bf16[2048,1024]{1,0:T(8,128)(2,1)} %refs_3_.3, ...), custom_call_target="tpu_custom_call" | custom-call | flops 2097152000 | bytes 6553600 | tf_op jit(solution)/shard_map/panel_products/pallas_call | solution.py:320
  25.0 0.9 constant_dynamic-slice_fusion.6
  26.1 3.4 %collective-permute-start.4 = (f32[136,256]{1,0:T(8,128)S(1)}, f32[136,256]{1,0:T(8,128)S(1)}, u32[]{:S(2)}, u32[]{:S(2)}) collective-permute-start(f32[136,256]{1,0:T(8,128)S(1)} %pad_maximum_fusion.2), channel_id=1, source_target_pairs={{0,6},{2,4},{4,2},{6,0},{8,14},{10,12},{12,10},{14,8},{16,22},{18,... | collective-permute-start | bytes 417800 | tf_op jit(solution)/shard_map/ppermute | solution.py:519
  29.4 0.1 collective-permute-start.2
  29.6 24.7 %column_products.1 = f32[2048,256]{1,0:T(8,128)} custom-call(bf16[3200,512]{1,0:T(8,128)(2,1)} %refs_0_.3, bf16[3200,512]{1,0:T(8,128)(2,1)} %collective-permute-done.refs_1_, bf16[3200,256]{1,0:T(8,128)(2,1)} %get-tuple-element.24.refs_2_, bf16[2048,1024]{1,0:T(8,128)(2,1)} %refs_3_.3), custom_call_target="tpu_custom_call" | custom-call | flops 16777216000 | bytes 6553600 | tf_op jit(solution)/shard_map/column_products/pallas_call | solution.py:369
  54.4 5.7 %collective-permute-start.7 = (f32[136,256]{1,0:T(8,128)S(1)}, f32[136,256]{1,0:T(8,128)S(1)}, u32[]{:S(2)}, u32[]{:S(2)}) collective-permute-start(f32[136,256]{1,0:T(8,128)S(1)} %add_add_fusion.2), channel_id=1, source_target_pairs={{0,24},{2,26},{4,28},{6,30},{8,16},{10,18},{12,20},{14,22},{16,8},... | collective-permute-start | bytes 417800 | tf_op jit(solution)/shard_map/ppermute | solution.py:519
  60.1 0.6 collective-permute-start.5
  60.7 1.5 constant_dynamic-slice_fusion.5
  62.3 2.9 %collective-permute-start.10 = (f32[512,256]{1,0:T(8,128)S(1)}, f32[512,256]{1,0:T(8,128)S(1)}, u32[]{:S(2)}, u32[]{:S(2)}) collective-permute-start(f32[512,256]{1,0:T(8,128)S(1)} %get-tuple-element.45), channel_id=1, source_target_pairs={{0,6},{2,4},{4,2},{6,0},{8,14},{10,12},{12,10},{14,8},{16,22},{18,... | collective-permute-start | bytes 1572872 | tf_op jit(solution)/shard_map/ppermute | solution.py:519
  65.2 8.2 %collective-permute-done.7 = f32[136,256]{1,0:T(8,128)S(1)} collective-permute-done((f32[136,256]{1,0:T(8,128)S(1)}, f32[136,256]{1,0:T(8,128)S(1)}, u32[]{:S(2)}, u32[]{:S(2)}) %collective-permute-start.7) | collective-permute-done | bytes 139296 | tf_op jit(solution)/shard_map/ppermute | solution.py:519
  73.3 5.2 %collective-permute-start.9 = (f32[512,256]{1,0:T(8,128)S(1)}, f32[512,256]{1,0:T(8,128)S(1)}, u32[]{:S(2)}, u32[]{:S(2)}) collective-permute-start(f32[512,256]{1,0:T(8,128)S(1)} %get-tuple-element.46), channel_id=1, source_target_pairs={{0,4},{2,6},{4,0},{6,2},{8,12},{10,14},{12,8},{14,10},{16,20},{18,... | collective-permute-start | bytes 1572872 | tf_op jit(solution)/shard_map/ppermute | solution.py:519
  78.5 17.7 %collective-permute-done.6 = f32[136,256]{1,0:T(8,128)S(1)} collective-permute-done((f32[136,256]{1,0:T(8,128)S(1)}, f32[136,256]{1,0:T(8,128)S(1)}, u32[]{:S(2)}, u32[]{:S(2)}) %collective-permute-start.6) | collective-permute-done | bytes 139296 | tf_op jit(solution)/shard_map/ppermute | solution.py:519
  96.4 0.6 broadcast_compare_fusion
  97.0 0.7 collective-permute-done.11
  97.8 0.7 maximum_select_fusion.gram_ref
  98.5 4.2 %collective-permute-done.9 = f32[512,256]{1,0:T(8,128)S(1)} collective-permute-done((f32[512,256]{1,0:T(8,128)S(1)}, f32[512,256]{1,0:T(8,128)S(1)}, u32[]{:S(2)}, u32[]{:S(2)}) %collective-permute-start.9) | collective-permute-done | bytes 524320 | tf_op jit(solution)/shard_map/ppermute | solution.py:519
  102.7 1.2 add_add_fusion
  104.0 0.8 constant_dynamic-slice_fusion.2
  104.8 7.9 %collective-permute-start.12 = (f32[128,256]{1,0:T(8,128)}, f32[128,256]{1,0:T(8,128)S(1)}, u32[]{:S(2)}, u32[]{:S(2)}) collective-permute-start(f32[128,256]{1,0:T(8,128)} %get-tuple-element.47), channel_id=1, source_target_pairs={{0,8},{2,10},{4,12},{6,14},{8,0},{10,2},{12,4},{14,6},{16,24},{18,... | collective-permute-start | bytes 393224 | tf_op jit(solution)/shard_map/ppermute | solution.py:519
  112.7 5.6 %collective-permute-start.14 = (f32[128,256]{1,0:T(8,128)}, f32[128,256]{1,0:T(8,128)}, u32[]{:S(2)}, u32[]{:S(2)}) collective-permute-start(f32[128,256]{1,0:T(8,128)} %get-tuple-element.48), channel_id=1, source_target_pairs={{0,24},{2,26},{4,28},{6,30},{8,16},{10,18},{12,20},{14,22},{16,8},... | collective-permute-start | bytes 393224 | tf_op jit(solution)/shard_map/ppermute | solution.py:519
  118.3 4.6 %all-to-all-start.1 = ((bf16[16,64,512]{2,1,0:T(8,128)(2,1)}), bf16[16,64,512]{2,1,0:T(8,128)(2,1)}, u32[]{:S(2)}, u32[]{:S(2)}) async-start(bf16[16,64,512]{2,1,0:T(8,128)(2,1)} %get-tuple-element.32), calls=%async_computation.1 | async-start | bytes 2097152 | tf_op jit(solution)/shard_map/all_to_all | solution.py:600
  122.9 24.0 %factor.1.inv_ref = f32[256,256]{1,0:T(8,128)} custom-call(f32[256,256]{1,0:T(8,128)} %maximum_select_fusion.gram_ref), custom_call_target="tpu_custom_call" | custom-call | flops 20000000000 | bytes 524288 | tf_op jit(solution)/shard_map/factor/pallas_call | solution.py:204
  146.9 1.6 convolution_convert_fusion
  148.5 3.6 %collective-permute-start.17 = (bf16[128,256]{1,0:T(8,128)(2,1)S(1)}, bf16[128,256]{1,0:T(8,128)(2,1)S(1)}, u32[]{:S(2)}, u32[]{:S(2)}) collective-permute-start(bf16[128,256]{1,0:T(8,128)(2,1)S(1)} %convolution_convert_fusion), channel_id=1, source_target_pairs={{0,24},{2,26},{4,28},{6,30},{8,16},{10,18},{12,20},{14,22},{16,8},... | collective-permute-start | bytes 196616 | tf_op jit(solution)/shard_map/ppermute | solution.py:519
  152.1 0.8 collective-permute-start.15
  153.0 0.7 select_reduce_fusion.pos_ref
  153.7 1.6 collective-permute-done.17
  155.2 2.4 %collective-permute-done.16 = bf16[128,256]{1,0:T(8,128)(2,1)S(1)} collective-permute-done((bf16[128,256]{1,0:T(8,128)(2,1)S(1)}, bf16[128,256]{1,0:T(8,128)(2,1)S(1)}, u32[]{:S(2)}, u32[]{:S(2)}) %collective-permute-start.16) | collective-permute-done | bytes 65568 | tf_op jit(solution)/shard_map/ppermute | solution.py:519
  157.8 3.6 %select.24 = bf16[13,128,512]{2,1,0:T(8,128)(2,1)} custom-call(s32[13]{0:T(128)} %select_reduce_fusion.pos_ref, bf16[16,192,512]{2,1,0:T(8,128)(2,1)} %copy-done, bf16[16,64,512]{2,1,0:T(8,128)(2,1)} %all-to-all-done.1.refs_1_), custom_call_target="tpu_custom_call" | custom-call | bytes 3407872 | tf_op jit(solution)/shard_map/select/pallas_call | solution.py:148
  161.5 0.7 select_reduce_fusion.1.w_ref
  162.2 2.2 %collective-permute-start.21 = (bf16[512,256]{1,0:T(8,128)(2,1)S(1)}, bf16[512,256]{1,0:T(8,128)(2,1)S(1)}, u32[]{:S(2)}, u32[]{:S(2)}) collective-permute-start(bf16[512,256]{1,0:T(8,128)(2,1)S(1)} %pad_maximum_fusion.1), channel_id=1, source_target_pairs={{0,6},{2,4},{4,2},{6,0},{8,14},{10,12},{12,10},{14,8},{16,22},{18,... | collective-permute-start | bytes 786440 | tf_op jit(solution)/shard_map/ppermute | solution.py:519
  164.4 0.6 collective-permute-start.20
  165.0 0.7 collective-permute-start.19
  165.7 1.2 copy-done.6
  166.9 14.6 %kernel_rows.1 = (bf16[1664,2048]{1,0:T(8,128)(2,1)}, bf16[1664,256]{1,0:T(8,128)(2,1)}) custom-call(f32[13]{0:T(128)} %select_reduce_fusion.1.w_ref, bf16[1664,512]{1,0:T(8,128)(2,1)} %bitcast.17, bf16[1664,512]{1,0:T(8,128)(2,1)} %copy-done.6, bf16[256,1024]{1,0:T(8,128)(2,1)} %get-tuple-element.33.refs_2_, bf16[2048,1024]{1,0:T(8,128)(2,1)} %refs_3_.3), custom_call_target="tpu_custom_call" | custom-call | flops 7851737088 | bytes 14417920 | tf_op jit(solution)/shard_map/kernel_rows/pallas_call | solution.py:427
  181.5 1.1 pad_maximum_fusion.rt_ref
  182.6 9.4 %remainder_rows.1 = (bf16[1664,2048]{1,0:T(8,128)(2,1)}, f32[256,2048]{1,0:T(8,128)}) custom-call(s32[1]{0:T(128)} %bitcast.quarter_ref, bf16[1664,2048]{1,0:T(8,128)(2,1)} %get-tuple-element.36.kern_ref, bf16[1664,256]{1,0:T(8,128)(2,1)} %get-tuple-element.37.p_ref, f32[256,256]{1,0:T(8,128)} %factor.1.inv_ref, bf16[4,512,256]{2,1,0:T(8,128)(2,1)} %pad_maximum_fusion.rt_ref), custom_call_target="tpu_custom_call" | custom-call | flops 1744830464 | bytes 13631488 | tf_op jit(solution)/shard_map/remainder_rows/pallas_call | solution.py:495
  (60 shorter events, 1.1 us)
Async XLA Ops:
  0.6 16.4 %collective-permute-start = (bf16[3200,512]{1,0:T(8,128)(2,1)}, bf16[3200,512]{1,0:T(8,128)(2,1)}, u32[]{:S(2)}, u32[]{:S(2)}) collective-permute-start(bf16[3200,512]{1,0:T(8,128)(2,1)} %refs_0_.3), channel_id=1, source_target_pairs={{0,1},{1,0},{2,3},{3,2},{4,5},{5,4},{6,7},{7,6},{8,9},{9,8},{10,11... | collective-permute-start | bytes 9830408 | tf_op jit(solution)/shard_map/ppermute | solution.py:217
  4.8 10.2 %copy-start.2 = (s32[16,25]{1,0:T(8,128)S(1)}, s32[16,25]{1,0:T(8,128)}, u32[]{:S(2)}) copy-start(s32[16,25]{1,0:T(8,128)} %dest_ref.1) | copy-start | bytes 4804
  4.8 10.2 %copy-start.3 = (s32[16]{0:T(128)S(1)}, s32[16]{0:T(128)}, u32[]{:S(2)}) copy-start(s32[16]{0:T(128)} %cnt_ref.3) | copy-start | bytes 196
  4.8 10.5 %copy-start.7 = (bf16[25]{0:T(256)(128)(2,1)S(1)}, bf16[25]{0:T(256)(128)(2,1)}, u32[]{:S(2)}) copy-start(bf16[25]{0:T(256)(128)(2,1)} %param.7) | copy-start | bytes 154
  4.9 113.4 %all-to-all-start = ((bf16[16,192,512]{2,1,0:T(8,128)(2,1)}), bf16[16,192,512]{2,1,0:T(8,128)(2,1)S(1)}, u32[]{:S(2)}, u32[]{:S(2)}) async-start(bf16[16,192,512]{2,1,0:T(8,128)(2,1)} %get-tuple-element.31), calls=%async_computation | async-start | bytes 6291456 | tf_op jit(solution)/shard_map/all_to_all | solution.py:568
  14.8 2.3 %collective-permute-start.1 = (bf16[256,1024]{1,0:T(8,128)(2,1)}, bf16[256,1024]{1,0:T(8,128)(2,1)}, u32[]{:S(2)}, u32[]{:S(2)}) collective-permute-start(bf16[256,1024]{1,0:T(8,128)(2,1)} %slice.25), channel_id=1, source_target_pairs={{0,1},{1,0},{2,3},{3,2},{4,5},{5,4},{6,7},{7,6},{8,9},{9,8},{10,11... | collective-permute-start | bytes 1572872 | tf_op jit(solution)/shard_map/ppermute | solution.py:563
  26.0 28.3 %collective-permute-start.3 = (f32[136,256]{1,0:T(8,128)S(1)}, f32[136,256]{1,0:T(8,128)S(1)}, u32[]{:S(2)}, u32[]{:S(2)}) collective-permute-start(f32[136,256]{1,0:T(8,128)S(1)} %pad_maximum_fusion.2), channel_id=1, source_target_pairs={{0,4},{2,6},{4,0},{6,2},{8,12},{10,14},{12,8},{14,10},{16,20},{18,... | collective-permute-start | bytes 417800 | tf_op jit(solution)/shard_map/ppermute | solution.py:519
  26.1 28.2 %collective-permute-start.4 = (f32[136,256]{1,0:T(8,128)S(1)}, f32[136,256]{1,0:T(8,128)S(1)}, u32[]{:S(2)}, u32[]{:S(2)}) collective-permute-start(f32[136,256]{1,0:T(8,128)S(1)} %pad_maximum_fusion.2), channel_id=1, source_target_pairs={{0,6},{2,4},{4,2},{6,0},{8,14},{10,12},{12,10},{14,8},{16,22},{18,... | collective-permute-start | bytes 417800 | tf_op jit(solution)/shard_map/ppermute | solution.py:519
  29.4 24.9 %collective-permute-start.2 = (f32[136,256]{1,0:T(8,128)S(1)}, f32[136,256]{1,0:T(8,128)S(1)}, u32[]{:S(2)}, u32[]{:S(2)}) collective-permute-start(f32[136,256]{1,0:T(8,128)S(1)} %pad_maximum_fusion.2), channel_id=1, source_target_pairs={{0,2},{2,0},{4,6},{6,4},{8,10},{10,8},{12,14},{14,12},{16,18},{18,... | collective-permute-start | bytes 417800 | tf_op jit(solution)/shard_map/ppermute | solution.py:519
  54.4 18.9 %collective-permute-start.7 = (f32[136,256]{1,0:T(8,128)S(1)}, f32[136,256]{1,0:T(8,128)S(1)}, u32[]{:S(2)}, u32[]{:S(2)}) collective-permute-start(f32[136,256]{1,0:T(8,128)S(1)} %add_add_fusion.2), channel_id=1, source_target_pairs={{0,24},{2,26},{4,28},{6,30},{8,16},{10,18},{12,20},{14,22},{16,8},... | collective-permute-start | bytes 417800 | tf_op jit(solution)/shard_map/ppermute | solution.py:519
  60.1 36.2 %collective-permute-start.6 = (f32[136,256]{1,0:T(8,128)S(1)}, f32[136,256]{1,0:T(8,128)S(1)}, u32[]{:S(2)}, u32[]{:S(2)}) collective-permute-start(f32[136,256]{1,0:T(8,128)S(1)} %add_add_fusion.2), channel_id=1, source_target_pairs={{0,16},{2,18},{4,20},{6,22},{8,24},{10,26},{12,28},{14,30},{16,0},... | collective-permute-start | bytes 417800 | tf_op jit(solution)/shard_map/ppermute | solution.py:519
  60.1 36.2 %collective-permute-start.5 = (f32[136,256]{1,0:T(8,128)S(1)}, f32[136,256]{1,0:T(8,128)S(1)}, u32[]{:S(2)}, u32[]{:S(2)}) collective-permute-start(f32[136,256]{1,0:T(8,128)S(1)} %add_add_fusion.2), channel_id=1, source_target_pairs={{0,8},{2,10},{4,12},{6,14},{8,0},{10,2},{12,4},{14,6},{16,24},{18,... | collective-permute-start | bytes 417800 | tf_op jit(solution)/shard_map/ppermute | solution.py:519
  62.2 36.3 %collective-permute-start.8 = (f32[512,256]{1,0:T(8,128)S(1)}, f32[512,256]{1,0:T(8,128)S(1)}, u32[]{:S(2)}, u32[]{:S(2)}) collective-permute-start(f32[512,256]{1,0:T(8,128)S(1)} %get-tuple-element.44), channel_id=1, source_target_pairs={{0,2},{2,0},{4,6},{6,4},{8,10},{10,8},{12,14},{14,12},{16,18},{18,... | collective-permute-start | bytes 1572872 | tf_op jit(solution)/shard_map/ppermute | solution.py:519
  62.3 36.2 %collective-permute-start.10 = (f32[512,256]{1,0:T(8,128)S(1)}, f32[512,256]{1,0:T(8,128)S(1)}, u32[]{:S(2)}, u32[]{:S(2)}) collective-permute-start(f32[512,256]{1,0:T(8,128)S(1)} %get-tuple-element.45), channel_id=1, source_target_pairs={{0,6},{2,4},{4,2},{6,0},{8,14},{10,12},{12,10},{14,8},{16,22},{18,... | collective-permute-start | bytes 1572872 | tf_op jit(solution)/shard_map/ppermute | solution.py:519
  73.3 29.4 %collective-permute-start.9 = (f32[512,256]{1,0:T(8,128)S(1)}, f32[512,256]{1,0:T(8,128)S(1)}, u32[]{:S(2)}, u32[]{:S(2)}) collective-permute-start(f32[512,256]{1,0:T(8,128)S(1)} %get-tuple-element.46), channel_id=1, source_target_pairs={{0,4},{2,6},{4,0},{6,2},{8,12},{10,14},{12,8},{14,10},{16,20},{18,... | collective-permute-start | bytes 1572872 | tf_op jit(solution)/shard_map/ppermute | solution.py:519
  96.3 1.4 collective-permute-start.11
  103.9 14.4 %copy-start.1 = (f32[512,256]{1,0:T(8,128)}, f32[512,256]{1,0:T(8,128)S(1)}, u32[]{:S(2)}) copy-start(f32[512,256]{1,0:T(8,128)S(1)} %add_add_fusion) | copy-start | bytes 1572868
  104.8 42.1 %collective-permute-start.12 = (f32[128,256]{1,0:T(8,128)}, f32[128,256]{1,0:T(8,128)S(1)}, u32[]{:S(2)}, u32[]{:S(2)}) collective-permute-start(f32[128,256]{1,0:T(8,128)} %get-tuple-element.47), channel_id=1, source_target_pairs={{0,8},{2,10},{4,12},{6,14},{8,0},{10,2},{12,4},{14,6},{16,24},{18,... | collective-permute-start | bytes 393224 | tf_op jit(solution)/shard_map/ppermute | solution.py:519
  112.7 34.2 %collective-permute-start.14 = (f32[128,256]{1,0:T(8,128)}, f32[128,256]{1,0:T(8,128)}, u32[]{:S(2)}, u32[]{:S(2)}) collective-permute-start(f32[128,256]{1,0:T(8,128)} %get-tuple-element.48), channel_id=1, source_target_pairs={{0,24},{2,26},{4,28},{6,30},{8,16},{10,18},{12,20},{14,22},{16,8},... | collective-permute-start | bytes 393224 | tf_op jit(solution)/shard_map/ppermute | solution.py:519
  118.3 28.6 %collective-permute-start.13 = (f32[128,256]{1,0:T(8,128)S(1)}, f32[128,256]{1,0:T(8,128)}, u32[]{:S(2)}, u32[]{:S(2)}) collective-permute-start(f32[128,256]{1,0:T(8,128)S(1)} %get-tuple-element.49), channel_id=1, source_target_pairs={{0,16},{2,18},{4,20},{6,22},{8,24},{10,26},{12,28},{14,30},{16,0},... | collective-permute-start | bytes 393224 | tf_op jit(solution)/shard_map/ppermute | solution.py:519
  118.3 28.6 %copy-start = (bf16[16,192,512]{2,1,0:T(8,128)(2,1)}, bf16[16,192,512]{2,1,0:T(8,128)(2,1)S(1)}, u32[]{:S(2)}) copy-start(bf16[16,192,512]{2,1,0:T(8,128)(2,1)S(1)} %all-to-all-done.refs_0_) | copy-start | bytes 9437188
  118.3 39.4 %all-to-all-start.1 = ((bf16[16,64,512]{2,1,0:T(8,128)(2,1)}), bf16[16,64,512]{2,1,0:T(8,128)(2,1)}, u32[]{:S(2)}, u32[]{:S(2)}) async-start(bf16[16,64,512]{2,1,0:T(8,128)(2,1)} %get-tuple-element.32), calls=%async_computation.1 | async-start | bytes 2097152 | tf_op jit(solution)/shard_map/all_to_all | solution.py:600
  122.9 30.1 %copy-start.4 = (pred[400]{0:T(512)(128)(4,1)S(1)}, pred[400]{0:T(512)(128)(4,1)}, u32[]{:S(2)}) copy-start(pred[400]{0:T(512)(128)(4,1)} %broadcast_compare_fusion) | copy-start | bytes 1204
  148.5 6.7 %collective-permute-start.17 = (bf16[128,256]{1,0:T(8,128)(2,1)S(1)}, bf16[128,256]{1,0:T(8,128)(2,1)S(1)}, u32[]{:S(2)}, u32[]{:S(2)}) collective-permute-start(bf16[128,256]{1,0:T(8,128)(2,1)S(1)} %convolution_convert_fusion), channel_id=1, source_target_pairs={{0,24},{2,26},{4,28},{6,30},{8,16},{10,18},{12,20},{14,22},{16,8},... | collective-permute-start | bytes 196616 | tf_op jit(solution)/shard_map/ppermute | solution.py:519
  152.1 5.5 %collective-permute-start.16 = (bf16[128,256]{1,0:T(8,128)(2,1)S(1)}, bf16[128,256]{1,0:T(8,128)(2,1)S(1)}, u32[]{:S(2)}, u32[]{:S(2)}) collective-permute-start(bf16[128,256]{1,0:T(8,128)(2,1)S(1)} %convolution_convert_fusion), channel_id=1, source_target_pairs={{0,16},{2,18},{4,20},{6,22},{8,24},{10,26},{12,28},{14,30},{16,0},... | collective-permute-start | bytes 196616 | tf_op jit(solution)/shard_map/ppermute | solution.py:519
  152.1 5.5 %collective-permute-start.15 = (bf16[128,256]{1,0:T(8,128)(2,1)S(1)}, bf16[128,256]{1,0:T(8,128)(2,1)S(1)}, u32[]{:S(2)}, u32[]{:S(2)}) collective-permute-start(bf16[128,256]{1,0:T(8,128)(2,1)S(1)} %convolution_convert_fusion), channel_id=1, source_target_pairs={{0,8},{2,10},{4,12},{6,14},{8,0},{10,2},{12,4},{14,6},{16,24},{18,... | collective-permute-start | bytes 196616 | tf_op jit(solution)/shard_map/ppermute | solution.py:519
  157.7 3.8 %copy-start.5 = (pred[400]{0:T(512)(128)(4,1)S(1)}, pred[400]{0:T(512)(128)(4,1)}, u32[]{:S(2)}) copy-start(pred[400]{0:T(512)(128)(4,1)} %broadcast_compare_fusion) | copy-start | bytes 1204
  161.4 4.3 %collective-permute-start.18 = (bf16[1664,512]{1,0:T(8,128)(2,1)}, bf16[1664,512]{1,0:T(8,128)(2,1)S(1)}, u32[]{:S(2)}, u32[]{:S(2)}) collective-permute-start(bf16[1664,512]{1,0:T(8,128)(2,1)} %bitcast.16), channel_id=1, source_target_pairs={{0,1},{1,0},{2,3},{3,2},{4,5},{5,4},{6,7},{7,6},{8,9},{9,8},{10,11... | collective-permute-start | bytes 5111816 | tf_op jit(solution)/shard_map/ppermute | solution.py:217
  162.2 19.3 %collective-permute-start.21 = (bf16[512,256]{1,0:T(8,128)(2,1)S(1)}, bf16[512,256]{1,0:T(8,128)(2,1)S(1)}, u32[]{:S(2)}, u32[]{:S(2)}) collective-permute-start(bf16[512,256]{1,0:T(8,128)(2,1)S(1)} %pad_maximum_fusion.1), channel_id=1, source_target_pairs={{0,6},{2,4},{4,2},{6,0},{8,14},{10,12},{12,10},{14,8},{16,22},{18,... | collective-permute-start | bytes 786440 | tf_op jit(solution)/shard_map/ppermute | solution.py:519
  164.4 17.0 %collective-permute-start.20 = (bf16[512,256]{1,0:T(8,128)(2,1)S(1)}, bf16[512,256]{1,0:T(8,128)(2,1)S(1)}, u32[]{:S(2)}, u32[]{:S(2)}) collective-permute-start(bf16[512,256]{1,0:T(8,128)(2,1)S(1)} %pad_maximum_fusion.1), channel_id=1, source_target_pairs={{0,4},{2,6},{4,0},{6,2},{8,12},{10,14},{12,8},{14,10},{16,20},{18,... | collective-permute-start | bytes 786440 | tf_op jit(solution)/shard_map/ppermute | solution.py:519
  165.0 16.5 %collective-permute-start.19 = (bf16[512,256]{1,0:T(8,128)(2,1)S(1)}, bf16[512,256]{1,0:T(8,128)(2,1)S(1)}, u32[]{:S(2)}, u32[]{:S(2)}) collective-permute-start(bf16[512,256]{1,0:T(8,128)(2,1)S(1)} %pad_maximum_fusion.1), channel_id=1, source_target_pairs={{0,2},{2,0},{4,6},{6,4},{8,10},{10,8},{12,14},{14,12},{16,18},{18,... | collective-permute-start | bytes 786440 | tf_op jit(solution)/shard_map/ppermute | solution.py:519
  165.7 1.2 copy-start.6

commit v6 on v5

--- a/solution.py
+++ b/solution.py
@@ -50,30 +50,15 @@
     return high, (x - high.astype(jnp.float32)).astype(jnp.bfloat16)
 
 
-HEAD = 64
-
-
-def block_copies(rank, whole_ref, outer, first_ref, last_ref, sems):
-    if rank == 0:
-        pairs = [(whole_ref, first_ref.at[outer, pl.ds(0, BLK)])]
-    else:
-        pairs = [
-            (whole_ref.at[pl.ds(0, HEAD)], first_ref.at[outer, pl.ds(BLK, HEAD)]),
-            (whole_ref.at[pl.ds(HEAD, BLK - HEAD)], last_ref.at[outer]),
-        ]
-    return [(a, b, sems.at[i]) for i, (a, b) in enumerate(pairs)]
-
-
 def pack_kernel(per_pair, dest_ref, cnt_ref, desc_ref, *refs):
-    out_refs, (ctr_ref, rank_ref, sems) = refs[:per_pair], refs[per_pair:]
+    out_refs, (ctr_ref, sems) = refs[:per_pair], refs[per_pair:]
     slots = desc_ref.shape[0]
     owners = ctr_ref.shape[0]
     me = lax.axis_index("rows")
     count = cnt_ref[me]
 
-    def copies(j, d, rank):
-        moves = block_copies(rank, desc_ref.at[j], d, out_refs[0], out_refs[-1], sems.at[j])
-        return [pltpu.make_async_copy(a, b, sem) for a, b, sem in moves]
+    def copy(j, d, rank):
+        return pltpu.make_async_copy(desc_ref.at[j], out_refs[rank].at[d], sems.at[j])
 
     @pl.loop(0, owners)
     def _(i):
@@ -86,39 +71,29 @@
             d = dest_ref[me, j]
             rank = ctr_ref[d]
             ctr_ref[d] = rank + 1
-            rank_ref[j] = rank
             for r in range(per_pair):
                 @pl.when(rank == r)
                 def _():
-                    for c in copies(j, d, r):
-                        c.start()
+                    copy(j, d, r).start()
 
     @pl.loop(0, slots)
     def _(j):
         @pl.when(j < count)
         def _():
-            for r in range(per_pair):
-                @pl.when(rank_ref[j] == r)
-                def _():
-                    for c in copies(j, 0, r):
-                        c.wait()
+            pltpu.make_async_copy(desc_ref.at[0], out_refs[0].at[0], sems.at[j]).wait()
 
 
 def pack(desc_blocks, destinations, counts, per_pair):
     slots, blk, feat = desc_blocks.shape
     owners = destinations.shape[0]
-    heights = [blk] if per_pair == 1 else [blk + HEAD, blk - HEAD]
     return pl.pallas_call(
         functools.partial(pack_kernel, per_pair),
-        out_shape=[
-            jax.ShapeDtypeStruct((owners, h, feat), desc_blocks.dtype) for h in heights
-        ],
+        out_shape=[jax.ShapeDtypeStruct((owners, blk, feat), desc_blocks.dtype)] * per_pair,
         in_specs=[SMEM, SMEM, VMEM],
         out_specs=[ANY] * per_pair,
         scratch_shapes=[
             pltpu.SMEM((owners,), jnp.int32),
-            pltpu.SMEM((slots,), jnp.int32),
-            pltpu.SemaphoreType.DMA((slots, 2)),
+            pltpu.SemaphoreType.DMA((slots,)),
         ],
         compiler_params=params(),
         cost_estimate=cost(0, 4 * slots * blk * feat),
@@ -129,18 +104,18 @@
 def select_kernel(per_pair, pos_ref, *refs):
     recv_refs, (out_ref, sems) = refs[:per_pair], refs[per_pair:]
 
-    def copies(p, rank):
+    def copy(p, rank):
         owner = pos_ref[p] // per_pair
-        moves = block_copies(rank, out_ref.at[p], owner, recv_refs[0], recv_refs[-1], sems.at[p])
-        return [pltpu.make_async_copy(b, a, sem) for a, b, sem in moves]
-
-    for act in ("start", "wait"):
-        for p in range(DST_BLK):
-            for r in range(per_pair):
-                @pl.when(pos_ref[p] % per_pair == r)
-                def _():
-                    for c in copies(p, r):
-                        getattr(c, act)()
+        return pltpu.make_async_copy(recv_refs[rank].at[owner], out_ref.at[p], sems.at[p])
+
+    for p in range(DST_BLK):
+        for r in range(per_pair):
+            @pl.when(pos_ref[p] % per_pair == r)
+            def _():
+                copy(p, r).start()
+
+    for p in range(DST_BLK):
+        pltpu.make_async_copy(recv_refs[0].at[0], out_ref.at[p], sems.at[p]).wait()
 
 
 def select(received, positions):
@@ -150,7 +125,7 @@
         out_shape=jax.ShapeDtypeStruct((DST_BLK, BLK, feat), received[0].dtype),
         in_specs=[SMEM] + [ANY] * len(received),
         out_specs=VMEM,
-        scratch_shapes=[pltpu.SemaphoreType.DMA((DST_BLK, 2))],
+        scratch_shapes=[pltpu.SemaphoreType.DMA((DST_BLK,))],
         compiler_params=params(),
         cost_estimate=cost(0, 4 * DST_BLK * BLK * feat),
         name="select",

time: 192 us -> 205 us (1.068)
  waiting for transfers between devices: 35.2 us -> 51.3 us
  starting transfers between devices: 53 us -> 43.1 us
  local copies, waits for them, and re-layouts: 6.72 us -> 9.3 us
  Pallas kernels: 88 us -> 90.1 us
    ppermute x18, waiting for transfers between devices: 34.2 us -> 50.3 us  [trade(): return lax.ppermute(x, 'rows', flips(bit, lax.axis_size('rows')))]
    ppermute x18, starting transfers between devices: 39.5 us -> 23.9 us  [trade(): return lax.ppermute(x, 'rows', flips(bit, lax.axis_size('rows')))]
    all_to_all x1, starting transfers between devices: 4.56 us -> 11.1 us  [on_device(): lax.all_to_all(last, 'rows', split_axis=0, concat_axis=0, tiled=True)]
    unnamed x18 -> x20, local copies, waits for them, and re-layouts: 1.23 us -> 3.35 us
  transfers between devices with their start and end apart: 24 -> 24, of which waited for: 7 -> 9; matrix products, arithmetic and copies ran while one was open for 7% -> 7% of each run, Pallas kernels for 39% -> 38%
where the time goes in v6:
time: 205 us
  Pallas kernels  90.1 us (44%)
  waiting for transfers between devices  51.3 us (25%)
  starting transfers between devices  43.1 us (21%)
  local copies, waits for them, and re-layouts  9.3 us (5%)
  other arithmetic  8.3 us (4%)
    ppermute x18, waiting for transfers between devices, trade(): return lax.ppermute(x, 'rows', flips(bit, lax.axis_size('rows')))  50.3 us
    pallas_call x1, Pallas kernels, column_products(): pl.pallas_call(functools.partial(column_kernel, len(parts)), grid=(size /...  24.7 us
    pallas_call x1, Pallas kernels, factor(): pl.pallas_call(functools.partial(factor_kernel, 64), out_shape=jax.ShapeD...  24 us
    ppermute x18, starting transfers between devices, trade(): return lax.ppermute(x, 'rows', flips(bit, lax.axis_size('rows')))  23.9 us
    pallas_call x1, Pallas kernels, kernel_rows(): pl.pallas_call(functools.partial(rows_kernel, len(parts)), grid=(cols //...  14.6 us
    all_to_all x1, starting transfers between devices, on_device(): lax.all_to_all(last, 'rows', split_axis=0, concat_axis=0, tiled=True)  11.1 us
    pallas_call x1, Pallas kernels, panel_products(): pl.pallas_call(functools.partial(panel_kernel, len(parts)), out_shape=(ja...  9.89 us
    pallas_call x1, Pallas kernels, remainder_rows(): pl.pallas_call(functools.partial(remainder_kernel, norm), grid_spec=spec,...  9.43 us
  transfers between devices with their start and end apart: 24, of which 9 were waited for; matrix products, arithmetic and copies ran while one was open for 7% of the time, Pallas kernels for 38%

profile of v6, /device:TPU:0, one launch (start us, length us, event | category | flops | bytes accessed | tf_op | source)
XLA Modules:
  0.0 204.5 jit_solution(17927247127104248601)
XLA Ops:
  0.6 0.5 collective-permute-start
  1.1 4.0 %pack.1 = (bf16[16,128,512]{2,1,0:T(8,128)(2,1)}, bf16[16,128,512]{2,1,0:T(8,128)(2,1)}) custom-call(s32[16,25]{1,0:T(8,128)} %dest_ref.1, s32[16]{0:T(128)} %cnt_ref.3, bf16[25,128,512]{2,1,0:T(8,128)(2,1)} %bitcast.15), custom_call_target="tpu_custom_call" | custom-call | bytes 6553600 | tf_op jit(solution)/shard_map/pack/pallas_call | solution.py:89
  5.1 7.2 %all-to-all-start = ((bf16[16,128,512]{2,1,0:T(8,128)(2,1)}), bf16[16,128,512]{2,1,0:T(8,128)(2,1)S(1)}, u32[]{:S(2)}, u32[]{:S(2)}) async-start(bf16[16,128,512]{2,1,0:T(8,128)(2,1)} %get-tuple-element.31), calls=%async_computation | async-start | bytes 4194304 | tf_op jit(solution)/shard_map/all_to_all | solution.py:543
  12.3 1.1 slice.25
  13.7 0.6 convert_element_type.10.w_ref
  14.4 1.0 collective-permute-done.1.refs_3_
  15.4 0.8 copy-done.1
  16.2 9.9 %panel_products.1 = (f32[256,256]{1,0:T(8,128)}, bf16[3200,256]{1,0:T(8,128)(2,1)}, bf16[256,1024]{1,0:T(8,128)(2,1)}) custom-call(s32[16]{0:T(128)} %cnt_ref.3, f32[25]{0:T(128)} %convert_element_type.10.w_ref, bf16[3200,512]{1,0:T(8,128)(2,1)} %refs_0_.3, bf16[3200,512]{1,0:T(8,128)(2,1)} %collective-permute-done.refs_1_, bf16[2048,1024]{1,0:T(8,128)(2,1)} %refs_3_.3, ...), custom_call_target="tpu_custom_call" | custom-call | flops 2097152000 | bytes 6553600 | tf_op jit(solution)/shard_map/panel_products/pallas_call | solution.py:295
  26.1 0.9 constant_dynamic-slice_fusion.6
  27.0 2.0 collective-permute-start.3
  29.0 1.0 collective-permute-start.4
  30.0 0.6 collective-permute-start.2
  30.6 24.7 %column_products.1 = f32[2048,256]{1,0:T(8,128)} custom-call(bf16[3200,512]{1,0:T(8,128)(2,1)} %refs_0_.3, bf16[3200,512]{1,0:T(8,128)(2,1)} %collective-permute-done.refs_1_, bf16[3200,256]{1,0:T(8,128)(2,1)} %get-tuple-element.24.refs_2_, bf16[2048,1024]{1,0:T(8,128)(2,1)} %refs_3_.3), custom_call_target="tpu_custom_call" | custom-call | flops 16777216000 | bytes 6553600 | tf_op jit(solution)/shard_map/column_products/pallas_call | solution.py:344
  55.8 3.1 %collective-permute-start.6 = (f32[136,256]{1,0:T(8,128)S(1)}, f32[136,256]{1,0:T(8,128)S(1)}, u32[]{:S(2)}, u32[]{:S(2)}) collective-permute-start(f32[136,256]{1,0:T(8,128)S(1)} %add_add_fusion.2), channel_id=1, source_target_pairs={{0,16},{2,18},{4,20},{6,22},{8,24},{10,26},{12,28},{14,30},{16,0},... | collective-permute-start | bytes 417800 | tf_op jit(solution)/shard_map/ppermute | solution.py:494
  58.9 1.0 collective-permute-start.5
  59.9 2.3 %constant_dynamic-slice_fusion.5 = (f32[512,256]{1,0:T(8,128)}, f32[512,256]{1,0:T(8,128)S(1)}, f32[512,256]{1,0:T(8,128)S(1)}) fusion(f32[2048,256]{1,0:T(8,128)} %column_products.1, s32[]{:T(128)S(6)} %select_n.211, s32[]{:T(128)S(6)} %select_n.213, s32[]{:T(128)S(6)} %select_n.212), kind=kLoop, calls=%fused_computation.31 | loop fusion | bytes 3145740 | tf_op jit(solution)/shard_map/dynamic_slice | solution.py:500
  62.1 1.4 collective-permute-start.8
  63.6 1.9 collective-permute-start.10
  65.8 7.3 %collective-permute-done.6 = f32[136,256]{1,0:T(8,128)S(1)} collective-permute-done((f32[136,256]{1,0:T(8,128)S(1)}, f32[136,256]{1,0:T(8,128)S(1)}, u32[]{:S(2)}, u32[]{:S(2)}) %collective-permute-start.6) | collective-permute-done | bytes 139296 | tf_op jit(solution)/shard_map/ppermute | solution.py:494
  73.2 0.7 fusion.6
  73.9 1.4 broadcast_in_dim_reshape.4
  75.3 1.5 reduce_window_sum.28
  76.7 0.7 maximum_select_fusion.gram_ref
  77.5 10.1 %collective-permute-done.10 = f32[512,256]{1,0:T(8,128)} collective-permute-done((f32[512,256]{1,0:T(8,128)S(1)}, f32[512,256]{1,0:T(8,128)}, u32[]{:S(2)}, u32[]{:S(2)}) %collective-permute-start.10) | collective-permute-done | bytes 524320 | tf_op jit(solution)/shard_map/ppermute | solution.py:494
  87.6 1.2 collective-permute-done.9
  88.7 1.7 add_add_fusion
  90.4 1.3 copy-done
  91.7 11.1 %all-to-all-start.1 = ((bf16[16,128,512]{2,1,0:T(8,128)(2,1)}), bf16[16,128,512]{2,1,0:T(8,128)(2,1)}, u32[]{:S(2)}, u32[]{:S(2)}) async-start(bf16[16,128,512]{2,1,0:T(8,128)(2,1)} %get-tuple-element.32), calls=%async_computation.1 | async-start | bytes 4194304 | tf_op jit(solution)/shard_map/all_to_all | solution.py:575
  103.7 1.9 collective-permute-start.12
  105.7 2.4 %collective-permute-start.14 = (f32[128,256]{1,0:T(8,128)S(1)}, f32[128,256]{1,0:T(8,128)S(1)}, u32[]{:S(2)}, u32[]{:S(2)}) collective-permute-start(f32[128,256]{1,0:T(8,128)S(1)} %get-tuple-element.48), channel_id=1, source_target_pairs={{0,24},{2,26},{4,28},{6,30},{8,16},{10,18},{12,20},{14,22},{16,8},... | collective-permute-start | bytes 393224 | tf_op jit(solution)/shard_map/ppermute | solution.py:494
  108.0 24.0 %factor.1.inv_ref = f32[256,256]{1,0:T(8,128)} custom-call(f32[256,256]{1,0:T(8,128)} %maximum_select_fusion.gram_ref), custom_call_target="tpu_custom_call" | custom-call | flops 20000000000 | bytes 524288 | tf_op jit(solution)/shard_map/factor/pallas_call | solution.py:179
  132.0 8.6 %collective-permute-done.12 = f32[128,256]{1,0:T(8,128)S(1)} collective-permute-done((f32[128,256]{1,0:T(8,128)S(1)}, f32[128,256]{1,0:T(8,128)S(1)}, u32[]{:S(2)}, u32[]{:S(2)}) %collective-permute-start.12) | collective-permute-done | bytes 131104 | tf_op jit(solution)/shard_map/ppermute | solution.py:494
  140.7 6.1 %collective-permute-done.14 = f32[128,256]{1,0:T(8,128)S(1)} collective-permute-done((f32[128,256]{1,0:T(8,128)S(1)}, f32[128,256]{1,0:T(8,128)S(1)}, u32[]{:S(2)}, u32[]{:S(2)}) %collective-permute-start.14) | collective-permute-done | bytes 131104 | tf_op jit(solution)/shard_map/ppermute | solution.py:494
  146.8 14.4 %collective-permute-done.13 = f32[128,256]{1,0:T(8,128)S(1)} collective-permute-done((f32[128,256]{1,0:T(8,128)S(1)}, f32[128,256]{1,0:T(8,128)S(1)}, u32[]{:S(2)}, u32[]{:S(2)}) %collective-permute-start.13) | collective-permute-done | bytes 131104 | tf_op jit(solution)/shard_map/ppermute | solution.py:494
  161.2 1.3 convolution_convert_fusion
  162.6 1.6 collective-permute-start.17
  164.2 2.8 %collective-permute-start.15 = (bf16[128,256]{1,0:T(8,128)(2,1)S(1)}, bf16[128,256]{1,0:T(8,128)(2,1)S(1)}, u32[]{:S(2)}, u32[]{:S(2)}) collective-permute-start(bf16[128,256]{1,0:T(8,128)(2,1)S(1)} %convolution_convert_fusion), channel_id=1, source_target_pairs={{0,8},{2,10},{4,12},{6,14},{8,0},{10,2},{12,4},{14,6},{16,24},{18,... | collective-permute-start | bytes 196616 | tf_op jit(solution)/shard_map/ppermute | solution.py:494
  167.0 0.7 select_reduce_fusion.pos_ref
  167.7 1.3 collective-permute-done.17
  168.9 1.3 collective-permute-done.16
  170.4 3.5 %select.24 = bf16[13,128,512]{2,1,0:T(8,128)(2,1)} custom-call(s32[13]{0:T(128)} %select_reduce_fusion.pos_ref, bf16[16,128,512]{2,1,0:T(8,128)(2,1)} %copy-done, bf16[16,128,512]{2,1,0:T(8,128)(2,1)} %all-to-all-done.1.refs_1_), custom_call_target="tpu_custom_call" | custom-call | bytes 3407872 | tf_op jit(solution)/shard_map/select/pallas_call | solution.py:123
  174.0 0.7 select_reduce_fusion.1.w_ref
  174.7 2.6 %collective-permute-start.21 = (bf16[512,256]{1,0:T(8,128)(2,1)S(1)}, bf16[512,256]{1,0:T(8,128)(2,1)S(1)}, u32[]{:S(2)}, u32[]{:S(2)}) collective-permute-start(bf16[512,256]{1,0:T(8,128)(2,1)S(1)} %pad_maximum_fusion.1), channel_id=1, source_target_pairs={{0,6},{2,4},{4,2},{6,0},{8,14},{10,12},{12,10},{14,8},{16,22},{18,... | collective-permute-start | bytes 786440 | tf_op jit(solution)/shard_map/ppermute | solution.py:494
  177.6 0.6 collective-permute-start.19
  178.1 1.2 copy-done.7
  179.3 14.6 %kernel_rows.1 = (bf16[1664,2048]{1,0:T(8,128)(2,1)}, bf16[1664,256]{1,0:T(8,128)(2,1)}) custom-call(f32[13]{0:T(128)} %select_reduce_fusion.1.w_ref, bf16[1664,512]{1,0:T(8,128)(2,1)} %bitcast.17, bf16[1664,512]{1,0:T(8,128)(2,1)} %copy-done.7, bf16[256,1024]{1,0:T(8,128)(2,1)} %get-tuple-element.33.refs_2_, bf16[2048,1024]{1,0:T(8,128)(2,1)} %refs_3_.3), custom_call_target="tpu_custom_call" | custom-call | flops 7851737088 | bytes 14417920 | tf_op jit(solution)/shard_map/kernel_rows/pallas_call | solution.py:402
  194.0 1.1 pad_maximum_fusion.rt_ref
  195.1 9.4 %remainder_rows.1 = (bf16[1664,2048]{1,0:T(8,128)(2,1)}, f32[256,2048]{1,0:T(8,128)}) custom-call(s32[1]{0:T(128)} %bitcast.quarter_ref, bf16[1664,2048]{1,0:T(8,128)(2,1)} %get-tuple-element.36.kern_ref, bf16[1664,256]{1,0:T(8,128)(2,1)} %get-tuple-element.37.p_ref, f32[256,256]{1,0:T(8,128)} %factor.1.inv_ref, bf16[4,512,256]{2,1,0:T(8,128)(2,1)} %pad_maximum_fusion.rt_ref), custom_call_target="tpu_custom_call" | custom-call | flops 1744830464 | bytes 13631488 | tf_op jit(solution)/shard_map/remainder_rows/pallas_call | solution.py:470
  (62 shorter events, 2.5 us)
Async XLA Ops:
  0.6 14.7 %collective-permute-start = (bf16[3200,512]{1,0:T(8,128)(2,1)}, bf16[3200,512]{1,0:T(8,128)(2,1)}, u32[]{:S(2)}, u32[]{:S(2)}) collective-permute-start(bf16[3200,512]{1,0:T(8,128)(2,1)} %refs_0_.3), channel_id=1, source_target_pairs={{0,1},{1,0},{2,3},{3,2},{4,5},{5,4},{6,7},{7,6},{8,9},{9,8},{10,11... | collective-permute-start | bytes 9830408 | tf_op jit(solution)/shard_map/ppermute | solution.py:192
  5.1 8.5 %copy-start.8 = (bf16[25]{0:T(256)(128)(2,1)S(1)}, bf16[25]{0:T(256)(128)(2,1)}, u32[]{:S(2)}) copy-start(bf16[25]{0:T(256)(128)(2,1)} %param.7) | copy-start | bytes 154
  5.1 85.3 %all-to-all-start = ((bf16[16,128,512]{2,1,0:T(8,128)(2,1)}), bf16[16,128,512]{2,1,0:T(8,128)(2,1)S(1)}, u32[]{:S(2)}, u32[]{:S(2)}) async-start(bf16[16,128,512]{2,1,0:T(8,128)(2,1)} %get-tuple-element.31), calls=%async_computation | async-start | bytes 4194304 | tf_op jit(solution)/shard_map/all_to_all | solution.py:543
  13.4 2.0 collective-permute-start.1
  15.4 0.8 copy-start.1
  27.0 28.3 %collective-permute-start.3 = (f32[136,256]{1,0:T(8,128)S(1)}, f32[136,256]{1,0:T(8,128)S(1)}, u32[]{:S(2)}, u32[]{:S(2)}) collective-permute-start(f32[136,256]{1,0:T(8,128)S(1)} %pad_maximum_fusion.2), channel_id=1, source_target_pairs={{0,4},{2,6},{4,0},{6,2},{8,12},{10,14},{12,8},{14,10},{16,20},{18,... | collective-permute-start | bytes 417800 | tf_op jit(solution)/shard_map/ppermute | solution.py:494
  29.0 26.3 %collective-permute-start.4 = (f32[136,256]{1,0:T(8,128)S(1)}, f32[136,256]{1,0:T(8,128)S(1)}, u32[]{:S(2)}, u32[]{:S(2)}) collective-permute-start(f32[136,256]{1,0:T(8,128)S(1)} %pad_maximum_fusion.2), channel_id=1, source_target_pairs={{0,6},{2,4},{4,2},{6,0},{8,14},{10,12},{12,10},{14,8},{16,22},{18,... | collective-permute-start | bytes 417800 | tf_op jit(solution)/shard_map/ppermute | solution.py:494
  30.0 25.4 %collective-permute-start.2 = (f32[136,256]{1,0:T(8,128)S(1)}, f32[136,256]{1,0:T(8,128)S(1)}, u32[]{:S(2)}, u32[]{:S(2)}) collective-permute-start(f32[136,256]{1,0:T(8,128)S(1)} %pad_maximum_fusion.2), channel_id=1, source_target_pairs={{0,2},{2,0},{4,6},{6,4},{8,10},{10,8},{12,14},{14,12},{16,18},{18,... | collective-permute-start | bytes 417800 | tf_op jit(solution)/shard_map/ppermute | solution.py:494
  55.4 17.8 %copy-start.2 = (s32[16,25]{1,0:T(8,128)S(1)}, s32[16,25]{1,0:T(8,128)}, u32[]{:S(2)}) copy-start(s32[16,25]{1,0:T(8,128)} %dest_ref.1) | copy-start | bytes 4804
  55.4 17.8 %copy-start.5 = (s32[16]{0:T(128)S(1)}, s32[16]{0:T(128)}, u32[]{:S(2)}) copy-start(s32[16]{0:T(128)} %cnt_ref.3) | copy-start | bytes 196
  55.4 10.1 %collective-permute-start.7 = (f32[136,256]{1,0:T(8,128)S(1)}, f32[136,256]{1,0:T(8,128)S(1)}, u32[]{:S(2)}, u32[]{:S(2)}) collective-permute-start(f32[136,256]{1,0:T(8,128)S(1)} %add_add_fusion.2), channel_id=1, source_target_pairs={{0,24},{2,26},{4,28},{6,30},{8,16},{10,18},{12,20},{14,22},{16,8},... | collective-permute-start | bytes 417800 | tf_op jit(solution)/shard_map/ppermute | solution.py:494
  55.8 17.3 %collective-permute-start.6 = (f32[136,256]{1,0:T(8,128)S(1)}, f32[136,256]{1,0:T(8,128)S(1)}, u32[]{:S(2)}, u32[]{:S(2)}) collective-permute-start(f32[136,256]{1,0:T(8,128)S(1)} %add_add_fusion.2), channel_id=1, source_target_pairs={{0,16},{2,18},{4,20},{6,22},{8,24},{10,26},{12,28},{14,30},{16,0},... | collective-permute-start | bytes 417800 | tf_op jit(solution)/shard_map/ppermute | solution.py:494
  58.9 14.2 %collective-permute-start.5 = (f32[136,256]{1,0:T(8,128)S(1)}, f32[136,256]{1,0:T(8,128)S(1)}, u32[]{:S(2)}, u32[]{:S(2)}) collective-permute-start(f32[136,256]{1,0:T(8,128)S(1)} %add_add_fusion.2), channel_id=1, source_target_pairs={{0,8},{2,10},{4,12},{6,14},{8,0},{10,2},{12,4},{14,6},{16,24},{18,... | collective-permute-start | bytes 417800 | tf_op jit(solution)/shard_map/ppermute | solution.py:494
  62.1 15.3 %collective-permute-start.8 = (f32[512,256]{1,0:T(8,128)}, f32[512,256]{1,0:T(8,128)}, u32[]{:S(2)}, u32[]{:S(2)}) collective-permute-start(f32[512,256]{1,0:T(8,128)} %get-tuple-element.44), channel_id=1, source_target_pairs={{0,2},{2,0},{4,6},{6,4},{8,10},{10,8},{12,14},{14,12},{16,18},{18,... | collective-permute-start | bytes 1572872 | tf_op jit(solution)/shard_map/ppermute | solution.py:494
  63.6 24.0 %collective-permute-start.10 = (f32[512,256]{1,0:T(8,128)S(1)}, f32[512,256]{1,0:T(8,128)}, u32[]{:S(2)}, u32[]{:S(2)}) collective-permute-start(f32[512,256]{1,0:T(8,128)S(1)} %get-tuple-element.45), channel_id=1, source_target_pairs={{0,6},{2,4},{4,2},{6,0},{8,14},{10,12},{12,10},{14,8},{16,22},{18,... | collective-permute-start | bytes 1572872 | tf_op jit(solution)/shard_map/ppermute | solution.py:494
  65.5 23.2 %collective-permute-start.9 = (f32[512,256]{1,0:T(8,128)S(1)}, f32[512,256]{1,0:T(8,128)}, u32[]{:S(2)}, u32[]{:S(2)}) collective-permute-start(f32[512,256]{1,0:T(8,128)S(1)} %get-tuple-element.46), channel_id=1, source_target_pairs={{0,4},{2,6},{4,0},{6,2},{8,12},{10,14},{12,8},{14,10},{16,20},{18,... | collective-permute-start | bytes 1572872 | tf_op jit(solution)/shard_map/ppermute | solution.py:494
  73.1 3.6 %collective-permute-start.11 = (f32[128,256]{1,0:T(8,128)S(1)}, f32[128,256]{1,0:T(8,128)S(1)}, u32[]{:S(2)}, u32[]{:S(2)}) collective-permute-start(f32[128,256]{1,0:T(8,128)S(1)} %slice.31), channel_id=1, source_target_pairs={{0,1},{1,0},{2,3},{3,2},{4,5},{5,4},{6,7},{7,6},{8,9},{9,8},{10,11... | collective-permute-start | bytes 393224 | tf_op jit(solution)/shard_map/ppermute | solution.py:563
  90.4 12.5 %copy-start.3 = (s32[16,25]{1,0:T(8,128)S(1)}, s32[16,25]{1,0:T(8,128)}, u32[]{:S(2)}) copy-start(s32[16,25]{1,0:T(8,128)} %reduce_window_sum.28) | copy-start | bytes 4804
  90.4 12.5 %copy-start.6 = (s32[16]{0:T(128)S(1)}, s32[16]{0:T(128)}, u32[]{:S(2)}) copy-start(s32[16]{0:T(128)} %cnt_ref.3) | copy-start | bytes 196
  90.4 12.7 %copy-start.4 = (s32[400]{0:T(512)S(1)}, s32[400]{0:T(512)}, u32[]{:S(2)}) copy-start(s32[400]{0:T(512)} %broadcast_in_dim_reshape.4) | copy-start | bytes 4804
  90.4 1.3 copy-start
  91.7 78.6 %all-to-all-start.1 = ((bf16[16,128,512]{2,1,0:T(8,128)(2,1)}), bf16[16,128,512]{2,1,0:T(8,128)(2,1)}, u32[]{:S(2)}, u32[]{:S(2)}) async-start(bf16[16,128,512]{2,1,0:T(8,128)(2,1)} %get-tuple-element.32), calls=%async_computation.1 | async-start | bytes 4194304 | tf_op jit(solution)/shard_map/all_to_all | solution.py:575
  103.7 36.9 %collective-permute-start.12 = (f32[128,256]{1,0:T(8,128)S(1)}, f32[128,256]{1,0:T(8,128)S(1)}, u32[]{:S(2)}, u32[]{:S(2)}) collective-permute-start(f32[128,256]{1,0:T(8,128)S(1)} %get-tuple-element.47), channel_id=1, source_target_pairs={{0,8},{2,10},{4,12},{6,14},{8,0},{10,2},{12,4},{14,6},{16,24},{18,... | collective-permute-start | bytes 393224 | tf_op jit(solution)/shard_map/ppermute | solution.py:494
  105.7 41.1 %collective-permute-start.14 = (f32[128,256]{1,0:T(8,128)S(1)}, f32[128,256]{1,0:T(8,128)S(1)}, u32[]{:S(2)}, u32[]{:S(2)}) collective-permute-start(f32[128,256]{1,0:T(8,128)S(1)} %get-tuple-element.48), channel_id=1, source_target_pairs={{0,24},{2,26},{4,28},{6,30},{8,16},{10,18},{12,20},{14,22},{16,8},... | collective-permute-start | bytes 393224 | tf_op jit(solution)/shard_map/ppermute | solution.py:494
  108.0 53.2 %collective-permute-start.13 = (f32[128,256]{1,0:T(8,128)S(1)}, f32[128,256]{1,0:T(8,128)S(1)}, u32[]{:S(2)}, u32[]{:S(2)}) collective-permute-start(f32[128,256]{1,0:T(8,128)S(1)} %get-tuple-element.49), channel_id=1, source_target_pairs={{0,16},{2,18},{4,20},{6,22},{8,24},{10,26},{12,28},{14,30},{16,0},... | collective-permute-start | bytes 393224 | tf_op jit(solution)/shard_map/ppermute | solution.py:494
  162.6 6.4 %collective-permute-start.17 = (bf16[128,256]{1,0:T(8,128)(2,1)S(1)}, bf16[128,256]{1,0:T(8,128)(2,1)S(1)}, u32[]{:S(2)}, u32[]{:S(2)}) collective-permute-start(bf16[128,256]{1,0:T(8,128)(2,1)S(1)} %convolution_convert_fusion), channel_id=1, source_target_pairs={{0,24},{2,26},{4,28},{6,30},{8,16},{10,18},{12,20},{14,22},{16,8},... | collective-permute-start | bytes 196616 | tf_op jit(solution)/shard_map/ppermute | solution.py:494
  164.2 6.1 %collective-permute-start.16 = (bf16[128,256]{1,0:T(8,128)(2,1)S(1)}, bf16[128,256]{1,0:T(8,128)(2,1)S(1)}, u32[]{:S(2)}, u32[]{:S(2)}) collective-permute-start(bf16[128,256]{1,0:T(8,128)(2,1)S(1)} %convolution_convert_fusion), channel_id=1, source_target_pairs={{0,16},{2,18},{4,20},{6,22},{8,24},{10,26},{12,28},{14,30},{16,0},... | collective-permute-start | bytes 196616 | tf_op jit(solution)/shard_map/ppermute | solution.py:494
  164.2 6.1 %collective-permute-start.15 = (bf16[128,256]{1,0:T(8,128)(2,1)S(1)}, bf16[128,256]{1,0:T(8,128)(2,1)S(1)}, u32[]{:S(2)}, u32[]{:S(2)}) collective-permute-start(bf16[128,256]{1,0:T(8,128)(2,1)S(1)} %convolution_convert_fusion), channel_id=1, source_target_pairs={{0,8},{2,10},{4,12},{6,14},{8,0},{10,2},{12,4},{14,6},{16,24},{18,... | collective-permute-start | bytes 196616 | tf_op jit(solution)/shard_map/ppermute | solution.py:494
  173.8 4.3 %collective-permute-start.18 = (bf16[1664,512]{1,0:T(8,128)(2,1)}, bf16[1664,512]{1,0:T(8,128)(2,1)S(1)}, u32[]{:S(2)}, u32[]{:S(2)}) collective-permute-start(bf16[1664,512]{1,0:T(8,128)(2,1)} %bitcast.16), channel_id=1, source_target_pairs={{0,1},{1,0},{2,3},{3,2},{4,5},{5,4},{6,7},{7,6},{8,9},{9,8},{10,11... | collective-permute-start | bytes 5111816 | tf_op jit(solution)/shard_map/ppermute | solution.py:192
  174.7 19.3 %collective-permute-start.21 = (bf16[512,256]{1,0:T(8,128)(2,1)S(1)}, bf16[512,256]{1,0:T(8,128)(2,1)S(1)}, u32[]{:S(2)}, u32[]{:S(2)}) collective-permute-start(bf16[512,256]{1,0:T(8,128)(2,1)S(1)} %pad_maximum_fusion.1), channel_id=1, source_target_pairs={{0,6},{2,4},{4,2},{6,0},{8,14},{10,12},{12,10},{14,8},{16,22},{18,... | collective-permute-start | bytes 786440 | tf_op jit(solution)/shard_map/ppermute | solution.py:494
  177.3 16.7 %collective-permute-start.20 = (bf16[512,256]{1,0:T(8,128)(2,1)S(1)}, bf16[512,256]{1,0:T(8,128)(2,1)S(1)}, u32[]{:S(2)}, u32[]{:S(2)}) collective-permute-start(bf16[512,256]{1,0:T(8,128)(2,1)S(1)} %pad_maximum_fusion.1), channel_id=1, source_target_pairs={{0,4},{2,6},{4,0},{6,2},{8,12},{10,14},{12,8},{14,10},{16,20},{18,... | collective-permute-start | bytes 786440 | tf_op jit(solution)/shard_map/ppermute | solution.py:494
  177.6 16.4 %collective-permute-start.19 = (bf16[512,256]{1,0:T(8,128)(2,1)S(1)}, bf16[512,256]{1,0:T(8,128)(2,1)S(1)}, u32[]{:S(2)}, u32[]{:S(2)}) collective-permute-start(bf16[512,256]{1,0:T(8,128)(2,1)S(1)} %pad_maximum_fusion.1), channel_id=1, source_target_pairs={{0,2},{2,0},{4,6},{6,4},{8,10},{10,8},{12,14},{14,12},{16,18},{18,... | collective-permute-start | bytes 786440 | tf_op jit(solution)/shard_map/ppermute | solution.py:494
  178.1 1.2 copy-start.7

commit v7 on v5

--- a/solution.py
+++ b/solution.py
@@ -50,7 +50,7 @@
     return high, (x - high.astype(jnp.float32)).astype(jnp.bfloat16)
 
 
-HEAD = 64
+HEAD = 48
 
 
 def block_copies(rank, whole_ref, outer, first_ref, last_ref, sems):
@@ -126,35 +126,34 @@
     )(destinations, counts, desc_blocks)
 
 
-def select_kernel(per_pair, pos_ref, *refs):
-    recv_refs, (out_ref, sems) = refs[:per_pair], refs[per_pair:]
-
-    def copies(p, rank):
-        owner = pos_ref[p] // per_pair
-        moves = block_copies(rank, out_ref.at[p], owner, recv_refs[0], recv_refs[-1], sems.at[p])
-        return [pltpu.make_async_copy(b, a, sem) for a, b, sem in moves]
-
-    for act in ("start", "wait"):
-        for p in range(DST_BLK):
-            for r in range(per_pair):
-                @pl.when(pos_ref[p] % per_pair == r)
-                def _():
-                    for c in copies(p, r):
-                        getattr(c, act)()
-
-
-def select(received, positions):
+def select_kernel(rows, owner_ref, *refs):
+    recv_refs, (out_ref, sems) = refs[: len(rows)], refs[len(rows) :]
+    copies = []
+    for p in range(out_ref.shape[0]):
+        at = 0
+        for i, (start, size) in enumerate(rows):
+            src = recv_refs[i].at[owner_ref[p], pl.ds(start, size)]
+            copies.append(pltpu.make_async_copy(src, out_ref.at[p, pl.ds(at, size)], sems.at[p, i]))
+            at += size
+    for c in copies:
+        c.start()
+    for c in copies:
+        c.wait()
+
+
+def select(received, rows, from_owner):
     feat = received[0].shape[-1]
+    count = from_owner.shape[0]
     return pl.pallas_call(
-        functools.partial(select_kernel, len(received)),
-        out_shape=jax.ShapeDtypeStruct((DST_BLK, BLK, feat), received[0].dtype),
-        in_specs=[SMEM] + [ANY] * len(received),
+        functools.partial(select_kernel, rows),
+        out_shape=jax.ShapeDtypeStruct((count, BLK, feat), received[0].dtype),
+        in_specs=[SMEM] + [ANY] * len(rows),
         out_specs=VMEM,
-        scratch_shapes=[pltpu.SemaphoreType.DMA((DST_BLK, 2))],
+        scratch_shapes=[pltpu.SemaphoreType.DMA((count, len(rows)))],
         compiler_params=params(),
-        cost_estimate=cost(0, 4 * DST_BLK * BLK * feat),
+        cost_estimate=cost(0, 4 * count * BLK * feat),
         name="select",
-    )(positions, *received)
+    )(from_owner, *received)
 
 
 def small_factor(a):
@@ -206,7 +205,7 @@
         out_shape=jax.ShapeDtypeStruct((n, n), jnp.float32),
         scratch_shapes=[pltpu.VMEM((n, n), jnp.float32)],
         compiler_params=params(),
-        cost_estimate=cost(2e10, 8 * n * n),
+        cost_estimate=cost(4 * n * n * n, 8 * n * n),
         name="factor",
     )(gram)
 
@@ -388,7 +387,7 @@
 
 def rows_kernel(nparts, w_ref, *refs):
     parts = refs[:nparts]
-    sp_ref, s_ref, kern_ref, p_ref, x_ref, rs_ref, sems = refs[nparts:]
+    sp_ref, s_ref, kern_ref, p_ref, cs_ref, csp_ref, x_ref, rs_ref, sems = refs[nparts:]
     rows_all = x_ref.shape[0]
     chunk = s_ref.shape[0]
     blocks = rows_all // BLK
@@ -402,6 +401,7 @@
             for c in moves:
                 c.start()
         points = column_scale(sp_ref[...])
+        csp_ref[...] = points
         for (a, b), moves in zip(spans, copies):
             for c in moves:
                 c.wait()
@@ -413,6 +413,7 @@
             p_ref[a:b, :] = (inner * inner * scale * points).astype(jnp.bfloat16)
 
     columns = column_scale(s_ref[...])
+    cs_ref[...] = columns
     for a, b in spans:
         inner = nt(x_ref[a:b, :], s_ref[...])
         scale = jnp.concatenate([rs_ref[a:b, :]] * (chunk // 128), axis=1)
@@ -430,6 +431,8 @@
         out_shape=(
             jax.ShapeDtypeStruct((rows, cols), jnp.bfloat16),
             jax.ShapeDtypeStruct((rows, PANEL), jnp.bfloat16),
+            jax.ShapeDtypeStruct((1, cols), jnp.float32),
+            jax.ShapeDtypeStruct((1, PANEL), jnp.float32),
         ),
         in_specs=[SMEM]
         + [ANY] * len(parts)
@@ -440,6 +443,8 @@
         out_specs=(
             pl.BlockSpec((rows, chunk), lambda i: (0, i)),
             pl.BlockSpec((rows, PANEL), lambda i: (0, 0)),
+            pl.BlockSpec((1, chunk), lambda i: (0, i)),
+            pl.BlockSpec((1, PANEL), lambda i: (0, 0)),
         ),
         scratch_shapes=[
             pltpu.VMEM((rows, width), jnp.bfloat16),
@@ -452,6 +457,82 @@
         ),
         name="kernel_rows",
     )(weights, *parts, sp, s)
+
+
+def seconds_kernel(nparts, place_ref, num_ref, w_ref, *refs):
+    parts = refs[:nparts]
+    sp_ref, csp_ref, s_ref, cs_ref = refs[nparts : nparts + 4]
+    kern_ref, p_ref, x_ref, kbuf_ref, pbuf_ref, sems, out_sems = refs[nparts + 6 :]
+    rows_all = x_ref.shape[0]
+    blocks = rows_all // BLK
+    num = num_ref[0]
+    spans = [(a, min(2, blocks - a)) for a in range(0, blocks, 2)]
+    copies = join_copies(parts, x_ref, sems, [(a * BLK, n * BLK) for a, n in spans])
+    for moves in copies:
+        for c in moves:
+            c.start()
+
+    def puts(j):
+        rows = pl.ds(j * BLK, BLK)
+        dst = pl.ds(pl.multiple_of(place_ref[j] * BLK, BLK), BLK)
+        return [
+            pltpu.make_async_copy(kbuf_ref.at[rows], kern_ref.at[dst], out_sems.at[j, 0]),
+            pltpu.make_async_copy(pbuf_ref.at[rows], p_ref.at[dst], out_sems.at[j, 1]),
+        ]
+
+    for t, (first, n) in enumerate(spans):
+        for c in copies[t]:
+            c.wait()
+
+        @pl.when(first < num)
+        def _():
+            a, b = first * BLK, (first + n) * BLK
+            scale = jnp.concatenate(
+                [row_scale(x_ref[j * BLK : (j + 1) * BLK, :], w_ref[j]) for j in range(first, first + n)],
+                axis=0,
+            )
+            inner = nt(x_ref[a:b, :], sp_ref[...])
+            pbuf_ref[a:b, :] = (inner * inner * scale * csp_ref[...]).astype(jnp.bfloat16)
+            inner = nt(x_ref[a:b, :], s_ref[...])
+            kbuf_ref[a:b, :] = (inner * inner * scale * cs_ref[...]).astype(jnp.bfloat16)
+
+        for j in range(first, first + n):
+            @pl.when(j < num)
+            def _():
+                for c in puts(j):
+                    c.start()
+
+    for j in range(blocks):
+        @pl.when(j < num)
+        def _():
+            for c in puts(j):
+                c.wait()
+
+
+def second_rows(parts, places, num, weights, sp, csp, s, cs, kern, panel):
+    rows, feat = parts[0].shape
+    cols, width = s.shape
+    n = len(parts)
+    return pl.pallas_call(
+        functools.partial(seconds_kernel, n),
+        out_shape=(
+            jax.ShapeDtypeStruct(kern.shape, kern.dtype),
+            jax.ShapeDtypeStruct(panel.shape, panel.dtype),
+        ),
+        in_specs=[SMEM] * 3 + [ANY] * n + [VMEM] * 4 + [ANY, ANY],
+        out_specs=(ANY, ANY),
+        input_output_aliases={n + 7: 0, n + 8: 1},
+        scratch_shapes=[
+            pltpu.VMEM((rows, width), jnp.bfloat16),
+            pltpu.VMEM((rows, cols), jnp.bfloat16),
+            pltpu.VMEM((rows, PANEL), jnp.bfloat16),
+            pltpu.SemaphoreType.DMA((-(-rows // (2 * BLK)), n)),
+            pltpu.SemaphoreType.DMA((rows // BLK, 2)),
+        ],
+        compiler_params=params(),
+        cost_estimate=cost(2 * rows * width * (cols + PANEL), 2 * cols * width),
+        name="second_rows",
+    )(places, num, weights, *parts, sp, csp, s, cs, kern, panel)
 
 
 def remainder_kernel(norm, quarter_ref, kern_ref, p_ref, inv_ref, rt_ref, out_ref, proj_ref):
@@ -519,10 +600,13 @@
     return lax.ppermute(x, "rows", flips(bit, lax.axis_size("rows")))
 
 
-def scatter_sum(x, pair):
+def quarters(x, pair):
     n = x.shape[0] // 4
     q = quarter_of(pair)
-    pieces = [lax.dynamic_slice_in_dim(x, (q ^ k) * n, n, 0) for k in range(4)]
+    return [lax.dynamic_slice_in_dim(x, (q ^ k) * n, n, 0) for k in range(4)]
+
+
+def quarter_sum(pieces, pair):
     got = [pieces[0]] + [trade(pieces[k], pair, k) for k in range(1, 4)]
     return (got[0] + got[1]) + (got[2] + got[3])
 
@@ -532,12 +616,9 @@
 
 
 def gather_back(x, pair):
-    n = x.shape[0]
     q = quarter_of(pair)
     pieces = gather_pieces(x, pair)
-    return jnp.concatenate(
-        [lax.select_n(q ^ i, *pieces) for i in range(4)], 0
-    )
+    return jnp.concatenate([lax.select_n(q ^ i, *pieces) for i in range(4)], 0)
 
 
 def pair_sum(x, pair):
@@ -571,7 +652,7 @@
     gram_part, pw, panel_points = panel_products(
         source_parts, block_counts, weights32, sparse_points, moved
     )
-    g = column_products(source_parts, pw, sparse_points)
+    sent = quarters(column_products(source_parts, pw, sparse_points), pairs[0])
 
     spare = -(-owners * slots // (PANEL * 8)) * 8
     table = lax.dynamic_update_slice(
@@ -580,7 +661,8 @@
     if groups == 2:
         gram_part = lax.dynamic_slice_in_dim(gram_part, group * (PANEL // 2), PANEL // 2, 0)
     summed = pair_sum(jnp.concatenate([gram_part, table], 0), pairs[0])
-    summed, g = lax.optimization_barrier((summed, g))
+    summed, *sent = lax.optimization_barrier((summed, *sent))
+    g = quarter_sum(sent, pairs[0])
     for pair in pairs[1:]:
         summed = pair_sum(summed, pair)
     gram, table = summed[:-spare], summed[-spare:]
@@ -591,17 +673,17 @@
         )
     all_weights = table.reshape(-1)[: owners * slots]
 
-    g = scatter_sum(g, pairs[0])
-    if per_pair > 1:
-        g, gram, last = lax.optimization_barrier((g, gram, outgoing[1]))
     for pair in pairs[1:]:
-        g = scatter_sum(g, pair)
+        sent = quarters(g, pair)
+        if per_pair > 1 and pair == pairs[-1]:
+            gram, last, received[0], *sent = lax.optimization_barrier(
+                (gram, outgoing[1], received[0], *sent)
+            )
+        g = quarter_sum(sent, pair)
     if per_pair > 1:
         received.append(lax.all_to_all(last, "rows", split_axis=0, concat_axis=0, tiled=True))
     inverse = factor(gram)
     rt = nt(g, inverse, HIGH).astype(jnp.bfloat16)
-    for pair in pairs[:0:-1]:
-        rt = gather_back(rt, pair)
 
     slot_ids = jnp.arange(slots, dtype=jnp.int32)
     toward = ((slot_ids[None, :] < block_counts[:, None]) & (destinations == me)).astype(jnp.int32)
@@ -612,15 +694,42 @@
     hit = (flat[None, :] == 1) & (place[None, :] == jnp.arange(DST_BLK, dtype=jnp.int32)[:, None])
     positions = jnp.sum(jnp.where(hit, where_from[None, :], 0), axis=1)
     weights_here = jnp.sum(jnp.where(hit, all_weights[None, :], 0.0), axis=1)
-
-    rt, positions = lax.optimization_barrier((rt, positions))
-    arrived = select(received, positions).reshape(DST_BLK * BLK, feat)
-    kern, panel = kernel_rows(share_parts(arrived), weights_here, panel_points, sparse_points)
+    from_owner = positions // per_pair
+    is_second = positions % per_pair == 1
+    order = jnp.cumsum(is_second.astype(jnp.int32))
+    most = DST_BLK // 2
+    pick = is_second[None, :] & (order[None, :] == 1 + jnp.arange(most, dtype=jnp.int32)[:, None])
+    places = jnp.sum(jnp.where(pick, jnp.arange(DST_BLK, dtype=jnp.int32)[None, :], 0), axis=1)
+    second_owner = jnp.sum(jnp.where(pick, from_owner[None, :], 0), axis=1)
+    second_weights = jnp.sum(jnp.where(pick, weights_here[None, :], 0.0), axis=1)
+
+    rt, from_owner = lax.optimization_barrier((rt, from_owner))
+    arrived = select(received[:1], [(0, BLK)], from_owner).reshape(DST_BLK * BLK, feat)
+    kern, panel, cs, csp = kernel_rows(
+        share_parts(arrived), weights_here, panel_points, sparse_points
+    )
+    for pair in pairs[:0:-1]:
+        rt = gather_back(rt, pair)
     pieces = gather_pieces(rt, pairs[0])
+    if per_pair > 1:
+        rt, kern, second_owner = lax.optimization_barrier((rt, kern, second_owner))
+        late = select(received, [(BLK, HEAD), (0, BLK - HEAD)], second_owner)
+        late = late.reshape(most * BLK, feat)
+        kern, panel = second_rows(
+            share_parts(late),
+            places,
+            order[-1:],
+            second_weights,
+            panel_points,
+            csp,
+            sparse_points,
+            cs,
+            kern,
+            panel,
+        )
     kern, *pieces = lax.optimization_barrier((kern, *pieces))
-    rt = jnp.stack(pieces)
     remainder, projected = remainder_rows(
-        kern, panel, quarter_of(pairs[0])[None], inverse, rt, norm
+        kern, panel, quarter_of(pairs[0])[None], inverse, jnp.stack(pieces), norm
     )
     return (projected, remainder)
 

time: 192 us -> 198 us (1.031)
  Pallas kernels: 88 us -> 102 us
  starting transfers between devices: 53 us -> 39.2 us
  other arithmetic: 6.57 us -> 11.7 us
  local copies, waits for them, and re-layouts: 6.72 us -> 11.6 us
  waiting for transfers between devices: 35.2 us -> 30.4 us
    ppermute x18, starting transfers between devices: 39.5 us -> 25 us  [trade(): return lax.ppermute(x, 'rows', flips(bit, lax.axis_size('rows')))]
    pallas_call x1 -> x3, Pallas kernels: 3.59 us -> 14.6 us  [the longest x1 8.34 us: second_rows(): pl.pallas_call(functools.partial(seconds_kernel, n), out_shape=(jax.Shape...]
    ppermute x18, waiting for transfers between devices: 34.2 us -> 30.2 us  [trade(): return lax.ppermute(x, 'rows', flips(bit, lax.axis_size('rows')))]
  transfers between devices with their start and end apart: 24 -> 25, of which waited for: 7 -> 7; matrix products, arithmetic and copies ran while one was open for 7% -> 10% of each run, Pallas kernels for 39% -> 45%
where the time goes in v7:
time: 198 us; the launch traced here: 197 us
  Pallas kernels  102 us (52%)
  starting transfers between devices  39.2 us (20%)
  waiting for transfers between devices  30.4 us (15%)
  other arithmetic  11.7 us (6%)
  local copies, waits for them, and re-layouts  11.6 us (6%)
    ppermute x18, waiting for transfers between devices, trade(): return lax.ppermute(x, 'rows', flips(bit, lax.axis_size('rows')))  30.2 us
    ppermute x18, starting transfers between devices, trade(): return lax.ppermute(x, 'rows', flips(bit, lax.axis_size('rows')))  25 us
    pallas_call x1, Pallas kernels, column_products(): pl.pallas_call(functools.partial(column_kernel, len(parts)), grid=(size /...  24.7 us
    pallas_call x1, Pallas kernels, factor(): pl.pallas_call(functools.partial(factor_kernel, 64), out_shape=jax.ShapeD...  24 us
    pallas_call x1, Pallas kernels, kernel_rows(): pl.pallas_call(functools.partial(rows_kernel, len(parts)), grid=(cols //...  14.8 us
    pallas_call x1, Pallas kernels, panel_products(): pl.pallas_call(functools.partial(panel_kernel, len(parts)), out_shape=(ja...  9.84 us
    pallas_call x1, Pallas kernels, remainder_rows(): pl.pallas_call(functools.partial(remainder_kernel, norm), grid_spec=spec,...  9.42 us
    pallas_call x1, Pallas kernels, second_rows(): pl.pallas_call(functools.partial(seconds_kernel, n), out_shape=(jax.Shape...  8.34 us
  transfers between devices with their start and end apart: 25, of which 7 were waited for; matrix products, arithmetic and copies ran while one was open for 10% of the time, Pallas kernels for 45%

profile of v7, /device:TPU:0, one launch (start us, length us, event | category | flops | bytes accessed | tf_op | source)
XLA Modules:
  0.0 196.8 jit_solution(668819638262512595)
XLA Ops:
  1.1 4.2 %pack.1 = (bf16[16,176,512]{2,1,0:T(8,128)(2,1)}, bf16[16,80,512]{2,1,0:T(8,128)(2,1)}) custom-call(s32[16,25]{1,0:T(8,128)} %dest_ref.1, s32[16]{0:T(128)} %cnt_ref.3, bf16[25,128,512]{2,1,0:T(8,128)(2,1)} %bitcast.20), custom_call_target="tpu_custom_call" | custom-call | bytes 6553600 | tf_op jit(solution)/shard_map/pack/pallas_call | solution.py:111
  5.4 7.4 %all-to-all-start = ((bf16[16,176,512]{2,1,0:T(8,128)(2,1)}), bf16[16,176,512]{2,1,0:T(8,128)(2,1)S(1)}, u32[]{:S(2)}, u32[]{:S(2)}) async-start(bf16[16,176,512]{2,1,0:T(8,128)(2,1)} %get-tuple-element.40), calls=%async_computation | async-start | bytes 5767168 | tf_op jit(solution)/shard_map/all_to_all | solution.py:649
  12.8 1.9 slice.33
  16.8 0.8 copy-done.2
  17.6 9.8 %panel_products.1 = (f32[256,256]{1,0:T(8,128)}, bf16[3200,256]{1,0:T(8,128)(2,1)}, bf16[256,1024]{1,0:T(8,128)(2,1)}) custom-call(s32[16]{0:T(128)} %cnt_ref.3, f32[25]{0:T(128)} %convert_element_type.21.w_ref, bf16[3200,512]{1,0:T(8,128)(2,1)} %refs_0_.3, bf16[3200,512]{1,0:T(8,128)(2,1)} %collective-permute-done.refs_1_, bf16[2048,1024]{1,0:T(8,128)(2,1)} %refs_4_.1, ...), custom_call_target="tpu_custom_call" | custom-call | flops 2097152000 | bytes 6553600 | tf_op jit(solution)/shard_map/panel_products/pallas_call | solution.py:319
  27.4 0.9 constant_dynamic-slice_fusion.8
  28.4 3.4 %collective-permute-start.3 = (f32[136,256]{1,0:T(8,128)S(1)}, f32[136,256]{1,0:T(8,128)S(1)}, u32[]{:S(2)}, u32[]{:S(2)}) collective-permute-start(f32[136,256]{1,0:T(8,128)S(1)} %pad_maximum_fusion.2), channel_id=1, source_target_pairs={{0,4},{2,6},{4,0},{6,2},{8,12},{10,14},{12,8},{14,10},{16,20},{18,... | collective-permute-start | bytes 417800 | tf_op jit(solution)/shard_map/ppermute | solution.py:600
  31.9 24.7 %column_products.1 = f32[2048,256]{1,0:T(8,128)} custom-call(bf16[3200,512]{1,0:T(8,128)(2,1)} %refs_0_.3, bf16[3200,512]{1,0:T(8,128)(2,1)} %collective-permute-done.refs_1_, bf16[3200,256]{1,0:T(8,128)(2,1)} %get-tuple-element.37.refs_2_, bf16[2048,1024]{1,0:T(8,128)(2,1)} %refs_4_.1), custom_call_target="tpu_custom_call" | custom-call | flops 16777216000 | bytes 6553600 | tf_op jit(solution)/shard_map/column_products/pallas_call | solution.py:368
  56.6 2.7 %constant_dynamic-slice_fusion.4 = (f32[512,256]{1,0:T(8,128)}, f32[512,256]{1,0:T(8,128)}, f32[512,256]{1,0:T(8,128)}, f32[512,256]{1,0:T(8,128)S(1)}) fusion(f32[2048,256]{1,0:T(8,128)} %column_products.1, s32[]{:T(128)S(6)} %select_n.247, s32[]{:T(128)S(6)} %select_n.246, s32[]{:T(128)S(6)} %select_n.245, s32[]{:T(128)S(6)} %select_n.244), kind=kLoop, calls=%fused_computation.32 | loop fusion | bytes 4194320 | tf_op jit(solution)/shard_map/dynamic_slice | solution.py:606
  59.4 2.0 %collective-permute-start.5 = (f32[136,256]{1,0:T(8,128)S(1)}, f32[136,256]{1,0:T(8,128)S(1)}, u32[]{:S(2)}, u32[]{:S(2)}) collective-permute-start(f32[136,256]{1,0:T(8,128)S(1)} %add_add_fusion.2), channel_id=1, source_target_pairs={{0,8},{2,10},{4,12},{6,14},{8,0},{10,2},{12,4},{14,6},{16,24},{18,... | collective-permute-start | bytes 417800 | tf_op jit(solution)/shard_map/ppermute | solution.py:600
  61.4 1.4 collective-permute-start.6
  62.8 1.1 collective-permute-start.7
  64.5 1.9 collective-permute-start.10
  66.4 0.9 collective-permute-start.11
  67.3 2.8 %collective-permute-done.5 = f32[136,256]{1,0:T(8,128)S(1)} collective-permute-done((f32[136,256]{1,0:T(8,128)S(1)}, f32[136,256]{1,0:T(8,128)S(1)}, u32[]{:S(2)}, u32[]{:S(2)}) %collective-permute-start.5) | collective-permute-done | bytes 139296 | tf_op jit(solution)/shard_map/ppermute | solution.py:600
  70.0 0.9 collective-permute-start.9
  71.0 17.9 %collective-permute-done.6 = f32[136,256]{1,0:T(8,128)S(1)} collective-permute-done((f32[136,256]{1,0:T(8,128)S(1)}, f32[136,256]{1,0:T(8,128)S(1)}, u32[]{:S(2)}, u32[]{:S(2)}) %collective-permute-start.6) | collective-permute-done | bytes 139296 | tf_op jit(solution)/shard_map/ppermute | solution.py:600
  88.9 0.7 slice.39
  89.6 1.3 broadcast_compare_fusion
  90.9 0.7 broadcast_in_dim.75
  91.5 0.8 select_reduce_fusion.1
  92.4 1.8 maximum_select_fusion.gram_ref
  94.2 1.5 collective-permute-done.9
  95.7 1.5 add_add_fusion
  97.2 0.8 constant_dynamic-slice_fusion
  97.9 2.8 %collective-permute-start.12 = (f32[128,256]{1,0:T(8,128)}, f32[128,256]{1,0:T(8,128)S(1)}, u32[]{:S(2)}, u32[]{:S(2)}) collective-permute-start(f32[128,256]{1,0:T(8,128)} %get-tuple-element.46), channel_id=1, source_target_pairs={{0,8},{2,10},{4,12},{6,14},{8,0},{10,2},{12,4},{14,6},{16,24},{18,... | collective-permute-start | bytes 393224 | tf_op jit(solution)/shard_map/ppermute | solution.py:600
  100.8 2.3 %collective-permute-start.13 = (f32[128,256]{1,0:T(8,128)}, f32[128,256]{1,0:T(8,128)S(1)}, u32[]{:S(2)}, u32[]{:S(2)}) collective-permute-start(f32[128,256]{1,0:T(8,128)} %get-tuple-element.47), channel_id=1, source_target_pairs={{0,16},{2,18},{4,20},{6,22},{8,24},{10,26},{12,28},{14,30},{16,0},... | collective-permute-start | bytes 393224 | tf_op jit(solution)/shard_map/ppermute | solution.py:600
  103.8 5.9 %all-to-all-start.1 = ((bf16[16,80,512]{2,1,0:T(8,128)(2,1)}), bf16[16,80,512]{2,1,0:T(8,128)(2,1)}, u32[]{:S(2)}, u32[]{:S(2)}) async-start(bf16[16,80,512]{2,1,0:T(8,128)(2,1)} %get-tuple-element.56), calls=%async_computation.1 | async-start | bytes 2621440 | tf_op jit(solution)/shard_map/all_to_all | solution.py:684
  109.7 24.0 %factor.1.inv_ref = f32[256,256]{1,0:T(8,128)} custom-call(f32[256,256]{1,0:T(8,128)} %maximum_select_fusion.gram_ref), custom_call_target="tpu_custom_call" | custom-call | flops 67108864 | bytes 524288 | tf_op jit(solution)/shard_map/factor/pallas_call | solution.py:203
  133.7 1.4 convolution_convert_fusion
  135.2 3.4 %select.64 = bf16[13,128,512]{2,1,0:T(8,128)(2,1)} custom-call(s32[13]{0:T(128)} %and_select_fusion.owner_ref, bf16[16,176,512]{2,1,0:T(8,128)(2,1)} %copy-done), custom_call_target="tpu_custom_call" | custom-call | bytes 3407872 | tf_op jit(solution)/shard_map/select/pallas_call | solution.py:147
  139.0 0.8 select_reduce_fusion.2
  139.7 1.9 collective-permute-start.15
  141.7 2.4 %collective-permute-start.16 = (bf16[128,256]{1,0:T(8,128)(2,1)S(1)}, bf16[128,256]{1,0:T(8,128)(2,1)S(1)}, u32[]{:S(2)}, u32[]{:S(2)}) collective-permute-start(bf16[128,256]{1,0:T(8,128)(2,1)S(1)} %convolution_convert_fusion), channel_id=1, source_target_pairs={{0,16},{2,18},{4,20},{6,22},{8,24},{10,26},{12,28},{14,30},{16,0},... | collective-permute-start | bytes 196616 | tf_op jit(solution)/shard_map/ppermute | solution.py:600
  144.2 0.7 select_reduce_fusion.w_ref
  144.9 4.5 %collective-permute-done.16 = bf16[128,256]{1,0:T(8,128)(2,1)S(1)} collective-permute-done((bf16[128,256]{1,0:T(8,128)(2,1)S(1)}, bf16[128,256]{1,0:T(8,128)(2,1)S(1)}, u32[]{:S(2)}, u32[]{:S(2)}) %collective-permute-start.16) | collective-permute-done | bytes 65568 | tf_op jit(solution)/shard_map/ppermute | solution.py:600
  149.4 0.8 collective-permute-done.17
  150.2 1.3 copy-done.10
  151.5 14.8 %kernel_rows.1 = (bf16[1664,2048]{1,0:T(8,128)(2,1)}, bf16[1664,256]{1,0:T(8,128)(2,1)}, f32[1,2048]{1,0:T(1,128)}, f32[1,256]{1,0:T(1,128)}) custom-call(f32[13]{0:T(128)} %select_reduce_fusion.w_ref, bf16[1664,512]{1,0:T(8,128)(2,1)} %bitcast.24, bf16[1664,512]{1,0:T(8,128)(2,1)} %copy-done.10, bf16[256,1024]{1,0:T(8,128)(2,1)} %get-tuple-element.53.refs_2_, ...), custom_call_target="tpu_custom_call" | custom-call | flops 7851737088 | bytes 14417920 | tf_op jit(solution)/shard_map/kernel_rows/pallas_call | solution.py:428
  166.3 2.9 %select.65 = bf16[6,128,512]{2,1,0:T(8,128)(2,1)} custom-call(s32[6]{0:T(128)} %get-tuple-element.55.owner_ref, bf16[16,176,512]{2,1,0:T(8,128)(2,1)} %copy-done, bf16[16,80,512]{2,1,0:T(8,128)(2,1)} %all-to-all-done.1.refs_1_), custom_call_target="tpu_custom_call" | custom-call | bytes 1572864 | tf_op jit(solution)/shard_map/select/pallas_call | solution.py:147
  169.9 0.8 select_reduce_fusion.3.w_ref
  170.7 1.5 collective-permute-start.20
  172.2 1.5 collective-permute-start.21
  174.2 0.9 copy-done.1
  175.1 8.3 %second_rows.1 = (bf16[1664,2048]{1,0:T(8,128)(2,1)}, bf16[1664,256]{1,0:T(8,128)(2,1)}) custom-call(s32[6]{0:T(128)} %get-tuple-element.71.place_ref, s32[1]{0:T(128)} %bitcast.5.num_ref, f32[6]{0:T(128)} %select_reduce_fusion.3.w_ref, bf16[768,512]{1,0:T(8,128)(2,1)} %bitcast.22, ...), custom_call_target="tpu_custom_call", output_to_operand_aliasing={{0}: (9, {}), {1}: (10, {})} | custom-call | flops 3623878656 | bytes 4194304 | tf_op jit(solution)/shard_map/second_rows/pallas_call | solution.py:516
  183.4 2.8 %collective-permute-done.21 = bf16[512,256]{1,0:T(8,128)(2,1)S(1)} collective-permute-done((bf16[512,256]{1,0:T(8,128)(2,1)S(1)}, bf16[512,256]{1,0:T(8,128)(2,1)S(1)}, u32[]{:S(2)}, u32[]{:S(2)}) %collective-permute-start.21) | collective-permute-done | bytes 262176 | tf_op jit(solution)/shard_map/ppermute | solution.py:600
  186.2 1.1 pad_maximum_fusion.rt_ref
  187.3 9.4 %remainder_rows.1 = (bf16[1664,2048]{1,0:T(8,128)(2,1)}, f32[256,2048]{1,0:T(8,128)}) custom-call(s32[1]{0:T(128)} %bitcast.quarter_ref, bf16[1664,2048]{1,0:T(8,128)(2,1)} %get-tuple-element.62.kern_ref, bf16[1664,256]{1,0:T(8,128)(2,1)} %get-tuple-element.63.p_ref, f32[256,256]{1,0:T(8,128)} %factor.1.inv_ref, bf16[4,512,256]{2,1,0:T(8,128)(2,1)} %pad_maximum_fusion.rt_ref), custom_call_target="tpu_custom_call" | custom-call | flops 1744830464 | bytes 13631488 | tf_op jit(solution)/shard_map/remainder_rows/pallas_call | solution.py:576
  (80 shorter events, 6.1 us)
Async XLA Ops:
  0.6 16.1 %collective-permute-start = (bf16[3200,512]{1,0:T(8,128)(2,1)}, bf16[3200,512]{1,0:T(8,128)(2,1)}, u32[]{:S(2)}, u32[]{:S(2)}) collective-permute-start(bf16[3200,512]{1,0:T(8,128)(2,1)} %refs_0_.3), channel_id=1, source_target_pairs={{0,1},{1,0},{2,3},{3,2},{4,5},{5,4},{6,7},{7,6},{8,9},{9,8},{10,11... | collective-permute-start | bytes 9830408 | tf_op jit(solution)/shard_map/ppermute | solution.py:216
  5.3 9.5 %copy-start.3 = (s32[16,25]{1,0:T(8,128)S(1)}, s32[16,25]{1,0:T(8,128)}, u32[]{:S(2)}) copy-start(s32[16,25]{1,0:T(8,128)} %dest_ref.1) | copy-start | bytes 4804
  5.3 9.5 %copy-start.6 = (s32[16]{0:T(128)S(1)}, s32[16]{0:T(128)}, u32[]{:S(2)}) copy-start(s32[16]{0:T(128)} %cnt_ref.3) | copy-start | bytes 196
  5.3 9.9 %copy-start.11 = (bf16[25]{0:T(256)(128)(2,1)S(1)}, bf16[25]{0:T(256)(128)(2,1)}, u32[]{:S(2)}) copy-start(bf16[25]{0:T(256)(128)(2,1)} %param.7) | copy-start | bytes 154
  5.4 92.6 %all-to-all-start = ((bf16[16,176,512]{2,1,0:T(8,128)(2,1)}), bf16[16,176,512]{2,1,0:T(8,128)(2,1)S(1)}, u32[]{:S(2)}, u32[]{:S(2)}) async-start(bf16[16,176,512]{2,1,0:T(8,128)(2,1)} %get-tuple-element.40), calls=%async_computation | async-start | bytes 5767168 | tf_op jit(solution)/shard_map/all_to_all | solution.py:649
  14.6 2.1 %collective-permute-start.1 = (bf16[256,1024]{1,0:T(8,128)(2,1)}, bf16[256,1024]{1,0:T(8,128)(2,1)S(1)}, u32[]{:S(2)}, u32[]{:S(2)}) collective-permute-start(bf16[256,1024]{1,0:T(8,128)(2,1)} %slice.33), channel_id=1, source_target_pairs={{0,1},{1,0},{2,3},{3,2},{4,5},{5,4},{6,7},{7,6},{8,9},{9,8},{10,11... | collective-permute-start | bytes 1572872 | tf_op jit(solution)/shard_map/ppermute | solution.py:644
  15.0 48.8 %copy-start.4 = (s32[400]{0:T(512)}, s32[400]{0:T(512)S(1)}, u32[]{:S(2)}) copy-start(s32[400]{0:T(512)S(1)} %broadcast_in_dim_reshape.4) | copy-start | bytes 4804
  16.8 0.8 copy-start.2
  28.3 31.0 %collective-permute-start.2 = (f32[136,256]{1,0:T(8,128)S(1)}, f32[136,256]{1,0:T(8,128)S(1)}, u32[]{:S(2)}, u32[]{:S(2)}) collective-permute-start(f32[136,256]{1,0:T(8,128)S(1)} %pad_maximum_fusion.2), channel_id=1, source_target_pairs={{0,2},{2,0},{4,6},{6,4},{8,10},{10,8},{12,14},{14,12},{16,18},{18,... | collective-permute-start | bytes 417800 | tf_op jit(solution)/shard_map/ppermute | solution.py:600
  28.4 30.9 %collective-permute-start.3 = (f32[136,256]{1,0:T(8,128)S(1)}, f32[136,256]{1,0:T(8,128)S(1)}, u32[]{:S(2)}, u32[]{:S(2)}) collective-permute-start(f32[136,256]{1,0:T(8,128)S(1)} %pad_maximum_fusion.2), channel_id=1, source_target_pairs={{0,4},{2,6},{4,0},{6,2},{8,12},{10,14},{12,8},{14,10},{16,20},{18,... | collective-permute-start | bytes 417800 | tf_op jit(solution)/shard_map/ppermute | solution.py:600
  31.8 27.6 %collective-permute-start.4 = (f32[136,256]{1,0:T(8,128)S(1)}, f32[136,256]{1,0:T(8,128)S(1)}, u32[]{:S(2)}, u32[]{:S(2)}) collective-permute-start(f32[136,256]{1,0:T(8,128)S(1)} %pad_maximum_fusion.2), channel_id=1, source_target_pairs={{0,6},{2,4},{4,2},{6,0},{8,14},{10,12},{12,10},{14,8},{16,22},{18,... | collective-permute-start | bytes 417800 | tf_op jit(solution)/shard_map/ppermute | solution.py:600
  59.4 10.6 %collective-permute-start.5 = (f32[136,256]{1,0:T(8,128)S(1)}, f32[136,256]{1,0:T(8,128)S(1)}, u32[]{:S(2)}, u32[]{:S(2)}) collective-permute-start(f32[136,256]{1,0:T(8,128)S(1)} %add_add_fusion.2), channel_id=1, source_target_pairs={{0,8},{2,10},{4,12},{6,14},{8,0},{10,2},{12,4},{14,6},{16,24},{18,... | collective-permute-start | bytes 417800 | tf_op jit(solution)/shard_map/ppermute | solution.py:600
  61.4 27.5 %collective-permute-start.6 = (f32[136,256]{1,0:T(8,128)S(1)}, f32[136,256]{1,0:T(8,128)S(1)}, u32[]{:S(2)}, u32[]{:S(2)}) collective-permute-start(f32[136,256]{1,0:T(8,128)S(1)} %add_add_fusion.2), channel_id=1, source_target_pairs={{0,16},{2,18},{4,20},{6,22},{8,24},{10,26},{12,28},{14,30},{16,0},... | collective-permute-start | bytes 417800 | tf_op jit(solution)/shard_map/ppermute | solution.py:600
  62.8 26.1 %collective-permute-start.7 = (f32[136,256]{1,0:T(8,128)S(1)}, f32[136,256]{1,0:T(8,128)S(1)}, u32[]{:S(2)}, u32[]{:S(2)}) collective-permute-start(f32[136,256]{1,0:T(8,128)S(1)} %add_add_fusion.2), channel_id=1, source_target_pairs={{0,24},{2,26},{4,28},{6,30},{8,16},{10,18},{12,20},{14,22},{16,8},... | collective-permute-start | bytes 417800 | tf_op jit(solution)/shard_map/ppermute | solution.py:600
  64.5 29.7 %collective-permute-start.10 = (f32[512,256]{1,0:T(8,128)}, f32[512,256]{1,0:T(8,128)}, u32[]{:S(2)}, u32[]{:S(2)}) collective-permute-start(f32[512,256]{1,0:T(8,128)} %get-tuple-element.43), channel_id=1, source_target_pairs={{0,4},{2,6},{4,0},{6,2},{8,12},{10,14},{12,8},{14,10},{16,20},{18,... | collective-permute-start | bytes 1572872 | tf_op jit(solution)/shard_map/ppermute | solution.py:600
  66.4 27.8 %collective-permute-start.11 = (f32[512,256]{1,0:T(8,128)}, f32[512,256]{1,0:T(8,128)}, u32[]{:S(2)}, u32[]{:S(2)}) collective-permute-start(f32[512,256]{1,0:T(8,128)} %get-tuple-element.44), channel_id=1, source_target_pairs={{0,6},{2,4},{4,2},{6,0},{8,14},{10,12},{12,10},{14,8},{16,22},{18,... | collective-permute-start | bytes 1572872 | tf_op jit(solution)/shard_map/ppermute | solution.py:600
  70.0 25.6 %collective-permute-start.9 = (f32[512,256]{1,0:T(8,128)}, f32[512,256]{1,0:T(8,128)}, u32[]{:S(2)}, u32[]{:S(2)}) collective-permute-start(f32[512,256]{1,0:T(8,128)} %get-tuple-element.42), channel_id=1, source_target_pairs={{0,2},{2,0},{4,6},{6,4},{8,10},{10,8},{12,14},{14,12},{16,18},{18,... | collective-permute-start | bytes 1572872 | tf_op jit(solution)/shard_map/ppermute | solution.py:600
  89.6 2.7 %collective-permute-start.8 = (f32[128,256]{1,0:T(8,128)}, f32[128,256]{1,0:T(8,128)}, u32[]{:S(2)}, u32[]{:S(2)}) collective-permute-start(f32[128,256]{1,0:T(8,128)} %slice.39), channel_id=1, source_target_pairs={{0,1},{1,0},{2,3},{3,2},{4,5},{5,4},{6,7},{7,6},{8,9},{9,8},{10,11... | collective-permute-start | bytes 393224 | tf_op jit(solution)/shard_map/ppermute | solution.py:670
  97.9 37.2 %copy-start = (bf16[16,176,512]{2,1,0:T(8,128)(2,1)}, bf16[16,176,512]{2,1,0:T(8,128)(2,1)S(1)}, u32[]{:S(2)}) copy-start(bf16[16,176,512]{2,1,0:T(8,128)(2,1)S(1)} %all-to-all-done.refs_0_) | copy-start | bytes 8650756
  97.9 35.8 %collective-permute-start.12 = (f32[128,256]{1,0:T(8,128)}, f32[128,256]{1,0:T(8,128)S(1)}, u32[]{:S(2)}, u32[]{:S(2)}) collective-permute-start(f32[128,256]{1,0:T(8,128)} %get-tuple-element.46), channel_id=1, source_target_pairs={{0,8},{2,10},{4,12},{6,14},{8,0},{10,2},{12,4},{14,6},{16,24},{18,... | collective-permute-start | bytes 393224 | tf_op jit(solution)/shard_map/ppermute | solution.py:600
  100.8 33.0 %collective-permute-start.13 = (f32[128,256]{1,0:T(8,128)}, f32[128,256]{1,0:T(8,128)S(1)}, u32[]{:S(2)}, u32[]{:S(2)}) collective-permute-start(f32[128,256]{1,0:T(8,128)} %get-tuple-element.47), channel_id=1, source_target_pairs={{0,16},{2,18},{4,20},{6,22},{8,24},{10,26},{12,28},{14,30},{16,0},... | collective-permute-start | bytes 393224 | tf_op jit(solution)/shard_map/ppermute | solution.py:600
  103.1 30.6 %collective-permute-start.14 = (f32[128,256]{1,0:T(8,128)}, f32[128,256]{1,0:T(8,128)}, u32[]{:S(2)}, u32[]{:S(2)}) collective-permute-start(f32[128,256]{1,0:T(8,128)} %get-tuple-element.48), channel_id=1, source_target_pairs={{0,24},{2,26},{4,28},{6,30},{8,16},{10,18},{12,20},{14,22},{16,8},... | collective-permute-start | bytes 393224 | tf_op jit(solution)/shard_map/ppermute | solution.py:600
  103.8 62.5 %all-to-all-start.1 = ((bf16[16,80,512]{2,1,0:T(8,128)(2,1)}), bf16[16,80,512]{2,1,0:T(8,128)(2,1)}, u32[]{:S(2)}, u32[]{:S(2)}) async-start(bf16[16,80,512]{2,1,0:T(8,128)(2,1)} %get-tuple-element.56), calls=%async_computation.1 | async-start | bytes 2621440 | tf_op jit(solution)/shard_map/all_to_all | solution.py:684
  109.7 29.3 %copy-start.8 = (s32[13]{0:T(128)S(1)}, s32[13]{0:T(128)}, u32[]{:S(2)}) copy-start(s32[13]{0:T(128)} %and_select_fusion.owner_ref) | copy-start | bytes 160
  133.7 10.5 %copy-start.5 = (s32[400]{0:T(512)S(1)}, s32[400]{0:T(512)}, u32[]{:S(2)}) copy-start(s32[400]{0:T(512)} %slice_subtract_fusion) | copy-start | bytes 4804
  133.7 10.5 %copy-start.7 = (pred[400]{0:T(512)(128)(4,1)S(1)}, pred[400]{0:T(512)(128)(4,1)}, u32[]{:S(2)}) copy-start(pred[400]{0:T(512)(128)(4,1)} %broadcast_compare_fusion) | copy-start | bytes 1204
  138.6 11.6 %collective-permute-start.18 = (bf16[1664,512]{1,0:T(8,128)(2,1)}, bf16[1664,512]{1,0:T(8,128)(2,1)S(1)}, u32[]{:S(2)}, u32[]{:S(2)}) collective-permute-start(bf16[1664,512]{1,0:T(8,128)(2,1)} %bitcast.23), channel_id=1, source_target_pairs={{0,1},{1,0},{2,3},{3,2},{4,5},{5,4},{6,7},{7,6},{8,9},{9,8},{10,11... | collective-permute-start | bytes 5111816 | tf_op jit(solution)/shard_map/ppermute | solution.py:216
  139.7 5.2 %collective-permute-start.15 = (bf16[128,256]{1,0:T(8,128)(2,1)S(1)}, bf16[128,256]{1,0:T(8,128)(2,1)S(1)}, u32[]{:S(2)}, u32[]{:S(2)}) collective-permute-start(bf16[128,256]{1,0:T(8,128)(2,1)S(1)} %convolution_convert_fusion), channel_id=1, source_target_pairs={{0,8},{2,10},{4,12},{6,14},{8,0},{10,2},{12,4},{14,6},{16,24},{18,... | collective-permute-start | bytes 196616 | tf_op jit(solution)/shard_map/ppermute | solution.py:600
  141.7 7.7 %collective-permute-start.16 = (bf16[128,256]{1,0:T(8,128)(2,1)S(1)}, bf16[128,256]{1,0:T(8,128)(2,1)S(1)}, u32[]{:S(2)}, u32[]{:S(2)}) collective-permute-start(bf16[128,256]{1,0:T(8,128)(2,1)S(1)} %convolution_convert_fusion), channel_id=1, source_target_pairs={{0,16},{2,18},{4,20},{6,22},{8,24},{10,26},{12,28},{14,30},{16,0},... | collective-permute-start | bytes 196616 | tf_op jit(solution)/shard_map/ppermute | solution.py:600
  144.0 6.1 %collective-permute-start.17 = (bf16[128,256]{1,0:T(8,128)(2,1)S(1)}, bf16[128,256]{1,0:T(8,128)(2,1)S(1)}, u32[]{:S(2)}, u32[]{:S(2)}) collective-permute-start(bf16[128,256]{1,0:T(8,128)(2,1)S(1)} %convolution_convert_fusion), channel_id=1, source_target_pairs={{0,24},{2,26},{4,28},{6,30},{8,16},{10,18},{12,20},{14,22},{16,8},... | collective-permute-start | bytes 196616 | tf_op jit(solution)/shard_map/ppermute | solution.py:600
  150.2 1.3 copy-start.10
  166.3 3.6 %copy-start.9 = (f32[13]{0:T(128)S(1)}, f32[13]{0:T(128)}, u32[]{:S(2)}) copy-start(f32[13]{0:T(128)} %select_reduce_fusion.w_ref) | copy-start | bytes 160
  169.2 5.0 %collective-permute-start.19 = (bf16[768,512]{1,0:T(8,128)(2,1)}, bf16[768,512]{1,0:T(8,128)(2,1)S(1)}, u32[]{:S(2)}, u32[]{:S(2)}) collective-permute-start(bf16[768,512]{1,0:T(8,128)(2,1)} %bitcast.21), channel_id=1, source_target_pairs={{0,1},{1,0},{2,3},{3,2},{4,5},{5,4},{6,7},{7,6},{8,9},{9,8},{10,11... | collective-permute-start | bytes 2359304 | tf_op jit(solution)/shard_map/ppermute | solution.py:216
  170.7 12.7 %collective-permute-start.20 = (bf16[512,256]{1,0:T(8,128)(2,1)S(1)}, bf16[512,256]{1,0:T(8,128)(2,1)S(1)}, u32[]{:S(2)}, u32[]{:S(2)}) collective-permute-start(bf16[512,256]{1,0:T(8,128)(2,1)S(1)} %pad_maximum_fusion.1), channel_id=1, source_target_pairs={{0,2},{2,0},{4,6},{6,4},{8,10},{10,8},{12,14},{14,12},{16,18},{18,... | collective-permute-start | bytes 786440 | tf_op jit(solution)/shard_map/ppermute | solution.py:600
  172.2 14.0 %collective-permute-start.21 = (bf16[512,256]{1,0:T(8,128)(2,1)S(1)}, bf16[512,256]{1,0:T(8,128)(2,1)S(1)}, u32[]{:S(2)}, u32[]{:S(2)}) collective-permute-start(bf16[512,256]{1,0:T(8,128)(2,1)S(1)} %pad_maximum_fusion.1), channel_id=1, source_target_pairs={{0,4},{2,6},{4,0},{6,2},{8,12},{10,14},{12,8},{14,10},{16,20},{18,... | collective-permute-start | bytes 786440 | tf_op jit(solution)/shard_map/ppermute | solution.py:600
  173.6 12.6 %collective-permute-start.22 = (bf16[512,256]{1,0:T(8,128)(2,1)S(1)}, bf16[512,256]{1,0:T(8,128)(2,1)S(1)}, u32[]{:S(2)}, u32[]{:S(2)}) collective-permute-start(bf16[512,256]{1,0:T(8,128)(2,1)S(1)} %pad_maximum_fusion.1), channel_id=1, source_target_pairs={{0,6},{2,4},{4,2},{6,0},{8,14},{10,12},{12,10},{14,8},{16,22},{18,... | collective-permute-start | bytes 786440 | tf_op jit(solution)/shard_map/ppermute | solution.py:600
  174.2 0.9 copy-start.1

commit v8 on v7

--- a/solution.py
+++ b/solution.py
@@ -50,30 +50,15 @@
     return high, (x - high.astype(jnp.float32)).astype(jnp.bfloat16)
 
 
-HEAD = 48
-
-
-def block_copies(rank, whole_ref, outer, first_ref, last_ref, sems):
-    if rank == 0:
-        pairs = [(whole_ref, first_ref.at[outer, pl.ds(0, BLK)])]
-    else:
-        pairs = [
-            (whole_ref.at[pl.ds(0, HEAD)], first_ref.at[outer, pl.ds(BLK, HEAD)]),
-            (whole_ref.at[pl.ds(HEAD, BLK - HEAD)], last_ref.at[outer]),
-        ]
-    return [(a, b, sems.at[i]) for i, (a, b) in enumerate(pairs)]
-
-
 def pack_kernel(per_pair, dest_ref, cnt_ref, desc_ref, *refs):
-    out_refs, (ctr_ref, rank_ref, sems) = refs[:per_pair], refs[per_pair:]
+    out_refs, (ctr_ref, sems) = refs[:per_pair], refs[per_pair:]
     slots = desc_ref.shape[0]
     owners = ctr_ref.shape[0]
     me = lax.axis_index("rows")
     count = cnt_ref[me]
 
-    def copies(j, d, rank):
-        moves = block_copies(rank, desc_ref.at[j], d, out_refs[0], out_refs[-1], sems.at[j])
-        return [pltpu.make_async_copy(a, b, sem) for a, b, sem in moves]
+    def copy(j, d, rank):
+        return pltpu.make_async_copy(desc_ref.at[j], out_refs[rank].at[d], sems.at[j])
 
     @pl.loop(0, owners)
     def _(i):
@@ -86,39 +71,29 @@
             d = dest_ref[me, j]
             rank = ctr_ref[d]
             ctr_ref[d] = rank + 1
-            rank_ref[j] = rank
             for r in range(per_pair):
                 @pl.when(rank == r)
                 def _():
-                    for c in copies(j, d, r):
-                        c.start()
+                    copy(j, d, r).start()
 
     @pl.loop(0, slots)
     def _(j):
         @pl.when(j < count)
         def _():
-            for r in range(per_pair):
-                @pl.when(rank_ref[j] == r)
-                def _():
-                    for c in copies(j, 0, r):
-                        c.wait()
+            pltpu.make_async_copy(desc_ref.at[0], out_refs[0].at[0], sems.at[j]).wait()
 
 
 def pack(desc_blocks, destinations, counts, per_pair):
     slots, blk, feat = desc_blocks.shape
     owners = destinations.shape[0]
-    heights = [blk] if per_pair == 1 else [blk + HEAD, blk - HEAD]
     return pl.pallas_call(
         functools.partial(pack_kernel, per_pair),
-        out_shape=[
-            jax.ShapeDtypeStruct((owners, h, feat), desc_blocks.dtype) for h in heights
-        ],
+        out_shape=[jax.ShapeDtypeStruct((owners, blk, feat), desc_blocks.dtype)] * per_pair,
         in_specs=[SMEM, SMEM, VMEM],
         out_specs=[ANY] * per_pair,
         scratch_shapes=[
             pltpu.SMEM((owners,), jnp.int32),
-            pltpu.SMEM((slots,), jnp.int32),
-            pltpu.SemaphoreType.DMA((slots, 2)),
+            pltpu.SemaphoreType.DMA((slots,)),
         ],
         compiler_params=params(),
         cost_estimate=cost(0, 4 * slots * blk * feat),
@@ -126,34 +101,30 @@
     )(destinations, counts, desc_blocks)
 
 
-def select_kernel(rows, owner_ref, *refs):
-    recv_refs, (out_ref, sems) = refs[: len(rows)], refs[len(rows) :]
-    copies = []
-    for p in range(out_ref.shape[0]):
-        at = 0
-        for i, (start, size) in enumerate(rows):
-            src = recv_refs[i].at[owner_ref[p], pl.ds(start, size)]
-            copies.append(pltpu.make_async_copy(src, out_ref.at[p, pl.ds(at, size)], sems.at[p, i]))
-            at += size
+def select_kernel(owner_ref, recv_ref, out_ref, sems):
+    copies = [
+        pltpu.make_async_copy(recv_ref.at[owner_ref[p]], out_ref.at[p], sems.at[p])
+        for p in range(out_ref.shape[0])
+    ]
     for c in copies:
         c.start()
     for c in copies:
         c.wait()
 
 
-def select(received, rows, from_owner):
-    feat = received[0].shape[-1]
+def select(received, from_owner):
+    feat = received.shape[-1]
     count = from_owner.shape[0]
     return pl.pallas_call(
-        functools.partial(select_kernel, rows),
-        out_shape=jax.ShapeDtypeStruct((count, BLK, feat), received[0].dtype),
-        in_specs=[SMEM] + [ANY] * len(rows),
+        select_kernel,
+        out_shape=jax.ShapeDtypeStruct((count, BLK, feat), received.dtype),
+        in_specs=[SMEM, ANY],
         out_specs=VMEM,
-        scratch_shapes=[pltpu.SemaphoreType.DMA((count, len(rows)))],
+        scratch_shapes=[pltpu.SemaphoreType.DMA((count,))],
         compiler_params=params(),
         cost_estimate=cost(0, 4 * count * BLK * feat),
         name="select",
-    )(from_owner, *received)
+    )(from_owner, received)
 
 
 def small_factor(a):
@@ -606,8 +577,11 @@
     return [lax.dynamic_slice_in_dim(x, (q ^ k) * n, n, 0) for k in range(4)]
 
 
-def quarter_sum(pieces, pair):
-    got = [pieces[0]] + [trade(pieces[k], pair, k) for k in range(1, 4)]
+def trades(pieces, pair):
+    return [pieces[0]] + [trade(pieces[k], pair, k) for k in range(1, 4)]
+
+
+def total(got):
     return (got[0] + got[1]) + (got[2] + got[3])
 
 
@@ -662,9 +636,15 @@
         gram_part = lax.dynamic_slice_in_dim(gram_part, group * (PANEL // 2), PANEL // 2, 0)
     summed = pair_sum(jnp.concatenate([gram_part, table], 0), pairs[0])
     summed, *sent = lax.optimization_barrier((summed, *sent))
-    g = quarter_sum(sent, pairs[0])
+    near = trades(sent, pairs[0])
     for pair in pairs[1:]:
-        summed = pair_sum(summed, pair)
+        got = gather_pieces(summed, pair)
+        if per_pair > 1 and pair == pairs[-1]:
+            got, last, received[0] = lax.optimization_barrier((got, outgoing[1], received[0]))
+            received.append(
+                lax.all_to_all(last, "rows", split_axis=0, concat_axis=0, tiled=True)
+            )
+        summed = total(got)
     gram, table = summed[:-spare], summed[-spare:]
     if groups == 2:
         other = lax.ppermute(gram, "cols", [(0, 1), (1, 0)])
@@ -673,17 +653,7 @@
         )
     all_weights = table.reshape(-1)[: owners * slots]
 
-    for pair in pairs[1:]:
-        sent = quarters(g, pair)
-        if per_pair > 1 and pair == pairs[-1]:
-            gram, last, received[0], *sent = lax.optimization_barrier(
-                (gram, outgoing[1], received[0], *sent)
-            )
-        g = quarter_sum(sent, pair)
-    if per_pair > 1:
-        received.append(lax.all_to_all(last, "rows", split_axis=0, concat_axis=0, tiled=True))
     inverse = factor(gram)
-    rt = nt(g, inverse, HIGH).astype(jnp.bfloat16)
 
     slot_ids = jnp.arange(slots, dtype=jnp.int32)
     toward = ((slot_ids[None, :] < block_counts[:, None]) & (destinations == me)).astype(jnp.int32)
@@ -703,20 +673,30 @@
     second_owner = jnp.sum(jnp.where(pick, from_owner[None, :], 0), axis=1)
     second_weights = jnp.sum(jnp.where(pick, weights_here[None, :], 0.0), axis=1)
 
-    rt, from_owner = lax.optimization_barrier((rt, from_owner))
-    arrived = select(received[:1], [(0, BLK)], from_owner).reshape(DST_BLK * BLK, feat)
+    inverse, *near = lax.optimization_barrier((inverse, *near))
+    g = total(near)
+    for pair in pairs[1:]:
+        sent = quarters(g, pair)
+        if pair == pairs[-1]:
+            from_owner, *sent = lax.optimization_barrier((from_owner, *sent))
+        far = trades(sent, pair)
+        g = total(far)
+    arrived = select(received[0], from_owner).reshape(DST_BLK * BLK, feat)
     kern, panel, cs, csp = kernel_rows(
         share_parts(arrived), weights_here, panel_points, sparse_points
     )
+    kern, *far = lax.optimization_barrier((kern, *far))
+    rt = nt(total(far), inverse, HIGH).astype(jnp.bfloat16)
+    if per_pair > 1:
+        rt, second_owner = lax.optimization_barrier((rt, second_owner))
+        late = share_parts(select(received[1], second_owner).reshape(most * BLK, feat))
     for pair in pairs[:0:-1]:
         rt = gather_back(rt, pair)
+    rt, kern = lax.optimization_barrier((rt, kern))
     pieces = gather_pieces(rt, pairs[0])
     if per_pair > 1:
-        rt, kern, second_owner = lax.optimization_barrier((rt, kern, second_owner))
-        late = select(received, [(BLK, HEAD), (0, BLK - HEAD)], second_owner)
-        late = late.reshape(most * BLK, feat)
         kern, panel = second_rows(
-            share_parts(late),
+            late,
             places,
             order[-1:],
             second_weights,

time: 198 us -> 195 us (0.985)
  waiting for transfers between devices: 30.4 us -> 36.4 us
  other arithmetic: 11.7 us -> 7.58 us
  local copies, waits for them, and re-layouts: 11.6 us -> 9.45 us
    ppermute x18, waiting for transfers between devices: 30.2 us -> 35.5 us  [trade(): return lax.ppermute(x, 'rows', flips(bit, lax.axis_size('rows')))]
  transfers between devices with their start and end apart: 25 -> 25, of which waited for: 7 -> 8; matrix products, arithmetic and copies ran while one was open for 10% -> 7% of each run, Pallas kernels for 45% -> 46%
where the time goes in v8:
time: 195 us; the launch traced here: 194 us
  Pallas kernels  101 us (52%)
  starting transfers between devices  37.9 us (19%)
  waiting for transfers between devices  36.4 us (19%)
  local copies, waits for them, and re-layouts  9.45 us (5%)
  other arithmetic  7.58 us (4%)
    ppermute x18, waiting for transfers between devices, trade(): return lax.ppermute(x, 'rows', flips(bit, lax.axis_size('rows')))  35.5 us
    pallas_call x1, Pallas kernels, column_products(): pl.pallas_call(functools.partial(column_kernel, len(parts)), grid=(size /...  24.8 us
    ppermute x18, starting transfers between devices, trade(): return lax.ppermute(x, 'rows', flips(bit, lax.axis_size('rows')))  24.6 us
    pallas_call x1, Pallas kernels, factor(): pl.pallas_call(functools.partial(factor_kernel, 64), out_shape=jax.ShapeD...  24 us
    pallas_call x1, Pallas kernels, kernel_rows(): pl.pallas_call(functools.partial(rows_kernel, len(parts)), grid=(cols //...  14.8 us
    pallas_call x1, Pallas kernels, panel_products(): pl.pallas_call(functools.partial(panel_kernel, len(parts)), out_shape=(ja...  9.93 us
    pallas_call x1, Pallas kernels, remainder_rows(): pl.pallas_call(functools.partial(remainder_kernel, norm), grid_spec=spec,...  9.43 us
    pallas_call x1, Pallas kernels, second_rows(): pl.pallas_call(functools.partial(seconds_kernel, n), out_shape=(jax.Shape...  8.03 us
  transfers between devices with their start and end apart: 25, of which 8 were waited for; matrix products, arithmetic and copies ran while one was open for 7% of the time, Pallas kernels for 46%

profile of v8, /device:TPU:0, one launch (start us, length us, event | category | flops | bytes accessed | tf_op | source)
XLA Modules:
  0.0 194.0 jit_solution(8976013066571672938)
XLA Ops:
  0.6 0.5 collective-permute-start
  1.1 4.0 %pack.1 = (bf16[16,128,512]{2,1,0:T(8,128)(2,1)}, bf16[16,128,512]{2,1,0:T(8,128)(2,1)}) custom-call(s32[16,25]{1,0:T(8,128)} %dest_ref.1, s32[16]{0:T(128)} %cnt_ref.3, bf16[25,128,512]{2,1,0:T(8,128)(2,1)} %bitcast.20), custom_call_target="tpu_custom_call" | custom-call | bytes 6553600 | tf_op jit(solution)/shard_map/pack/pallas_call | solution.py:89
  5.1 7.0 %all-to-all-start = ((bf16[16,128,512]{2,1,0:T(8,128)(2,1)}), bf16[16,128,512]{2,1,0:T(8,128)(2,1)S(1)}, u32[]{:S(2)}, u32[]{:S(2)}) async-start(bf16[16,128,512]{2,1,0:T(8,128)(2,1)} %get-tuple-element.54), calls=%async_computation | async-start | bytes 4194304 | tf_op jit(solution)/shard_map/all_to_all | solution.py:623
  12.2 1.1 slice.33
  13.9 0.6 convert_element_type.21.w_ref
  15.4 0.8 copy-done.3
  16.2 9.9 %panel_products.1 = (f32[256,256]{1,0:T(8,128)}, bf16[3200,256]{1,0:T(8,128)(2,1)}, bf16[256,1024]{1,0:T(8,128)(2,1)}) custom-call(s32[16]{0:T(128)} %cnt_ref.3, f32[25]{0:T(128)} %convert_element_type.21.w_ref, bf16[3200,512]{1,0:T(8,128)(2,1)} %refs_0_.3, bf16[3200,512]{1,0:T(8,128)(2,1)} %collective-permute-done.refs_1_, bf16[2048,1024]{1,0:T(8,128)(2,1)} %refs_4_.1, ...), custom_call_target="tpu_custom_call" | custom-call | flops 2097152000 | bytes 6553600 | tf_op jit(solution)/shard_map/panel_products/pallas_call | solution.py:290
  26.1 0.9 constant_dynamic-slice_fusion.8
  27.1 3.3 %collective-permute-start.3 = (f32[136,256]{1,0:T(8,128)S(1)}, f32[136,256]{1,0:T(8,128)S(1)}, u32[]{:S(2)}, u32[]{:S(2)}) collective-permute-start(f32[136,256]{1,0:T(8,128)S(1)} %pad_maximum_fusion.2), channel_id=1, source_target_pairs={{0,4},{2,6},{4,0},{6,2},{8,12},{10,14},{12,8},{14,10},{16,20},{18,... | collective-permute-start | bytes 417800 | tf_op jit(solution)/shard_map/ppermute | solution.py:571
  30.6 24.8 %column_products.1 = f32[2048,256]{1,0:T(8,128)} custom-call(bf16[3200,512]{1,0:T(8,128)(2,1)} %refs_0_.3, bf16[3200,512]{1,0:T(8,128)(2,1)} %collective-permute-done.refs_1_, bf16[3200,256]{1,0:T(8,128)(2,1)} %get-tuple-element.51.refs_2_, bf16[2048,1024]{1,0:T(8,128)(2,1)} %refs_4_.1), custom_call_target="tpu_custom_call" | custom-call | flops 16777216000 | bytes 6553600 | tf_op jit(solution)/shard_map/column_products/pallas_call | solution.py:339
  55.4 2.7 %constant_dynamic-slice_fusion.4 = (f32[512,256]{1,0:T(8,128)}, f32[512,256]{1,0:T(8,128)}, f32[512,256]{1,0:T(8,128)S(1)}, f32[512,256]{1,0:T(8,128)S(1)}) fusion(f32[2048,256]{1,0:T(8,128)} %column_products.1, s32[]{:T(128)S(6)} %select_n.247, s32[]{:T(128)S(6)} %select_n.246, s32[]{:T(128)S(6)} %select_n.245, s32[]{:T(128)S(6)} %select_n.244), kind=kLoop, calls=%fused_computation.32 | loop fusion | bytes 4194320 | tf_op jit(solution)/shard_map/dynamic_slice | solution.py:577
  58.1 1.4 collective-permute-start.5
  59.5 2.9 %collective-permute-start.6 = (f32[136,256]{1,0:T(8,128)S(1)}, f32[136,256]{1,0:T(8,128)S(1)}, u32[]{:S(2)}, u32[]{:S(2)}) collective-permute-start(f32[136,256]{1,0:T(8,128)S(1)} %add_add_fusion.2), channel_id=1, source_target_pairs={{0,16},{2,18},{4,20},{6,22},{8,24},{10,26},{12,28},{14,30},{16,0},... | collective-permute-start | bytes 417800 | tf_op jit(solution)/shard_map/ppermute | solution.py:571
  62.6 3.0 %collective-permute-done.5 = f32[136,256]{1,0:T(8,128)S(1)} collective-permute-done((f32[136,256]{1,0:T(8,128)S(1)}, f32[136,256]{1,0:T(8,128)S(1)}, u32[]{:S(2)}, u32[]{:S(2)}) %collective-permute-start.5) | collective-permute-done | bytes 139296 | tf_op jit(solution)/shard_map/ppermute | solution.py:571
  65.6 7.3 %collective-permute-done.6 = f32[136,256]{1,0:T(8,128)S(1)} collective-permute-done((f32[136,256]{1,0:T(8,128)S(1)}, f32[136,256]{1,0:T(8,128)S(1)}, u32[]{:S(2)}, u32[]{:S(2)}) %collective-permute-start.6) | collective-permute-done | bytes 139296 | tf_op jit(solution)/shard_map/ppermute | solution.py:571
  73.0 0.7 copy-done.4
  73.6 1.3 copy-done
  75.0 5.2 %all-to-all-start.1 = ((bf16[16,128,512]{2,1,0:T(8,128)(2,1)}), bf16[16,128,512]{2,1,0:T(8,128)(2,1)}, u32[]{:S(2)}, u32[]{:S(2)}) async-start(bf16[16,128,512]{2,1,0:T(8,128)(2,1)} %get-tuple-element.81), calls=%async_computation.1 | async-start | bytes 4194304 | tf_op jit(solution)/shard_map/all_to_all | solution.py:645
  80.3 1.9 collective-permute-start.10
  82.2 1.5 collective-permute-start.11
  83.9 1.0 add_add_fusion.1
  85.0 0.5 and_select_fusion.owner_ref
  85.5 0.8 collective-permute-done.8
  86.3 0.7 maximum_select_fusion.gram_ref
  87.0 24.0 %factor.1.inv_ref = f32[256,256]{1,0:T(8,128)} custom-call(f32[256,256]{1,0:T(8,128)} %maximum_select_fusion.gram_ref), custom_call_target="tpu_custom_call" | custom-call | flops 67108864 | bytes 524288 | tf_op jit(solution)/shard_map/factor/pallas_call | solution.py:174
  111.0 15.4 %collective-permute-done.10 = f32[512,256]{1,0:T(8,128)S(1)} collective-permute-done((f32[512,256]{1,0:T(8,128)}, f32[512,256]{1,0:T(8,128)S(1)}, u32[]{:S(2)}, u32[]{:S(2)}) %collective-permute-start.10) | collective-permute-done | bytes 524320 | tf_op jit(solution)/shard_map/ppermute | solution.py:571
  126.5 4.6 %collective-permute-done.9 = f32[512,256]{1,0:T(8,128)S(1)} collective-permute-done((f32[512,256]{1,0:T(8,128)S(1)}, f32[512,256]{1,0:T(8,128)S(1)}, u32[]{:S(2)}, u32[]{:S(2)}) %collective-permute-start.9) | collective-permute-done | bytes 524320 | tf_op jit(solution)/shard_map/ppermute | solution.py:571
  131.3 3.5 %select.64 = bf16[13,128,512]{2,1,0:T(8,128)(2,1)} custom-call(s32[13]{0:T(128)} %and_select_fusion.owner_ref, bf16[16,128,512]{2,1,0:T(8,128)(2,1)} %copy-done), custom_call_target="tpu_custom_call" | custom-call | bytes 3407872 | tf_op jit(solution)/shard_map/select/pallas_call | solution.py:118
  135.2 0.8 select_reduce_fusion.2
  135.9 0.7 select_reduce_fusion.w_ref
  136.6 2.5 %collective-permute-start.14 = (f32[128,256]{1,0:T(8,128)S(1)}, f32[128,256]{1,0:T(8,128)S(1)}, u32[]{:S(2)}, u32[]{:S(2)}) collective-permute-start(f32[128,256]{1,0:T(8,128)S(1)} %get-tuple-element.73), channel_id=1, source_target_pairs={{0,16},{2,18},{4,20},{6,22},{8,24},{10,26},{12,28},{14,30},{16,0},... | collective-permute-start | bytes 393224 | tf_op jit(solution)/shard_map/ppermute | solution.py:571
  139.1 1.9 collective-permute-start.15
  141.0 14.8 %kernel_rows.1 = (bf16[1664,2048]{1,0:T(8,128)(2,1)}, bf16[1664,256]{1,0:T(8,128)(2,1)}, f32[1,2048]{1,0:T(1,128)}, f32[1,256]{1,0:T(1,128)}) custom-call(f32[13]{0:T(128)} %select_reduce_fusion.w_ref, bf16[1664,512]{1,0:T(8,128)(2,1)} %bitcast.24, bf16[1664,512]{1,0:T(8,128)(2,1)} %collective-permute-done.12.refs_1_, ...), custom_call_target="tpu_custom_call" | custom-call | flops 7851737088 | bytes 14417920 | tf_op jit(solution)/shard_map/kernel_rows/pallas_call | solution.py:399
  155.9 0.4 convolution_convert_fusion
  156.4 2.8 %select.65 = bf16[6,128,512]{2,1,0:T(8,128)(2,1)} custom-call(s32[6]{0:T(128)} %get-tuple-element.80.owner_ref, bf16[16,128,512]{2,1,0:T(8,128)(2,1)} %all-to-all-done.1.recv_ref), custom_call_target="tpu_custom_call" | custom-call | bytes 1572864 | tf_op jit(solution)/shard_map/select/pallas_call | solution.py:118
  159.3 0.6 slice.31
  159.9 2.4 %collective-permute-start.18 = (bf16[128,256]{1,0:T(8,128)(2,1)S(1)}, bf16[128,256]{1,0:T(8,128)(2,1)S(1)}, u32[]{:S(2)}, u32[]{:S(2)}) collective-permute-start(bf16[128,256]{1,0:T(8,128)(2,1)S(1)} %convolution_convert_fusion), channel_id=1, source_target_pairs={{0,16},{2,18},{4,20},{6,22},{8,24},{10,26},{12,28},{14,30},{16,0},... | collective-permute-start | bytes 196616 | tf_op jit(solution)/shard_map/ppermute | solution.py:571
  162.4 2.0 %collective-permute-start.19 = (bf16[128,256]{1,0:T(8,128)(2,1)S(1)}, bf16[128,256]{1,0:T(8,128)(2,1)S(1)}, u32[]{:S(2)}, u32[]{:S(2)}) collective-permute-start(bf16[128,256]{1,0:T(8,128)(2,1)S(1)} %convolution_convert_fusion), channel_id=1, source_target_pairs={{0,24},{2,26},{4,28},{6,30},{8,16},{10,18},{12,20},{14,22},{16,8},... | collective-permute-start | bytes 196616 | tf_op jit(solution)/shard_map/ppermute | solution.py:571
  164.3 0.7 select_reduce_fusion.3.w_ref
  165.0 0.5 collective-permute-done.17
  165.6 2.9 %collective-permute-done.18 = bf16[128,256]{1,0:T(8,128)(2,1)S(1)} collective-permute-done((bf16[128,256]{1,0:T(8,128)(2,1)S(1)}, bf16[128,256]{1,0:T(8,128)(2,1)S(1)}, u32[]{:S(2)}, u32[]{:S(2)}) %collective-permute-start.18) | collective-permute-done | bytes 65568 | tf_op jit(solution)/shard_map/ppermute | solution.py:571
  168.5 2.0 %collective-permute-start.20 = (bf16[512,256]{1,0:T(8,128)(2,1)S(1)}, bf16[512,256]{1,0:T(8,128)(2,1)S(1)}, u32[]{:S(2)}, u32[]{:S(2)}) collective-permute-start(bf16[512,256]{1,0:T(8,128)(2,1)S(1)} %pad_maximum_fusion.1), channel_id=1, source_target_pairs={{0,2},{2,0},{4,6},{6,4},{8,10},{10,8},{12,14},{14,12},{16,18},{18,... | collective-permute-start | bytes 786440 | tf_op jit(solution)/shard_map/ppermute | solution.py:571
  170.5 2.4 %collective-permute-start.21 = (bf16[512,256]{1,0:T(8,128)(2,1)S(1)}, bf16[512,256]{1,0:T(8,128)(2,1)S(1)}, u32[]{:S(2)}, u32[]{:S(2)}) collective-permute-start(bf16[512,256]{1,0:T(8,128)(2,1)S(1)} %pad_maximum_fusion.1), channel_id=1, source_target_pairs={{0,4},{2,6},{4,0},{6,2},{8,12},{10,14},{12,8},{14,10},{16,20},{18,... | collective-permute-start | bytes 786440 | tf_op jit(solution)/shard_map/ppermute | solution.py:571
  172.8 0.9 copy-done.2
  173.7 8.0 %second_rows.1 = (bf16[1664,2048]{1,0:T(8,128)(2,1)}, bf16[1664,256]{1,0:T(8,128)(2,1)}) custom-call(s32[6]{0:T(128)} %get-tuple-element.99.place_ref, s32[1]{0:T(128)} %bitcast.5.num_ref, f32[6]{0:T(128)} %select_reduce_fusion.3.w_ref, bf16[768,512]{1,0:T(8,128)(2,1)} %bitcast.22, ...), custom_call_target="tpu_custom_call", output_to_operand_aliasing={{0}: (9, {}), {1}: (10, {})} | custom-call | flops 3623878656 | bytes 4194304 | tf_op jit(solution)/shard_map/second_rows/pallas_call | solution.py:487
  181.8 1.7 collective-permute-done.21
  183.4 1.1 pad_maximum_fusion.rt_ref
  184.6 9.4 %remainder_rows.1 = (bf16[1664,2048]{1,0:T(8,128)(2,1)}, f32[256,2048]{1,0:T(8,128)}) custom-call(s32[1]{0:T(128)} %bitcast.quarter_ref, bf16[1664,2048]{1,0:T(8,128)(2,1)} %get-tuple-element.90.kern_ref, bf16[1664,256]{1,0:T(8,128)(2,1)} %get-tuple-element.91.p_ref, f32[256,256]{1,0:T(8,128)} %factor.1.inv_ref, bf16[4,512,256]{2,1,0:T(8,128)(2,1)} %pad_maximum_fusion.rt_ref), custom_call_target="tpu_custom_call" | custom-call | flops 1744830464 | bytes 13631488 | tf_op jit(solution)/shard_map/remainder_rows/pallas_call | solution.py:547
  (76 shorter events, 3.0 us)
Async XLA Ops:
  0.6 14.8 %collective-permute-start = (bf16[3200,512]{1,0:T(8,128)(2,1)}, bf16[3200,512]{1,0:T(8,128)(2,1)}, u32[]{:S(2)}, u32[]{:S(2)}) collective-permute-start(bf16[3200,512]{1,0:T(8,128)(2,1)} %refs_0_.3), channel_id=1, source_target_pairs={{0,1},{1,0},{2,3},{3,2},{4,5},{5,4},{6,7},{7,6},{8,9},{9,8},{10,11... | collective-permute-start | bytes 9830408 | tf_op jit(solution)/shard_map/ppermute | solution.py:187
  5.1 8.4 %copy-start.5 = (s32[16,25]{1,0:T(8,128)S(1)}, s32[16,25]{1,0:T(8,128)}, u32[]{:S(2)}) copy-start(s32[16,25]{1,0:T(8,128)} %dest_ref.1) | copy-start | bytes 4804
  5.1 8.4 %copy-start.6 = (s32[16]{0:T(128)S(1)}, s32[16]{0:T(128)}, u32[]{:S(2)}) copy-start(s32[16]{0:T(128)} %cnt_ref.3) | copy-start | bytes 196
  5.1 8.7 %copy-start.9 = (bf16[25]{0:T(256)(128)(2,1)S(1)}, bf16[25]{0:T(256)(128)(2,1)}, u32[]{:S(2)}) copy-start(bf16[25]{0:T(256)(128)(2,1)} %param.7) | copy-start | bytes 154
  5.1 68.5 %all-to-all-start = ((bf16[16,128,512]{2,1,0:T(8,128)(2,1)}), bf16[16,128,512]{2,1,0:T(8,128)(2,1)S(1)}, u32[]{:S(2)}, u32[]{:S(2)}) async-start(bf16[16,128,512]{2,1,0:T(8,128)(2,1)} %get-tuple-element.54), calls=%async_computation | async-start | bytes 4194304 | tf_op jit(solution)/shard_map/all_to_all | solution.py:623
  13.2 2.1 %collective-permute-start.1 = (bf16[256,1024]{1,0:T(8,128)(2,1)S(1)}, bf16[256,1024]{1,0:T(8,128)(2,1)S(1)}, u32[]{:S(2)}, u32[]{:S(2)}) collective-permute-start(bf16[256,1024]{1,0:T(8,128)(2,1)S(1)} %slice.33), channel_id=1, source_target_pairs={{0,1},{1,0},{2,3},{3,2},{4,5},{5,4},{6,7},{7,6},{8,9},{9,8},{10,11... | collective-permute-start | bytes 1572872 | tf_op jit(solution)/shard_map/ppermute | solution.py:618
  15.4 0.8 copy-start.3
  27.1 31.0 %collective-permute-start.2 = (f32[136,256]{1,0:T(8,128)S(1)}, f32[136,256]{1,0:T(8,128)S(1)}, u32[]{:S(2)}, u32[]{:S(2)}) collective-permute-start(f32[136,256]{1,0:T(8,128)S(1)} %pad_maximum_fusion.2), channel_id=1, source_target_pairs={{0,2},{2,0},{4,6},{6,4},{8,10},{10,8},{12,14},{14,12},{16,18},{18,... | collective-permute-start | bytes 417800 | tf_op jit(solution)/shard_map/ppermute | solution.py:571
  27.1 30.9 %collective-permute-start.3 = (f32[136,256]{1,0:T(8,128)S(1)}, f32[136,256]{1,0:T(8,128)S(1)}, u32[]{:S(2)}, u32[]{:S(2)}) collective-permute-start(f32[136,256]{1,0:T(8,128)S(1)} %pad_maximum_fusion.2), channel_id=1, source_target_pairs={{0,4},{2,6},{4,0},{6,2},{8,12},{10,14},{12,8},{14,10},{16,20},{18,... | collective-permute-start | bytes 417800 | tf_op jit(solution)/shard_map/ppermute | solution.py:571
  30.5 27.6 %collective-permute-start.4 = (f32[136,256]{1,0:T(8,128)S(1)}, f32[136,256]{1,0:T(8,128)S(1)}, u32[]{:S(2)}, u32[]{:S(2)}) collective-permute-start(f32[136,256]{1,0:T(8,128)S(1)} %pad_maximum_fusion.2), channel_id=1, source_target_pairs={{0,6},{2,4},{4,2},{6,0},{8,14},{10,12},{12,10},{14,8},{16,22},{18,... | collective-permute-start | bytes 417800 | tf_op jit(solution)/shard_map/ppermute | solution.py:571
  58.1 7.5 %collective-permute-start.5 = (f32[136,256]{1,0:T(8,128)S(1)}, f32[136,256]{1,0:T(8,128)S(1)}, u32[]{:S(2)}, u32[]{:S(2)}) collective-permute-start(f32[136,256]{1,0:T(8,128)S(1)} %add_add_fusion.2), channel_id=1, source_target_pairs={{0,8},{2,10},{4,12},{6,14},{8,0},{10,2},{12,4},{14,6},{16,24},{18,... | collective-permute-start | bytes 417800 | tf_op jit(solution)/shard_map/ppermute | solution.py:571
  59.5 13.4 %collective-permute-start.6 = (f32[136,256]{1,0:T(8,128)S(1)}, f32[136,256]{1,0:T(8,128)S(1)}, u32[]{:S(2)}, u32[]{:S(2)}) collective-permute-start(f32[136,256]{1,0:T(8,128)S(1)} %add_add_fusion.2), channel_id=1, source_target_pairs={{0,16},{2,18},{4,20},{6,22},{8,24},{10,26},{12,28},{14,30},{16,0},... | collective-permute-start | bytes 417800 | tf_op jit(solution)/shard_map/ppermute | solution.py:571
  62.4 11.2 %collective-permute-start.7 = (f32[136,256]{1,0:T(8,128)S(1)}, f32[136,256]{1,0:T(8,128)}, u32[]{:S(2)}, u32[]{:S(2)}) collective-permute-start(f32[136,256]{1,0:T(8,128)S(1)} %add_add_fusion.2), channel_id=1, source_target_pairs={{0,24},{2,26},{4,28},{6,30},{8,16},{10,18},{12,20},{14,22},{16,8},... | collective-permute-start | bytes 417800 | tf_op jit(solution)/shard_map/ppermute | solution.py:571
  73.0 0.7 copy-start.4
  73.6 1.3 copy-start
  75.0 81.4 %all-to-all-start.1 = ((bf16[16,128,512]{2,1,0:T(8,128)(2,1)}), bf16[16,128,512]{2,1,0:T(8,128)(2,1)}, u32[]{:S(2)}, u32[]{:S(2)}) async-start(bf16[16,128,512]{2,1,0:T(8,128)(2,1)} %get-tuple-element.81), calls=%async_computation.1 | async-start | bytes 4194304 | tf_op jit(solution)/shard_map/all_to_all | solution.py:645
  80.3 46.2 %collective-permute-start.10 = (f32[512,256]{1,0:T(8,128)}, f32[512,256]{1,0:T(8,128)S(1)}, u32[]{:S(2)}, u32[]{:S(2)}) collective-permute-start(f32[512,256]{1,0:T(8,128)} %get-tuple-element.61), channel_id=1, source_target_pairs={{0,4},{2,6},{4,0},{6,2},{8,12},{10,14},{12,8},{14,10},{16,20},{18,... | collective-permute-start | bytes 1572872 | tf_op jit(solution)/shard_map/ppermute | solution.py:571
  82.2 44.2 %collective-permute-start.11 = (f32[512,256]{1,0:T(8,128)}, f32[512,256]{1,0:T(8,128)S(1)}, u32[]{:S(2)}, u32[]{:S(2)}) collective-permute-start(f32[512,256]{1,0:T(8,128)} %get-tuple-element.62), channel_id=1, source_target_pairs={{0,6},{2,4},{4,2},{6,0},{8,14},{10,12},{12,10},{14,8},{16,22},{18,... | collective-permute-start | bytes 1572872 | tf_op jit(solution)/shard_map/ppermute | solution.py:571
  83.7 47.4 %collective-permute-start.9 = (f32[512,256]{1,0:T(8,128)S(1)}, f32[512,256]{1,0:T(8,128)S(1)}, u32[]{:S(2)}, u32[]{:S(2)}) collective-permute-start(f32[512,256]{1,0:T(8,128)S(1)} %get-tuple-element.60), channel_id=1, source_target_pairs={{0,2},{2,0},{4,6},{6,4},{8,10},{10,8},{12,14},{14,12},{16,18},{18,... | collective-permute-start | bytes 1572872 | tf_op jit(solution)/shard_map/ppermute | solution.py:571
  84.9 1.4 collective-permute-start.8
  131.3 3.8 %copy-start.7 = (s32[13]{0:T(128)S(1)}, s32[13]{0:T(128)}, u32[]{:S(2)}) copy-start(s32[13]{0:T(128)} %and_select_fusion.owner_ref) | copy-start | bytes 160
  134.8 6.2 %collective-permute-start.12 = (bf16[1664,512]{1,0:T(8,128)(2,1)}, bf16[1664,512]{1,0:T(8,128)(2,1)}, u32[]{:S(2)}, u32[]{:S(2)}) collective-permute-start(bf16[1664,512]{1,0:T(8,128)(2,1)} %bitcast.23), channel_id=1, source_target_pairs={{0,1},{1,0},{2,3},{3,2},{4,5},{5,4},{6,7},{7,6},{8,9},{9,8},{10,11... | collective-permute-start | bytes 5111816 | tf_op jit(solution)/shard_map/ppermute | solution.py:187
  136.6 19.3 %collective-permute-start.13 = (f32[128,256]{1,0:T(8,128)S(1)}, f32[128,256]{1,0:T(8,128)S(1)}, u32[]{:S(2)}, u32[]{:S(2)}) collective-permute-start(f32[128,256]{1,0:T(8,128)S(1)} %get-tuple-element.72), channel_id=1, source_target_pairs={{0,8},{2,10},{4,12},{6,14},{8,0},{10,2},{12,4},{14,6},{16,24},{18,... | collective-permute-start | bytes 393224 | tf_op jit(solution)/shard_map/ppermute | solution.py:571
  136.6 19.3 %collective-permute-start.14 = (f32[128,256]{1,0:T(8,128)S(1)}, f32[128,256]{1,0:T(8,128)S(1)}, u32[]{:S(2)}, u32[]{:S(2)}) collective-permute-start(f32[128,256]{1,0:T(8,128)S(1)} %get-tuple-element.73), channel_id=1, source_target_pairs={{0,16},{2,18},{4,20},{6,22},{8,24},{10,26},{12,28},{14,30},{16,0},... | collective-permute-start | bytes 393224 | tf_op jit(solution)/shard_map/ppermute | solution.py:571
  139.1 16.8 %collective-permute-start.15 = (f32[128,256]{1,0:T(8,128)S(1)}, f32[128,256]{1,0:T(8,128)S(1)}, u32[]{:S(2)}, u32[]{:S(2)}) collective-permute-start(f32[128,256]{1,0:T(8,128)S(1)} %get-tuple-element.74), channel_id=1, source_target_pairs={{0,24},{2,26},{4,28},{6,30},{8,16},{10,18},{12,20},{14,22},{16,8},... | collective-permute-start | bytes 393224 | tf_op jit(solution)/shard_map/ppermute | solution.py:571
  141.0 14.9 %copy-start.1 = (f32[256,256]{1,0:T(8,128)S(1)}, f32[256,256]{1,0:T(8,128)}, u32[]{:S(2)}) copy-start(f32[256,256]{1,0:T(8,128)} %factor.1.inv_ref) | copy-start | bytes 786436
  155.9 8.4 %copy-start.8 = (f32[13]{0:T(128)S(1)}, f32[13]{0:T(128)}, u32[]{:S(2)}) copy-start(f32[13]{0:T(128)} %select_reduce_fusion.w_ref) | copy-start | bytes 160
  159.2 13.6 %collective-permute-start.16 = (bf16[768,512]{1,0:T(8,128)(2,1)}, bf16[768,512]{1,0:T(8,128)(2,1)S(1)}, u32[]{:S(2)}, u32[]{:S(2)}) collective-permute-start(bf16[768,512]{1,0:T(8,128)(2,1)} %bitcast.21), channel_id=1, source_target_pairs={{0,1},{1,0},{2,3},{3,2},{4,5},{5,4},{6,7},{7,6},{8,9},{9,8},{10,11... | collective-permute-start | bytes 2359304 | tf_op jit(solution)/shard_map/ppermute | solution.py:187
  159.9 5.6 %collective-permute-start.17 = (bf16[128,256]{1,0:T(8,128)(2,1)S(1)}, bf16[128,256]{1,0:T(8,128)(2,1)S(1)}, u32[]{:S(2)}, u32[]{:S(2)}) collective-permute-start(bf16[128,256]{1,0:T(8,128)(2,1)S(1)} %convolution_convert_fusion), channel_id=1, source_target_pairs={{0,8},{2,10},{4,12},{6,14},{8,0},{10,2},{12,4},{14,6},{16,24},{18,... | collective-permute-start | bytes 196616 | tf_op jit(solution)/shard_map/ppermute | solution.py:571
  159.9 8.5 %collective-permute-start.18 = (bf16[128,256]{1,0:T(8,128)(2,1)S(1)}, bf16[128,256]{1,0:T(8,128)(2,1)S(1)}, u32[]{:S(2)}, u32[]{:S(2)}) collective-permute-start(bf16[128,256]{1,0:T(8,128)(2,1)S(1)} %convolution_convert_fusion), channel_id=1, source_target_pairs={{0,16},{2,18},{4,20},{6,22},{8,24},{10,26},{12,28},{14,30},{16,0},... | collective-permute-start | bytes 196616 | tf_op jit(solution)/shard_map/ppermute | solution.py:571
  162.4 6.1 %collective-permute-start.19 = (bf16[128,256]{1,0:T(8,128)(2,1)S(1)}, bf16[128,256]{1,0:T(8,128)(2,1)S(1)}, u32[]{:S(2)}, u32[]{:S(2)}) collective-permute-start(bf16[128,256]{1,0:T(8,128)(2,1)S(1)} %convolution_convert_fusion), channel_id=1, source_target_pairs={{0,24},{2,26},{4,28},{6,30},{8,16},{10,18},{12,20},{14,22},{16,8},... | collective-permute-start | bytes 196616 | tf_op jit(solution)/shard_map/ppermute | solution.py:571
  168.5 13.3 %collective-permute-start.20 = (bf16[512,256]{1,0:T(8,128)(2,1)S(1)}, bf16[512,256]{1,0:T(8,128)(2,1)S(1)}, u32[]{:S(2)}, u32[]{:S(2)}) collective-permute-start(bf16[512,256]{1,0:T(8,128)(2,1)S(1)} %pad_maximum_fusion.1), channel_id=1, source_target_pairs={{0,2},{2,0},{4,6},{6,4},{8,10},{10,8},{12,14},{14,12},{16,18},{18,... | collective-permute-start | bytes 786440 | tf_op jit(solution)/shard_map/ppermute | solution.py:571
  170.5 13.0 %collective-permute-start.21 = (bf16[512,256]{1,0:T(8,128)(2,1)S(1)}, bf16[512,256]{1,0:T(8,128)(2,1)S(1)}, u32[]{:S(2)}, u32[]{:S(2)}) collective-permute-start(bf16[512,256]{1,0:T(8,128)(2,1)S(1)} %pad_maximum_fusion.1), channel_id=1, source_target_pairs={{0,4},{2,6},{4,0},{6,2},{8,12},{10,14},{12,8},{14,10},{16,20},{18,... | collective-permute-start | bytes 786440 | tf_op jit(solution)/shard_map/ppermute | solution.py:571
  172.8 10.6 %collective-permute-start.22 = (bf16[512,256]{1,0:T(8,128)(2,1)S(1)}, bf16[512,256]{1,0:T(8,128)(2,1)S(1)}, u32[]{:S(2)}, u32[]{:S(2)}) collective-permute-start(bf16[512,256]{1,0:T(8,128)(2,1)S(1)} %pad_maximum_fusion.1), channel_id=1, source_target_pairs={{0,6},{2,4},{4,2},{6,0},{8,14},{10,12},{12,10},{14,8},{16,22},{18,... | collective-permute-start | bytes 786440 | tf_op jit(solution)/shard_map/ppermute | solution.py:571
  172.8 0.9 copy-start.2

commit v9 on v7

--- a/solution.py
+++ b/solution.py
@@ -50,7 +50,7 @@
     return high, (x - high.astype(jnp.float32)).astype(jnp.bfloat16)
 
 
-HEAD = 48
+HEAD = 32
 
 
 def block_copies(rank, whole_ref, outer, first_ref, last_ref, sems):
@@ -205,7 +205,7 @@
         out_shape=jax.ShapeDtypeStruct((n, n), jnp.float32),
         scratch_shapes=[pltpu.VMEM((n, n), jnp.float32)],
         compiler_params=params(),
-        cost_estimate=cost(4 * n * n * n, 8 * n * n),
+        cost_estimate=cost(1e11, 8 * n * n),
         name="factor",
     )(gram)
 
@@ -606,8 +606,11 @@
     return [lax.dynamic_slice_in_dim(x, (q ^ k) * n, n, 0) for k in range(4)]
 
 
-def quarter_sum(pieces, pair):
-    got = [pieces[0]] + [trade(pieces[k], pair, k) for k in range(1, 4)]
+def trades(pieces, pair):
+    return [pieces[0]] + [trade(pieces[k], pair, k) for k in range(1, 4)]
+
+
+def total(got):
     return (got[0] + got[1]) + (got[2] + got[3])
 
 
@@ -645,45 +648,25 @@
     else:
         moved = lax.all_gather(first, "cols", axis=0, tiled=False)[0]
     desc_blocks = descriptors.reshape(slots, BLK, feat)
-    outgoing = pack(desc_blocks, destinations, block_counts, per_pair)
+    outgoing = list(pack(desc_blocks, destinations, block_counts, per_pair))
+
+    weights32 = block_weights.astype(jnp.float32)
+    spare = -(-owners * slots // (PANEL * 8)) * 8
+    table = lax.dynamic_update_slice(
+        jnp.zeros((spare * PANEL,), jnp.float32), weights32, (me * slots,)
+    ).reshape(spare, PANEL)
+    for pair in pairs[::-1]:
+        table = pair_sum(table, pair)
+    table, outgoing[0], source_parts = lax.optimization_barrier(
+        (table, outgoing[0], source_parts)
+    )
+    all_weights = table.reshape(-1)[: owners * slots]
     received = [lax.all_to_all(outgoing[0], "rows", split_axis=0, concat_axis=0, tiled=True)]
 
-    weights32 = block_weights.astype(jnp.float32)
     gram_part, pw, panel_points = panel_products(
         source_parts, block_counts, weights32, sparse_points, moved
     )
     sent = quarters(column_products(source_parts, pw, sparse_points), pairs[0])
-
-    spare = -(-owners * slots // (PANEL * 8)) * 8
-    table = lax.dynamic_update_slice(
-        jnp.zeros((spare * PANEL,), jnp.float32), weights32, (me * slots,)
-    ).reshape(spare, PANEL)
-    if groups == 2:
-        gram_part = lax.dynamic_slice_in_dim(gram_part, group * (PANEL // 2), PANEL // 2, 0)
-    summed = pair_sum(jnp.concatenate([gram_part, table], 0), pairs[0])
-    summed, *sent = lax.optimization_barrier((summed, *sent))
-    g = quarter_sum(sent, pairs[0])
-    for pair in pairs[1:]:
-        summed = pair_sum(summed, pair)
-    gram, table = summed[:-spare], summed[-spare:]
-    if groups == 2:
-        other = lax.ppermute(gram, "cols", [(0, 1), (1, 0)])
-        gram = jnp.where(
-            group == 0, jnp.concatenate([gram, other], 0), jnp.concatenate([other, gram], 0)
-        )
-    all_weights = table.reshape(-1)[: owners * slots]
-
-    for pair in pairs[1:]:
-        sent = quarters(g, pair)
-        if per_pair > 1 and pair == pairs[-1]:
-            gram, last, received[0], *sent = lax.optimization_barrier(
-                (gram, outgoing[1], received[0], *sent)
-            )
-        g = quarter_sum(sent, pair)
-    if per_pair > 1:
-        received.append(lax.all_to_all(last, "rows", split_axis=0, concat_axis=0, tiled=True))
-    inverse = factor(gram)
-    rt = nt(g, inverse, HIGH).astype(jnp.bfloat16)
 
     slot_ids = jnp.arange(slots, dtype=jnp.int32)
     toward = ((slot_ids[None, :] < block_counts[:, None]) & (destinations == me)).astype(jnp.int32)
@@ -703,20 +686,48 @@
     second_owner = jnp.sum(jnp.where(pick, from_owner[None, :], 0), axis=1)
     second_weights = jnp.sum(jnp.where(pick, weights_here[None, :], 0.0), axis=1)
 
-    rt, from_owner = lax.optimization_barrier((rt, from_owner))
+    if groups == 2:
+        gram_part = lax.dynamic_slice_in_dim(gram_part, group * (PANEL // 2), PANEL // 2, 0)
+    gram = pair_sum(gram_part, pairs[0])
+    gram, from_owner, *sent = lax.optimization_barrier((gram, from_owner, *sent))
+    for pair in pairs[1:-1]:
+        gram = pair_sum(gram, pair)
+    far = gather_pieces(gram, pairs[-1])
+    near = trades(sent, pairs[0])
+
     arrived = select(received[:1], [(0, BLK)], from_owner).reshape(DST_BLK * BLK, feat)
     kern, panel, cs, csp = kernel_rows(
         share_parts(arrived), weights_here, panel_points, sparse_points
     )
+    kern, far, near = lax.optimization_barrier((kern, far, near))
+    gram = total(far)
+    if groups == 2:
+        other = lax.ppermute(gram, "cols", [(0, 1), (1, 0)])
+        gram = jnp.where(
+            group == 0, jnp.concatenate([gram, other], 0), jnp.concatenate([other, gram], 0)
+        )
+    g = total(near)
+    for pair in pairs[1:]:
+        sent = quarters(g, pair)
+        if per_pair > 1 and pair == pairs[-1]:
+            gram, last, received[0], *sent = lax.optimization_barrier(
+                (gram, outgoing[1], received[0], *sent)
+            )
+        far = trades(sent, pair)
+    if per_pair > 1:
+        received.append(lax.all_to_all(last, "rows", split_axis=0, concat_axis=0, tiled=True))
+    inverse = factor(gram)
+    inverse, *far = lax.optimization_barrier((inverse, *far))
+    rt = nt(total(far), inverse, HIGH).astype(jnp.bfloat16)
     for pair in pairs[:0:-1]:
         rt = gather_back(rt, pair)
+    if per_pair > 1:
+        rt, kern, second_owner = lax.optimization_barrier((rt, kern, second_owner))
     pieces = gather_pieces(rt, pairs[0])
     if per_pair > 1:
-        rt, kern, second_owner = lax.optimization_barrier((rt, kern, second_owner))
         late = select(received, [(BLK, HEAD), (0, BLK - HEAD)], second_owner)
-        late = late.reshape(most * BLK, feat)
         kern, panel = second_rows(
-            share_parts(late),
+            share_parts(late.reshape(most * BLK, feat)),
             places,
             order[-1:],
             second_weights,

time: 198 us -> 209 us (1.056)
  starting transfers between devices: 39.2 us -> 50.6 us
  waiting for transfers between devices: 30.4 us -> 38 us
  other arithmetic: 11.7 us -> 7.07 us
  Pallas kernels: 102 us -> 97.5 us
    ppermute x18 -> x24, starting transfers between devices: 25 us -> 39.3 us  [trade(): return lax.ppermute(x, 'rows', flips(bit, lax.axis_size('rows')))]
    all_to_all x1, waiting for transfers between devices: 0.01 us -> 4.96 us  [on_device(): lax.all_to_all(outgoing[0], 'rows', split_axis=0, concat_axis=0, tiled=True)]
    all_to_all x1, starting transfers between devices: 7.4 us -> 3.73 us  [on_device(): lax.all_to_all(outgoing[0], 'rows', split_axis=0, concat_axis=0, tiled=True)]
    unnamed x26 -> x23, local copies, waits for them, and re-layouts: 2.99 us -> 6 us
    ppermute x18 -> x24, waiting for transfers between devices: 30.2 us -> 31.9 us  [trade(): return lax.ppermute(x, 'rows', flips(bit, lax.axis_size('rows')))]
  transfers between devices with their start and end apart: 25 -> 31, of which waited for: 7 -> 10; matrix products, arithmetic and copies ran while one was open for 10% -> 6% of each run, Pallas kernels for 45% -> 39%
where the time goes in v9:
time: 209 us; the launch traced here: 208 us
  Pallas kernels  97.5 us (47%)
  starting transfers between devices  50.6 us (24%)
  waiting for transfers between devices  38 us (18%)
  local copies, waits for them, and re-layouts  12.7 us (6%)
  other arithmetic  7.07 us (3%)
    ppermute x24, starting transfers between devices, trade(): return lax.ppermute(x, 'rows', flips(bit, lax.axis_size('rows')))  39.3 us
    ppermute x24, waiting for transfers between devices, trade(): return lax.ppermute(x, 'rows', flips(bit, lax.axis_size('rows')))  31.9 us
    pallas_call x1, Pallas kernels, column_products(): pl.pallas_call(functools.partial(column_kernel, len(parts)), grid=(size /...  24.7 us
    pallas_call x1, Pallas kernels, factor(): pl.pallas_call(functools.partial(factor_kernel, 64), out_shape=jax.ShapeD...  24 us
    pallas_call x1, Pallas kernels, kernel_rows(): pl.pallas_call(functools.partial(rows_kernel, len(parts)), grid=(cols //...  14.8 us
    pallas_call x1, Pallas kernels, remainder_rows(): pl.pallas_call(functools.partial(remainder_kernel, norm), grid_spec=spec,...  9.42 us
    pallas_call x1, Pallas kernels, panel_products(): pl.pallas_call(functools.partial(panel_kernel, len(parts)), out_shape=(ja...  8.11 us
    all_to_all x1, starting transfers between devices, on_device(): lax.all_to_all(last, 'rows', split_axis=0, concat_axis=0, tiled=True)  6.86 us
  transfers between devices with their start and end apart: 31, of which 10 were waited for; matrix products, arithmetic and copies ran while one was open for 6% of the time, Pallas kernels for 39%

profile of v9, /device:TPU:0, one launch (start us, length us, event | category | flops | bytes accessed | tf_op | source)
XLA Modules:
  0.0 208.2 jit_solution(7404938362730176905)
XLA Ops:
  1.1 0.7 convert_dynamic-update-slice_fusion
  1.9 2.7 %collective-permute-start = (f32[8,256]{1,0:T(8,128)S(1)}, f32[8,256]{1,0:T(8,128)S(1)}, u32[]{:S(2)}, u32[]{:S(2)}) collective-permute-start(f32[8,256]{1,0:T(8,128)S(1)} %reshape.137), channel_id=1, source_target_pairs={{0,8},{2,10},{4,12},{6,14},{8,0},{10,2},{12,4},{14,6},{16,24},{18,... | collective-permute-start | bytes 24584 | tf_op jit(solution)/shard_map/ppermute | solution.py:600
  4.6 2.6 %collective-permute-start.1 = (f32[8,256]{1,0:T(8,128)S(1)}, f32[8,256]{1,0:T(8,128)S(1)}, u32[]{:S(2)}, u32[]{:S(2)}) collective-permute-start(f32[8,256]{1,0:T(8,128)S(1)} %reshape.137), channel_id=1, source_target_pairs={{0,16},{2,18},{4,20},{6,22},{8,24},{10,26},{12,28},{14,30},{16,0},... | collective-permute-start | bytes 24584 | tf_op jit(solution)/shard_map/ppermute | solution.py:600
  7.2 2.0 collective-permute-done.1
  9.1 3.5 %collective-permute-done.2 = f32[8,256]{1,0:T(8,128)S(1)} collective-permute-done((f32[8,256]{1,0:T(8,128)S(1)}, f32[8,256]{1,0:T(8,128)S(1)}, u32[]{:S(2)}, u32[]{:S(2)}) %collective-permute-start.2) | collective-permute-done | bytes 8224 | tf_op jit(solution)/shard_map/ppermute | solution.py:600
  12.6 1.5 collective-permute-start.3
  14.1 1.5 collective-permute-start.4
  16.1 3.6 %pack.1 = (bf16[16,160,512]{2,1,0:T(8,128)(2,1)}, bf16[16,96,512]{2,1,0:T(8,128)(2,1)}) custom-call(s32[16,25]{1,0:T(8,128)} %dest_ref.1, s32[16]{0:T(128)} %cnt_ref.3, bf16[25,128,512]{2,1,0:T(8,128)(2,1)} %bitcast.19), custom_call_target="tpu_custom_call" | custom-call | bytes 6553600 | tf_op jit(solution)/shard_map/pack/pallas_call | solution.py:111
  20.3 1.7 copy-done.2
  21.9 3.7 %all-to-all-start = ((bf16[16,160,512]{2,1,0:T(8,128)(2,1)}), bf16[16,160,512]{2,1,0:T(8,128)(2,1)S(1)}, u32[]{:S(2)}, u32[]{:S(2)}) async-start(bf16[16,160,512]{2,1,0:T(8,128)(2,1)} %get-tuple-element.61), calls=%async_computation | async-start | bytes 5242880 | tf_op jit(solution)/shard_map/all_to_all | solution.py:664
  25.7 1.9 slice.28
  29.9 0.8 copy-done.4
  30.7 8.1 %panel_products.1 = (f32[256,256]{1,0:T(8,128)}, bf16[3200,256]{1,0:T(8,128)(2,1)}, bf16[256,1024]{1,0:T(8,128)(2,1)}) custom-call(s32[16]{0:T(128)} %cnt_ref.3, f32[25]{0:T(128)} %convert_element_type.21.w_ref, bf16[3200,512]{1,0:T(8,128)(2,1)} %refs_0_.1, bf16[3200,512]{1,0:T(8,128)(2,1)} %copy-done.2, bf16[2048,1024]{1,0:T(8,128)(2,1)} %refs_4_.1, ...), custom_call_target="tpu_custom_call" | custom-call | flops 2097152000 | bytes 6553600 | tf_op jit(solution)/shard_map/panel_products/pallas_call | solution.py:319
  38.8 0.9 constant_dynamic-slice_fusion.8
  39.7 1.8 collective-permute-start.10
  41.6 1.7 collective-permute-start.9
  43.3 24.7 %column_products.1 = f32[2048,256]{1,0:T(8,128)} custom-call(bf16[3200,512]{1,0:T(8,128)(2,1)} %refs_0_.1, bf16[3200,512]{1,0:T(8,128)(2,1)} %copy-done.2, bf16[3200,256]{1,0:T(8,128)(2,1)} %get-tuple-element.59.refs_2_, bf16[2048,1024]{1,0:T(8,128)(2,1)} %refs_4_.1), custom_call_target="tpu_custom_call" | custom-call | flops 16777216000 | bytes 6553600 | tf_op jit(solution)/shard_map/column_products/pallas_call | solution.py:368
  68.0 2.9 %constant_dynamic-slice_fusion.4 = (f32[512,256]{1,0:T(8,128)}, f32[512,256]{1,0:T(8,128)}, f32[512,256]{1,0:T(8,128)}, f32[512,256]{1,0:T(8,128)S(1)}) fusion(f32[2048,256]{1,0:T(8,128)} %column_products.1, s32[]{:T(128)S(6)} %select_n.259, s32[]{:T(128)S(6)} %select_n.258, s32[]{:T(128)S(6)} %select_n.257, s32[]{:T(128)S(6)} %select_n.256), kind=kLoop, calls=%fused_computation.32 | loop fusion | bytes 4194320 | tf_op jit(solution)/shard_map/dynamic_slice | solution.py:606
  71.0 5.0 %all-to-all-done.refs_0_ = bf16[16,160,512]{2,1,0:T(8,128)(2,1)S(1)} async-done(((bf16[16,160,512]{2,1,0:T(8,128)(2,1)}), bf16[16,160,512]{2,1,0:T(8,128)(2,1)S(1)}, u32[]{:S(2)}, u32[]{:S(2)}) %all-to-all-start) | async-done | bytes 2621472 | tf_op jit(solution)/shard_map/all_to_all | solution.py:664
  75.9 1.5 copy-done
  77.4 3.4 %select.64 = bf16[13,128,512]{2,1,0:T(8,128)(2,1)} custom-call(s32[13]{0:T(128)} %and_select_fusion.owner_ref, bf16[16,160,512]{2,1,0:T(8,128)(2,1)} %copy-done), custom_call_target="tpu_custom_call" | custom-call | bytes 3407872 | tf_op jit(solution)/shard_map/select/pallas_call | solution.py:147
  81.0 7.6 %collective-permute-start.12 = (f32[128,256]{1,0:T(8,128)S(1)}, f32[128,256]{1,0:T(8,128)S(1)}, u32[]{:S(2)}, u32[]{:S(2)}) collective-permute-start(f32[128,256]{1,0:T(8,128)S(1)} %add_add_fusion.2), channel_id=1, source_target_pairs={{0,8},{2,10},{4,12},{6,14},{8,0},{10,2},{12,4},{14,6},{16,24},{18,... | collective-permute-start | bytes 393224 | tf_op jit(solution)/shard_map/ppermute | solution.py:600
  89.5 2.2 %collective-permute-start.13 = (f32[128,256]{1,0:T(8,128)S(1)}, f32[128,256]{1,0:T(8,128)S(1)}, u32[]{:S(2)}, u32[]{:S(2)}) collective-permute-start(f32[128,256]{1,0:T(8,128)S(1)} %add_add_fusion.2), channel_id=1, source_target_pairs={{0,16},{2,18},{4,20},{6,22},{8,24},{10,26},{12,28},{14,30},{16,0},... | collective-permute-start | bytes 393224 | tf_op jit(solution)/shard_map/ppermute | solution.py:600
  91.7 1.3 collective-permute-start.14
  93.0 1.4 collective-permute-start.15
  94.4 1.7 collective-permute-start.16
  96.5 14.8 %kernel_rows.1 = (bf16[1664,2048]{1,0:T(8,128)(2,1)}, bf16[1664,256]{1,0:T(8,128)(2,1)}, f32[1,2048]{1,0:T(1,128)}, f32[1,256]{1,0:T(1,128)}) custom-call(f32[13]{0:T(128)} %select_reduce_fusion.w_ref, bf16[1664,512]{1,0:T(8,128)(2,1)} %bitcast.23, bf16[1664,512]{1,0:T(8,128)(2,1)} %collective-permute-done.11.refs_1_, ...), custom_call_target="tpu_custom_call" | custom-call | flops 7851737088 | bytes 14417920 | tf_op jit(solution)/shard_map/kernel_rows/pallas_call | solution.py:428
  111.3 7.3 %collective-permute-done.16 = f32[512,256]{1,0:T(8,128)S(1)} collective-permute-done((f32[512,256]{1,0:T(8,128)}, f32[512,256]{1,0:T(8,128)S(1)}, u32[]{:S(2)}, u32[]{:S(2)}) %collective-permute-start.16) | collective-permute-done | bytes 524320 | tf_op jit(solution)/shard_map/ppermute | solution.py:600
  118.6 1.0 collective-permute-done.17
  119.9 1.1 collective-permute-done.18
  121.8 1.1 collective-permute-start.19
  122.9 3.2 %collective-permute-start.20 = (f32[128,256]{1,0:T(8,128)S(1)}, f32[128,256]{1,0:T(8,128)S(1)}, u32[]{:S(2)}, u32[]{:S(2)}) collective-permute-start(f32[128,256]{1,0:T(8,128)S(1)} %get-tuple-element.81), channel_id=1, source_target_pairs={{0,16},{2,18},{4,20},{6,22},{8,24},{10,26},{12,28},{14,30},{16,0},... | collective-permute-start | bytes 393224 | tf_op jit(solution)/shard_map/ppermute | solution.py:600
  126.2 6.9 %all-to-all-start.1 = ((bf16[16,96,512]{2,1,0:T(8,128)(2,1)}), bf16[16,96,512]{2,1,0:T(8,128)(2,1)S(1)}, u32[]{:S(2)}, u32[]{:S(2)}) async-start(bf16[16,96,512]{2,1,0:T(8,128)(2,1)} %get-tuple-element.91), calls=%async_computation.1 | async-start | bytes 3145728 | tf_op jit(solution)/shard_map/all_to_all | solution.py:718
  133.0 24.0 %factor.1.inv_ref = f32[256,256]{1,0:T(8,128)} custom-call(f32[256,256]{1,0:T(8,128)} %maximum_select_fusion.gram_ref), custom_call_target="tpu_custom_call" | custom-call | flops 99999997952 | bytes 524288 | tf_op jit(solution)/shard_map/factor/pallas_call | solution.py:203
  157.1 1.3 convolution_convert_fusion
  158.4 2.0 collective-permute-start.22
  160.4 2.4 %collective-permute-start.23 = (bf16[128,256]{1,0:T(8,128)(2,1)S(1)}, bf16[128,256]{1,0:T(8,128)(2,1)S(1)}, u32[]{:S(2)}, u32[]{:S(2)}) collective-permute-start(bf16[128,256]{1,0:T(8,128)(2,1)S(1)} %convolution_convert_fusion), channel_id=1, source_target_pairs={{0,16},{2,18},{4,20},{6,22},{8,24},{10,26},{12,28},{14,30},{16,0},... | collective-permute-start | bytes 196616 | tf_op jit(solution)/shard_map/ppermute | solution.py:600
  163.6 13.2 %collective-permute-done.23 = bf16[128,256]{1,0:T(8,128)(2,1)S(1)} collective-permute-done((bf16[128,256]{1,0:T(8,128)(2,1)S(1)}, bf16[128,256]{1,0:T(8,128)(2,1)S(1)}, u32[]{:S(2)}, u32[]{:S(2)}) %collective-permute-start.23) | collective-permute-done | bytes 65568 | tf_op jit(solution)/shard_map/ppermute | solution.py:600
  176.9 1.1 copy-done.1
  178.0 2.9 %select.65 = bf16[6,128,512]{2,1,0:T(8,128)(2,1)} custom-call(s32[6]{0:T(128)} %get-tuple-element.89.owner_ref, bf16[16,160,512]{2,1,0:T(8,128)(2,1)} %copy-done, bf16[16,96,512]{2,1,0:T(8,128)(2,1)} %copy-done.1), custom_call_target="tpu_custom_call" | custom-call | bytes 1572864 | tf_op jit(solution)/shard_map/select/pallas_call | solution.py:147
  182.2 1.1 collective-permute-start.26
  183.3 1.7 collective-permute-start.27
  185.7 0.9 copy-done.3
  186.6 6.5 %second_rows.1 = (bf16[1664,2048]{1,0:T(8,128)(2,1)}, bf16[1664,256]{1,0:T(8,128)(2,1)}) custom-call(s32[6]{0:T(128)} %get-tuple-element.107.place_ref, s32[1]{0:T(128)} %bitcast.5.num_ref, f32[6]{0:T(128)} %select_reduce_fusion.3.w_ref, bf16[768,512]{1,0:T(8,128)(2,1)} %bitcast.21, ...), custom_call_target="tpu_custom_call", output_to_operand_aliasing={{0}: (9, {}), {1}: (10, {})} | custom-call | flops 3623878656 | bytes 4194304 | tf_op jit(solution)/shard_map/second_rows/pallas_call | solution.py:516
  193.1 3.5 %collective-permute-done.27 = bf16[512,256]{1,0:T(8,128)(2,1)S(1)} collective-permute-done((bf16[512,256]{1,0:T(8,128)(2,1)S(1)}, bf16[512,256]{1,0:T(8,128)(2,1)S(1)}, u32[]{:S(2)}, u32[]{:S(2)}) %collective-permute-start.27) | collective-permute-done | bytes 262176 | tf_op jit(solution)/shard_map/ppermute | solution.py:600
  196.6 1.1 collective-permute-done.28
  197.7 1.1 pad_maximum_fusion.rt_ref
  198.8 9.4 %remainder_rows.1 = (bf16[1664,2048]{1,0:T(8,128)(2,1)}, f32[256,2048]{1,0:T(8,128)}) custom-call(s32[1]{0:T(128)} %bitcast.quarter_ref, bf16[1664,2048]{1,0:T(8,128)(2,1)} %get-tuple-element.98.kern_ref, bf16[1664,256]{1,0:T(8,128)(2,1)} %get-tuple-element.99.p_ref, f32[256,256]{1,0:T(8,128)} %factor.1.inv_ref, bf16[4,512,256]{2,1,0:T(8,128)(2,1)} %pad_maximum_fusion.rt_ref), custom_call_target="tpu_custom_call" | custom-call | flops 1744830464 | bytes 13631488 | tf_op jit(solution)/shard_map/remainder_rows/pallas_call | solution.py:576
  (89 shorter events, 9.3 us)
Async XLA Ops:
  0.6 19.6 %collective-permute-start.6 = (bf16[3200,512]{1,0:T(8,128)(2,1)}, bf16[3200,512]{1,0:T(8,128)(2,1)S(1)}, u32[]{:S(2)}, u32[]{:S(2)}) collective-permute-start(bf16[3200,512]{1,0:T(8,128)(2,1)} %refs_0_.1), channel_id=1, source_target_pairs={{0,1},{1,0},{2,3},{3,2},{4,5},{5,4},{6,7},{7,6},{8,9},{9,8},{10,11... | collective-permute-start | bytes 9830408 | tf_op jit(solution)/shard_map/ppermute | solution.py:216
  1.9 5.3 %collective-permute-start = (f32[8,256]{1,0:T(8,128)S(1)}, f32[8,256]{1,0:T(8,128)S(1)}, u32[]{:S(2)}, u32[]{:S(2)}) collective-permute-start(f32[8,256]{1,0:T(8,128)S(1)} %reshape.137), channel_id=1, source_target_pairs={{0,8},{2,10},{4,12},{6,14},{8,0},{10,2},{12,4},{14,6},{16,24},{18,... | collective-permute-start | bytes 24584 | tf_op jit(solution)/shard_map/ppermute | solution.py:600
  4.6 4.5 %collective-permute-start.1 = (f32[8,256]{1,0:T(8,128)S(1)}, f32[8,256]{1,0:T(8,128)S(1)}, u32[]{:S(2)}, u32[]{:S(2)}) collective-permute-start(f32[8,256]{1,0:T(8,128)S(1)} %reshape.137), channel_id=1, source_target_pairs={{0,16},{2,18},{4,20},{6,22},{8,24},{10,26},{12,28},{14,30},{16,0},... | collective-permute-start | bytes 24584 | tf_op jit(solution)/shard_map/ppermute | solution.py:600
  7.2 5.4 %collective-permute-start.2 = (f32[8,256]{1,0:T(8,128)S(1)}, f32[8,256]{1,0:T(8,128)S(1)}, u32[]{:S(2)}, u32[]{:S(2)}) collective-permute-start(f32[8,256]{1,0:T(8,128)S(1)} %reshape.137), channel_id=1, source_target_pairs={{0,24},{2,26},{4,28},{6,30},{8,16},{10,18},{12,20},{14,22},{16,8},... | collective-permute-start | bytes 24584 | tf_op jit(solution)/shard_map/ppermute | solution.py:600
  12.6 7.1 %collective-permute-start.3 = (f32[8,256]{1,0:T(8,128)S(1)}, f32[8,256]{1,0:T(8,128)S(1)}, u32[]{:S(2)}, u32[]{:S(2)}) collective-permute-start(f32[8,256]{1,0:T(8,128)S(1)} %add_add_fusion.4), channel_id=1, source_target_pairs={{0,2},{2,0},{4,6},{6,4},{8,10},{10,8},{12,14},{14,12},{16,18},{18,... | collective-permute-start | bytes 24584 | tf_op jit(solution)/shard_map/ppermute | solution.py:600
  14.1 5.6 %collective-permute-start.4 = (f32[8,256]{1,0:T(8,128)S(1)}, f32[8,256]{1,0:T(8,128)S(1)}, u32[]{:S(2)}, u32[]{:S(2)}) collective-permute-start(f32[8,256]{1,0:T(8,128)S(1)} %add_add_fusion.4), channel_id=1, source_target_pairs={{0,4},{2,6},{4,0},{6,2},{8,12},{10,14},{12,8},{14,10},{16,20},{18,... | collective-permute-start | bytes 24584 | tf_op jit(solution)/shard_map/ppermute | solution.py:600
  15.7 4.5 %collective-permute-start.5 = (f32[8,256]{1,0:T(8,128)S(1)}, f32[8,256]{1,0:T(8,128)S(1)}, u32[]{:S(2)}, u32[]{:S(2)}) collective-permute-start(f32[8,256]{1,0:T(8,128)S(1)} %add_add_fusion.4), channel_id=1, source_target_pairs={{0,6},{2,4},{4,2},{6,0},{8,14},{10,12},{12,10},{14,8},{16,22},{18,... | collective-permute-start | bytes 24584 | tf_op jit(solution)/shard_map/ppermute | solution.py:600
  20.2 1.7 copy-start.2
  20.2 7.3 %copy-start.10 = (bf16[25]{0:T(256)(128)(2,1)S(1)}, bf16[25]{0:T(256)(128)(2,1)}, u32[]{:S(2)}) copy-start(bf16[25]{0:T(256)(128)(2,1)} %param.7) | copy-start | bytes 154
  20.2 7.9 %copy-start.6 = (s32[16,25]{1,0:T(8,128)S(1)}, s32[16,25]{1,0:T(8,128)}, u32[]{:S(2)}) copy-start(s32[16,25]{1,0:T(8,128)} %dest_ref.1) | copy-start | bytes 4804
  20.2 7.8 %copy-start.7 = (s32[16]{0:T(128)S(1)}, s32[16]{0:T(128)}, u32[]{:S(2)}) copy-start(s32[16]{0:T(128)} %cnt_ref.3) | copy-start | bytes 196
  21.9 54.0 %all-to-all-start = ((bf16[16,160,512]{2,1,0:T(8,128)(2,1)}), bf16[16,160,512]{2,1,0:T(8,128)(2,1)S(1)}, u32[]{:S(2)}, u32[]{:S(2)}) async-start(bf16[16,160,512]{2,1,0:T(8,128)(2,1)} %get-tuple-element.61), calls=%async_computation | async-start | bytes 5242880 | tf_op jit(solution)/shard_map/all_to_all | solution.py:664
  27.5 2.4 %collective-permute-start.7 = (bf16[256,1024]{1,0:T(8,128)(2,1)}, bf16[256,1024]{1,0:T(8,128)(2,1)S(1)}, u32[]{:S(2)}, u32[]{:S(2)}) collective-permute-start(bf16[256,1024]{1,0:T(8,128)(2,1)} %slice.28), channel_id=1, source_target_pairs={{0,1},{1,0},{2,3},{3,2},{4,5},{5,4},{6,7},{7,6},{8,9},{9,8},{10,11... | collective-permute-start | bytes 1572872 | tf_op jit(solution)/shard_map/ppermute | solution.py:647
  29.9 0.8 copy-start.4
  39.7 31.2 %collective-permute-start.10 = (f32[128,256]{1,0:T(8,128)S(1)}, f32[128,256]{1,0:T(8,128)S(1)}, u32[]{:S(2)}, u32[]{:S(2)}) collective-permute-start(f32[128,256]{1,0:T(8,128)S(1)} %constant_dynamic-slice_fusion.8), channel_id=1, source_target_pairs={{0,6},{2,4},{4,2},{6,0},{8,14},{10,12},{12,10},{14,8},{16,22},{18,... | collective-permute-start | bytes 393224 | tf_op jit(solution)/shard_map/ppermute | solution.py:600
  41.6 29.3 %collective-permute-start.8 = (f32[128,256]{1,0:T(8,128)S(1)}, f32[128,256]{1,0:T(8,128)S(1)}, u32[]{:S(2)}, u32[]{:S(2)}) collective-permute-start(f32[128,256]{1,0:T(8,128)S(1)} %constant_dynamic-slice_fusion.8), channel_id=1, source_target_pairs={{0,2},{2,0},{4,6},{6,4},{8,10},{10,8},{12,14},{14,12},{16,18},{18,... | collective-permute-start | bytes 393224 | tf_op jit(solution)/shard_map/ppermute | solution.py:600
  41.6 29.4 %collective-permute-start.9 = (f32[128,256]{1,0:T(8,128)S(1)}, f32[128,256]{1,0:T(8,128)S(1)}, u32[]{:S(2)}, u32[]{:S(2)}) collective-permute-start(f32[128,256]{1,0:T(8,128)S(1)} %constant_dynamic-slice_fusion.8), channel_id=1, source_target_pairs={{0,4},{2,6},{4,0},{6,2},{8,12},{10,14},{12,8},{14,10},{16,20},{18,... | collective-permute-start | bytes 393224 | tf_op jit(solution)/shard_map/ppermute | solution.py:600
  68.0 2.9 %copy-start.5 = (f32[256,256]{1,0:T(8,128)S(1)}, f32[256,256]{1,0:T(8,128)}, u32[]{:S(2)}) copy-start(f32[256,256]{1,0:T(8,128)} %get-tuple-element.58) | copy-start | bytes 786436
  75.9 1.5 copy-start
  80.9 15.2 %collective-permute-start.11 = (bf16[1664,512]{1,0:T(8,128)(2,1)}, bf16[1664,512]{1,0:T(8,128)(2,1)}, u32[]{:S(2)}, u32[]{:S(2)}) collective-permute-start(bf16[1664,512]{1,0:T(8,128)(2,1)} %bitcast.22), channel_id=1, source_target_pairs={{0,1},{1,0},{2,3},{3,2},{4,5},{5,4},{6,7},{7,6},{8,9},{9,8},{10,11... | collective-permute-start | bytes 5111816 | tf_op jit(solution)/shard_map/ppermute | solution.py:216
  81.0 13.4 %collective-permute-start.12 = (f32[128,256]{1,0:T(8,128)S(1)}, f32[128,256]{1,0:T(8,128)S(1)}, u32[]{:S(2)}, u32[]{:S(2)}) collective-permute-start(f32[128,256]{1,0:T(8,128)S(1)} %add_add_fusion.2), channel_id=1, source_target_pairs={{0,8},{2,10},{4,12},{6,14},{8,0},{10,2},{12,4},{14,6},{16,24},{18,... | collective-permute-start | bytes 393224 | tf_op jit(solution)/shard_map/ppermute | solution.py:600
  89.5 21.8 %collective-permute-start.13 = (f32[128,256]{1,0:T(8,128)S(1)}, f32[128,256]{1,0:T(8,128)S(1)}, u32[]{:S(2)}, u32[]{:S(2)}) collective-permute-start(f32[128,256]{1,0:T(8,128)S(1)} %add_add_fusion.2), channel_id=1, source_target_pairs={{0,16},{2,18},{4,20},{6,22},{8,24},{10,26},{12,28},{14,30},{16,0},... | collective-permute-start | bytes 393224 | tf_op jit(solution)/shard_map/ppermute | solution.py:600
  91.7 19.6 %collective-permute-start.14 = (f32[128,256]{1,0:T(8,128)S(1)}, f32[128,256]{1,0:T(8,128)S(1)}, u32[]{:S(2)}, u32[]{:S(2)}) collective-permute-start(f32[128,256]{1,0:T(8,128)S(1)} %add_add_fusion.2), channel_id=1, source_target_pairs={{0,24},{2,26},{4,28},{6,30},{8,16},{10,18},{12,20},{14,22},{16,8},... | collective-permute-start | bytes 393224 | tf_op jit(solution)/shard_map/ppermute | solution.py:600
  93.0 18.3 %collective-permute-start.15 = (f32[512,256]{1,0:T(8,128)}, f32[512,256]{1,0:T(8,128)S(1)}, u32[]{:S(2)}, u32[]{:S(2)}) collective-permute-start(f32[512,256]{1,0:T(8,128)} %get-tuple-element.66), channel_id=1, source_target_pairs={{0,2},{2,0},{4,6},{6,4},{8,10},{10,8},{12,14},{14,12},{16,18},{18,... | collective-permute-start | bytes 1572872 | tf_op jit(solution)/shard_map/ppermute | solution.py:600
  94.4 24.2 %collective-permute-start.16 = (f32[512,256]{1,0:T(8,128)}, f32[512,256]{1,0:T(8,128)S(1)}, u32[]{:S(2)}, u32[]{:S(2)}) collective-permute-start(f32[512,256]{1,0:T(8,128)} %get-tuple-element.67), channel_id=1, source_target_pairs={{0,4},{2,6},{4,0},{6,2},{8,12},{10,14},{12,8},{14,10},{16,20},{18,... | collective-permute-start | bytes 1572872 | tf_op jit(solution)/shard_map/ppermute | solution.py:600
  96.0 23.6 %collective-permute-start.17 = (f32[512,256]{1,0:T(8,128)}, f32[512,256]{1,0:T(8,128)S(1)}, u32[]{:S(2)}, u32[]{:S(2)}) collective-permute-start(f32[512,256]{1,0:T(8,128)} %get-tuple-element.68), channel_id=1, source_target_pairs={{0,6},{2,4},{4,2},{6,0},{8,14},{10,12},{12,10},{14,8},{16,22},{18,... | collective-permute-start | bytes 1572872 | tf_op jit(solution)/shard_map/ppermute | solution.py:600
  119.6 1.4 collective-permute-start.18
  121.8 35.3 %collective-permute-start.19 = (f32[128,256]{1,0:T(8,128)S(1)}, f32[128,256]{1,0:T(8,128)S(1)}, u32[]{:S(2)}, u32[]{:S(2)}) collective-permute-start(f32[128,256]{1,0:T(8,128)S(1)} %get-tuple-element.80), channel_id=1, source_target_pairs={{0,8},{2,10},{4,12},{6,14},{8,0},{10,2},{12,4},{14,6},{16,24},{18,... | collective-permute-start | bytes 393224 | tf_op jit(solution)/shard_map/ppermute | solution.py:600
  122.9 34.2 %collective-permute-start.20 = (f32[128,256]{1,0:T(8,128)S(1)}, f32[128,256]{1,0:T(8,128)S(1)}, u32[]{:S(2)}, u32[]{:S(2)}) collective-permute-start(f32[128,256]{1,0:T(8,128)S(1)} %get-tuple-element.81), channel_id=1, source_target_pairs={{0,16},{2,18},{4,20},{6,22},{8,24},{10,26},{12,28},{14,30},{16,0},... | collective-permute-start | bytes 393224 | tf_op jit(solution)/shard_map/ppermute | solution.py:600
  126.1 31.0 %collective-permute-start.21 = (f32[128,256]{1,0:T(8,128)S(1)}, f32[128,256]{1,0:T(8,128)S(1)}, u32[]{:S(2)}, u32[]{:S(2)}) collective-permute-start(f32[128,256]{1,0:T(8,128)S(1)} %get-tuple-element.82), channel_id=1, source_target_pairs={{0,24},{2,26},{4,28},{6,30},{8,16},{10,18},{12,20},{14,22},{16,8},... | collective-permute-start | bytes 393224 | tf_op jit(solution)/shard_map/ppermute | solution.py:600
  126.2 50.7 %all-to-all-start.1 = ((bf16[16,96,512]{2,1,0:T(8,128)(2,1)}), bf16[16,96,512]{2,1,0:T(8,128)(2,1)S(1)}, u32[]{:S(2)}, u32[]{:S(2)}) async-start(bf16[16,96,512]{2,1,0:T(8,128)(2,1)} %get-tuple-element.91), calls=%async_computation.1 | async-start | bytes 3145728 | tf_op jit(solution)/shard_map/all_to_all | solution.py:718
  133.0 29.9 %copy-start.8 = (s32[13]{0:T(128)S(1)}, s32[13]{0:T(128)}, u32[]{:S(2)}) copy-start(s32[13]{0:T(128)} %and_select_fusion.owner_ref) | copy-start | bytes 160
  158.4 5.2 %collective-permute-start.22 = (bf16[128,256]{1,0:T(8,128)(2,1)S(1)}, bf16[128,256]{1,0:T(8,128)(2,1)S(1)}, u32[]{:S(2)}, u32[]{:S(2)}) collective-permute-start(bf16[128,256]{1,0:T(8,128)(2,1)S(1)} %convolution_convert_fusion), channel_id=1, source_target_pairs={{0,8},{2,10},{4,12},{6,14},{8,0},{10,2},{12,4},{14,6},{16,24},{18,... | collective-permute-start | bytes 196616 | tf_op jit(solution)/shard_map/ppermute | solution.py:600
  160.4 16.3 %collective-permute-start.23 = (bf16[128,256]{1,0:T(8,128)(2,1)S(1)}, bf16[128,256]{1,0:T(8,128)(2,1)S(1)}, u32[]{:S(2)}, u32[]{:S(2)}) collective-permute-start(bf16[128,256]{1,0:T(8,128)(2,1)S(1)} %convolution_convert_fusion), channel_id=1, source_target_pairs={{0,16},{2,18},{4,20},{6,22},{8,24},{10,26},{12,28},{14,30},{16,0},... | collective-permute-start | bytes 196616 | tf_op jit(solution)/shard_map/ppermute | solution.py:600
  162.8 14.0 %collective-permute-start.24 = (bf16[128,256]{1,0:T(8,128)(2,1)S(1)}, bf16[128,256]{1,0:T(8,128)(2,1)S(1)}, u32[]{:S(2)}, u32[]{:S(2)}) collective-permute-start(bf16[128,256]{1,0:T(8,128)(2,1)S(1)} %convolution_convert_fusion), channel_id=1, source_target_pairs={{0,24},{2,26},{4,28},{6,30},{8,16},{10,18},{12,20},{14,22},{16,8},... | collective-permute-start | bytes 196616 | tf_op jit(solution)/shard_map/ppermute | solution.py:600
  176.8 4.7 %copy-start.9 = (f32[13]{0:T(128)S(1)}, f32[13]{0:T(128)}, u32[]{:S(2)}) copy-start(f32[13]{0:T(128)} %select_reduce_fusion.w_ref) | copy-start | bytes 160
  176.9 1.1 copy-start.1
  180.9 4.8 %collective-permute-start.25 = (bf16[768,512]{1,0:T(8,128)(2,1)}, bf16[768,512]{1,0:T(8,128)(2,1)S(1)}, u32[]{:S(2)}, u32[]{:S(2)}) collective-permute-start(bf16[768,512]{1,0:T(8,128)(2,1)} %bitcast.20), channel_id=1, source_target_pairs={{0,1},{1,0},{2,3},{3,2},{4,5},{5,4},{6,7},{7,6},{8,9},{9,8},{10,11... | collective-permute-start | bytes 2359304 | tf_op jit(solution)/shard_map/ppermute | solution.py:216
  182.2 10.9 %collective-permute-start.26 = (bf16[512,256]{1,0:T(8,128)(2,1)S(1)}, bf16[512,256]{1,0:T(8,128)(2,1)S(1)}, u32[]{:S(2)}, u32[]{:S(2)}) collective-permute-start(bf16[512,256]{1,0:T(8,128)(2,1)S(1)} %pad_maximum_fusion.1), channel_id=1, source_target_pairs={{0,2},{2,0},{4,6},{6,4},{8,10},{10,8},{12,14},{14,12},{16,18},{18,... | collective-permute-start | bytes 786440 | tf_op jit(solution)/shard_map/ppermute | solution.py:600
  183.3 13.3 %collective-permute-start.27 = (bf16[512,256]{1,0:T(8,128)(2,1)S(1)}, bf16[512,256]{1,0:T(8,128)(2,1)S(1)}, u32[]{:S(2)}, u32[]{:S(2)}) collective-permute-start(bf16[512,256]{1,0:T(8,128)(2,1)S(1)} %pad_maximum_fusion.1), channel_id=1, source_target_pairs={{0,4},{2,6},{4,0},{6,2},{8,12},{10,14},{12,8},{14,10},{16,20},{18,... | collective-permute-start | bytes 786440 | tf_op jit(solution)/shard_map/ppermute | solution.py:600
  185.0 12.7 %collective-permute-start.28 = (bf16[512,256]{1,0:T(8,128)(2,1)S(1)}, bf16[512,256]{1,0:T(8,128)(2,1)S(1)}, u32[]{:S(2)}, u32[]{:S(2)}) collective-permute-start(bf16[512,256]{1,0:T(8,128)(2,1)S(1)} %pad_maximum_fusion.1), channel_id=1, source_target_pairs={{0,6},{2,4},{4,2},{6,0},{8,14},{10,12},{12,10},{14,8},{16,22},{18,... | collective-permute-start | bytes 786440 | tf_op jit(solution)/shard_map/ppermute | solution.py:600
  185.7 0.9 copy-start.3

commit v10 on v5

--- a/solution.py
+++ b/solution.py
@@ -50,7 +50,7 @@
     return high, (x - high.astype(jnp.float32)).astype(jnp.bfloat16)
 
 
-HEAD = 64
+HEAD = 48
 
 
 def block_copies(rank, whole_ref, outer, first_ref, last_ref, sems):

time: 192 us -> 193 us (level)
  starting transfers between devices: 53 us -> 49.8 us
  Pallas kernels: 88 us -> 90.4 us
    ppermute x18, starting transfers between devices: 39.5 us -> 34.7 us  [trade(): return lax.ppermute(x, 'rows', flips(bit, lax.axis_size('rows')))]
    pallas_call x1, Pallas kernels: 7.97 us -> 9.92 us  [panel_products(): pl.pallas_call(functools.partial(panel_kernel, len(parts)), out_shape=(ja...]
  transfers between devices with their start and end apart: 24 -> 24, of which waited for: 7 -> 6; matrix products, arithmetic and copies ran while one was open for 7% -> 7% of each run, Pallas kernels for 39% -> 40%
where the time goes in v10:
time: 193 us
  Pallas kernels  90.4 us (47%)
  starting transfers between devices  49.8 us (26%)
  waiting for transfers between devices  35.3 us (18%)
  local copies, waits for them, and re-layouts  8 us (4%)
  other arithmetic  6.52 us (3%)
    ppermute x18, starting transfers between devices, trade(): return lax.ppermute(x, 'rows', flips(bit, lax.axis_size('rows')))  34.7 us
    ppermute x18, waiting for transfers between devices, trade(): return lax.ppermute(x, 'rows', flips(bit, lax.axis_size('rows')))  34.5 us
    pallas_call x1, Pallas kernels, column_products(): pl.pallas_call(functools.partial(column_kernel, len(parts)), grid=(size /...  24.7 us
    pallas_call x1, Pallas kernels, factor(): pl.pallas_call(functools.partial(factor_kernel, 64), out_shape=jax.ShapeD...  24 us
    pallas_call x1, Pallas kernels, kernel_rows(): pl.pallas_call(functools.partial(rows_kernel, len(parts)), grid=(cols //...  14.6 us
    pallas_call x1, Pallas kernels, panel_products(): pl.pallas_call(functools.partial(panel_kernel, len(parts)), out_shape=(ja...  9.92 us
    pallas_call x1, Pallas kernels, remainder_rows(): pl.pallas_call(functools.partial(remainder_kernel, norm), grid_spec=spec,...  9.43 us
    all_to_all x1, starting transfers between devices, on_device(): lax.all_to_all(outgoing[0], 'rows', split_axis=0, concat_axis=0, tiled=True)  8.08 us
  transfers between devices with their start and end apart: 24, of which 6 were waited for; matrix products, arithmetic and copies ran while one was open for 7% of the time, Pallas kernels for 40%

profile of v10, /device:TPU:0, one launch (start us, length us, event | category | flops | bytes accessed | tf_op | source)
XLA Modules:
  0.0 192.5 jit_solution(18304613890261078523)
XLA Ops:
  0.6 0.5 collective-permute-start
  1.1 4.1 %pack.1 = (bf16[16,176,512]{2,1,0:T(8,128)(2,1)}, bf16[16,80,512]{2,1,0:T(8,128)(2,1)}) custom-call(s32[16,25]{1,0:T(8,128)} %dest_ref.1, s32[16]{0:T(128)} %cnt_ref.3, bf16[25,128,512]{2,1,0:T(8,128)(2,1)} %bitcast.15), custom_call_target="tpu_custom_call" | custom-call | bytes 6553600 | tf_op jit(solution)/shard_map/pack/pallas_call | solution.py:111
  5.3 8.1 %all-to-all-start = ((bf16[16,176,512]{2,1,0:T(8,128)(2,1)}), bf16[16,176,512]{2,1,0:T(8,128)(2,1)S(1)}, u32[]{:S(2)}, u32[]{:S(2)}) async-start(bf16[16,176,512]{2,1,0:T(8,128)(2,1)} %get-tuple-element.31), calls=%async_computation | async-start | bytes 5767168 | tf_op jit(solution)/shard_map/all_to_all | solution.py:568
  13.4 1.9 slice.25
  15.8 0.5 convert_element_type.10.w_ref
  16.5 0.7 broadcast_in_dim.42
  17.2 0.3 reduce-window.9
  17.9 0.8 copy-done.1
  18.7 9.9 %panel_products.1 = (f32[256,256]{1,0:T(8,128)}, bf16[3200,256]{1,0:T(8,128)(2,1)}, bf16[256,1024]{1,0:T(8,128)(2,1)}) custom-call(s32[16]{0:T(128)} %cnt_ref.3, f32[25]{0:T(128)} %convert_element_type.10.w_ref, bf16[3200,512]{1,0:T(8,128)(2,1)} %refs_0_.3, bf16[3200,512]{1,0:T(8,128)(2,1)} %collective-permute-done.refs_1_, bf16[2048,1024]{1,0:T(8,128)(2,1)} %refs_3_.3, ...), custom_call_target="tpu_custom_call" | custom-call | flops 2097152000 | bytes 6553600 | tf_op jit(solution)/shard_map/panel_products/pallas_call | solution.py:320
  28.6 0.9 constant_dynamic-slice_fusion.6
  29.7 0.8 collective-permute-start.4
  30.4 2.7 %collective-permute-start.2 = (f32[136,256]{1,0:T(8,128)S(1)}, f32[136,256]{1,0:T(8,128)S(1)}, u32[]{:S(2)}, u32[]{:S(2)}) collective-permute-start(f32[136,256]{1,0:T(8,128)S(1)} %pad_maximum_fusion.2), channel_id=1, source_target_pairs={{0,2},{2,0},{4,6},{6,4},{8,10},{10,8},{12,14},{14,12},{16,18},{18,... | collective-permute-start | bytes 417800 | tf_op jit(solution)/shard_map/ppermute | solution.py:519
  33.1 24.7 %column_products.1 = f32[2048,256]{1,0:T(8,128)} custom-call(bf16[3200,512]{1,0:T(8,128)(2,1)} %refs_0_.3, bf16[3200,512]{1,0:T(8,128)(2,1)} %collective-permute-done.refs_1_, bf16[3200,256]{1,0:T(8,128)(2,1)} %get-tuple-element.24.refs_2_, bf16[2048,1024]{1,0:T(8,128)(2,1)} %refs_3_.3), custom_call_target="tpu_custom_call" | custom-call | flops 16777216000 | bytes 6553600 | tf_op jit(solution)/shard_map/column_products/pallas_call | solution.py:369
  58.0 3.0 %collective-permute-start.7 = (f32[136,256]{1,0:T(8,128)S(1)}, f32[136,256]{1,0:T(8,128)S(1)}, u32[]{:S(2)}, u32[]{:S(2)}) collective-permute-start(f32[136,256]{1,0:T(8,128)S(1)} %add_add_fusion.2), channel_id=1, source_target_pairs={{0,24},{2,26},{4,28},{6,30},{8,16},{10,18},{12,20},{14,22},{16,8},... | collective-permute-start | bytes 417800 | tf_op jit(solution)/shard_map/ppermute | solution.py:519
  61.0 0.2 collective-permute-start.6
  61.2 1.2 collective-permute-start.5
  62.4 1.5 constant_dynamic-slice_fusion.5
  63.9 0.8 collective-permute-start.8
  64.7 1.5 collective-permute-start.10
  66.2 2.8 %collective-permute-done.7 = f32[136,256]{1,0:T(8,128)S(1)} collective-permute-done((f32[136,256]{1,0:T(8,128)S(1)}, f32[136,256]{1,0:T(8,128)S(1)}, u32[]{:S(2)}, u32[]{:S(2)}) %collective-permute-start.7) | collective-permute-done | bytes 139296 | tf_op jit(solution)/shard_map/ppermute | solution.py:519
  69.0 3.9 %collective-permute-start.9 = (f32[512,256]{1,0:T(8,128)S(1)}, f32[512,256]{1,0:T(8,128)S(1)}, u32[]{:S(2)}, u32[]{:S(2)}) collective-permute-start(f32[512,256]{1,0:T(8,128)S(1)} %get-tuple-element.46), channel_id=1, source_target_pairs={{0,4},{2,6},{4,0},{6,2},{8,12},{10,14},{12,8},{14,10},{16,20},{18,... | collective-permute-start | bytes 1572872 | tf_op jit(solution)/shard_map/ppermute | solution.py:519
  72.9 19.3 %collective-permute-done.6 = f32[136,256]{1,0:T(8,128)S(1)} collective-permute-done((f32[136,256]{1,0:T(8,128)S(1)}, f32[136,256]{1,0:T(8,128)S(1)}, u32[]{:S(2)}, u32[]{:S(2)}) %collective-permute-start.6) | collective-permute-done | bytes 139296 | tf_op jit(solution)/shard_map/ppermute | solution.py:519
  92.3 0.5 broadcast_compare_fusion
  92.9 0.8 collective-permute-done.11
  93.7 0.7 maximum_select_fusion.gram_ref
  94.4 3.5 %collective-permute-done.9 = f32[512,256]{1,0:T(8,128)S(1)} collective-permute-done((f32[512,256]{1,0:T(8,128)S(1)}, f32[512,256]{1,0:T(8,128)S(1)}, u32[]{:S(2)}, u32[]{:S(2)}) %collective-permute-start.9) | collective-permute-done | bytes 524320 | tf_op jit(solution)/shard_map/ppermute | solution.py:519
  98.0 1.2 add_add_fusion
  99.2 0.8 constant_dynamic-slice_fusion.2
  99.9 11.0 %collective-permute-start.12 = (f32[128,256]{1,0:T(8,128)}, f32[128,256]{1,0:T(8,128)}, u32[]{:S(2)}, u32[]{:S(2)}) collective-permute-start(f32[128,256]{1,0:T(8,128)} %get-tuple-element.47), channel_id=1, source_target_pairs={{0,8},{2,10},{4,12},{6,14},{8,0},{10,2},{12,4},{14,6},{16,24},{18,... | collective-permute-start | bytes 393224 | tf_op jit(solution)/shard_map/ppermute | solution.py:519
  111.0 0.9 collective-permute-start.14
  111.9 0.5 collective-permute-start.13
  112.4 6.2 %all-to-all-start.1 = ((bf16[16,80,512]{2,1,0:T(8,128)(2,1)}), bf16[16,80,512]{2,1,0:T(8,128)(2,1)}, u32[]{:S(2)}, u32[]{:S(2)}) async-start(bf16[16,80,512]{2,1,0:T(8,128)(2,1)} %get-tuple-element.32), calls=%async_computation.1 | async-start | bytes 2621440 | tf_op jit(solution)/shard_map/all_to_all | solution.py:600
  118.6 24.0 %factor.1.inv_ref = f32[256,256]{1,0:T(8,128)} custom-call(f32[256,256]{1,0:T(8,128)} %maximum_select_fusion.gram_ref), custom_call_target="tpu_custom_call" | custom-call | flops 20000000000 | bytes 524288 | tf_op jit(solution)/shard_map/factor/pallas_call | solution.py:204
  142.6 1.6 convolution_convert_fusion
  144.2 3.7 %collective-permute-start.17 = (bf16[128,256]{1,0:T(8,128)(2,1)S(1)}, bf16[128,256]{1,0:T(8,128)(2,1)S(1)}, u32[]{:S(2)}, u32[]{:S(2)}) collective-permute-start(bf16[128,256]{1,0:T(8,128)(2,1)S(1)} %convolution_convert_fusion), channel_id=1, source_target_pairs={{0,24},{2,26},{4,28},{6,30},{8,16},{10,18},{12,20},{14,22},{16,8},... | collective-permute-start | bytes 196616 | tf_op jit(solution)/shard_map/ppermute | solution.py:519
  147.9 0.7 collective-permute-start.15
  148.7 0.7 select_reduce_fusion.pos_ref
  149.4 1.0 collective-permute-done.17
  150.4 7.8 %collective-permute-done.16 = bf16[128,256]{1,0:T(8,128)(2,1)S(1)} collective-permute-done((bf16[128,256]{1,0:T(8,128)(2,1)S(1)}, bf16[128,256]{1,0:T(8,128)(2,1)S(1)}, u32[]{:S(2)}, u32[]{:S(2)}) %collective-permute-start.16) | collective-permute-done | bytes 65568 | tf_op jit(solution)/shard_map/ppermute | solution.py:519
  158.3 3.6 %select.24 = bf16[13,128,512]{2,1,0:T(8,128)(2,1)} custom-call(s32[13]{0:T(128)} %select_reduce_fusion.pos_ref, bf16[16,176,512]{2,1,0:T(8,128)(2,1)} %copy-done, bf16[16,80,512]{2,1,0:T(8,128)(2,1)} %all-to-all-done.1.refs_1_), custom_call_target="tpu_custom_call" | custom-call | bytes 3407872 | tf_op jit(solution)/shard_map/select/pallas_call | solution.py:148
  162.0 0.7 select_reduce_fusion.1.w_ref
  162.6 1.7 collective-permute-start.21
  164.4 1.5 collective-permute-start.20
  165.8 0.3 collective-permute-start.19
  166.1 1.2 copy-done.7
  167.3 14.6 %kernel_rows.1 = (bf16[1664,2048]{1,0:T(8,128)(2,1)}, bf16[1664,256]{1,0:T(8,128)(2,1)}) custom-call(f32[13]{0:T(128)} %select_reduce_fusion.1.w_ref, bf16[1664,512]{1,0:T(8,128)(2,1)} %bitcast.17, bf16[1664,512]{1,0:T(8,128)(2,1)} %copy-done.7, bf16[256,1024]{1,0:T(8,128)(2,1)} %get-tuple-element.33.refs_2_, bf16[2048,1024]{1,0:T(8,128)(2,1)} %refs_3_.3), custom_call_target="tpu_custom_call" | custom-call | flops 7851737088 | bytes 14417920 | tf_op jit(solution)/shard_map/kernel_rows/pallas_call | solution.py:427
  182.0 1.1 pad_maximum_fusion.rt_ref
  183.1 9.4 %remainder_rows.1 = (bf16[1664,2048]{1,0:T(8,128)(2,1)}, f32[256,2048]{1,0:T(8,128)}) custom-call(s32[1]{0:T(128)} %bitcast.quarter_ref, bf16[1664,2048]{1,0:T(8,128)(2,1)} %get-tuple-element.36.kern_ref, bf16[1664,256]{1,0:T(8,128)(2,1)} %get-tuple-element.37.p_ref, f32[256,256]{1,0:T(8,128)} %factor.1.inv_ref, bf16[4,512,256]{2,1,0:T(8,128)(2,1)} %pad_maximum_fusion.rt_ref), custom_call_target="tpu_custom_call" | custom-call | flops 1744830464 | bytes 13631488 | tf_op jit(solution)/shard_map/remainder_rows/pallas_call | solution.py:495
  (62 shorter events, 1.5 us)
Async XLA Ops:
  0.6 17.3 %collective-permute-start = (bf16[3200,512]{1,0:T(8,128)(2,1)}, bf16[3200,512]{1,0:T(8,128)(2,1)}, u32[]{:S(2)}, u32[]{:S(2)}) collective-permute-start(bf16[3200,512]{1,0:T(8,128)(2,1)} %refs_0_.3), channel_id=1, source_target_pairs={{0,1},{1,0},{2,3},{3,2},{4,5},{5,4},{6,7},{7,6},{8,9},{9,8},{10,11... | collective-permute-start | bytes 9830408 | tf_op jit(solution)/shard_map/ppermute | solution.py:217
  5.3 10.2 %copy-start.2 = (s32[16,25]{1,0:T(8,128)S(1)}, s32[16,25]{1,0:T(8,128)}, u32[]{:S(2)}) copy-start(s32[16,25]{1,0:T(8,128)} %dest_ref.1) | copy-start | bytes 4804
  5.3 10.2 %copy-start.4 = (s32[16]{0:T(128)S(1)}, s32[16]{0:T(128)}, u32[]{:S(2)}) copy-start(s32[16]{0:T(128)} %cnt_ref.3) | copy-start | bytes 196
  5.3 10.5 %copy-start.8 = (bf16[25]{0:T(256)(128)(2,1)S(1)}, bf16[25]{0:T(256)(128)(2,1)}, u32[]{:S(2)}) copy-start(bf16[25]{0:T(256)(128)(2,1)} %param.7) | copy-start | bytes 154
  5.3 107.1 %all-to-all-start = ((bf16[16,176,512]{2,1,0:T(8,128)(2,1)}), bf16[16,176,512]{2,1,0:T(8,128)(2,1)S(1)}, u32[]{:S(2)}, u32[]{:S(2)}) async-start(bf16[16,176,512]{2,1,0:T(8,128)(2,1)} %get-tuple-element.31), calls=%async_computation | async-start | bytes 5767168 | tf_op jit(solution)/shard_map/all_to_all | solution.py:568
  15.3 2.6 %collective-permute-start.1 = (bf16[256,1024]{1,0:T(8,128)(2,1)}, bf16[256,1024]{1,0:T(8,128)(2,1)S(1)}, u32[]{:S(2)}, u32[]{:S(2)}) collective-permute-start(bf16[256,1024]{1,0:T(8,128)(2,1)} %slice.25), channel_id=1, source_target_pairs={{0,1},{1,0},{2,3},{3,2},{4,5},{5,4},{6,7},{7,6},{8,9},{9,8},{10,11... | collective-permute-start | bytes 1572872 | tf_op jit(solution)/shard_map/ppermute | solution.py:563
  17.9 0.8 copy-start.1
  29.6 28.3 %collective-permute-start.3 = (f32[136,256]{1,0:T(8,128)S(1)}, f32[136,256]{1,0:T(8,128)S(1)}, u32[]{:S(2)}, u32[]{:S(2)}) collective-permute-start(f32[136,256]{1,0:T(8,128)S(1)} %pad_maximum_fusion.2), channel_id=1, source_target_pairs={{0,4},{2,6},{4,0},{6,2},{8,12},{10,14},{12,8},{14,10},{16,20},{18,... | collective-permute-start | bytes 417800 | tf_op jit(solution)/shard_map/ppermute | solution.py:519
  29.7 28.2 %collective-permute-start.4 = (f32[136,256]{1,0:T(8,128)S(1)}, f32[136,256]{1,0:T(8,128)S(1)}, u32[]{:S(2)}, u32[]{:S(2)}) collective-permute-start(f32[136,256]{1,0:T(8,128)S(1)} %pad_maximum_fusion.2), channel_id=1, source_target_pairs={{0,6},{2,4},{4,2},{6,0},{8,14},{10,12},{12,10},{14,8},{16,22},{18,... | collective-permute-start | bytes 417800 | tf_op jit(solution)/shard_map/ppermute | solution.py:519
  30.4 27.5 %collective-permute-start.2 = (f32[136,256]{1,0:T(8,128)S(1)}, f32[136,256]{1,0:T(8,128)S(1)}, u32[]{:S(2)}, u32[]{:S(2)}) collective-permute-start(f32[136,256]{1,0:T(8,128)S(1)} %pad_maximum_fusion.2), channel_id=1, source_target_pairs={{0,2},{2,0},{4,6},{6,4},{8,10},{10,8},{12,14},{14,12},{16,18},{18,... | collective-permute-start | bytes 417800 | tf_op jit(solution)/shard_map/ppermute | solution.py:519
  58.0 11.0 %collective-permute-start.7 = (f32[136,256]{1,0:T(8,128)S(1)}, f32[136,256]{1,0:T(8,128)S(1)}, u32[]{:S(2)}, u32[]{:S(2)}) collective-permute-start(f32[136,256]{1,0:T(8,128)S(1)} %add_add_fusion.2), channel_id=1, source_target_pairs={{0,24},{2,26},{4,28},{6,30},{8,16},{10,18},{12,20},{14,22},{16,8},... | collective-permute-start | bytes 417800 | tf_op jit(solution)/shard_map/ppermute | solution.py:519
  61.0 31.2 %collective-permute-start.6 = (f32[136,256]{1,0:T(8,128)S(1)}, f32[136,256]{1,0:T(8,128)S(1)}, u32[]{:S(2)}, u32[]{:S(2)}) collective-permute-start(f32[136,256]{1,0:T(8,128)S(1)} %add_add_fusion.2), channel_id=1, source_target_pairs={{0,16},{2,18},{4,20},{6,22},{8,24},{10,26},{12,28},{14,30},{16,0},... | collective-permute-start | bytes 417800 | tf_op jit(solution)/shard_map/ppermute | solution.py:519
  61.2 31.0 %collective-permute-start.5 = (f32[136,256]{1,0:T(8,128)S(1)}, f32[136,256]{1,0:T(8,128)S(1)}, u32[]{:S(2)}, u32[]{:S(2)}) collective-permute-start(f32[136,256]{1,0:T(8,128)S(1)} %add_add_fusion.2), channel_id=1, source_target_pairs={{0,8},{2,10},{4,12},{6,14},{8,0},{10,2},{12,4},{14,6},{16,24},{18,... | collective-permute-start | bytes 417800 | tf_op jit(solution)/shard_map/ppermute | solution.py:519
  63.9 30.5 %collective-permute-start.8 = (f32[512,256]{1,0:T(8,128)S(1)}, f32[512,256]{1,0:T(8,128)S(1)}, u32[]{:S(2)}, u32[]{:S(2)}) collective-permute-start(f32[512,256]{1,0:T(8,128)S(1)} %get-tuple-element.44), channel_id=1, source_target_pairs={{0,2},{2,0},{4,6},{6,4},{8,10},{10,8},{12,14},{14,12},{16,18},{18,... | collective-permute-start | bytes 1572872 | tf_op jit(solution)/shard_map/ppermute | solution.py:519
  64.7 29.7 %collective-permute-start.10 = (f32[512,256]{1,0:T(8,128)S(1)}, f32[512,256]{1,0:T(8,128)S(1)}, u32[]{:S(2)}, u32[]{:S(2)}) collective-permute-start(f32[512,256]{1,0:T(8,128)S(1)} %get-tuple-element.45), channel_id=1, source_target_pairs={{0,6},{2,4},{4,2},{6,0},{8,14},{10,12},{12,10},{14,8},{16,22},{18,... | collective-permute-start | bytes 1572872 | tf_op jit(solution)/shard_map/ppermute | solution.py:519
  69.0 29.0 %collective-permute-start.9 = (f32[512,256]{1,0:T(8,128)S(1)}, f32[512,256]{1,0:T(8,128)S(1)}, u32[]{:S(2)}, u32[]{:S(2)}) collective-permute-start(f32[512,256]{1,0:T(8,128)S(1)} %get-tuple-element.46), channel_id=1, source_target_pairs={{0,4},{2,6},{4,0},{6,2},{8,12},{10,14},{12,8},{14,10},{16,20},{18,... | collective-permute-start | bytes 1572872 | tf_op jit(solution)/shard_map/ppermute | solution.py:519
  92.3 1.4 collective-permute-start.11
  99.9 42.7 %collective-permute-start.12 = (f32[128,256]{1,0:T(8,128)}, f32[128,256]{1,0:T(8,128)}, u32[]{:S(2)}, u32[]{:S(2)}) collective-permute-start(f32[128,256]{1,0:T(8,128)} %get-tuple-element.47), channel_id=1, source_target_pairs={{0,8},{2,10},{4,12},{6,14},{8,0},{10,2},{12,4},{14,6},{16,24},{18,... | collective-permute-start | bytes 393224 | tf_op jit(solution)/shard_map/ppermute | solution.py:519
  111.0 31.7 %collective-permute-start.14 = (f32[128,256]{1,0:T(8,128)}, f32[128,256]{1,0:T(8,128)}, u32[]{:S(2)}, u32[]{:S(2)}) collective-permute-start(f32[128,256]{1,0:T(8,128)} %get-tuple-element.48), channel_id=1, source_target_pairs={{0,24},{2,26},{4,28},{6,30},{8,16},{10,18},{12,20},{14,22},{16,8},... | collective-permute-start | bytes 393224 | tf_op jit(solution)/shard_map/ppermute | solution.py:519
  111.9 30.8 %collective-permute-start.13 = (f32[128,256]{1,0:T(8,128)}, f32[128,256]{1,0:T(8,128)}, u32[]{:S(2)}, u32[]{:S(2)}) collective-permute-start(f32[128,256]{1,0:T(8,128)} %get-tuple-element.49), channel_id=1, source_target_pairs={{0,16},{2,18},{4,20},{6,22},{8,24},{10,26},{12,28},{14,30},{16,0},... | collective-permute-start | bytes 393224 | tf_op jit(solution)/shard_map/ppermute | solution.py:519
  112.4 30.2 %copy-start = (bf16[16,176,512]{2,1,0:T(8,128)(2,1)}, bf16[16,176,512]{2,1,0:T(8,128)(2,1)S(1)}, u32[]{:S(2)}) copy-start(bf16[16,176,512]{2,1,0:T(8,128)(2,1)S(1)} %all-to-all-done.refs_0_) | copy-start | bytes 8650756
  112.4 45.8 %all-to-all-start.1 = ((bf16[16,80,512]{2,1,0:T(8,128)(2,1)}), bf16[16,80,512]{2,1,0:T(8,128)(2,1)}, u32[]{:S(2)}, u32[]{:S(2)}) async-start(bf16[16,80,512]{2,1,0:T(8,128)(2,1)} %get-tuple-element.32), calls=%async_computation.1 | async-start | bytes 2621440 | tf_op jit(solution)/shard_map/all_to_all | solution.py:600
  118.6 30.1 %copy-start.3 = (s32[400]{0:T(512)S(1)}, s32[400]{0:T(512)}, u32[]{:S(2)}) copy-start(s32[400]{0:T(512)} %broadcast_in_dim.42) | copy-start | bytes 4804
  118.6 30.1 %copy-start.5 = (pred[400]{0:T(512)(128)(4,1)S(1)}, pred[400]{0:T(512)(128)(4,1)}, u32[]{:S(2)}) copy-start(pred[400]{0:T(512)(128)(4,1)} %broadcast_compare_fusion) | copy-start | bytes 1204
  144.2 6.2 %collective-permute-start.17 = (bf16[128,256]{1,0:T(8,128)(2,1)S(1)}, bf16[128,256]{1,0:T(8,128)(2,1)S(1)}, u32[]{:S(2)}, u32[]{:S(2)}) collective-permute-start(bf16[128,256]{1,0:T(8,128)(2,1)S(1)} %convolution_convert_fusion), channel_id=1, source_target_pairs={{0,24},{2,26},{4,28},{6,30},{8,16},{10,18},{12,20},{14,22},{16,8},... | collective-permute-start | bytes 196616 | tf_op jit(solution)/shard_map/ppermute | solution.py:519
  147.9 10.2 %collective-permute-start.16 = (bf16[128,256]{1,0:T(8,128)(2,1)S(1)}, bf16[128,256]{1,0:T(8,128)(2,1)S(1)}, u32[]{:S(2)}, u32[]{:S(2)}) collective-permute-start(bf16[128,256]{1,0:T(8,128)(2,1)S(1)} %convolution_convert_fusion), channel_id=1, source_target_pairs={{0,16},{2,18},{4,20},{6,22},{8,24},{10,26},{12,28},{14,30},{16,0},... | collective-permute-start | bytes 196616 | tf_op jit(solution)/shard_map/ppermute | solution.py:519
  147.9 10.2 %collective-permute-start.15 = (bf16[128,256]{1,0:T(8,128)(2,1)S(1)}, bf16[128,256]{1,0:T(8,128)(2,1)S(1)}, u32[]{:S(2)}, u32[]{:S(2)}) collective-permute-start(bf16[128,256]{1,0:T(8,128)(2,1)S(1)} %convolution_convert_fusion), channel_id=1, source_target_pairs={{0,8},{2,10},{4,12},{6,14},{8,0},{10,2},{12,4},{14,6},{16,24},{18,... | collective-permute-start | bytes 196616 | tf_op jit(solution)/shard_map/ppermute | solution.py:519
  158.2 3.7 %copy-start.6 = (pred[400]{0:T(512)(128)(4,1)S(1)}, pred[400]{0:T(512)(128)(4,1)}, u32[]{:S(2)}) copy-start(pred[400]{0:T(512)(128)(4,1)} %broadcast_compare_fusion) | copy-start | bytes 1204
  161.9 4.3 %collective-permute-start.18 = (bf16[1664,512]{1,0:T(8,128)(2,1)}, bf16[1664,512]{1,0:T(8,128)(2,1)S(1)}, u32[]{:S(2)}, u32[]{:S(2)}) collective-permute-start(bf16[1664,512]{1,0:T(8,128)(2,1)} %bitcast.16), channel_id=1, source_target_pairs={{0,1},{1,0},{2,3},{3,2},{4,5},{5,4},{6,7},{7,6},{8,9},{9,8},{10,11... | collective-permute-start | bytes 5111816 | tf_op jit(solution)/shard_map/ppermute | solution.py:217
  162.6 19.3 %collective-permute-start.21 = (bf16[512,256]{1,0:T(8,128)(2,1)S(1)}, bf16[512,256]{1,0:T(8,128)(2,1)S(1)}, u32[]{:S(2)}, u32[]{:S(2)}) collective-permute-start(bf16[512,256]{1,0:T(8,128)(2,1)S(1)} %pad_maximum_fusion.1), channel_id=1, source_target_pairs={{0,6},{2,4},{4,2},{6,0},{8,14},{10,12},{12,10},{14,8},{16,22},{18,... | collective-permute-start | bytes 786440 | tf_op jit(solution)/shard_map/ppermute | solution.py:519
  164.4 17.6 %collective-permute-start.20 = (bf16[512,256]{1,0:T(8,128)(2,1)S(1)}, bf16[512,256]{1,0:T(8,128)(2,1)S(1)}, u32[]{:S(2)}, u32[]{:S(2)}) collective-permute-start(bf16[512,256]{1,0:T(8,128)(2,1)S(1)} %pad_maximum_fusion.1), channel_id=1, source_target_pairs={{0,4},{2,6},{4,0},{6,2},{8,12},{10,14},{12,8},{14,10},{16,20},{18,... | collective-permute-start | bytes 786440 | tf_op jit(solution)/shard_map/ppermute | solution.py:519
  165.8 16.1 %collective-permute-start.19 = (bf16[512,256]{1,0:T(8,128)(2,1)S(1)}, bf16[512,256]{1,0:T(8,128)(2,1)S(1)}, u32[]{:S(2)}, u32[]{:S(2)}) collective-permute-start(bf16[512,256]{1,0:T(8,128)(2,1)S(1)} %pad_maximum_fusion.1), channel_id=1, source_target_pairs={{0,2},{2,0},{4,6},{6,4},{8,10},{10,8},{12,14},{14,12},{16,18},{18,... | collective-permute-start | bytes 786440 | tf_op jit(solution)/shard_map/ppermute | solution.py:519
  166.1 1.2 copy-start.7

commit v11 on v10

--- a/solution.py
+++ b/solution.py
@@ -595,13 +595,15 @@
     if per_pair > 1:
         g, gram, last = lax.optimization_barrier((g, gram, outgoing[1]))
     for pair in pairs[1:]:
-        g = scatter_sum(g, pair)
+        n = g.shape[0] // 4
+        q = quarter_of(pair)
+        far = [lax.dynamic_slice_in_dim(g, (q ^ k) * n, n, 0) for k in range(4)]
+        far = [far[0]] + [trade(far[k], pair, k) for k in range(1, 4)]
+        if pair != pairs[-1]:
+            g = (far[0] + far[1]) + (far[2] + far[3])
     if per_pair > 1:
         received.append(lax.all_to_all(last, "rows", split_axis=0, concat_axis=0, tiled=True))
     inverse = factor(gram)
-    rt = nt(g, inverse, HIGH).astype(jnp.bfloat16)
-    for pair in pairs[:0:-1]:
-        rt = gather_back(rt, pair)
 
     slot_ids = jnp.arange(slots, dtype=jnp.int32)
     toward = ((slot_ids[None, :] < block_counts[:, None]) & (destinations == me)).astype(jnp.int32)
@@ -613,9 +615,14 @@
     positions = jnp.sum(jnp.where(hit, where_from[None, :], 0), axis=1)
     weights_here = jnp.sum(jnp.where(hit, all_weights[None, :], 0.0), axis=1)
 
-    rt, positions = lax.optimization_barrier((rt, positions))
+    inverse, positions = lax.optimization_barrier((inverse, positions))
     arrived = select(received, positions).reshape(DST_BLK * BLK, feat)
     kern, panel = kernel_rows(share_parts(arrived), weights_here, panel_points, sparse_points)
+    kern, *far = lax.optimization_barrier((kern, *far))
+    g = (far[0] + far[1]) + (far[2] + far[3])
+    rt = nt(g, inverse, HIGH).astype(jnp.bfloat16)
+    for pair in pairs[:0:-1]:
+        rt = gather_back(rt, pair)
     pieces = gather_pieces(rt, pairs[0])
     kern, *pieces = lax.optimization_barrier((kern, *pieces))
     rt = jnp.stack(pieces)

time: 193 us -> 203 us (1.052)
  waiting for transfers between devices: 35.3 us -> 43.8 us
  other arithmetic: 6.52 us -> 9.07 us
    ppermute x18, waiting for transfers between devices: 34.5 us -> 42.2 us  [trade(): return lax.ppermute(x, 'rows', flips(bit, lax.axis_size('rows')))]
    ppermute x18, starting transfers between devices: 34.7 us -> 27 us  [trade(): return lax.ppermute(x, 'rows', flips(bit, lax.axis_size('rows')))]
    all_to_all x1, starting transfers between devices: 6.16 us -> 13.2 us  [on_device(): lax.all_to_all(last, 'rows', split_axis=0, concat_axis=0, tiled=True)]
  transfers between devices with their start and end apart: 24 -> 24, of which waited for: 6 -> 10; matrix products, arithmetic and copies ran while one was open for 7% -> 7% of each run, Pallas kernels for 40% -> 38%
where the time goes in v11:
time: 203 us; the launch traced here: 202 us
  Pallas kernels  90.4 us (45%)
  starting transfers between devices  48.8 us (24%)
  waiting for transfers between devices  43.8 us (22%)
  other arithmetic  9.07 us (4%)
  local copies, waits for them, and re-layouts  8.54 us (4%)
    ppermute x18, waiting for transfers between devices, trade(): return lax.ppermute(x, 'rows', flips(bit, lax.axis_size('rows')))  42.2 us
    ppermute x18, starting transfers between devices, trade(): return lax.ppermute(x, 'rows', flips(bit, lax.axis_size('rows')))  27 us
    pallas_call x1, Pallas kernels, column_products(): pl.pallas_call(functools.partial(column_kernel, len(parts)), grid=(size /...  24.7 us
    pallas_call x1, Pallas kernels, factor(): pl.pallas_call(functools.partial(factor_kernel, 64), out_shape=jax.ShapeD...  24 us
    pallas_call x1, Pallas kernels, kernel_rows(): pl.pallas_call(functools.partial(rows_kernel, len(parts)), grid=(cols //...  14.6 us
    all_to_all x1, starting transfers between devices, on_device(): lax.all_to_all(last, 'rows', split_axis=0, concat_axis=0, tiled=True)  13.2 us
    pallas_call x1, Pallas kernels, panel_products(): pl.pallas_call(functools.partial(panel_kernel, len(parts)), out_shape=(ja...  9.88 us
    pallas_call x1, Pallas kernels, remainder_rows(): pl.pallas_call(functools.partial(remainder_kernel, norm), grid_spec=spec,...  9.44 us
  transfers between devices with their start and end apart: 24, of which 10 were waited for; matrix products, arithmetic and copies ran while one was open for 7% of the time, Pallas kernels for 38%

profile of v11, /device:TPU:0, one launch (start us, length us, event | category | flops | bytes accessed | tf_op | source)
XLA Modules:
  0.0 202.1 jit_solution(1295322240689657694)
XLA Ops:
  1.1 4.1 %pack.1 = (bf16[16,176,512]{2,1,0:T(8,128)(2,1)}, bf16[16,80,512]{2,1,0:T(8,128)(2,1)}) custom-call(s32[16,25]{1,0:T(8,128)} %dest_ref.1, s32[16]{0:T(128)} %cnt_ref.3, bf16[25,128,512]{2,1,0:T(8,128)(2,1)} %bitcast.15), custom_call_target="tpu_custom_call" | custom-call | bytes 6553600 | tf_op jit(solution)/shard_map/pack/pallas_call | solution.py:111
  5.3 7.7 %all-to-all-start = ((bf16[16,176,512]{2,1,0:T(8,128)(2,1)}), bf16[16,176,512]{2,1,0:T(8,128)(2,1)S(1)}, u32[]{:S(2)}, u32[]{:S(2)}) async-start(bf16[16,176,512]{2,1,0:T(8,128)(2,1)} %get-tuple-element.35), calls=%async_computation | async-start | bytes 5767168 | tf_op jit(solution)/shard_map/all_to_all | solution.py:568
  13.0 1.9 slice.25
  15.5 0.5 convert_element_type.10.w_ref
  16.4 0.6 reduce-window.12
  17.2 0.8 copy-done.2
  18.0 9.9 %panel_products.1 = (f32[256,256]{1,0:T(8,128)}, bf16[3200,256]{1,0:T(8,128)(2,1)}, bf16[256,1024]{1,0:T(8,128)(2,1)}) custom-call(s32[16]{0:T(128)} %cnt_ref.3, f32[25]{0:T(128)} %convert_element_type.10.w_ref, bf16[3200,512]{1,0:T(8,128)(2,1)} %refs_0_.3, bf16[3200,512]{1,0:T(8,128)(2,1)} %collective-permute-done.refs_1_, bf16[2048,1024]{1,0:T(8,128)(2,1)} %refs_3_.3, ...), custom_call_target="tpu_custom_call" | custom-call | flops 2097152000 | bytes 6553600 | tf_op jit(solution)/shard_map/panel_products/pallas_call | solution.py:320
  27.9 0.9 constant_dynamic-slice_fusion.7
  28.9 3.2 %collective-permute-start.4 = (f32[136,256]{1,0:T(8,128)S(1)}, f32[136,256]{1,0:T(8,128)S(1)}, u32[]{:S(2)}, u32[]{:S(2)}) collective-permute-start(f32[136,256]{1,0:T(8,128)S(1)} %pad_maximum_fusion.2), channel_id=1, source_target_pairs={{0,6},{2,4},{4,2},{6,0},{8,14},{10,12},{12,10},{14,8},{16,22},{18,... | collective-permute-start | bytes 417800 | tf_op jit(solution)/shard_map/ppermute | solution.py:519
  32.4 24.7 %column_products.1 = f32[2048,256]{1,0:T(8,128)} custom-call(bf16[3200,512]{1,0:T(8,128)(2,1)} %refs_0_.3, bf16[3200,512]{1,0:T(8,128)(2,1)} %collective-permute-done.refs_1_, bf16[3200,256]{1,0:T(8,128)(2,1)} %get-tuple-element.29.refs_2_, bf16[2048,1024]{1,0:T(8,128)(2,1)} %refs_3_.3), custom_call_target="tpu_custom_call" | custom-call | flops 16777216000 | bytes 6553600 | tf_op jit(solution)/shard_map/column_products/pallas_call | solution.py:369
  57.2 3.6 %collective-permute-start.7 = (f32[136,256]{1,0:T(8,128)S(1)}, f32[136,256]{1,0:T(8,128)S(1)}, u32[]{:S(2)}, u32[]{:S(2)}) collective-permute-start(f32[136,256]{1,0:T(8,128)S(1)} %add_add_fusion.2), channel_id=1, source_target_pairs={{0,24},{2,26},{4,28},{6,30},{8,16},{10,18},{12,20},{14,22},{16,8},... | collective-permute-start | bytes 417800 | tf_op jit(solution)/shard_map/ppermute | solution.py:519
  60.8 0.8 collective-permute-start.5
  61.7 1.5 constant_dynamic-slice_fusion.6
  63.1 1.8 collective-permute-start.8
  65.0 3.6 %collective-permute-done.7 = f32[136,256]{1,0:T(8,128)S(1)} collective-permute-done((f32[136,256]{1,0:T(8,128)S(1)}, f32[136,256]{1,0:T(8,128)S(1)}, u32[]{:S(2)}, u32[]{:S(2)}) %collective-permute-start.7) | collective-permute-done | bytes 139296 | tf_op jit(solution)/shard_map/ppermute | solution.py:519
  68.6 3.7 %collective-permute-start.9 = (f32[512,256]{1,0:T(8,128)S(1)}, f32[512,256]{1,0:T(8,128)S(1)}, u32[]{:S(2)}, u32[]{:S(2)}) collective-permute-start(f32[512,256]{1,0:T(8,128)S(1)} %get-tuple-element.56), channel_id=1, source_target_pairs={{0,4},{2,6},{4,0},{6,2},{8,12},{10,14},{12,8},{14,10},{16,20},{18,... | collective-permute-start | bytes 1572872 | tf_op jit(solution)/shard_map/ppermute | solution.py:519
  72.3 19.3 %collective-permute-done.6 = f32[136,256]{1,0:T(8,128)S(1)} collective-permute-done((f32[136,256]{1,0:T(8,128)S(1)}, f32[136,256]{1,0:T(8,128)S(1)}, u32[]{:S(2)}, u32[]{:S(2)}) %collective-permute-start.6) | collective-permute-done | bytes 139296 | tf_op jit(solution)/shard_map/ppermute | solution.py:519
  91.8 0.5 broadcast_compare_fusion
  92.3 0.8 collective-permute-done.11
  93.1 0.7 maximum_select_fusion.gram_ref
  93.9 3.5 %collective-permute-done.9 = f32[512,256]{1,0:T(8,128)S(1)} collective-permute-done((f32[512,256]{1,0:T(8,128)S(1)}, f32[512,256]{1,0:T(8,128)S(1)}, u32[]{:S(2)}, u32[]{:S(2)}) %collective-permute-start.9) | collective-permute-done | bytes 524320 | tf_op jit(solution)/shard_map/ppermute | solution.py:519
  97.4 1.2 add_add_fusion
  98.6 13.2 %all-to-all-start.1 = ((bf16[16,80,512]{2,1,0:T(8,128)(2,1)}), bf16[16,80,512]{2,1,0:T(8,128)(2,1)}, u32[]{:S(2)}, u32[]{:S(2)}) async-start(bf16[16,80,512]{2,1,0:T(8,128)(2,1)} %get-tuple-element.36), calls=%async_computation.1 | async-start | bytes 2621440 | tf_op jit(solution)/shard_map/all_to_all | solution.py:605
  111.8 1.4 slice_reduce_fusion
  113.2 0.7 broadcast_in_dim.42
  113.9 0.7 add_bitcast_fusion
  114.6 0.7 slice_subtract_fusion
  115.3 1.3 select_reduce_fusion.pos_ref
  116.6 24.0 %factor.1.inv_ref = f32[256,256]{1,0:T(8,128)} custom-call(f32[256,256]{1,0:T(8,128)} %maximum_select_fusion.gram_ref), custom_call_target="tpu_custom_call" | custom-call | flops 20000000000 | bytes 524288 | tf_op jit(solution)/shard_map/factor/pallas_call | solution.py:204
  140.6 0.7 all-to-all-done.1.refs_1_
  141.4 3.6 %select.24 = bf16[13,128,512]{2,1,0:T(8,128)(2,1)} custom-call(s32[13]{0:T(128)} %select_reduce_fusion.pos_ref, bf16[16,176,512]{2,1,0:T(8,128)(2,1)} %copy-done, bf16[16,80,512]{2,1,0:T(8,128)(2,1)} %all-to-all-done.1.refs_1_), custom_call_target="tpu_custom_call" | custom-call | bytes 3407872 | tf_op jit(solution)/shard_map/select/pallas_call | solution.py:148
  145.2 0.7 select_reduce_fusion.1.w_ref
  145.9 3.7 %collective-permute-start.15 = (f32[128,256]{1,0:T(8,128)S(1)}, f32[128,256]{1,0:T(8,128)S(1)}, u32[]{:S(2)}, u32[]{:S(2)}) collective-permute-start(f32[128,256]{1,0:T(8,128)S(1)} %get-tuple-element.57), channel_id=1, source_target_pairs={{0,24},{2,26},{4,28},{6,30},{8,16},{10,18},{12,20},{14,22},{16,8},... | collective-permute-start | bytes 393224 | tf_op jit(solution)/shard_map/ppermute | solution.py:519
  149.7 1.7 collective-permute-start.14
  151.4 1.2 copy-done.9
  152.6 14.6 %kernel_rows.1 = (bf16[1664,2048]{1,0:T(8,128)(2,1)}, bf16[1664,256]{1,0:T(8,128)(2,1)}) custom-call(f32[13]{0:T(128)} %select_reduce_fusion.1.w_ref, bf16[1664,512]{1,0:T(8,128)(2,1)} %bitcast.17, bf16[1664,512]{1,0:T(8,128)(2,1)} %copy-done.9, bf16[256,1024]{1,0:T(8,128)(2,1)} %get-tuple-element.37.refs_2_, bf16[2048,1024]{1,0:T(8,128)(2,1)} %refs_3_.3), custom_call_target="tpu_custom_call" | custom-call | flops 7851737088 | bytes 14417920 | tf_op jit(solution)/shard_map/kernel_rows/pallas_call | solution.py:427
  167.7 2.7 %collective-permute-start.18 = (bf16[128,256]{1,0:T(8,128)(2,1)S(1)}, bf16[128,256]{1,0:T(8,128)(2,1)S(1)}, u32[]{:S(2)}, u32[]{:S(2)}) collective-permute-start(bf16[128,256]{1,0:T(8,128)(2,1)S(1)} %convolution_convert_fusion), channel_id=1, source_target_pairs={{0,24},{2,26},{4,28},{6,30},{8,16},{10,18},{12,20},{14,22},{16,8},... | collective-permute-start | bytes 196616 | tf_op jit(solution)/shard_map/ppermute | solution.py:519
  170.4 0.8 collective-permute-start.17
  171.2 0.9 collective-permute-start.16
  172.1 2.1 %collective-permute-done.18 = bf16[128,256]{1,0:T(8,128)(2,1)S(1)} collective-permute-done((bf16[128,256]{1,0:T(8,128)(2,1)S(1)}, bf16[128,256]{1,0:T(8,128)(2,1)S(1)}, u32[]{:S(2)}, u32[]{:S(2)}) %collective-permute-start.18) | collective-permute-done | bytes 65568 | tf_op jit(solution)/shard_map/ppermute | solution.py:519
  174.3 2.7 %collective-permute-done.17 = bf16[128,256]{1,0:T(8,128)(2,1)S(1)} collective-permute-done((bf16[128,256]{1,0:T(8,128)(2,1)S(1)}, bf16[128,256]{1,0:T(8,128)(2,1)S(1)}, u32[]{:S(2)}, u32[]{:S(2)}) %collective-permute-start.17) | collective-permute-done | bytes 65568 | tf_op jit(solution)/shard_map/ppermute | solution.py:519
  177.1 1.8 collective-permute-start.21
  178.9 0.6 collective-permute-start.20
  179.5 1.2 collective-permute-start.19
  180.6 6.7 %collective-permute-done.21 = bf16[512,256]{1,0:T(8,128)(2,1)S(1)} collective-permute-done((bf16[512,256]{1,0:T(8,128)(2,1)S(1)}, bf16[512,256]{1,0:T(8,128)(2,1)S(1)}, u32[]{:S(2)}, u32[]{:S(2)}) %collective-permute-start.21) | collective-permute-done | bytes 262176 | tf_op jit(solution)/shard_map/ppermute | solution.py:519
  187.3 4.0 %collective-permute-done.20 = bf16[512,256]{1,0:T(8,128)(2,1)S(1)} collective-permute-done((bf16[512,256]{1,0:T(8,128)(2,1)S(1)}, bf16[512,256]{1,0:T(8,128)(2,1)S(1)}, u32[]{:S(2)}, u32[]{:S(2)}) %collective-permute-start.20) | collective-permute-done | bytes 262176 | tf_op jit(solution)/shard_map/ppermute | solution.py:519
  191.5 1.1 pad_maximum_fusion.rt_ref
  192.6 9.4 %remainder_rows.1 = (bf16[1664,2048]{1,0:T(8,128)(2,1)}, f32[256,2048]{1,0:T(8,128)}) custom-call(s32[1]{0:T(128)} %bitcast.quarter_ref, bf16[1664,2048]{1,0:T(8,128)(2,1)} %get-tuple-element.46.kern_ref, bf16[1664,256]{1,0:T(8,128)(2,1)} %get-tuple-element.47.p_ref, f32[256,256]{1,0:T(8,128)} %factor.1.inv_ref, bf16[4,512,256]{2,1,0:T(8,128)(2,1)} %pad_maximum_fusion.rt_ref), custom_call_target="tpu_custom_call" | custom-call | flops 1744830464 | bytes 13631488 | tf_op jit(solution)/shard_map/remainder_rows/pallas_call | solution.py:495
  (66 shorter events, 3.0 us)
Async XLA Ops:
  0.6 16.6 %collective-permute-start = (bf16[3200,512]{1,0:T(8,128)(2,1)}, bf16[3200,512]{1,0:T(8,128)(2,1)}, u32[]{:S(2)}, u32[]{:S(2)}) collective-permute-start(bf16[3200,512]{1,0:T(8,128)(2,1)} %refs_0_.3), channel_id=1, source_target_pairs={{0,1},{1,0},{2,3},{3,2},{4,5},{5,4},{6,7},{7,6},{8,9},{9,8},{10,11... | collective-permute-start | bytes 9830408 | tf_op jit(solution)/shard_map/ppermute | solution.py:217
  5.3 9.8 %copy-start.3 = (s32[16,25]{1,0:T(8,128)S(1)}, s32[16,25]{1,0:T(8,128)}, u32[]{:S(2)}) copy-start(s32[16,25]{1,0:T(8,128)} %dest_ref.1) | copy-start | bytes 4804
  5.3 9.8 %copy-start.7 = (s32[16]{0:T(128)S(1)}, s32[16]{0:T(128)}, u32[]{:S(2)}) copy-start(s32[16]{0:T(128)} %cnt_ref.3) | copy-start | bytes 196
  5.3 10.2 %copy-start.10 = (bf16[25]{0:T(256)(128)(2,1)S(1)}, bf16[25]{0:T(256)(128)(2,1)}, u32[]{:S(2)}) copy-start(bf16[25]{0:T(256)(128)(2,1)} %param.7) | copy-start | bytes 154
  5.3 93.3 %all-to-all-start = ((bf16[16,176,512]{2,1,0:T(8,128)(2,1)}), bf16[16,176,512]{2,1,0:T(8,128)(2,1)S(1)}, u32[]{:S(2)}, u32[]{:S(2)}) async-start(bf16[16,176,512]{2,1,0:T(8,128)(2,1)} %get-tuple-element.35), calls=%async_computation | async-start | bytes 5767168 | tf_op jit(solution)/shard_map/all_to_all | solution.py:568
  14.9 2.3 %collective-permute-start.1 = (bf16[256,1024]{1,0:T(8,128)(2,1)}, bf16[256,1024]{1,0:T(8,128)(2,1)S(1)}, u32[]{:S(2)}, u32[]{:S(2)}) collective-permute-start(bf16[256,1024]{1,0:T(8,128)(2,1)} %slice.25), channel_id=1, source_target_pairs={{0,1},{1,0},{2,3},{3,2},{4,5},{5,4},{6,7},{7,6},{8,9},{9,8},{10,11... | collective-permute-start | bytes 1572872 | tf_op jit(solution)/shard_map/ppermute | solution.py:563
  15.3 12.6 %copy-start.4 = (s32[400]{0:T(512)}, s32[400]{0:T(512)S(1)}, u32[]{:S(2)}) copy-start(s32[400]{0:T(512)S(1)} %broadcast_in_dim_reshape.4) | copy-start | bytes 4804
  16.3 0.7 copy-start.6
  17.2 0.8 copy-start.2
  28.8 28.3 %collective-permute-start.3 = (f32[136,256]{1,0:T(8,128)S(1)}, f32[136,256]{1,0:T(8,128)S(1)}, u32[]{:S(2)}, u32[]{:S(2)}) collective-permute-start(f32[136,256]{1,0:T(8,128)S(1)} %pad_maximum_fusion.2), channel_id=1, source_target_pairs={{0,4},{2,6},{4,0},{6,2},{8,12},{10,14},{12,8},{14,10},{16,20},{18,... | collective-permute-start | bytes 417800 | tf_op jit(solution)/shard_map/ppermute | solution.py:519
  28.9 28.2 %collective-permute-start.4 = (f32[136,256]{1,0:T(8,128)S(1)}, f32[136,256]{1,0:T(8,128)S(1)}, u32[]{:S(2)}, u32[]{:S(2)}) collective-permute-start(f32[136,256]{1,0:T(8,128)S(1)} %pad_maximum_fusion.2), channel_id=1, source_target_pairs={{0,6},{2,4},{4,2},{6,0},{8,14},{10,12},{12,10},{14,8},{16,22},{18,... | collective-permute-start | bytes 417800 | tf_op jit(solution)/shard_map/ppermute | solution.py:519
  32.1 25.0 %collective-permute-start.2 = (f32[136,256]{1,0:T(8,128)S(1)}, f32[136,256]{1,0:T(8,128)S(1)}, u32[]{:S(2)}, u32[]{:S(2)}) collective-permute-start(f32[136,256]{1,0:T(8,128)S(1)} %pad_maximum_fusion.2), channel_id=1, source_target_pairs={{0,2},{2,0},{4,6},{6,4},{8,10},{10,8},{12,14},{14,12},{16,18},{18,... | collective-permute-start | bytes 417800 | tf_op jit(solution)/shard_map/ppermute | solution.py:519
  57.2 34.6 %copy-start.5 = (s32[400]{0:T(512)S(1)}, s32[400]{0:T(512)}, u32[]{:S(2)}) copy-start(s32[400]{0:T(512)} %copy-done.4) | copy-start | bytes 4804
  57.2 11.4 %collective-permute-start.7 = (f32[136,256]{1,0:T(8,128)S(1)}, f32[136,256]{1,0:T(8,128)S(1)}, u32[]{:S(2)}, u32[]{:S(2)}) collective-permute-start(f32[136,256]{1,0:T(8,128)S(1)} %add_add_fusion.2), channel_id=1, source_target_pairs={{0,24},{2,26},{4,28},{6,30},{8,16},{10,18},{12,20},{14,22},{16,8},... | collective-permute-start | bytes 417800 | tf_op jit(solution)/shard_map/ppermute | solution.py:519
  60.8 30.8 %collective-permute-start.6 = (f32[136,256]{1,0:T(8,128)S(1)}, f32[136,256]{1,0:T(8,128)S(1)}, u32[]{:S(2)}, u32[]{:S(2)}) collective-permute-start(f32[136,256]{1,0:T(8,128)S(1)} %add_add_fusion.2), channel_id=1, source_target_pairs={{0,16},{2,18},{4,20},{6,22},{8,24},{10,26},{12,28},{14,30},{16,0},... | collective-permute-start | bytes 417800 | tf_op jit(solution)/shard_map/ppermute | solution.py:519
  60.8 30.8 %collective-permute-start.5 = (f32[136,256]{1,0:T(8,128)S(1)}, f32[136,256]{1,0:T(8,128)S(1)}, u32[]{:S(2)}, u32[]{:S(2)}) collective-permute-start(f32[136,256]{1,0:T(8,128)S(1)} %add_add_fusion.2), channel_id=1, source_target_pairs={{0,8},{2,10},{4,12},{6,14},{8,0},{10,2},{12,4},{14,6},{16,24},{18,... | collective-permute-start | bytes 417800 | tf_op jit(solution)/shard_map/ppermute | solution.py:519
  63.1 30.7 %collective-permute-start.8 = (f32[512,256]{1,0:T(8,128)S(1)}, f32[512,256]{1,0:T(8,128)S(1)}, u32[]{:S(2)}, u32[]{:S(2)}) collective-permute-start(f32[512,256]{1,0:T(8,128)S(1)} %get-tuple-element.54), channel_id=1, source_target_pairs={{0,2},{2,0},{4,6},{6,4},{8,10},{10,8},{12,14},{14,12},{16,18},{18,... | collective-permute-start | bytes 1572872 | tf_op jit(solution)/shard_map/ppermute | solution.py:519
  65.0 28.9 %collective-permute-start.10 = (f32[512,256]{1,0:T(8,128)S(1)}, f32[512,256]{1,0:T(8,128)S(1)}, u32[]{:S(2)}, u32[]{:S(2)}) collective-permute-start(f32[512,256]{1,0:T(8,128)S(1)} %get-tuple-element.55), channel_id=1, source_target_pairs={{0,6},{2,4},{4,2},{6,0},{8,14},{10,12},{12,10},{14,8},{16,22},{18,... | collective-permute-start | bytes 1572872 | tf_op jit(solution)/shard_map/ppermute | solution.py:519
  68.6 28.8 %collective-permute-start.9 = (f32[512,256]{1,0:T(8,128)S(1)}, f32[512,256]{1,0:T(8,128)S(1)}, u32[]{:S(2)}, u32[]{:S(2)}) collective-permute-start(f32[512,256]{1,0:T(8,128)S(1)} %get-tuple-element.56), channel_id=1, source_target_pairs={{0,4},{2,6},{4,0},{6,2},{8,12},{10,14},{12,8},{14,10},{16,20},{18,... | collective-permute-start | bytes 1572872 | tf_op jit(solution)/shard_map/ppermute | solution.py:519
  91.7 1.4 collective-permute-start.11
  98.6 42.1 %copy-start = (bf16[16,176,512]{2,1,0:T(8,128)(2,1)}, bf16[16,176,512]{2,1,0:T(8,128)(2,1)S(1)}, u32[]{:S(2)}) copy-start(bf16[16,176,512]{2,1,0:T(8,128)(2,1)S(1)} %all-to-all-done.refs_0_) | copy-start | bytes 8650756
  98.6 42.8 %all-to-all-start.1 = ((bf16[16,80,512]{2,1,0:T(8,128)(2,1)}), bf16[16,80,512]{2,1,0:T(8,128)(2,1)}, u32[]{:S(2)}, u32[]{:S(2)}) async-start(bf16[16,80,512]{2,1,0:T(8,128)(2,1)} %get-tuple-element.36), calls=%async_computation.1 | async-start | bytes 2621440 | tf_op jit(solution)/shard_map/all_to_all | solution.py:605
  140.6 4.5 %copy-start.8 = (pred[400]{0:T(512)(128)(4,1)S(1)}, pred[400]{0:T(512)(128)(4,1)}, u32[]{:S(2)}) copy-start(pred[400]{0:T(512)(128)(4,1)} %broadcast_compare_fusion) | copy-start | bytes 1204
  145.0 6.4 %collective-permute-start.12 = (bf16[1664,512]{1,0:T(8,128)(2,1)}, bf16[1664,512]{1,0:T(8,128)(2,1)S(1)}, u32[]{:S(2)}, u32[]{:S(2)}) collective-permute-start(bf16[1664,512]{1,0:T(8,128)(2,1)} %bitcast.16), channel_id=1, source_target_pairs={{0,1},{1,0},{2,3},{3,2},{4,5},{5,4},{6,7},{7,6},{8,9},{9,8},{10,11... | collective-permute-start | bytes 5111816 | tf_op jit(solution)/shard_map/ppermute | solution.py:217
  145.9 21.3 %collective-permute-start.15 = (f32[128,256]{1,0:T(8,128)S(1)}, f32[128,256]{1,0:T(8,128)S(1)}, u32[]{:S(2)}, u32[]{:S(2)}) collective-permute-start(f32[128,256]{1,0:T(8,128)S(1)} %get-tuple-element.57), channel_id=1, source_target_pairs={{0,24},{2,26},{4,28},{6,30},{8,16},{10,18},{12,20},{14,22},{16,8},... | collective-permute-start | bytes 393224 | tf_op jit(solution)/shard_map/ppermute | solution.py:519
  149.7 17.6 %collective-permute-start.14 = (f32[128,256]{1,0:T(8,128)S(1)}, f32[128,256]{1,0:T(8,128)S(1)}, u32[]{:S(2)}, u32[]{:S(2)}) collective-permute-start(f32[128,256]{1,0:T(8,128)S(1)} %get-tuple-element.58), channel_id=1, source_target_pairs={{0,16},{2,18},{4,20},{6,22},{8,24},{10,26},{12,28},{14,30},{16,0},... | collective-permute-start | bytes 393224 | tf_op jit(solution)/shard_map/ppermute | solution.py:519
  151.4 15.9 %collective-permute-start.13 = (f32[128,256]{1,0:T(8,128)S(1)}, f32[128,256]{1,0:T(8,128)S(1)}, u32[]{:S(2)}, u32[]{:S(2)}) collective-permute-start(f32[128,256]{1,0:T(8,128)S(1)} %get-tuple-element.59), channel_id=1, source_target_pairs={{0,8},{2,10},{4,12},{6,14},{8,0},{10,2},{12,4},{14,6},{16,24},{18,... | collective-permute-start | bytes 393224 | tf_op jit(solution)/shard_map/ppermute | solution.py:519
  151.4 1.2 copy-start.9
  152.6 14.7 %copy-start.1 = (f32[256,256]{1,0:T(8,128)S(1)}, f32[256,256]{1,0:T(8,128)}, u32[]{:S(2)}) copy-start(f32[256,256]{1,0:T(8,128)} %factor.1.inv_ref) | copy-start | bytes 786436
  167.7 6.6 %collective-permute-start.18 = (bf16[128,256]{1,0:T(8,128)(2,1)S(1)}, bf16[128,256]{1,0:T(8,128)(2,1)S(1)}, u32[]{:S(2)}, u32[]{:S(2)}) collective-permute-start(bf16[128,256]{1,0:T(8,128)(2,1)S(1)} %convolution_convert_fusion), channel_id=1, source_target_pairs={{0,24},{2,26},{4,28},{6,30},{8,16},{10,18},{12,20},{14,22},{16,8},... | collective-permute-start | bytes 196616 | tf_op jit(solution)/shard_map/ppermute | solution.py:519
  170.4 6.6 %collective-permute-start.17 = (bf16[128,256]{1,0:T(8,128)(2,1)S(1)}, bf16[128,256]{1,0:T(8,128)(2,1)S(1)}, u32[]{:S(2)}, u32[]{:S(2)}) collective-permute-start(bf16[128,256]{1,0:T(8,128)(2,1)S(1)} %convolution_convert_fusion), channel_id=1, source_target_pairs={{0,16},{2,18},{4,20},{6,22},{8,24},{10,26},{12,28},{14,30},{16,0},... | collective-permute-start | bytes 196616 | tf_op jit(solution)/shard_map/ppermute | solution.py:519
  171.2 5.8 %collective-permute-start.16 = (bf16[128,256]{1,0:T(8,128)(2,1)S(1)}, bf16[128,256]{1,0:T(8,128)(2,1)S(1)}, u32[]{:S(2)}, u32[]{:S(2)}) collective-permute-start(bf16[128,256]{1,0:T(8,128)(2,1)S(1)} %convolution_convert_fusion), channel_id=1, source_target_pairs={{0,8},{2,10},{4,12},{6,14},{8,0},{10,2},{12,4},{14,6},{16,24},{18,... | collective-permute-start | bytes 196616 | tf_op jit(solution)/shard_map/ppermute | solution.py:519
  177.1 10.3 %collective-permute-start.21 = (bf16[512,256]{1,0:T(8,128)(2,1)S(1)}, bf16[512,256]{1,0:T(8,128)(2,1)S(1)}, u32[]{:S(2)}, u32[]{:S(2)}) collective-permute-start(bf16[512,256]{1,0:T(8,128)(2,1)S(1)} %pad_maximum_fusion.1), channel_id=1, source_target_pairs={{0,6},{2,4},{4,2},{6,0},{8,14},{10,12},{12,10},{14,8},{16,22},{18,... | collective-permute-start | bytes 786440 | tf_op jit(solution)/shard_map/ppermute | solution.py:519
  178.9 12.4 %collective-permute-start.20 = (bf16[512,256]{1,0:T(8,128)(2,1)S(1)}, bf16[512,256]{1,0:T(8,128)(2,1)S(1)}, u32[]{:S(2)}, u32[]{:S(2)}) collective-permute-start(bf16[512,256]{1,0:T(8,128)(2,1)S(1)} %pad_maximum_fusion.1), channel_id=1, source_target_pairs={{0,4},{2,6},{4,0},{6,2},{8,12},{10,14},{12,8},{14,10},{16,20},{18,... | collective-permute-start | bytes 786440 | tf_op jit(solution)/shard_map/ppermute | solution.py:519
  179.5 12.0 %collective-permute-start.19 = (bf16[512,256]{1,0:T(8,128)(2,1)S(1)}, bf16[512,256]{1,0:T(8,128)(2,1)S(1)}, u32[]{:S(2)}, u32[]{:S(2)}) collective-permute-start(bf16[512,256]{1,0:T(8,128)(2,1)S(1)} %pad_maximum_fusion.1), channel_id=1, source_target_pairs={{0,2},{2,0},{4,6},{6,4},{8,10},{10,8},{12,14},{14,12},{16,18},{18,... | collective-permute-start | bytes 786440 | tf_op jit(solution)/shard_map/ppermute | solution.py:519

commit v12 on v10

--- a/solution.py
+++ b/solution.py
@@ -454,11 +454,17 @@
     )(weights, *parts, sp, s)
 
 
-def remainder_kernel(norm, quarter_ref, kern_ref, p_ref, inv_ref, rt_ref, out_ref, proj_ref):
+def remainder_kernel(norm, quarter_ref, kern_ref, p_ref, inv_ref, *refs):
+    pieces, (out_ref, proj_ref, rt_ref) = refs[:4], refs[4:]
     chunk = kern_ref.shape[1]
     step = pl.program_id(0)
     inv_high, inv_low = split(inv_ref[...])
-    rt = rt_ref[0]
+    for k in range(4):
+        @pl.when((step ^ quarter_ref[0]) == k)
+        def _():
+            rt_ref[...] = pieces[k][...]
+
+    rt = rt_ref[...]
     coef = (nn(rt, inv_high) + nn(rt, inv_low)).astype(jnp.bfloat16)
     proj_ref[...] = rt.astype(jnp.float32).T * (1.0 / norm)
     fit = nt(p_ref[...], coef)
@@ -474,9 +480,9 @@
             out_ref[:, :part] = (basis * norm).astype(out_ref.dtype)
 
 
-def remainder_rows(kern, panel, quarter, inverse, rt, norm):
+def remainder_rows(kern, panel, quarter, inverse, pieces, norm):
     rows, cols = kern.shape
-    chunk = rt.shape[1]
+    chunk = pieces[0].shape[0]
     once = pl.Buffered(1)
     spec = pltpu.PrefetchScalarGridSpec(
         num_scalar_prefetch=1,
@@ -485,12 +491,13 @@
             pl.BlockSpec((rows, chunk), lambda i, q: (0, i)),
             pl.BlockSpec((rows, PANEL), lambda i, q: (0, 0), pipeline_mode=once),
             pl.BlockSpec((PANEL, PANEL), lambda i, q: (0, 0), pipeline_mode=once),
-            pl.BlockSpec((1, chunk, PANEL), lambda i, q: (i ^ q[0], 0, 0)),
-        ],
+        ]
+        + [pl.BlockSpec((chunk, PANEL), lambda i, q: (0, 0), pipeline_mode=once)] * 4,
         out_specs=(
             pl.BlockSpec((rows, chunk), lambda i, q: (0, i)),
             pl.BlockSpec((PANEL, chunk), lambda i, q: (0, i)),
         ),
+        scratch_shapes=[pltpu.VMEM((chunk, PANEL), jnp.bfloat16)],
     )
     return pl.pallas_call(
         functools.partial(remainder_kernel, norm),
@@ -502,7 +509,7 @@
         compiler_params=params(dimension_semantics=("arbitrary",)),
         cost_estimate=cost(2 * rows * PANEL * cols, 4 * rows * cols),
         name="remainder_rows",
-    )(quarter, kern, panel, inverse, rt)
+    )(quarter, kern, panel, inverse, *pieces)
 
 
 def flips(bit, size):
@@ -618,9 +625,8 @@
     kern, panel = kernel_rows(share_parts(arrived), weights_here, panel_points, sparse_points)
     pieces = gather_pieces(rt, pairs[0])
     kern, *pieces = lax.optimization_barrier((kern, *pieces))
-    rt = jnp.stack(pieces)
     remainder, projected = remainder_rows(
-        kern, panel, quarter_of(pairs[0])[None], inverse, rt, norm
+        kern, panel, quarter_of(pairs[0])[None], inverse, pieces, norm
     )
     return (projected, remainder)
 

time: 193 us -> 193 us (level)
  no operation moved by 1% of the time
where the time goes in v12:
time: 193 us
  Pallas kernels  90.8 us (47%)
  starting transfers between devices  50 us (26%)
  waiting for transfers between devices  34.8 us (18%)
  local copies, waits for them, and re-layouts  8.92 us (5%)
  other arithmetic  5.4 us (3%)
    ppermute x18, starting transfers between devices, trade(): return lax.ppermute(x, 'rows', flips(bit, lax.axis_size('rows')))  35.1 us
    ppermute x18, waiting for transfers between devices, trade(): return lax.ppermute(x, 'rows', flips(bit, lax.axis_size('rows')))  34 us
    pallas_call x1, Pallas kernels, column_products(): pl.pallas_call(functools.partial(column_kernel, len(parts)), grid=(size /...  24.7 us
    pallas_call x1, Pallas kernels, factor(): pl.pallas_call(functools.partial(factor_kernel, 64), out_shape=jax.ShapeD...  24 us
    pallas_call x1, Pallas kernels, kernel_rows(): pl.pallas_call(functools.partial(rows_kernel, len(parts)), grid=(cols //...  14.6 us
    pallas_call x1, Pallas kernels, panel_products(): pl.pallas_call(functools.partial(panel_kernel, len(parts)), out_shape=(ja...  9.95 us
    pallas_call x1, Pallas kernels, remainder_rows(): pl.pallas_call(functools.partial(remainder_kernel, norm), grid_spec=spec,...  9.72 us
    all_to_all x1, starting transfers between devices, on_device(): lax.all_to_all(outgoing[0], 'rows', split_axis=0, concat_axis=0, tiled=True)  7.89 us
  transfers between devices with their start and end apart: 24, of which 6 were waited for; matrix products, arithmetic and copies ran while one was open for 7% of the time, Pallas kernels for 40%

profile of v12, /device:TPU:0, one launch (start us, length us, event | category | flops | bytes accessed | tf_op | source)
XLA Modules:
  0.0 192.5 jit_solution(17787009728803168255)
XLA Ops:
  0.6 0.5 collective-permute-start
  1.1 4.2 %pack.1 = (bf16[16,176,512]{2,1,0:T(8,128)(2,1)}, bf16[16,80,512]{2,1,0:T(8,128)(2,1)}) custom-call(s32[16,25]{1,0:T(8,128)} %dest_ref.1, s32[16]{0:T(128)} %cnt_ref.3, bf16[25,128,512]{2,1,0:T(8,128)(2,1)} %bitcast.11), custom_call_target="tpu_custom_call" | custom-call | bytes 6553600 | tf_op jit(solution)/shard_map/pack/pallas_call | solution.py:111
  5.4 7.9 %all-to-all-start = ((bf16[16,176,512]{2,1,0:T(8,128)(2,1)}), bf16[16,176,512]{2,1,0:T(8,128)(2,1)S(1)}, u32[]{:S(2)}, u32[]{:S(2)}) async-start(bf16[16,176,512]{2,1,0:T(8,128)(2,1)} %get-tuple-element.31), calls=%async_computation | async-start | bytes 5767168 | tf_op jit(solution)/shard_map/all_to_all | solution.py:575
  13.3 1.9 slice.25
  15.1 0.2 collective-permute-start.1
  15.7 0.5 convert_element_type.10.w_ref
  16.3 0.7 broadcast_in_dim.42
  17.0 0.3 reduce-window.9
  17.8 0.8 copy-done.2
  18.6 9.9 %panel_products.1 = (f32[256,256]{1,0:T(8,128)}, bf16[3200,256]{1,0:T(8,128)(2,1)}, bf16[256,1024]{1,0:T(8,128)(2,1)}) custom-call(s32[16]{0:T(128)} %cnt_ref.3, f32[25]{0:T(128)} %convert_element_type.10.w_ref, bf16[3200,512]{1,0:T(8,128)(2,1)} %refs_0_.3, bf16[3200,512]{1,0:T(8,128)(2,1)} %collective-permute-done.refs_1_, bf16[2048,1024]{1,0:T(8,128)(2,1)} %refs_3_.3, ...), custom_call_target="tpu_custom_call" | custom-call | flops 2097152000 | bytes 6553600 | tf_op jit(solution)/shard_map/panel_products/pallas_call | solution.py:320
  28.5 0.9 constant_dynamic-slice_fusion.6
  29.5 2.7 %collective-permute-start.4 = (f32[136,256]{1,0:T(8,128)S(1)}, f32[136,256]{1,0:T(8,128)S(1)}, u32[]{:S(2)}, u32[]{:S(2)}) collective-permute-start(f32[136,256]{1,0:T(8,128)S(1)} %pad_maximum_fusion.1), channel_id=1, source_target_pairs={{0,6},{2,4},{4,2},{6,0},{8,14},{10,12},{12,10},{14,8},{16,22},{18,... | collective-permute-start | bytes 417800 | tf_op jit(solution)/shard_map/ppermute | solution.py:526
  32.2 0.8 collective-permute-start.2
  33.0 24.7 %column_products.1 = f32[2048,256]{1,0:T(8,128)} custom-call(bf16[3200,512]{1,0:T(8,128)(2,1)} %refs_0_.3, bf16[3200,512]{1,0:T(8,128)(2,1)} %collective-permute-done.refs_1_, bf16[3200,256]{1,0:T(8,128)(2,1)} %get-tuple-element.24.refs_2_, bf16[2048,1024]{1,0:T(8,128)(2,1)} %refs_3_.3), custom_call_target="tpu_custom_call" | custom-call | flops 16777216000 | bytes 6553600 | tf_op jit(solution)/shard_map/column_products/pallas_call | solution.py:369
  57.8 3.6 %collective-permute-start.7 = (f32[136,256]{1,0:T(8,128)S(1)}, f32[136,256]{1,0:T(8,128)S(1)}, u32[]{:S(2)}, u32[]{:S(2)}) collective-permute-start(f32[136,256]{1,0:T(8,128)S(1)} %add_add_fusion.2), channel_id=1, source_target_pairs={{0,24},{2,26},{4,28},{6,30},{8,16},{10,18},{12,20},{14,22},{16,8},... | collective-permute-start | bytes 417800 | tf_op jit(solution)/shard_map/ppermute | solution.py:526
  61.4 0.8 collective-permute-start.5
  62.3 1.5 constant_dynamic-slice_fusion.5
  63.7 1.3 collective-permute-start.8
  65.1 1.5 collective-permute-start.10
  66.5 2.4 %collective-permute-done.7 = f32[136,256]{1,0:T(8,128)S(1)} collective-permute-done((f32[136,256]{1,0:T(8,128)S(1)}, f32[136,256]{1,0:T(8,128)S(1)}, u32[]{:S(2)}, u32[]{:S(2)}) %collective-permute-start.7) | collective-permute-done | bytes 139296 | tf_op jit(solution)/shard_map/ppermute | solution.py:526
  68.9 3.9 %collective-permute-start.9 = (f32[512,256]{1,0:T(8,128)S(1)}, f32[512,256]{1,0:T(8,128)S(1)}, u32[]{:S(2)}, u32[]{:S(2)}) collective-permute-start(f32[512,256]{1,0:T(8,128)S(1)} %get-tuple-element.46), channel_id=1, source_target_pairs={{0,4},{2,6},{4,0},{6,2},{8,12},{10,14},{12,8},{14,10},{16,20},{18,... | collective-permute-start | bytes 1572872 | tf_op jit(solution)/shard_map/ppermute | solution.py:526
  72.8 19.3 %collective-permute-done.6 = f32[136,256]{1,0:T(8,128)S(1)} collective-permute-done((f32[136,256]{1,0:T(8,128)S(1)}, f32[136,256]{1,0:T(8,128)S(1)}, u32[]{:S(2)}, u32[]{:S(2)}) %collective-permute-start.6) | collective-permute-done | bytes 139296 | tf_op jit(solution)/shard_map/ppermute | solution.py:526
  92.3 0.5 broadcast_compare_fusion
  92.8 0.8 collective-permute-done.11
  93.6 0.7 maximum_select_fusion.gram_ref
  94.4 3.5 %collective-permute-done.9 = f32[512,256]{1,0:T(8,128)S(1)} collective-permute-done((f32[512,256]{1,0:T(8,128)S(1)}, f32[512,256]{1,0:T(8,128)S(1)}, u32[]{:S(2)}, u32[]{:S(2)}) %collective-permute-start.9) | collective-permute-done | bytes 524320 | tf_op jit(solution)/shard_map/ppermute | solution.py:526
  97.9 1.2 add_add_fusion
  99.1 0.8 constant_dynamic-slice_fusion.2
  99.8 11.0 %collective-permute-start.12 = (f32[128,256]{1,0:T(8,128)}, f32[128,256]{1,0:T(8,128)}, u32[]{:S(2)}, u32[]{:S(2)}) collective-permute-start(f32[128,256]{1,0:T(8,128)} %get-tuple-element.47), channel_id=1, source_target_pairs={{0,8},{2,10},{4,12},{6,14},{8,0},{10,2},{12,4},{14,6},{16,24},{18,... | collective-permute-start | bytes 393224 | tf_op jit(solution)/shard_map/ppermute | solution.py:526
  110.9 1.1 collective-permute-start.14
  111.9 0.4 collective-permute-start.13
  112.3 6.2 %all-to-all-start.1 = ((bf16[16,80,512]{2,1,0:T(8,128)(2,1)}), bf16[16,80,512]{2,1,0:T(8,128)(2,1)}, u32[]{:S(2)}, u32[]{:S(2)}) async-start(bf16[16,80,512]{2,1,0:T(8,128)(2,1)} %get-tuple-element.32), calls=%async_computation.1 | async-start | bytes 2621440 | tf_op jit(solution)/shard_map/all_to_all | solution.py:607
  118.6 24.0 %factor.1.inv_ref = f32[256,256]{1,0:T(8,128)} custom-call(f32[256,256]{1,0:T(8,128)} %maximum_select_fusion.gram_ref), custom_call_target="tpu_custom_call" | custom-call | flops 20000000000 | bytes 524288 | tf_op jit(solution)/shard_map/factor/pallas_call | solution.py:204
  142.6 1.6 convolution_convert_fusion
  144.1 3.7 %collective-permute-start.17 = (bf16[128,256]{1,0:T(8,128)(2,1)S(1)}, bf16[128,256]{1,0:T(8,128)(2,1)S(1)}, u32[]{:S(2)}, u32[]{:S(2)}) collective-permute-start(bf16[128,256]{1,0:T(8,128)(2,1)S(1)} %convolution_convert_fusion), channel_id=1, source_target_pairs={{0,24},{2,26},{4,28},{6,30},{8,16},{10,18},{12,20},{14,22},{16,8},... | collective-permute-start | bytes 196616 | tf_op jit(solution)/shard_map/ppermute | solution.py:526
  147.9 0.7 collective-permute-start.15
  148.6 0.7 select_reduce_fusion.pos_ref
  149.3 1.0 collective-permute-done.17
  150.3 7.7 %collective-permute-done.16 = bf16[128,256]{1,0:T(8,128)(2,1)S(1)} collective-permute-done((bf16[128,256]{1,0:T(8,128)(2,1)S(1)}, bf16[128,256]{1,0:T(8,128)(2,1)S(1)}, u32[]{:S(2)}, u32[]{:S(2)}) %collective-permute-start.16) | collective-permute-done | bytes 65568 | tf_op jit(solution)/shard_map/ppermute | solution.py:526
  158.2 3.6 %select.24 = bf16[13,128,512]{2,1,0:T(8,128)(2,1)} custom-call(s32[13]{0:T(128)} %select_reduce_fusion.pos_ref, bf16[16,176,512]{2,1,0:T(8,128)(2,1)} %copy-done, bf16[16,80,512]{2,1,0:T(8,128)(2,1)} %all-to-all-done.1.refs_1_), custom_call_target="tpu_custom_call" | custom-call | bytes 3407872 | tf_op jit(solution)/shard_map/select/pallas_call | solution.py:148
  161.9 0.7 select_reduce_fusion.1.w_ref
  162.5 1.8 collective-permute-start.21
  164.3 1.4 collective-permute-start.20
  165.8 0.3 collective-permute-start.19
  166.0 1.2 copy-done.11
  167.2 14.6 %kernel_rows.1 = (bf16[1664,2048]{1,0:T(8,128)(2,1)}, bf16[1664,256]{1,0:T(8,128)(2,1)}) custom-call(f32[13]{0:T(128)} %select_reduce_fusion.1.w_ref, bf16[1664,512]{1,0:T(8,128)(2,1)} %bitcast.13, bf16[1664,512]{1,0:T(8,128)(2,1)} %copy-done.11, bf16[256,1024]{1,0:T(8,128)(2,1)} %get-tuple-element.33.refs_2_, bf16[2048,1024]{1,0:T(8,128)(2,1)} %refs_3_.3), custom_call_target="tpu_custom_call" | custom-call | flops 7851737088 | bytes 14417920 | tf_op jit(solution)/shard_map/kernel_rows/pallas_call | solution.py:427
  181.9 0.7 copy-done.3
  182.8 9.7 %remainder_rows.1 = (bf16[1664,2048]{1,0:T(8,128)(2,1)}, f32[256,2048]{1,0:T(8,128)}) custom-call(s32[1]{0:T(128)} %bitcast.quarter_ref, bf16[1664,2048]{1,0:T(8,128)(2,1)} %get-tuple-element.36.kern_ref, bf16[1664,256]{1,0:T(8,128)(2,1)} %get-tuple-element.37.p_ref, f32[256,256]{1,0:T(8,128)} %factor.1.inv_ref, bf16[512,256]{1,0:T(8,128)(2,1)} %copy-done.1, ...), custom_call_target="tpu_custom_call" | custom-call | flops 1744830464 | bytes 13631488 | tf_op jit(solution)/shard_map/remainder_rows/pallas_call | solution.py:502
  (69 shorter events, 1.6 us)
Async XLA Ops:
  0.6 17.1 %collective-permute-start = (bf16[3200,512]{1,0:T(8,128)(2,1)}, bf16[3200,512]{1,0:T(8,128)(2,1)}, u32[]{:S(2)}, u32[]{:S(2)}) collective-permute-start(bf16[3200,512]{1,0:T(8,128)(2,1)} %refs_0_.3), channel_id=1, source_target_pairs={{0,1},{1,0},{2,3},{3,2},{4,5},{5,4},{6,7},{7,6},{8,9},{9,8},{10,11... | collective-permute-start | bytes 9830408 | tf_op jit(solution)/shard_map/ppermute | solution.py:217
  5.3 10.0 %copy-start.6 = (s32[16,25]{1,0:T(8,128)S(1)}, s32[16,25]{1,0:T(8,128)}, u32[]{:S(2)}) copy-start(s32[16,25]{1,0:T(8,128)} %dest_ref.1) | copy-start | bytes 4804
  5.3 10.0 %copy-start.8 = (s32[16]{0:T(128)S(1)}, s32[16]{0:T(128)}, u32[]{:S(2)}) copy-start(s32[16]{0:T(128)} %cnt_ref.3) | copy-start | bytes 196
  5.4 10.3 %copy-start.12 = (bf16[25]{0:T(256)(128)(2,1)S(1)}, bf16[25]{0:T(256)(128)(2,1)}, u32[]{:S(2)}) copy-start(bf16[25]{0:T(256)(128)(2,1)} %param.7) | copy-start | bytes 154
  5.4 107.0 %all-to-all-start = ((bf16[16,176,512]{2,1,0:T(8,128)(2,1)}), bf16[16,176,512]{2,1,0:T(8,128)(2,1)S(1)}, u32[]{:S(2)}, u32[]{:S(2)}) async-start(bf16[16,176,512]{2,1,0:T(8,128)(2,1)} %get-tuple-element.31), calls=%async_computation | async-start | bytes 5767168 | tf_op jit(solution)/shard_map/all_to_all | solution.py:575
  15.1 2.6 %collective-permute-start.1 = (bf16[256,1024]{1,0:T(8,128)(2,1)}, bf16[256,1024]{1,0:T(8,128)(2,1)S(1)}, u32[]{:S(2)}, u32[]{:S(2)}) collective-permute-start(bf16[256,1024]{1,0:T(8,128)(2,1)} %slice.25), channel_id=1, source_target_pairs={{0,1},{1,0},{2,3},{3,2},{4,5},{5,4},{6,7},{7,6},{8,9},{9,8},{10,11... | collective-permute-start | bytes 1572872 | tf_op jit(solution)/shard_map/ppermute | solution.py:570
  17.8 0.8 copy-start.2
  29.5 28.3 %collective-permute-start.3 = (f32[136,256]{1,0:T(8,128)S(1)}, f32[136,256]{1,0:T(8,128)S(1)}, u32[]{:S(2)}, u32[]{:S(2)}) collective-permute-start(f32[136,256]{1,0:T(8,128)S(1)} %pad_maximum_fusion.1), channel_id=1, source_target_pairs={{0,4},{2,6},{4,0},{6,2},{8,12},{10,14},{12,8},{14,10},{16,20},{18,... | collective-permute-start | bytes 417800 | tf_op jit(solution)/shard_map/ppermute | solution.py:526
  29.5 28.2 %collective-permute-start.4 = (f32[136,256]{1,0:T(8,128)S(1)}, f32[136,256]{1,0:T(8,128)S(1)}, u32[]{:S(2)}, u32[]{:S(2)}) collective-permute-start(f32[136,256]{1,0:T(8,128)S(1)} %pad_maximum_fusion.1), channel_id=1, source_target_pairs={{0,6},{2,4},{4,2},{6,0},{8,14},{10,12},{12,10},{14,8},{16,22},{18,... | collective-permute-start | bytes 417800 | tf_op jit(solution)/shard_map/ppermute | solution.py:526
  32.2 25.5 %collective-permute-start.2 = (f32[136,256]{1,0:T(8,128)S(1)}, f32[136,256]{1,0:T(8,128)S(1)}, u32[]{:S(2)}, u32[]{:S(2)}) collective-permute-start(f32[136,256]{1,0:T(8,128)S(1)} %pad_maximum_fusion.1), channel_id=1, source_target_pairs={{0,2},{2,0},{4,6},{6,4},{8,10},{10,8},{12,14},{14,12},{16,18},{18,... | collective-permute-start | bytes 417800 | tf_op jit(solution)/shard_map/ppermute | solution.py:526
  57.8 11.1 %collective-permute-start.7 = (f32[136,256]{1,0:T(8,128)S(1)}, f32[136,256]{1,0:T(8,128)S(1)}, u32[]{:S(2)}, u32[]{:S(2)}) collective-permute-start(f32[136,256]{1,0:T(8,128)S(1)} %add_add_fusion.2), channel_id=1, source_target_pairs={{0,24},{2,26},{4,28},{6,30},{8,16},{10,18},{12,20},{14,22},{16,8},... | collective-permute-start | bytes 417800 | tf_op jit(solution)/shard_map/ppermute | solution.py:526
  61.4 30.7 %collective-permute-start.6 = (f32[136,256]{1,0:T(8,128)S(1)}, f32[136,256]{1,0:T(8,128)S(1)}, u32[]{:S(2)}, u32[]{:S(2)}) collective-permute-start(f32[136,256]{1,0:T(8,128)S(1)} %add_add_fusion.2), channel_id=1, source_target_pairs={{0,16},{2,18},{4,20},{6,22},{8,24},{10,26},{12,28},{14,30},{16,0},... | collective-permute-start | bytes 417800 | tf_op jit(solution)/shard_map/ppermute | solution.py:526
  61.4 30.7 %collective-permute-start.5 = (f32[136,256]{1,0:T(8,128)S(1)}, f32[136,256]{1,0:T(8,128)S(1)}, u32[]{:S(2)}, u32[]{:S(2)}) collective-permute-start(f32[136,256]{1,0:T(8,128)S(1)} %add_add_fusion.2), channel_id=1, source_target_pairs={{0,8},{2,10},{4,12},{6,14},{8,0},{10,2},{12,4},{14,6},{16,24},{18,... | collective-permute-start | bytes 417800 | tf_op jit(solution)/shard_map/ppermute | solution.py:526
  63.7 30.6 %collective-permute-start.8 = (f32[512,256]{1,0:T(8,128)S(1)}, f32[512,256]{1,0:T(8,128)S(1)}, u32[]{:S(2)}, u32[]{:S(2)}) collective-permute-start(f32[512,256]{1,0:T(8,128)S(1)} %get-tuple-element.44), channel_id=1, source_target_pairs={{0,2},{2,0},{4,6},{6,4},{8,10},{10,8},{12,14},{14,12},{16,18},{18,... | collective-permute-start | bytes 1572872 | tf_op jit(solution)/shard_map/ppermute | solution.py:526
  65.1 29.3 %collective-permute-start.10 = (f32[512,256]{1,0:T(8,128)S(1)}, f32[512,256]{1,0:T(8,128)S(1)}, u32[]{:S(2)}, u32[]{:S(2)}) collective-permute-start(f32[512,256]{1,0:T(8,128)S(1)} %get-tuple-element.45), channel_id=1, source_target_pairs={{0,6},{2,4},{4,2},{6,0},{8,14},{10,12},{12,10},{14,8},{16,22},{18,... | collective-permute-start | bytes 1572872 | tf_op jit(solution)/shard_map/ppermute | solution.py:526
  68.9 28.9 %collective-permute-start.9 = (f32[512,256]{1,0:T(8,128)S(1)}, f32[512,256]{1,0:T(8,128)S(1)}, u32[]{:S(2)}, u32[]{:S(2)}) collective-permute-start(f32[512,256]{1,0:T(8,128)S(1)} %get-tuple-element.46), channel_id=1, source_target_pairs={{0,4},{2,6},{4,0},{6,2},{8,12},{10,14},{12,8},{14,10},{16,20},{18,... | collective-permute-start | bytes 1572872 | tf_op jit(solution)/shard_map/ppermute | solution.py:526
  92.2 1.4 collective-permute-start.11
  99.8 42.7 %collective-permute-start.12 = (f32[128,256]{1,0:T(8,128)}, f32[128,256]{1,0:T(8,128)}, u32[]{:S(2)}, u32[]{:S(2)}) collective-permute-start(f32[128,256]{1,0:T(8,128)} %get-tuple-element.47), channel_id=1, source_target_pairs={{0,8},{2,10},{4,12},{6,14},{8,0},{10,2},{12,4},{14,6},{16,24},{18,... | collective-permute-start | bytes 393224 | tf_op jit(solution)/shard_map/ppermute | solution.py:526
  110.9 31.7 %collective-permute-start.14 = (f32[128,256]{1,0:T(8,128)}, f32[128,256]{1,0:T(8,128)}, u32[]{:S(2)}, u32[]{:S(2)}) collective-permute-start(f32[128,256]{1,0:T(8,128)} %get-tuple-element.48), channel_id=1, source_target_pairs={{0,24},{2,26},{4,28},{6,30},{8,16},{10,18},{12,20},{14,22},{16,8},... | collective-permute-start | bytes 393224 | tf_op jit(solution)/shard_map/ppermute | solution.py:526
  111.9 30.6 %collective-permute-start.13 = (f32[128,256]{1,0:T(8,128)}, f32[128,256]{1,0:T(8,128)}, u32[]{:S(2)}, u32[]{:S(2)}) collective-permute-start(f32[128,256]{1,0:T(8,128)} %get-tuple-element.49), channel_id=1, source_target_pairs={{0,16},{2,18},{4,20},{6,22},{8,24},{10,26},{12,28},{14,30},{16,0},... | collective-permute-start | bytes 393224 | tf_op jit(solution)/shard_map/ppermute | solution.py:526
  112.3 30.2 %copy-start = (bf16[16,176,512]{2,1,0:T(8,128)(2,1)}, bf16[16,176,512]{2,1,0:T(8,128)(2,1)S(1)}, u32[]{:S(2)}) copy-start(bf16[16,176,512]{2,1,0:T(8,128)(2,1)S(1)} %all-to-all-done.refs_0_) | copy-start | bytes 8650756
  112.3 45.8 %all-to-all-start.1 = ((bf16[16,80,512]{2,1,0:T(8,128)(2,1)}), bf16[16,80,512]{2,1,0:T(8,128)(2,1)}, u32[]{:S(2)}, u32[]{:S(2)}) async-start(bf16[16,80,512]{2,1,0:T(8,128)(2,1)} %get-tuple-element.32), calls=%async_computation.1 | async-start | bytes 2621440 | tf_op jit(solution)/shard_map/all_to_all | solution.py:607
  118.5 30.1 %copy-start.7 = (s32[400]{0:T(512)S(1)}, s32[400]{0:T(512)}, u32[]{:S(2)}) copy-start(s32[400]{0:T(512)} %broadcast_in_dim.42) | copy-start | bytes 4804
  118.5 30.1 %copy-start.9 = (pred[400]{0:T(512)(128)(4,1)S(1)}, pred[400]{0:T(512)(128)(4,1)}, u32[]{:S(2)}) copy-start(pred[400]{0:T(512)(128)(4,1)} %broadcast_compare_fusion) | copy-start | bytes 1204
  144.1 6.2 %collective-permute-start.17 = (bf16[128,256]{1,0:T(8,128)(2,1)S(1)}, bf16[128,256]{1,0:T(8,128)(2,1)S(1)}, u32[]{:S(2)}, u32[]{:S(2)}) collective-permute-start(bf16[128,256]{1,0:T(8,128)(2,1)S(1)} %convolution_convert_fusion), channel_id=1, source_target_pairs={{0,24},{2,26},{4,28},{6,30},{8,16},{10,18},{12,20},{14,22},{16,8},... | collective-permute-start | bytes 196616 | tf_op jit(solution)/shard_map/ppermute | solution.py:526
  147.9 10.2 %collective-permute-start.16 = (bf16[128,256]{1,0:T(8,128)(2,1)S(1)}, bf16[128,256]{1,0:T(8,128)(2,1)S(1)}, u32[]{:S(2)}, u32[]{:S(2)}) collective-permute-start(bf16[128,256]{1,0:T(8,128)(2,1)S(1)} %convolution_convert_fusion), channel_id=1, source_target_pairs={{0,16},{2,18},{4,20},{6,22},{8,24},{10,26},{12,28},{14,30},{16,0},... | collective-permute-start | bytes 196616 | tf_op jit(solution)/shard_map/ppermute | solution.py:526
  147.9 10.2 %collective-permute-start.15 = (bf16[128,256]{1,0:T(8,128)(2,1)S(1)}, bf16[128,256]{1,0:T(8,128)(2,1)S(1)}, u32[]{:S(2)}, u32[]{:S(2)}) collective-permute-start(bf16[128,256]{1,0:T(8,128)(2,1)S(1)} %convolution_convert_fusion), channel_id=1, source_target_pairs={{0,8},{2,10},{4,12},{6,14},{8,0},{10,2},{12,4},{14,6},{16,24},{18,... | collective-permute-start | bytes 196616 | tf_op jit(solution)/shard_map/ppermute | solution.py:526
  158.1 7.6 %copy-start.1 = (bf16[512,256]{1,0:T(8,128)(2,1)}, bf16[512,256]{1,0:T(8,128)(2,1)S(1)}, u32[]{:S(2)}) copy-start(bf16[512,256]{1,0:T(8,128)(2,1)S(1)} %pad_maximum_fusion.refs_0_) | copy-start | bytes 786436
  158.1 3.7 %copy-start.10 = (pred[400]{0:T(512)(128)(4,1)S(1)}, pred[400]{0:T(512)(128)(4,1)}, u32[]{:S(2)}) copy-start(pred[400]{0:T(512)(128)(4,1)} %broadcast_compare_fusion) | copy-start | bytes 1204
  161.8 4.3 %collective-permute-start.18 = (bf16[1664,512]{1,0:T(8,128)(2,1)}, bf16[1664,512]{1,0:T(8,128)(2,1)S(1)}, u32[]{:S(2)}, u32[]{:S(2)}) collective-permute-start(bf16[1664,512]{1,0:T(8,128)(2,1)} %bitcast.12), channel_id=1, source_target_pairs={{0,1},{1,0},{2,3},{3,2},{4,5},{5,4},{6,7},{7,6},{8,9},{9,8},{10,11... | collective-permute-start | bytes 5111816 | tf_op jit(solution)/shard_map/ppermute | solution.py:217
  162.5 19.3 %collective-permute-start.21 = (bf16[512,256]{1,0:T(8,128)(2,1)S(1)}, bf16[512,256]{1,0:T(8,128)(2,1)S(1)}, u32[]{:S(2)}, u32[]{:S(2)}) collective-permute-start(bf16[512,256]{1,0:T(8,128)(2,1)S(1)} %pad_maximum_fusion.refs_0_), channel_id=1, source_target_pairs={{0,6},{2,4},{4,2},{6,0},{8,14},{10,12},{12,10},{14,8},{16,22},{18,... | collective-permute-start | bytes 786440 | tf_op jit(solution)/shard_map/ppermute | solution.py:526
  164.3 17.6 %collective-permute-start.20 = (bf16[512,256]{1,0:T(8,128)(2,1)S(1)}, bf16[512,256]{1,0:T(8,128)(2,1)S(1)}, u32[]{:S(2)}, u32[]{:S(2)}) collective-permute-start(bf16[512,256]{1,0:T(8,128)(2,1)S(1)} %pad_maximum_fusion.refs_0_), channel_id=1, source_target_pairs={{0,4},{2,6},{4,0},{6,2},{8,12},{10,14},{12,8},{14,10},{16,20},{18,... | collective-permute-start | bytes 786440 | tf_op jit(solution)/shard_map/ppermute | solution.py:526
  165.8 16.1 %collective-permute-start.19 = (bf16[512,256]{1,0:T(8,128)(2,1)S(1)}, bf16[512,256]{1,0:T(8,128)(2,1)S(1)}, u32[]{:S(2)}, u32[]{:S(2)}) collective-permute-start(bf16[512,256]{1,0:T(8,128)(2,1)S(1)} %pad_maximum_fusion.refs_0_), channel_id=1, source_target_pairs={{0,2},{2,0},{4,6},{6,4},{8,10},{10,8},{12,14},{14,12},{16,18},{18,... | collective-permute-start | bytes 786440 | tf_op jit(solution)/shard_map/ppermute | solution.py:526
  166.0 1.2 copy-start.11
  181.9 0.7 copy-start.3
  181.9 0.8 copy-start.4
  181.9 0.9 copy-start.5
